TPU v7x, 32 devices: a whole 2x2x4 slice. The times are simulated.
32 devices in a mesh: dp: 4 (over z), seq: 8 (over y, x, core).
Axes of the slice: x: 2, y: 2, z: 4, core: 2. Of those that a mesh axis runs over, the one named last changes fastest.
Arguments:
- tokens: bfloat16 [4, 3072, 512], P('dp', 'seq'), may hold values from -6 to 6
- doc_lengths: int32 [4, 8], P('dp'), may hold values from 3 to 3051, as said below
- cotangent: bfloat16 [4, 3072, 512], P('dp', 'seq'), may hold values from -6 to 6
- norm_gain: bfloat16 [3, 2, 512], replicated, may hold values from 0.099609375 to 1.8984375
- norm_shift: bfloat16 [3, 2, 512], replicated, may hold values from -1.75 to 1.75
- relative_bias: bfloat16 [3, 2, 512], replicated, may hold values from -3 to 3
- attention_in: bfloat16 [512, 3, 2048], replicated, may hold values from -0.25 to 0.25
- attention_out: bfloat16 [512, 3, 512], replicated, may hold values from -1 to 1
- expand_weight: bfloat16 [512, 3, 2048], replicated, may hold values from -0.25 to 0.25
- expand_bias: bfloat16 [3, 2048], replicated, may hold values from -1.75 to 1.75
- contract_weight: bfloat16 [2048, 3, 512], replicated, may hold values from -0.125 to 0.125
- contract_bias: bfloat16 [3, 512], replicated, may hold values from -1.75 to 1.75
- pool_weight: bfloat16 [1536, 512], replicated, may hold values from -0.15625 to 0.15625
- pool_bias: bfloat16 [512], replicated, may hold values from -1.75 to 1.75
- upsample_weight: bfloat16 [512, 1536], replicated, may hold values from -0.25 to 0.25
- upsample_bias: bfloat16 [1536], replicated, may hold values from -1.75 to 1.75
Outputs:
- output: bfloat16 [4, 3072, 512], P('dp', 'seq')
- tokens_grad: bfloat16 [4, 3072, 512], P('dp', 'seq')
- norm_gain_grad: float32 [3, 2, 512], replicated
- norm_shift_grad: float32 [3, 2, 512], replicated
- relative_bias_grad: float32 [3, 2, 512], replicated
- attention_in_grad: float32 [512, 3, 2048], P('seq')
- attention_out_grad: float32 [512, 3, 512], P('seq')
- expand_weight_grad: float32 [512, 3, 2048], P('seq')
- expand_bias_grad: float32 [3, 2048], replicated
- contract_weight_grad: float32 [2048, 3, 512], P('seq')
- contract_bias_grad: float32 [3, 512], replicated
- pool_weight_grad: float32 [1536, 512], P('seq')
- pool_bias_grad: float32 [512], replicated
- upsample_weight_grad: float32 [512, 1536], P('seq')
- upsample_bias_grad: float32 [1536], replicated
- rms: float32 [3], replicated
Inputs may be any that keep to these rules, and one draw needn't show every extreme that they name: `doc_lengths`: in each row the 8 lengths are multiples of 3 that sum to 3072. One of them, neither the first nor the last and at a place drawn from the seed, starts among the first 384 places and ends among the last 384; every other one is at most 3 * (16) long. In one row, drawn from the seed, every other one is 3 long.
All inputs are finite; a program needn't handle non-finite values.
Results may differ from a plain program's by a relative error of at most 0.023.
Values may be sent and summed in bfloat16 or wider, within the bound.
No kernel may reach another device: no remote copies, remote signals or barrier semaphores. Data moves between devices by JAX's collectives and lax.ppermute only.
A program may use at most 320 MiB of HBM per device.

v0:
```python
from functools import partial

import jax
import jax.numpy as jnp
from jax import lax
from jax.sharding import PartitionSpec as P

D = 512
HEADS = 8
HD = 64
WIN = 256
QBLK = 384


epsilon = 1e-05
masked_score = -1e30


def passed_along(block, axis, distance):
    devices = range(lax.axis_size(axis))
    route = [(i - distance, i) for i in devices if i - distance in devices]
    return lax.ppermute(block, axis, route)


def layer_norm(values, scaling, offset):
    centre = values - jnp.mean(values, axis=-1, keepdims=True)
    spread = jnp.mean(centre * centre, axis=-1, keepdims=True)
    return centre * lax.rsqrt(spread + epsilon) * scaling + offset


def sinusoid(distance):
    halfway = D // 2
    frequency = jnp.power(10000.0, -2.0 * jnp.arange(halfway, dtype=jnp.float32) / D)
    phases = distance[:, None] * frequency[None, :]
    return jnp.concatenate([jnp.sin(phases), jnp.cos(phases)], axis=1)


def skewed(table_scores, key_count):
    head_count, query_count, table_length = table_scores.shape
    flattened = table_scores.reshape(head_count, query_count * table_length)
    flattened = flattened[:, query_count - 1 : query_count - 1 + query_count * (table_length - 1)]
    return flattened.reshape(head_count, query_count, table_length - 1)[:, :, :key_count]


def split_into_heads(matrix):
    return matrix.reshape(matrix.shape[0], HEADS, matrix.shape[1] // HEADS)


def document_of(places, lengths):
    ending = jnp.cumsum(lengths)
    return jnp.sum((places[:, None] >= ending[None, :]).astype(jnp.int32), axis=1)


def window_visible(query_place, key_place, lengths):
    behind = query_place[:, None] - key_place[None, :]
    same_document = (
        document_of(query_place, lengths)[:, None] == document_of(key_place, lengths)[None, :]
    )
    return (key_place[None, :] >= 0) & (behind >= 0) & (behind <= WIN) & same_document


def pooled_visible(query_place, key_place, lengths):
    same_document = (
        document_of(3 * query_place, lengths)[:, None]
        == document_of(3 * key_place, lengths)[None, :]
    )
    return (key_place[None, :] <= query_place[:, None]) & same_document


def window_block_visible(token_start, first_row, lengths):
    query_place = token_start + first_row + jnp.arange(QBLK)
    key_place = token_start + first_row - WIN + jnp.arange(QBLK + WIN)
    return window_visible(query_place, key_place, lengths)


def pooled_block_visible(block_index, pooled_start, query_count, block_rows, lengths):
    query_place = pooled_start + jnp.arange(query_count)
    key_place = block_index * block_rows + jnp.arange(block_rows)
    return pooled_visible(query_place, key_place, lengths)


def dot_float(first_matrix, second_matrix):
    return jnp.dot(first_matrix, second_matrix, preferred_element_type=jnp.float32)


def outer_float(first_matrix, second_matrix):
    return jnp.einsum("rc,re->ce", first_matrix, second_matrix, preferred_element_type=jnp.float32)


def dot_back(first_matrix, second_matrix):
    return jnp.einsum("rc,ec->re", first_matrix, second_matrix, preferred_element_type=jnp.float32)


def add_rows(target, addend):
    return target + addend


def block_scores(query_content, query_token_position, key_block, table_block, visible):
    content = jnp.einsum(
        "qhd,khd->hqk",
        split_into_heads(query_content),
        split_into_heads(key_block),
        preferred_element_type=jnp.float32,
    )
    token_position = jnp.einsum(
        "eay,cay->aec",
        split_into_heads(query_token_position),
        split_into_heads(table_block),
        preferred_element_type=jnp.float32,
    )
    combined = (content + skewed(token_position, key_block.shape[0])) * HD ** (-0.5)
    return jnp.where(visible[None], combined, masked_score)


def attention_forward_pass(
    query_content, query_token_position, key_row_matrix, value_rows, lookup_table_rows, visible_of
):
    query_count = query_content.shape[0]
    scores = block_scores(
        query_content, query_token_position, key_row_matrix, lookup_table_rows, visible_of(0)
    )
    highest = jnp.max(scores, axis=2)
    summed = jnp.sum(jnp.exp(scores - highest[:, :, None]), axis=2)
    log_total = highest + jnp.log(summed)
    weights = jnp.exp(scores - log_total[:, :, None]).astype(jnp.bfloat16)
    mixed_rows = jnp.einsum(
        "hqk,khd->qhd", weights, split_into_heads(value_rows), preferred_element_type=jnp.float32
    )
    return (mixed_rows.reshape(query_count, D).astype(jnp.bfloat16), log_total)


def attend_backward(
    query_content,
    query_token_position,
    key_row_matrix,
    value_rows,
    lookup_table_rows,
    visible_of,
    block_rows,
    log_total,
    grad_mixed,
):
    query_count = query_content.shape[0]
    table_length = query_count + block_rows - 1
    score_scale = HD ** (-0.5)
    grad_heads = split_into_heads(grad_mixed)
    unskew = jax.vjp(
        lambda table_scores: skewed(table_scores, block_rows),
        jnp.zeros((HEADS, query_count, table_length), jnp.float32),
    )[1]
    key_block = key_row_matrix
    table_block = lookup_table_rows
    scores = block_scores(
        query_content, query_token_position, key_block, table_block, visible_of(0)
    )
    weights = jnp.exp(scores - log_total[:, :, None])
    grad_weights = jnp.einsum(
        "qhd,khd->hqk", grad_heads, split_into_heads(value_rows), preferred_element_type=jnp.float32
    )
    parts = (key_block, table_block, weights, grad_weights)
    row_delta = jnp.sum(parts[2] * parts[3], axis=2)
    grad_keys = jnp.zeros(key_row_matrix.shape, jnp.float32)
    grad_values = jnp.zeros(value_rows.shape, jnp.float32)
    grad_table = jnp.zeros(lookup_table_rows.shape, jnp.float32)
    key_block, table_block, weights, grad_weights = parts
    grad_scores = (weights * (grad_weights - row_delta[:, :, None])).astype(jnp.bfloat16)
    grad_table_scores = unskew(grad_scores.astype(jnp.float32))[0].astype(jnp.bfloat16)
    grad_content = (
        jnp.einsum(
            "hqk,khd->qhd",
            grad_scores,
            split_into_heads(key_block),
            preferred_element_type=jnp.float32,
        )
        * score_scale
    )
    grad_position = (
        jnp.einsum(
            "xru,uxw->rxw",
            grad_table_scores,
            split_into_heads(table_block),
            preferred_element_type=jnp.float32,
        )
        * score_scale
    )
    key_piece = (
        jnp.einsum(
            "hqk,qhd->khd",
            grad_scores,
            split_into_heads(query_content),
            preferred_element_type=jnp.float32,
        )
        * score_scale
    )
    value_piece = jnp.einsum(
        "hqk,qhd->khd", weights.astype(jnp.bfloat16), grad_heads, preferred_element_type=jnp.float32
    )
    table_piece = (
        jnp.einsum(
            "fjb,jfg->bfg",
            grad_table_scores,
            split_into_heads(query_token_position),
            preferred_element_type=jnp.float32,
        )
        * score_scale
    )
    grad_keys = add_rows(grad_keys, key_piece.reshape(block_rows, D))
    grad_values = add_rows(grad_values, value_piece.reshape(block_rows, D))
    grad_table = add_rows(grad_table, table_piece.reshape(table_length, D))
    finished = (grad_content, grad_position, grad_keys, grad_values, grad_table)
    grad_content, grad_position, grad_keys, grad_values, grad_table = finished
    return (
        grad_content.reshape(query_count, D),
        grad_position.reshape(query_count, D),
        grad_keys,
        grad_values,
        grad_table,
    )


def window_forward(
    normed,
    key_row_matrix,
    value_rows,
    layer_in,
    query_content,
    query_token_position,
    token_start,
    lengths,
):
    row_count = key_row_matrix.shape[0]
    border = passed_along(
        jnp.stack([key_row_matrix[row_count - WIN :], value_rows[row_count - WIN :]]), "seq", 1
    )
    border_keys = border[0]
    border_values = border[1]
    keys_all = jnp.concatenate([border_keys, key_row_matrix], axis=0)
    values_all = jnp.concatenate([border_values, value_rows], axis=0)
    distance = (QBLK - 1 + WIN - jnp.arange(2 * QBLK + WIN - 1)).astype(jnp.float32)
    embed_rows = sinusoid(distance).astype(jnp.bfloat16)
    lookup_table_rows = dot_float(embed_rows, layer_in[:, 3 * D :]).astype(jnp.bfloat16)

    def one_block(block_index):
        first_row = block_index * QBLK
        visible = window_block_visible(token_start, first_row, lengths)
        return attention_forward_pass(
            query_content,
            query_token_position,
            keys_all,
            values_all,
            lookup_table_rows,
            lambda unused: visible,
        )

    mixed_blocks, log_totals = lax.map(one_block, jnp.arange(row_count // QBLK))
    stored = (keys_all, values_all, embed_rows, lookup_table_rows, log_totals)
    return (mixed_blocks.reshape(row_count, D), stored)


def window_backward(stored, query_content, query_token_position, grad_mixed, token_start, lengths):
    keys_all, values_all, embed_rows, lookup_table_rows, log_totals = stored
    row_count = query_content.shape[0]

    def one_block(carried, block_index):
        grad_keys, grad_values, grad_weight = carried
        first_row = block_index * QBLK
        visible = window_block_visible(token_start, first_row, lengths)
        gradients = attend_backward(
            query_content,
            query_token_position,
            keys_all,
            values_all,
            lookup_table_rows,
            lambda unused: visible,
            QBLK + WIN,
            log_totals[block_index],
            grad_mixed,
        )
        grad_keys = add_rows(grad_keys, gradients[2])
        grad_values = add_rows(grad_values, gradients[3])
        grad_weight = grad_weight + outer_float(embed_rows, gradients[4].astype(jnp.bfloat16))
        return ((grad_keys, grad_values, grad_weight), (gradients[0], gradients[1]))

    initial = (
        jnp.zeros(keys_all.shape, jnp.float32),
        jnp.zeros(values_all.shape, jnp.float32),
        jnp.zeros((D, D), jnp.float32),
    )
    carried, per_block = lax.scan(one_block, initial, jnp.arange(row_count // QBLK))
    grad_keys, grad_values, grad_weight = carried
    returned = passed_along(
        jnp.stack([grad_keys[:WIN], grad_values[:WIN]]).astype(jnp.bfloat16), "seq", -1
    ).astype(jnp.float32)
    own_keys = grad_keys[WIN:].at[row_count - WIN :].add(returned[0])
    own_values = grad_values[WIN:].at[row_count - WIN :].add(returned[1])
    return (
        per_block[0].reshape(row_count, D),
        per_block[1].reshape(row_count, D),
        own_keys,
        own_values,
        grad_weight,
    )


def pooled_forward(
    normed,
    key_row_matrix,
    value_rows,
    layer_in,
    query_content,
    query_token_position,
    pooled_start,
    lengths,
):
    query_count = key_row_matrix.shape[0]
    keys_all, values_all = (
        lax.all_gather(key_row_matrix, "seq", axis=0, tiled=True),
        lax.all_gather(value_rows, "seq", axis=0, tiled=True),
    )
    pooled_total = keys_all.shape[0]
    distance = (pooled_start + query_count - 1 - jnp.arange(query_count + pooled_total - 1)).astype(
        jnp.float32
    )
    embed_rows = sinusoid(distance).astype(jnp.bfloat16)
    lookup_table_rows = dot_float(embed_rows, layer_in[:, 3 * D :]).astype(jnp.bfloat16)
    visible_of = partial(
        pooled_block_visible,
        pooled_start=pooled_start,
        query_count=query_count,
        block_rows=pooled_total,
        lengths=lengths,
    )
    mixed_rows, log_total = attention_forward_pass(
        query_content, query_token_position, keys_all, values_all, lookup_table_rows, visible_of
    )
    stored = (keys_all, values_all, embed_rows, lookup_table_rows, log_total, pooled_total)
    return (mixed_rows, stored)


def pooled_backward(stored, query_content, query_token_position, grad_mixed, pooled_start, lengths):
    keys_all, values_all, embed_rows, lookup_table_rows, log_total, block_rows = stored
    query_count = query_content.shape[0]
    visible_of = partial(
        pooled_block_visible,
        pooled_start=pooled_start,
        query_count=query_count,
        block_rows=block_rows,
        lengths=lengths,
    )
    gradients = attend_backward(
        query_content,
        query_token_position,
        keys_all,
        values_all,
        lookup_table_rows,
        visible_of,
        block_rows,
        log_total,
        grad_mixed,
    )
    own_keys, own_values = (
        lax.psum_scatter(
            gradients[2].astype(jnp.bfloat16), "seq", scatter_dimension=0, tiled=True
        ).astype(jnp.float32),
        lax.psum_scatter(
            gradients[3].astype(jnp.bfloat16), "seq", scatter_dimension=0, tiled=True
        ).astype(jnp.float32),
    )
    grad_weight = outer_float(embed_rows, gradients[4].astype(jnp.bfloat16))
    return (gradients[0], gradients[1], own_keys, own_values, grad_weight)


def block_forward(inputs, layer_index, params, attention_level_apply):
    (
        norm_gain,
        norm_shift,
        relative_bias,
        attention_in,
        attention_out,
        expand_weight,
        expand_bias,
        contract_weight,
        contract_bias,
    ) = params
    layer_in = attention_in[:, layer_index, :]
    normed = layer_norm(inputs, norm_gain[layer_index, 0], norm_shift[layer_index, 0]).astype(
        jnp.bfloat16
    )
    projected = dot_float(normed, layer_in[:, : 3 * D])
    queries = projected[:, :D]
    key_row_matrix = projected[:, D : 2 * D].astype(jnp.bfloat16)
    value_rows = projected[:, 2 * D :].astype(jnp.bfloat16)
    query_content = (queries + relative_bias[layer_index, 0]).astype(jnp.bfloat16)
    query_token_position = (queries + relative_bias[layer_index, 1]).astype(jnp.bfloat16)
    mixed_rows, attention_stored = attention_level_apply(
        normed, key_row_matrix, value_rows, layer_in, query_content, query_token_position
    )
    middle = inputs + dot_float(mixed_rows, attention_out[:, layer_index, :])
    normed_two = layer_norm(middle, norm_gain[layer_index, 1], norm_shift[layer_index, 1]).astype(
        jnp.bfloat16
    )
    expanded = dot_float(normed_two, expand_weight[:, layer_index, :]) + expand_bias[layer_index]
    activated = jax.nn.gelu(expanded, approximate=False).astype(jnp.bfloat16)
    result = (
        middle
        + dot_float(activated, contract_weight[:, layer_index, :])
        + contract_bias[layer_index]
    )
    stored = (
        inputs,
        normed,
        query_content,
        query_token_position,
        attention_stored,
        mixed_rows,
        middle,
        normed_two,
        expanded,
        activated,
    )
    return (result, stored)


def block_backward(grad_result, layer_index, params, stored, attend_back):
    (
        norm_gain,
        norm_shift,
        relative_bias,
        attention_in,
        attention_out,
        expand_weight,
        expand_bias,
        contract_weight,
        contract_bias,
    ) = params
    (
        inputs,
        normed,
        query_content,
        query_token_position,
        attention_stored,
        mixed_rows,
        middle,
        normed_two,
        expanded,
        activated,
    ) = stored
    layer_in = attention_in[:, layer_index, :]
    grad_branch = grad_result.astype(jnp.bfloat16)
    grad_contract = outer_float(activated, grad_branch)
    grad_contract_bias = jnp.sum(grad_branch.astype(jnp.float32), axis=0)
    grad_activated = dot_back(grad_branch, contract_weight[:, layer_index, :])
    gelu_pull = jax.vjp(lambda argument: jax.nn.gelu(argument, approximate=False), expanded)[1]
    grad_expanded = gelu_pull(grad_activated)[0].astype(jnp.bfloat16)
    grad_expand = outer_float(normed_two, grad_expanded)
    grad_expand_bias = jnp.sum(grad_expanded.astype(jnp.float32), axis=0)
    grad_normed_two = dot_back(grad_expanded, expand_weight[:, layer_index, :])
    second_pull = jax.vjp(
        layer_norm,
        middle,
        norm_gain[layer_index, 1].astype(jnp.float32),
        norm_shift[layer_index, 1].astype(jnp.float32),
    )[1]
    grad_middle_norm, grad_gain_two, grad_shift_two = second_pull(grad_normed_two)
    grad_middle = grad_result + grad_middle_norm
    grad_attend = grad_middle.astype(jnp.bfloat16)
    grad_out_weight = outer_float(mixed_rows, grad_attend)
    grad_mixed = dot_back(grad_attend, attention_out[:, layer_index, :]).astype(jnp.bfloat16)
    grad_content, grad_position, own_keys, own_values, grad_table_weight = attend_back(
        attention_stored, query_content, query_token_position, grad_mixed
    )
    grad_bias_pair = jnp.stack([jnp.sum(grad_content, axis=0), jnp.sum(grad_position, axis=0)])
    grad_projected = jnp.concatenate(
        [
            (grad_content + grad_position).astype(jnp.bfloat16),
            own_keys.astype(jnp.bfloat16),
            own_values.astype(jnp.bfloat16),
        ],
        axis=1,
    )
    grad_in_weight = jnp.concatenate(
        [outer_float(normed, grad_projected), grad_table_weight], axis=1
    )
    grad_normed = dot_back(grad_projected, layer_in[:, : 3 * D])
    first_pull = jax.vjp(
        layer_norm,
        inputs,
        norm_gain[layer_index, 0].astype(jnp.float32),
        norm_shift[layer_index, 0].astype(jnp.float32),
    )[1]
    grad_inputs_norm, grad_gain_one, grad_shift_one = first_pull(grad_normed)
    grad_inputs = grad_middle + grad_inputs_norm
    gradients = (
        jnp.stack([grad_gain_one, grad_gain_two]),
        jnp.stack([grad_shift_one, grad_shift_two]),
        grad_bias_pair,
        grad_in_weight,
        grad_out_weight,
        grad_expand,
        grad_expand_bias,
        grad_contract,
        grad_contract_bias,
    )
    return (grad_inputs, gradients)


def per_device(
    tokens,
    doc_lengths,
    cotangent,
    norm_gain,
    norm_shift,
    relative_bias,
    attention_in,
    attention_out,
    expand_weight,
    expand_bias,
    contract_weight,
    contract_bias,
    pool_weight,
    pool_bias,
    upsample_weight,
    upsample_bias,
):
    params = (
        norm_gain,
        norm_shift,
        relative_bias,
        attention_in,
        attention_out,
        expand_weight,
        expand_bias,
        contract_weight,
        contract_bias,
    )
    inputs = tokens[0].astype(jnp.float32)
    lengths = doc_lengths[0]
    row_count = inputs.shape[0]
    pooled_count = row_count // 3
    device = lax.axis_index("seq")
    token_start = device * row_count
    pooled_start = device * pooled_count
    token_place = token_start + jnp.arange(row_count)
    window_level = partial(window_forward, token_start=token_start, lengths=lengths)
    window_back = partial(window_backward, token_start=token_start, lengths=lengths)
    pooled_level = partial(pooled_forward, pooled_start=pooled_start, lengths=lengths)
    pooled_back = partial(pooled_backward, pooled_start=pooled_start, lengths=lengths)
    first_out, first_stored = block_forward(inputs, 0, params, window_level)
    first_low = first_out.astype(jnp.bfloat16)
    edge_rows = passed_along(first_low[row_count - 2 :], "seq", 1)
    keep_mask = (token_place >= 2) & (
        document_of(token_place - 2, lengths) == document_of(token_place, lengths)
    )
    shifted = jnp.concatenate([edge_rows, first_low[: row_count - 2]], axis=0)
    shifted = jnp.where(keep_mask[:, None], shifted, jnp.zeros_like(shifted))
    grouped = shifted.reshape(pooled_count, 3 * D)
    pooled = dot_float(grouped, pool_weight) + pool_bias
    short_out, short_stored = block_forward(pooled, 1, params, pooled_level)
    short_low = short_out.astype(jnp.bfloat16)
    upsampled = (dot_float(short_low, upsample_weight) + upsample_bias).reshape(row_count, D)
    output, last_stored = block_forward(first_out + upsampled, 2, params, window_level)
    level_squares = jnp.stack(
        [jnp.sum(first_out * first_out), jnp.sum(short_out * short_out), jnp.sum(output * output)]
    )
    grad_joined, grads_last = block_backward(
        cotangent[0].astype(jnp.float32), 2, params, last_stored, window_back
    )
    grad_upsampled = grad_joined.reshape(pooled_count, 3 * D).astype(jnp.bfloat16)
    grad_upsample_weight = outer_float(short_low, grad_upsampled)
    grad_upsample_bias = jnp.sum(grad_upsampled.astype(jnp.float32), axis=0)
    grad_short = dot_back(grad_upsampled, upsample_weight)
    grad_pooled, grads_short = block_backward(grad_short, 1, params, short_stored, pooled_back)
    grad_pooled_low = grad_pooled.astype(jnp.bfloat16)
    grad_pool_weight = outer_float(grouped, grad_pooled_low)
    grad_pool_bias = jnp.sum(grad_pooled_low.astype(jnp.float32), axis=0)
    grad_shifted = dot_back(grad_pooled_low, pool_weight).reshape(row_count, D)
    grad_shifted = jnp.where(keep_mask[:, None], grad_shifted, 0.0)
    came_back = passed_along(grad_shifted[:2], "seq", -1)
    grad_first = grad_joined + jnp.concatenate([grad_shifted[2:], came_back], axis=0)
    grad_inputs, grads_first = block_backward(grad_first, 0, params, first_stored, window_back)
    stack_axes = (0, 0, 0, 1, 1, 1, 0, 1, 0)
    stacked = [
        jnp.stack(
            [grads_first[index], grads_short[index], grads_last[index]], axis=stack_axes[index]
        )
        for index in range(9)
    ]
    attention_shares = (
        lax.psum_scatter(
            stacked[3].astype(jnp.bfloat16), "seq", scatter_dimension=0, tiled=True
        ).astype(jnp.float32),
        lax.psum_scatter(
            stacked[4].astype(jnp.bfloat16), "seq", scatter_dimension=0, tiled=True
        ).astype(jnp.float32),
        lax.psum_scatter(
            stacked[5].astype(jnp.bfloat16), "seq", scatter_dimension=0, tiled=True
        ).astype(jnp.float32),
        lax.psum_scatter(
            stacked[7].astype(jnp.bfloat16), "seq", scatter_dimension=0, tiled=True
        ).astype(jnp.float32),
        lax.psum_scatter(
            grad_pool_weight.astype(jnp.bfloat16), "seq", scatter_dimension=0, tiled=True
        ).astype(jnp.float32),
        lax.psum_scatter(
            grad_upsample_weight.astype(jnp.bfloat16), "seq", scatter_dimension=0, tiled=True
        ).astype(jnp.float32),
    )
    attention_shares = (
        lax.psum(attention_shares[0].astype(jnp.bfloat16), "dp").astype(jnp.float32),
        lax.psum(attention_shares[1].astype(jnp.bfloat16), "dp").astype(jnp.float32),
        lax.psum(attention_shares[2].astype(jnp.bfloat16), "dp").astype(jnp.float32),
        lax.psum(attention_shares[3].astype(jnp.bfloat16), "dp").astype(jnp.float32),
        lax.psum(attention_shares[4].astype(jnp.bfloat16), "dp").astype(jnp.float32),
        lax.psum(attention_shares[5].astype(jnp.bfloat16), "dp").astype(jnp.float32),
    )
    small_sums = lax.psum(
        (
            stacked[0],
            stacked[1],
            stacked[2],
            stacked[6],
            stacked[8],
            grad_pool_bias,
            grad_upsample_bias,
            level_squares,
        ),
        ("dp", "seq"),
    )
    whole_rows = lax.axis_size("dp") * lax.axis_size("seq") * row_count * D
    counts = jnp.array([whole_rows, whole_rows // 3, whole_rows], jnp.float32)
    rms = jnp.sqrt(small_sums[7] / counts)
    return (
        output[None].astype(jnp.bfloat16),
        grad_inputs[None].astype(jnp.bfloat16),
        small_sums[0],
        small_sums[1],
        small_sums[2],
        attention_shares[0],
        attention_shares[1],
        attention_shares[2],
        small_sums[3],
        attention_shares[3],
        small_sums[4],
        attention_shares[4],
        small_sums[5],
        attention_shares[5],
        small_sums[6],
        rms,
    )


def solution(mesh):
    in_specs = (
        P("dp", "seq", None),
        P("dp", None),
        P("dp", "seq", None),
        P(),
        P(),
        P(),
        P(),
        P(),
        P(),
        P(),
        P(),
        P(),
        P(),
        P(),
        P(),
        P(),
    )
    out_specs = (
        P("dp", "seq", None),
        P("dp", "seq", None),
        P(),
        P(),
        P(),
        P("seq", None, None),
        P("seq", None, None),
        P("seq", None, None),
        P(),
        P("seq", None, None),
        P(),
        P("seq", None),
        P(),
        P("seq", None),
        P(),
        P(),
    )
    return jax.shard_map(
        per_device, mesh=mesh, in_specs=in_specs, out_specs=out_specs, check_vma=False
    )
```

profile of v0, /device:TPU:0, one launch (start us, length us, event | category | flops | bytes accessed | tf_op | source)
XLA Modules:
  0.0 1139.9 jit_solution(14316606339164874039)
XLA Ops:
  7.3 6.1 slice_bitcast_fusion
  26.7 5.1 fusion.108
  34.5 6.4 fusion.238
  42.9 13.7 %reshape.1054 = f32[3142656]{0:T(1024)} reshape(f32[8,384,1023]{2,1,0:T(8,128)} %fusion.238) | data formatting | bytes 25141248
  56.6 12.7 %reshape.984 = f32[8,392832]{1,0:T(8,128)} reshape(f32[3142656]{0:T(1024)} %reshape.1054) | data formatting | bytes 25141248 | tf_op jit(solution)/shard_map/while/body/eval_jaxpr/reshape | solution.py:40
  69.2 11.7 %slice.490 = f32[8,392448]{1,0:T(8,128)} slice(f32[8,392832]{1,0:T(8,128)} %reshape.984), slice={[0:8], [383:392831]} | slice | bytes 25116672 | tf_op jit(solution)/shard_map/while/body/eval_jaxpr/slice | solution.py:41
  81.0 9.9 reshape.1056
  90.9 14.6 %reshape.985 = f32[8,384,1022]{2,1,0:T(8,128)} reshape(f32[3139584]{0:T(1024)} %reshape.1056) | data formatting | bytes 25116672 | tf_op jit(solution)/shard_map/while/body/eval_jaxpr/reshape | solution.py:42
  110.8 4.7 fusion.226
  118.9 4.7 convolution_convert_fusion.24
  125.6 10.5 multiply_convert_fusion.4
  152.1 4.9 fusion.98
  167.6 6.9 reshape.991
  179.0 9.4 reshape.992
  206.6 5.5 multiply_convert_fusion.8
  229.5 7.8 fusion.240
  237.2 14.0 %reshape.1058 = f32[3142656]{0:T(1024)} reshape(f32[8,384,1023]{2,1,0:T(8,128)} %fusion.240) | data formatting | bytes 25141248
  251.2 12.7 %reshape.997 = f32[8,392832]{1,0:T(8,128)} reshape(f32[3142656]{0:T(1024)} %reshape.1058) | data formatting | bytes 25141248 | tf_op jit(solution)/shard_map/while/body/eval_jaxpr/reshape | solution.py:40
  263.9 11.6 %slice.510 = f32[8,392448]{1,0:T(8,128)} slice(f32[8,392832]{1,0:T(8,128)} %reshape.997), slice={[0:8], [383:392831]} | slice | bytes 25116672 | tf_op jit(solution)/shard_map/while/body/eval_jaxpr/slice | solution.py:41
  275.5 9.9 reshape.1060
  285.5 14.2 %reshape.998 = f32[8,384,1022]{2,1,0:T(8,128)} reshape(f32[3139584]{0:T(1024)} %reshape.1060) | data formatting | bytes 25116672 | tf_op jit(solution)/shard_map/while/body/eval_jaxpr/reshape | solution.py:42
  311.1 5.8 fusion.234
  321.9 4.9 convolution_convert_fusion.23
  327.7 10.1 multiply_convert_fusion.3
  351.6 6.3 multiply_reduce_fusion.1
  372.1 11.2 reshape.1062
  383.3 12.1 %reshape.1000 = bf16[8,392448]{1,0:T(8,128)(2,1)} reshape(bf16[3139584]{0:T(1024)(128)(2,1)} %reshape.1062) | data formatting | bytes 12558336 | tf_op jit(solution)/shard_map/while/body/eval_jaxpr/transpose(jvp())/reshape | solution.py:42
  395.3 7.4 pad.37
  402.8 14.8 %reshape.1064 = bf16[3142656]{0:T(1024)(128)(2,1)} reshape(bf16[8,392832]{1,0:T(8,128)(2,1)} %pad.37) | data formatting | bytes 12570624
  417.6 13.9 %convert_element_type.704 = bf16[8,384,1023]{2,1,0:T(8,128)(2,1)} reshape(bf16[3142656]{0:T(1024)(128)(2,1)} %reshape.1064) | data formatting | bytes 12570624 | tf_op jit(solution)/shard_map/while/body/eval_jaxpr/convert_element_type | solution.py:167
  431.5 5.3 fusion.82
  481.7 5.9 reshape.1066
  487.5 5.6 reshape.1006
  496.4 6.6 reshape.1068
  503.0 7.6 convert_element_type.717
  522.7 23.3 %reduce-scatter.25.cloned.1.call-done = bf16[128,512]{1,0:T(8,128)(2,1)} async-done(((bf16[1024,512]{1,0:T(8,128)(2,1)}), bf16[128,512]{1,0:T(8,128)(2,1)}) %reduce-scatter.25.cloned.1.call-update) | async-done | bytes 131088
  565.1 6.1 convert_reduce_fusion.1
  612.4 5.6 multiply_reduce_fusion
  631.7 11.2 reshape.1070
  642.9 12.2 %reshape.1009 = bf16[8,392448]{1,0:T(8,128)(2,1)} reshape(bf16[3139584]{0:T(1024)(128)(2,1)} %reshape.1070) | data formatting | bytes 12558336 | tf_op jit(solution)/shard_map/while/body/eval_jaxpr/transpose(jvp())/reshape | solution.py:42
  655.0 7.5 pad.41
  662.6 14.8 %reshape.1072 = bf16[3142656]{0:T(1024)(128)(2,1)} reshape(bf16[8,392832]{1,0:T(8,128)(2,1)} %pad.41) | data formatting | bytes 12570624
  677.4 14.0 %convert_element_type.732 = bf16[8,384,1023]{2,1,0:T(8,128)(2,1)} reshape(bf16[3142656]{0:T(1024)(128)(2,1)} %reshape.1072) | data formatting | bytes 12570624 | tf_op jit(solution)/shard_map/while/body/eval_jaxpr/convert_element_type | solution.py:167
  713.4 4.7 multiply_reduce_fusion.3
  739.5 62.7 %reduce-scatter.19.cloned.1.call-done = bf16[256,3,512]{2,0,1:T(8,128)(2,1)} async-done(((bf16[2048,3,512]{2,0,1:T(8,128)(2,1)}), bf16[256,3,512]{2,0,1:T(8,128)(2,1)}) %reduce-scatter.19.cloned.1.call-update) | async-done | bytes 786448 | tf_op jit(solution)/shard_map/reduce_scatter | solution.py:598
  802.2 65.0 %reduce-scatter.13.cloned.1.call-done = bf16[64,3,2048]{2,0,1:T(8,128)(2,1)} async-done(((bf16[512,3,2048]{2,0,1:T(8,128)(2,1)}), bf16[64,3,2048]{2,0,1:T(8,128)(2,1)}) %reduce-scatter.13.cloned.1.call-update) | async-done | bytes 786448 | tf_op jit(solution)/shard_map/reduce_scatter | solution.py:589
  869.4 130.0 %all-reduce.11.cloned.1.call-done = (f32[3,2,512]{2,1,0:T(2,128)}, f32[3,2,512]{2,1,0:T(2,128)}, f32[3,2,512]{2,1,0:T(2,128)}, f32[3,2048]{1,0:T(4,128)}, f32[3,...) async-done(((f32[3,2,512]{2,1,0:T(2,128)}, f32[3,2,512]{2,1,0:T(2,128)}, f32[3,2,512]{2,1,0:T(2,128)}, f32[3,2048]{1,0:T(4,128)}, f32[3,512]{1,0:T(4,128)}, ...) | async-done | bytes 75804 | tf_op jit(solution)/shard_map/psum | solution.py:616
  1000.6 119.3 %all-reduce.13.cloned.1.call-done = (bf16[64,3,2048]{2,0,1:T(8,128)(2,1)}, bf16[64,3,512]{2,0,1:T(8,128)(2,1)}, bf16[64,3,2048]{2,0,1:T(8,128)(2,1)}, bf16[256,3...) async-done(((bf16[64,3,2048]{2,0,1:T(8,128)(2,1)}, bf16[64,3,512]{2,0,1:T(8,128)(2,1)}, bf16[64,3,2048]{2,0,1:T(8,128)(2,1)}, ...) | async-done | bytes 2949136 | tf_op jit(solution)/shard_map/psum | solution.py:609
  (756 shorter events, 331.2 us)
Async XLA Ops:
  7.2 138.9 %copy-start = (bf16[1536,512]{1,0:T(8,128)(2,1)S(1)}, bf16[1536,512]{1,0:T(8,128)(2,1)}, u32[]{:S(2)}) copy-start(bf16[1536,512]{1,0:T(8,128)(2,1)} %param.37) | copy-start | bytes 4718596
  7.2 181.4 %all-gather.5.cloned.1.call-start = ((), (), s32[]{:S(2)}) async-start(), calls=%async_computation.9 | async-start | bytes 1179648 | tf_op jit(solution)/shard_map/all_gather | solution.py:317
  18.9 89.0 %collective-permute-start = (bf16[2,256,512]{2,1,0:T(8,128)(2,1)}, bf16[2,256,512]{2,1,0:T(8,128)(2,1)}, u32[]{:S(2)}, u32[]{:S(2)}) collective-permute-start(bf16[2,256,512]{2,1,0:T(8,128)(2,1)} %pad_maximum_fusion.14), channel_id=1, source_target_pairs={{0,1},{1,2},{2,3},{3,4},{4,5},{5,6},{6,7},{8,9},{9,10},{10,11},{11... | collective-permute-start | bytes 1572872 | tf_op jit(solution)/shard_map/ppermute | solution.py:22
  26.7 14.1 %copy-start.37 = (bf16[384,512]{0,1:T(8,128)(2,1)}, bf16[384,512]{0,1:T(8,128)(2,1)S(1)}, u32[]{:S(2)}) copy-start(bf16[384,512]{0,1:T(8,128)(2,1)S(1)} %copy.143) | copy-start | bytes 1179652
  41.0 15.5 %copy-start.196 = (s32[8,1]{0,1:T(1,128)}, s32[8,1]{0,1:T(1,128)S(1)}, u32[]{:S(2)}) copy-start(s32[8,1]{0,1:T(1,128)S(1)} %reduce-window.8) | copy-start | bytes 100
  90.9 14.9 %copy-start.79 = (bf16[384,512]{1,0:T(8,128)(2,1)S(1)}, bf16[384,512]{1,0:T(8,128)(2,1)}, u32[]{:S(2)}) copy-start(bf16[384,512]{1,0:T(8,128)(2,1)} %get-tuple-element.293) | copy-start | bytes 1179652
  90.9 16.3 %copy-start.134 = (bf16[3,2048]{1,0:T(4,128)(2,1)S(1)}, bf16[3,2048]{1,0:T(4,128)(2,1)}, u32[]{:S(2)}) copy-start(bf16[3,2048]{1,0:T(4,128)(2,1)} %param.34) | copy-start | bytes 36868
  106.2 12.7 %copy-start.56 = (bf16[384,512]{0,1:T(8,128)(2,1)}, bf16[384,512]{0,1:T(8,128)(2,1)S(1)}, u32[]{:S(2)}) copy-start(bf16[384,512]{0,1:T(8,128)(2,1)S(1)} %copy.139) | copy-start | bytes 1179652
  123.6 12.6 %copy-start.53 = (bf16[8,64,384]{2,1,0:T(8,128)(2,1)}, bf16[8,64,384]{2,1,0:T(8,128)(2,1)S(1)}, u32[]{:S(2)}) copy-start(bf16[8,64,384]{2,1,0:T(8,128)(2,1)S(1)} %convolution_convert_fusion.24) | copy-start | bytes 1179652
  125.3 10.9 copy-start.21
  125.3 10.9 copy-start.152
  125.5 10.6 copy-start.147
  125.6 10.6 copy-start.189
  125.6 10.6 copy-start.210
  140.2 4.5 collective-permute-start.1
  148.5 51.5 %all-gather.3.cloned.1.call-start = ((), (), s32[]{:S(2)}) async-start(), calls=%async_computation.8 | async-start | bytes 1179648 | tf_op jit(solution)/shard_map/all_gather | solution.py:318
  159.9 361.7 %reduce-scatter.27.cloned.1.call-start = ((), (), s32[]{:S(2)}) async-start(), calls=%async_computation.17 | async-start | bytes 1179648
  179.0 11.1 copy-start.96
  206.3 250.6 %copy-start.198 = (f32[128]{0:T(128)}, f32[128]{0:T(128)S(1)}, u32[]{:S(2)}) copy-start(f32[128]{0:T(128)S(1)} %broadcast_multiply_fusion.5) | copy-start | bytes 1540
  206.5 250.4 %copy-start.211 = (f32[128]{0:T(128)}, f32[128]{0:T(128)S(1)}, u32[]{:S(2)}) copy-start(f32[128]{0:T(128)S(1)} %fusion.183) | copy-start | bytes 1540
  219.7 223.7 %copy-start.155 = (f32[384]{0:T(512)}, f32[384]{0:T(512)S(1)}, u32[]{:S(2)}) copy-start(f32[384]{0:T(512)S(1)} %fusion.180) | copy-start | bytes 4612
  226.5 81.0 %collective-permute-start.2 = (bf16[2,256,512]{2,1,0:T(8,128)(2,1)}, bf16[2,256,512]{2,1,0:T(8,128)(2,1)}, u32[]{:S(2)}, u32[]{:S(2)}) collective-permute-start(bf16[2,256,512]{2,1,0:T(8,128)(2,1)} %pad_maximum_fusion.15), channel_id=1, source_target_pairs={{0,1},{1,2},{2,3},{3,4},{4,5},{5,6},{6,7},{8,9},{9,10},{10,11},{11... | collective-permute-start | bytes 1572872 | tf_op jit(solution)/shard_map/ppermute | solution.py:22
  326.8 11.0 copy-start.55
  327.4 19.0 %copy-start.26 = (f32[384,512]{1,0:T(8,128)}, f32[384,512]{1,0:T(8,128)S(1)}, u32[]{:S(2)}) copy-start(f32[384,512]{1,0:T(8,128)S(1)} %get-tuple-element.374) | copy-start | bytes 2359300
  327.4 19.0 %copy-start.157 = (f32[384]{0:T(512)}, f32[384]{0:T(512)S(1)}, u32[]{:S(2)}) copy-start(f32[384]{0:T(512)S(1)} %broadcast_multiply_fusion) | copy-start | bytes 4612
  327.7 18.7 %copy-start.192 = (f32[384]{0:T(512)}, f32[384]{0:T(512)S(1)}, u32[]{:S(2)}) copy-start(f32[384]{0:T(512)S(1)} %fusion.181) | copy-start | bytes 4612
  351.6 10.5 slice-start.2
  351.6 10.5 slice-start.3
  367.2 72.8 %collective-permute-start.3 = (bf16[2,256,512]{1,2,0:T(8,128)(2,1)}, bf16[2,256,512]{1,2,0:T(8,128)(2,1)}, u32[]{:S(2)}, u32[]{:S(2)}) collective-permute-start(bf16[2,256,512]{1,2,0:T(8,128)(2,1)} %pad_maximum_fusion.16), channel_id=1, source_target_pairs={{1,0},{2,1},{3,2},{4,3},{5,4},{6,5},{7,6},{9,8},{10,9},{11,10},{12... | collective-permute-start | bytes 1572872 | tf_op jit(solution)/shard_map/ppermute | solution.py:22
  467.9 78.0 %reduce-scatter.25.cloned.1.call-start = ((), (), s32[]{:S(2)}) async-start(), calls=%async_computation.16 | async-start | bytes 1179648
  475.9 263.5 %reduce-scatter.23.cloned.1.call-start = ((), (), s32[]{:S(2)}) async-start(), calls=%async_computation.15 | async-start | bytes 1769472 | tf_op jit(solution)/shard_map/reduce_scatter | solution.py:604
  516.2 30.7 %copy-start.141 = (f32[1,1,512]{2,1,0:T(1,128)S(1)}, f32[1,1,512]{2,1,0:T(1,128)}, u32[]{:S(2)}) copy-start(f32[1,1,512]{2,1,0:T(1,128)} %get-tuple-element.330) | copy-start | bytes 6148
  516.2 30.7 %copy-start.194 = (f32[128]{0:T(128)S(1)}, f32[128]{0:T(128)}, u32[]{:S(2)}) copy-start(f32[128]{0:T(128)} %copy-done.193) | copy-start | bytes 1540
  516.3 223.2 %reduce-scatter.21.cloned.1.call-start = ((), (), s32[]{:S(2)}) async-start(), calls=%async_computation.14 | async-start | bytes 1769472 | tf_op jit(solution)/shard_map/reduce_scatter | solution.py:601
  521.6 28.9 %copy-start.18 = (f32[128,512]{1,0:T(8,128)S(1)}, f32[128,512]{1,0:T(8,128)}, u32[]{:S(2)}) copy-start(f32[128,512]{1,0:T(8,128)} %copy-done.16) | copy-start | bytes 786436
  521.6 29.7 %copy-start.47 = (f32[128,512]{1,0:T(8,128)S(1)}, f32[128,512]{1,0:T(8,128)}, u32[]{:S(2)}) copy-start(f32[128,512]{1,0:T(8,128)} %copy-done.46) | copy-start | bytes 786436
  522.6 28.6 %copy-start.107 = (bf16[128,512]{0,1:T(8,128)(2,1)}, bf16[128,512]{0,1:T(8,128)(2,1)S(1)}, u32[]{:S(2)}) copy-start(bf16[128,512]{0,1:T(8,128)(2,1)S(1)} %copy.168) | copy-start | bytes 393220
  558.5 4.5 collective-permute-start.4
  563.0 176.5 %reduce-scatter.15.cloned.1.call-start = ((), (), s32[]{:S(2)}) async-start(), calls=%async_computation.11 | async-start | bytes 1769472 | tf_op jit(solution)/shard_map/reduce_scatter | solution.py:592
  578.0 161.5 %reduce-scatter.17.cloned.1.call-start = ((), (), s32[]{:S(2)}) async-start(), calls=%async_computation.12 | async-start | bytes 7077888 | tf_op jit(solution)/shard_map/reduce_scatter | solution.py:595
  587.0 215.2 %reduce-scatter.19.cloned.1.call-start = ((), (), s32[]{:S(2)}) async-start(), calls=%async_computation.13 | async-start | bytes 7077888 | tf_op jit(solution)/shard_map/reduce_scatter | solution.py:598
  595.3 271.9 %reduce-scatter.13.cloned.1.call-start = ((), (), s32[]{:S(2)}) async-start(), calls=%async_computation.10 | async-start | bytes 7077888 | tf_op jit(solution)/shard_map/reduce_scatter | solution.py:589
  630.2 73.0 %collective-permute-start.5 = (bf16[2,256,512]{1,2,0:T(8,128)(2,1)}, bf16[2,256,512]{1,2,0:T(8,128)(2,1)}, u32[]{:S(2)}, u32[]{:S(2)}) collective-permute-start(bf16[2,256,512]{1,2,0:T(8,128)(2,1)} %pad_maximum_fusion.17), channel_id=1, source_target_pairs={{1,0},{2,1},{3,2},{4,3},{5,4},{6,5},{7,6},{9,8},{10,9},{11,10},{12... | collective-permute-start | bytes 1572872 | tf_op jit(solution)/shard_map/ppermute | solution.py:22
  677.4 14.0 %copy-start.38 = (bf16[384,512]{0,1:T(8,128)(2,1)S(1)}, bf16[384,512]{0,1:T(8,128)(2,1)}, u32[]{:S(2)}) copy-start(bf16[384,512]{0,1:T(8,128)(2,1)} %copy-done.37) | copy-start | bytes 1179652
  711.4 288.0 %all-reduce.11.cloned.1.call-start = ((), (), s32[]{:S(2)}) async-start(), calls=%async_computation.18 | async-start | bytes 177152 | tf_op jit(solution)/shard_map/psum | solution.py:616
  713.4 13.0 %copy-start.36 = (bf16[128,1536]{1,0:T(8,128)(2,1)S(1)}, bf16[128,1536]{1,0:T(8,128)(2,1)}, u32[]{:S(2)}) copy-start(bf16[128,1536]{1,0:T(8,128)(2,1)} %convert_element_type.711) | copy-start | bytes 1179652
  737.6 261.9 %copy-start.217 = (f32[3]{0:T(128)S(1)}, f32[3]{0:T(128)}, u32[]{:S(2)}) copy-start(f32[3]{0:T(128)} %constant.402) | copy-start | bytes 40
  739.3 380.6 %all-reduce.13.cloned.1.call-start = ((), (), s32[]{:S(2)}) async-start(), calls=%async_computation.19 | async-start | bytes 5898240 | tf_op jit(solution)/shard_map/psum | solution.py:609
  (200 other events, 778.4 us)
Sparse Core Ops, SparseCore 0:
  148.6 25.3 all-gather.4
  176.4 23.4 all-gather.2
  468.0 38.1 reduce-scatter.26
  509.9 36.0 reduce-scatter.24
  549.1 38.4 reduce-scatter.22
  590.7 38.4 reduce-scatter.20
  633.0 38.4 reduce-scatter.14
  674.9 61.7 reduce-scatter.16
  740.4 61.7 reduce-scatter.18
  805.4 61.7 reduce-scatter.12
  875.9 123.4 all-reduce.10
  1002.1 117.7 all-reduce.12
where the time goes:
time: 1150 us; the launch traced here: 1140 us
  waiting for transfers between devices  404 us (35%)
  local copies, waits for them, and re-layouts  392 us (34%)
  matrix products  218 us (19%)
  other arithmetic  92.1 us (8%)
  between operations  17.6 us (2%)
  starting transfers between devices  15.4 us (1%)
    unnamed x475, local copies, waits for them, and re-layouts  147 us
    psum x1, waiting for transfers between devices, per_device(): lax.psum((stacked[0], stacked[1], stacked[2], stacked[6], stacked[8], gra...  130 us
    psum x1, waiting for transfers between devices, per_device(): lax.psum(attention_shares[0].astype(jnp.bfloat16), 'dp').astype(jnp.float32)  119 us
    reshape x6, local copies, waits for them, and re-layouts, skewed(): flattened.reshape(head_count, query_count, table_length - 1)  68.1 us
    reduce_scatter x1, waiting for transfers between devices, per_device(): lax.psum_scatter(stacked[3].astype(jnp.bfloat16), 'seq', scatter_dimensio...  65 us
    reduce_scatter x1, waiting for transfers between devices, per_device(): lax.psum_scatter(stacked[7].astype(jnp.bfloat16), 'seq', scatter_dimensio...  62.7 us
    dot_general x17, matrix products, dot_float(): jnp.dot(first_matrix, second_matrix, preferred_element_type=jnp.float32)  53.3 us
    dot_general x14, matrix products, dot_back(): jnp.einsum('rc,ec->re', first_matrix, second_matrix, preferred_element_ty...  41.7 us
  transfers between devices with their start and end apart: 18, of which 7 were waited for; matrix products, arithmetic and copies ran while one was open for 45% of the time, Pallas kernels for 0%

commit v1 on v0

v1 whole, which is shorter than its diff:
```python
from functools import partial

import jax
import jax.numpy as jnp
from jax import lax
from jax.experimental import pallas as pl
from jax.experimental.pallas import tpu as pltpu
from jax.sharding import PartitionSpec as P

D = 512
HEADS = 8
HD = 64
WIN = 256
QBLK = 384
DOCS = 8
VMEM_BYTES = 48 * 2**20
epsilon = 1e-05


LANES = 128
PAIR = 2 * HD
MASKED = -1e30


def nt(first, second):
    return lax.dot_general(
        first, second, (((1,), (1,)), ((), ())), preferred_element_type=jnp.float32
    )


def nn(first, second):
    return lax.dot_general(
        first, second, (((1,), (0,)), ((), ())), preferred_element_type=jnp.float32
    )


def tn(first, second):
    return lax.dot_general(
        first, second, (((0,), (0,)), ((), ())), preferred_element_type=jnp.float32
    )


def document(places, info):
    total = jnp.zeros(places.shape, jnp.int32)
    for index in range(DOCS):
        total = total + (places >= info[1 + index]).astype(jnp.int32)
    return total


def lanes_and_rows():
    lane = lax.broadcasted_iota(jnp.int32, (LANES, LANES), 1)
    row = lax.broadcasted_iota(jnp.int32, (LANES, LANES), 0)
    return lane, row


def turned(values, index):
    return [
        jnp.take_along_axis(values[:, m * LANES : (m + 1) * LANES], index, axis=1)
        for m in range(values.shape[1] // LANES)
    ]


def skew_window(table):
    lane, row = lanes_and_rows()
    blocks = turned(table, (lane - row + LANES) % LANES)
    out = [blocks[0]] + [
        jnp.where(lane >= row, here, before) for before, here in zip(blocks, blocks[1:])
    ]
    return jnp.concatenate(out, axis=1)


def unskew_window(scores):
    lane, row = lanes_and_rows()
    blocks = turned(scores, (lane + row) % LANES)
    blocks.append(jnp.zeros_like(blocks[0]))
    out = [
        jnp.where(lane + row < LANES, here, after) for here, after in zip(blocks, blocks[1:])
    ]
    return jnp.concatenate(out, axis=1)


def skew_pooled(table):
    lane, row = lanes_and_rows()
    here, after = turned(table, (lane + LANES - 1 - row) % LANES)
    return jnp.where(lane <= row, here, after)


def unskew_pooled(scores):
    lane, row = lanes_and_rows()
    (block,) = turned(scores, (lane + row + 1) % LANES)
    zero = jnp.zeros_like(block)
    first = lane + row >= LANES - 1
    return jnp.concatenate([jnp.where(first, block, zero), jnp.where(first, zero, block)], axis=1)


def head_lanes(rows):
    return lax.broadcasted_iota(jnp.int32, (rows, PAIR), 1) // HD


def softmax_rows(scores):
    highest = jnp.max(scores, axis=1, keepdims=True)
    powers = jnp.exp(scores - highest)
    return powers / jnp.sum(powers, axis=1, keepdims=True)


def window_mask(info, part):
    place = info[0] + part * LANES
    row = lax.broadcasted_iota(jnp.int32, (LANES, LANES + WIN), 0)
    column = lax.broadcasted_iota(jnp.int32, (LANES, LANES + WIN), 1)
    behind = row + WIN - column
    query = place + lax.broadcasted_iota(jnp.int32, (LANES, 1), 0)
    key = place - WIN + lax.broadcasted_iota(jnp.int32, (1, LANES + WIN), 1)
    same = document(query, info) == document(key, info)
    return (behind >= 0) & (behind <= WIN) & same & (key >= 0)


def pooled_mask(info, start):
    query = info[0] + lax.broadcasted_iota(jnp.int32, (LANES, 1), 0)
    key = start + lax.broadcasted_iota(jnp.int32, (1, LANES), 1)
    return (key <= query) & (document(3 * query, info) == document(3 * key, info))


def heads_forward(content, position, keys, values, table, visible, skew):
    head = head_lanes(LANES)
    weights, mixed = [], []
    for index in range(2):
        mine = head == index
        score = nt(jnp.where(mine, content, 0), keys)
        place = nt(jnp.where(mine, position, 0), table)
        score = jnp.where(visible, (score + skew(place)) * HD**-0.5, MASKED)
        weight = softmax_rows(score).astype(jnp.bfloat16)
        weights.append(weight)
        mixed.append(nn(weight, values))
    return weights, jnp.where(head == 0, mixed[0], mixed[1])


def heads_backward(content, position, keys, values, table, weights, grad, unskew):
    head = head_lanes(LANES)
    scores, places, contents, positions, grads, to_content, to_position = ([] for _ in range(7))
    for index in range(2):
        mine = head == index
        grads.append(jnp.where(mine, grad, 0))
        contents.append(jnp.where(mine, content, 0))
        positions.append(jnp.where(mine, position, 0))
        grad_weight = nt(grads[index], values)
        weight = weights[index].astype(jnp.float32)
        delta = jnp.sum(weight * grad_weight, axis=1, keepdims=True)
        score = (weight * (grad_weight - delta)).astype(jnp.bfloat16)
        place = unskew(score.astype(jnp.float32)).astype(jnp.bfloat16)
        scores.append(score)
        places.append(place)
        to_content.append(nn(score, keys))
        to_position.append(nn(place, table))
    scale = HD**-0.5
    grad_content = jnp.where(head == 0, to_content[0], to_content[1]) * scale
    grad_position = jnp.where(head == 0, to_position[0], to_position[1]) * scale

    def summed(first, second):
        return tn(jnp.concatenate(first, axis=0), jnp.concatenate(second, axis=0))

    grad_keys = summed(scores, contents) * scale
    grad_values = summed(weights, grads)
    grad_table = summed(places, positions) * scale
    return grad_content, grad_position, grad_keys, grad_values, grad_table


def window_forward_kernel(
    info, content, position, keys, values, table, mixed_ref, weights_ref
):
    for part in range(QBLK // LANES):
        rows = pl.ds(part * LANES, LANES)
        seen = pl.ds(part * LANES, LANES + WIN)
        weights, mixed = heads_forward(
            content[rows, :],
            position[rows, :],
            keys[seen, :],
            values[seen, :],
            table[...],
            window_mask(info, part),
            skew_window,
        )
        for index in range(2):
            weights_ref[index, part] = weights[index]
        mixed_ref[rows, :] = mixed.astype(jnp.bfloat16)


def window_backward_kernel(
    content,
    position,
    keys,
    values,
    table,
    weights,
    grad,
    dq_ref,
    bias_ref,
    dk_ref,
    dv_ref,
    dt_ref,
):
    dk_ref[...] = jnp.zeros_like(dk_ref)
    dv_ref[...] = jnp.zeros_like(dv_ref)
    total = jnp.zeros(table.shape, jnp.float32)
    bias = jnp.zeros((2, PAIR), jnp.float32)
    for part in range(QBLK // LANES):
        rows = pl.ds(part * LANES, LANES)
        seen = pl.ds(part * LANES, LANES + WIN)
        grad_content, grad_position, grad_keys, grad_values, grad_table = heads_backward(
            content[rows, :],
            position[rows, :],
            keys[seen, :],
            values[seen, :],
            table[...],
            [weights[0, part], weights[1, part]],
            grad[rows, :],
            unskew_window,
        )
        dq_ref[rows, :] = (grad_content + grad_position).astype(jnp.bfloat16)
        bias = bias + jnp.concatenate(
            [
                jnp.sum(grad_content, axis=0, keepdims=True),
                jnp.sum(grad_position, axis=0, keepdims=True),
            ],
            axis=0,
        )
        dk_ref[seen, :] += grad_keys
        dv_ref[seen, :] += grad_values
        total = total + grad_table
    bias_ref[...] = bias
    dt_ref[...] = total.astype(dt_ref.dtype)


def table_rows(order, block, count):
    start = order[block] + count - 1 - order[count]
    return pl.ds(pl.multiple_of(LANES * jnp.minimum(start, count - 1), LANES), 2 * LANES)


def pooled_forward_kernel(
    info, order, content, position, keys, values, table, mixed_ref, weights_ref
):
    head = head_lanes(LANES)
    count = keys.shape[0] // LANES
    mixed = []
    visible = [pooled_mask(info, LANES * order[block]) for block in range(count)]
    for index in range(2):
        mine = head == index
        here = jnp.where(mine, content[...], 0)
        there = jnp.where(mine, position[...], 0)
        scores = []
        for block in range(count):
            score = nt(here, keys[pl.ds(block * LANES, LANES), :])
            place = nt(there, table[table_rows(order, block, count), :])
            score = (score + skew_pooled(place)) * HD**-0.5
            scores.append(jnp.where(visible[block], score, MASKED))
        weight = softmax_rows(jnp.concatenate(scores, axis=1)).astype(jnp.bfloat16)
        weights_ref[index] = weight
        mixed.append(nn(weight, values[...]))
    mixed_ref[...] = jnp.where(head == 0, mixed[0], mixed[1]).astype(jnp.bfloat16)


def pooled_backward_kernel(
    order,
    content,
    position,
    keys,
    values,
    table,
    weights,
    grad,
    dq_ref,
    bias_ref,
    dk_ref,
    dv_ref,
    dt_ref,
    sum_ref,
):
    head = head_lanes(LANES)
    count = keys.shape[0] // LANES
    scale = HD**-0.5
    sum_ref[...] = jnp.zeros_like(sum_ref)
    contents, grads, positions, scores, to_content, to_position = ([] for _ in range(6))
    for index in range(2):
        mine = head == index
        contents.append(jnp.where(mine, content[...], 0))
        positions.append(jnp.where(mine, position[...], 0))
        grads.append(jnp.where(mine, grad[...], 0))
        grad_weight = nt(grads[index], values[...])
        weight = weights[index].astype(jnp.float32)
        delta = jnp.sum(weight * grad_weight, axis=1, keepdims=True)
        score = weight * (grad_weight - delta)
        scores.append(score.astype(jnp.bfloat16))
        to_content.append(nn(scores[index], keys[...]))
    positions = jnp.concatenate(positions, axis=0)
    to_position = [jnp.zeros((LANES, PAIR), jnp.float32) for _ in range(2)]
    for block in range(count):
        rows = table_rows(order, block, count)
        places = []
        for index in range(2):
            score = scores[index][:, block * LANES : (block + 1) * LANES]
            place = unskew_pooled(score.astype(jnp.float32)).astype(jnp.bfloat16)
            to_position[index] = to_position[index] + nn(place, table[rows, :])
            places.append(place)
        sum_ref[rows, :] += tn(jnp.concatenate(places, axis=0), positions)
    grad_content = jnp.where(head == 0, to_content[0], to_content[1]) * scale
    grad_position = jnp.where(head == 0, to_position[0], to_position[1]) * scale
    grad_keys = tn(jnp.concatenate(scores, axis=0), jnp.concatenate(contents, axis=0)) * scale
    grad_values = tn(
        jnp.concatenate([weights[0], weights[1]], axis=0), jnp.concatenate(grads, axis=0)
    )
    dq_ref[...] = (grad_content + grad_position).astype(jnp.bfloat16)
    bias_ref[...] = jnp.concatenate(
        [
            jnp.sum(grad_content, axis=0, keepdims=True),
            jnp.sum(grad_position, axis=0, keepdims=True),
        ],
        axis=0,
    )
    dk_ref[...] = grad_keys.astype(dk_ref.dtype)
    dv_ref[...] = grad_values.astype(dv_ref.dtype)
    dt_ref[...] = (sum_ref[...] * scale).astype(dt_ref.dtype)


def by_pair(array):
    return pl.BlockSpec((array.shape[0], PAIR), lambda pair: (0, pair))


def weights_block(shape):
    return pl.BlockSpec((2,) + shape[1:], lambda pair: (pair,) + (0,) * (len(shape) - 1))


def attention_forward(kernel, scalars, operands, weights_shape):
    content = operands[0]
    return pl.pallas_call(
        kernel,
        grid=(HEADS // 2,),
        in_specs=[pl.BlockSpec(memory_space=pltpu.SMEM)] * len(scalars)
        + [by_pair(a) for a in operands],
        out_specs=[by_pair(content), weights_block(weights_shape)],
        out_shape=[
            jax.ShapeDtypeStruct(content.shape, jnp.bfloat16),
            jax.ShapeDtypeStruct(weights_shape, jnp.bfloat16),
        ],
        compiler_params=pltpu.CompilerParams(vmem_limit_bytes=VMEM_BYTES),
    )(*scalars, *operands)


def attention_backward(kernel, scalars, operands, weights, grad, types, scratch=()):
    content, _, keys, values, table = operands
    bias = jax.ShapeDtypeStruct((2, D), jnp.float32)
    summed = [jax.ShapeDtypeStruct(a.shape, t) for a, t in zip((keys, values, table), types)]
    return pl.pallas_call(
        kernel,
        grid=(HEADS // 2,),
        in_specs=[pl.BlockSpec(memory_space=pltpu.SMEM)] * len(scalars)
        + [by_pair(a) for a in operands]
        + [weights_block(weights.shape), by_pair(grad)],
        out_specs=[by_pair(content), by_pair(bias)] + [by_pair(a) for a in summed],
        out_shape=[jax.ShapeDtypeStruct(content.shape, jnp.bfloat16), bias] + summed,
        scratch_shapes=scratch,
        compiler_params=pltpu.CompilerParams(vmem_limit_bytes=VMEM_BYTES),
    )(*scalars, *operands, weights, grad)


def crossed(block, axis, bit):
    count = lax.axis_size(axis)
    return lax.ppermute(block, axis, [(index, index ^ bit) for index in range(count)])


def both(low, high, bit):
    return jnp.where(bit, high, low), jnp.where(bit, low, high)


def halves(matrix, bit):
    middle = matrix.shape[1] // 2
    return both(matrix[:, :middle], matrix[:, middle:], bit)


def rounded_sum(*terms):
    return sum(term.astype(jnp.float32) for term in terms).astype(jnp.bfloat16)


def gather_pooled(rows):
    half = rows.shape[0] // 2
    from_x = crossed(rows, "seq", 2)
    from_y = crossed(rows, "seq", 4)
    from_core = crossed(rows, "seq", 1)
    first = crossed(from_x[:half], "seq", 4)
    second = crossed(from_y[half:], "seq", 2)
    core_x = crossed(from_x, "seq", 1)
    core_y = crossed(from_y, "seq", 1)
    opposite = jnp.concatenate([first, second], axis=0)
    core_opposite = crossed(opposite, "seq", 1)
    return jnp.concatenate(
        [rows, from_core, from_x, core_x, from_y, core_y, opposite, core_opposite], axis=0
    )


def scatter_pooled(rows):
    count = rows.shape[0] // 8
    blocks = rows.reshape(4, 2, count, rows.shape[1])
    arrived = crossed(blocks[:, 1], "seq", 1)
    blocks = rounded_sum(blocks[:, 0], arrived)
    middle = rows.shape[1] // 2
    left, right = blocks[:, :, :middle], blocks[:, :, middle:]
    left_arrived = crossed(jnp.stack([left[1], left[3]]), "seq", 2)
    right_arrived = crossed(right[2:], "seq", 4)
    left_next = crossed(rounded_sum(left[2], left_arrived[1]), "seq", 4)
    right_next = crossed(rounded_sum(right[1], right_arrived[1]), "seq", 2)
    sums = [
        left[0].astype(jnp.float32)
        + left_arrived[0].astype(jnp.float32)
        + left_next.astype(jnp.float32),
        right[0].astype(jnp.float32)
        + right_arrived[0].astype(jnp.float32)
        + right_next.astype(jnp.float32),
    ]
    return jnp.concatenate(sums, axis=1)


def piece_lanes(piece):
    features, columns = piece[0].shape[1], piece[2].shape[1] * 2
    return features // D * (columns // 4)


def pair_kernel(count, place, *refs):
    inputs, (keep_one, send_one, keep_two, send_two) = refs[: 4 * count], refs[4 * count :]
    offset = 0
    for index in range(count):
        own_x, pair_x, own_dy, pair_dy = inputs[4 * index : 4 * index + 4]
        height = own_x.shape[1] // 4
        quarter = own_dy.shape[1] // 2
        groups = height // LANES
        for block in range(4):
            columns = pl.ds(pl.multiple_of((place[0] ^ block) * height, LANES), height)
            total = tn(own_x[:, columns], own_dy[...]) + tn(pair_x[:, columns], pair_dy[...])
            total = total.astype(jnp.bfloat16)
            first = (keep_one, send_one)[block % 2]
            second = (keep_two, send_two)[block // 2]
            for out, slot, lanes in (
                (first, block // 2, total[:, :quarter]),
                (second, block % 2, total[:, quarter:]),
            ):
                if groups == 1:
                    out[slot, :, offset : offset + quarter] = lanes
                else:
                    for group in range(groups):
                        start = offset + quarter * group
                        low = HD * group
                        high = height // 2 + low
                        out[slot, :HD, start : start + quarter] = lanes[low : low + HD]
                        out[slot, HD:, start : start + quarter] = lanes[high : high + HD]
        offset += groups * quarter


def pair_gradients(place, pieces):
    lanes = sum(piece_lanes(piece) for piece in pieces)
    out = jax.ShapeDtypeStruct((2, LANES, lanes), jnp.bfloat16)
    operands = [array for piece in pieces for array in piece]
    return pl.pallas_call(
        partial(pair_kernel, len(pieces)),
        in_specs=[pl.BlockSpec(memory_space=pltpu.SMEM)]
        + [pl.BlockSpec(memory_space=pltpu.VMEM)] * len(operands),
        out_specs=[pl.BlockSpec(memory_space=pltpu.VMEM)] * 4,
        out_shape=[out] * 4,
        compiler_params=pltpu.CompilerParams(vmem_limit_bytes=VMEM_BYTES),
    )(place, *operands)


def reduced(pieces, place, core, depth):
    keep_one, send_one, keep_two, send_two = pair_gradients(place, pieces)
    one = crossed(send_one, "seq", 2)
    two = crossed(send_two, "seq", 4)
    next_one = crossed(rounded_sum(keep_one[1], one[1]), "seq", 4)
    next_two = crossed(rounded_sum(keep_two[1], two[1]), "seq", 2)
    first = rounded_sum(keep_one[0], one[0], next_one)
    second = rounded_sum(keep_two[0], two[0], next_two)
    keep, send = both(first, second, depth)
    keep = rounded_sum(keep, crossed(send, "dp", 1))
    keep = rounded_sum(keep, crossed(keep, "dp", 2))
    other = crossed(keep, "dp", 1)
    first, second = both(keep, other, depth)
    share = jnp.concatenate([first, second], axis=1)
    keep, send = both(share[:HD], share[HD:], core)
    return both(keep, crossed(send, "seq", 1), core)


def final_kernel(plan, *refs):
    groups = len(plan)
    buffers, outs = refs[: 2 * groups], refs[2 * groups :]
    for index, pieces in enumerate(plan):
        lanes = buffers[2 * index].shape[1] // 2
        offset = 0
        for out_index, layer, first_column, columns, height in pieces:
            out = outs[out_index]
            quarter = columns // 4
            for group in range(height // HD):
                rows = pl.ds(HD * group, HD)
                for part in range(4):
                    buffer = buffers[2 * index + part // 2]
                    start = (part % 2) * lanes + offset
                    value = buffer[:, start : start + quarter].astype(jnp.float32)
                    begin = first_column + part * quarter
                    if layer is None:
                        out[rows, begin : begin + quarter] = value
                    else:
                        out[layer, rows, begin : begin + quarter] = value
                offset += quarter


def final_outputs(plan, buffers, shapes):
    flat = [array for pair in buffers for array in pair]
    return pl.pallas_call(
        partial(final_kernel, plan),
        in_specs=[pl.BlockSpec(memory_space=pltpu.VMEM)] * len(flat),
        out_specs=[pl.BlockSpec(memory_space=pltpu.VMEM)] * len(shapes),
        out_shape=[jax.ShapeDtypeStruct(shape, jnp.float32) for shape in shapes],
        compiler_params=pltpu.CompilerParams(vmem_limit_bytes=VMEM_BYTES),
    )(*flat)


def summed_everywhere(values):
    flat = jnp.concatenate([value.reshape(-1) for value in values])
    size = flat.shape[0]
    rows = -(-size // (8 * LANES)) * 8
    flat = jnp.pad(flat, (0, rows * LANES - size)).reshape(rows, LANES)
    for axis in ("seq", "dp"):
        count = lax.axis_size(axis)
        for bit in range(count.bit_length() - 1):
            flat = flat + crossed(flat, axis, 1 << bit)
    flat = flat.reshape(-1)
    out, start = [], 0
    for value in values:
        out.append(flat[start : start + value.size].reshape(value.shape))
        start += value.size
    return out


def passed_along(block, axis, distance):
    devices = range(lax.axis_size(axis))
    route = [(i - distance, i) for i in devices if i - distance in devices]
    return lax.ppermute(block, axis, route)


def layer_norm(values, scaling, offset):
    centre = values - jnp.mean(values, axis=-1, keepdims=True)
    spread = jnp.mean(centre * centre, axis=-1, keepdims=True)
    return centre * lax.rsqrt(spread + epsilon) * scaling + offset


def sinusoid(distance):
    halfway = D // 2
    frequency = jnp.power(10000.0, -2.0 * jnp.arange(halfway, dtype=jnp.float32) / D)
    phases = distance[:, None] * frequency[None, :]
    return jnp.concatenate([jnp.sin(phases), jnp.cos(phases)], axis=1)


def embedding(first, count):
    distance = first - jnp.arange(count)
    return sinusoid(distance.astype(jnp.float32)).astype(jnp.bfloat16)


def document_of(places, ending):
    return jnp.sum((places[:, None] >= ending[None, :]).astype(jnp.int32), axis=1)


def dot_float(first_matrix, second_matrix):
    return jnp.dot(first_matrix, second_matrix, preferred_element_type=jnp.float32)


def outer_float(first_matrix, second_matrix):
    return jnp.einsum("rc,re->ce", first_matrix, second_matrix, preferred_element_type=jnp.float32)


def dot_back(first_matrix, second_matrix):
    return jnp.einsum("rc,ec->re", first_matrix, second_matrix, preferred_element_type=jnp.float32)


class Window:
    def __init__(self, start, ends, table):
        self.info = jnp.concatenate([start[None], ends]).astype(jnp.int32)
        self.embedded = table

    def forward(self, content, position, keys, values, weight):
        border = passed_along(jnp.stack([keys[-WIN:], values[-WIN:]]), "seq", 1)
        keys_all = jnp.concatenate([border[0], keys], axis=0)
        values_all = jnp.concatenate([border[1], values], axis=0)
        table = dot_float(self.embedded, weight).astype(jnp.bfloat16)
        operands = (content, position, keys_all, values_all, table)
        shape = (HEADS, QBLK // LANES, LANES, LANES + WIN)
        mixed, weights = attention_forward(window_forward_kernel, [self.info], operands, shape)
        return mixed, (operands, weights)

    def backward(self, stored, grad):
        operands, weights = stored
        types = (jnp.float32, jnp.float32, jnp.bfloat16)
        dq, bias, dk, dv, dt = attention_backward(
            window_backward_kernel, [], operands, weights, grad, types
        )
        returned = passed_along(
            jnp.stack([dk[:WIN], dv[:WIN]]).astype(jnp.bfloat16), "seq", -1
        ).astype(jnp.float32)
        rest = QBLK - WIN
        dk = jnp.concatenate([dk[WIN : WIN + rest], dk[WIN + rest :] + returned[0]], axis=0)
        dv = jnp.concatenate([dv[WIN : WIN + rest], dv[WIN + rest :] + returned[1]], axis=0)
        return dq, bias, dk.astype(jnp.bfloat16), dv.astype(jnp.bfloat16), dt


class Pooled:
    def __init__(self, device, count, rows, ends, crossing):
        self.crossing = crossing
        order = jnp.arange(count)
        if crossing:
            order = order ^ device
        self.order = jnp.concatenate([order, device[None]]).astype(jnp.int32)
        self.info = jnp.concatenate([device[None] * rows, ends]).astype(jnp.int32)
        self.embedded = embedding(count * rows - 1, (count + 1) * rows)

    def forward(self, content, position, keys, values, weight):
        both_rows = jnp.concatenate([keys, values], axis=1)
        if self.crossing:
            both_rows = gather_pooled(both_rows)
        else:
            both_rows = lax.all_gather(both_rows, "seq", axis=0, tiled=True)
        table = dot_float(self.embedded, weight).astype(jnp.bfloat16)
        operands = (content, position, both_rows[:, :D], both_rows[:, D:], table)
        shape = (HEADS, LANES, both_rows.shape[0])
        mixed, weights = attention_forward(
            pooled_forward_kernel, [self.info, self.order], operands, shape
        )
        return mixed, (operands, weights)

    def backward(self, stored, grad):
        operands, weights = stored
        types = (jnp.bfloat16,) * 3
        scratch = [pltpu.VMEM((operands[4].shape[0], PAIR), jnp.float32)]
        dq, bias, dk, dv, dt = attention_backward(
            pooled_backward_kernel, [self.order], operands, weights, grad, types, scratch
        )
        joined = jnp.concatenate([dk, dv], axis=1)
        if self.crossing:
            joined = scatter_pooled(joined)
        else:
            joined = lax.psum_scatter(joined, "seq", scatter_dimension=0, tiled=True)
        joined = joined.astype(jnp.bfloat16)
        return dq, bias, joined[:, :D], joined[:, D:], dt


def block_forward(inputs, layer, params, attention):
    gain, shift, bias, w_in, w_out, w_expand, b_expand, w_contract, b_contract = params
    layer_in = w_in[layer]
    normed = layer_norm(inputs, gain[layer, 0], shift[layer, 0]).astype(jnp.bfloat16)
    projected = dot_float(normed, layer_in[:, : 3 * D])
    queries = projected[:, :D]
    keys = projected[:, D : 2 * D].astype(jnp.bfloat16)
    values = projected[:, 2 * D :].astype(jnp.bfloat16)
    content = (queries + bias[layer, 0]).astype(jnp.bfloat16)
    position = (queries + bias[layer, 1]).astype(jnp.bfloat16)
    mixed, kept = attention.forward(content, position, keys, values, layer_in[:, 3 * D :])
    middle = inputs + dot_float(mixed, w_out[layer])
    normed_two = layer_norm(middle, gain[layer, 1], shift[layer, 1]).astype(jnp.bfloat16)
    expanded = dot_float(normed_two, w_expand[layer]) + b_expand[layer]
    activated = jax.nn.gelu(expanded, approximate=False).astype(jnp.bfloat16)
    result = middle + dot_float(activated, w_contract[layer]) + b_contract[layer]
    return result, (inputs, normed, kept, mixed, middle, normed_two, expanded, activated)


def norm_backward(inputs, gain, shift, grad):
    pull = jax.vjp(layer_norm, inputs, gain.astype(jnp.float32), shift.astype(jnp.float32))[1]
    return pull(grad)


def block_backward(grad_result, layer, params, stored, attention, near):
    gain, shift, bias, w_in, w_out, w_expand, b_expand, w_contract, b_contract = params
    inputs, normed, kept, mixed, middle, normed_two, expanded, activated = stored
    layer_in = w_in[layer]
    branch = grad_result.astype(jnp.bfloat16)
    contract_bias = jnp.sum(branch.astype(jnp.float32), axis=0)
    grad_activated = dot_back(branch, w_contract[layer])
    gelu_pull = jax.vjp(lambda value: jax.nn.gelu(value, approximate=False), expanded)[1]
    grad_expanded = gelu_pull(grad_activated)[0].astype(jnp.bfloat16)
    expand_bias = jnp.sum(grad_expanded.astype(jnp.float32), axis=0)
    grad_normed_two = dot_back(grad_expanded, w_expand[layer])
    grad_norm, gain_two, shift_two = norm_backward(
        middle, gain[layer, 1], shift[layer, 1], grad_normed_two
    )
    grad_middle = grad_result + grad_norm
    grad_attend = grad_middle.astype(jnp.bfloat16)
    grad_mixed = dot_back(grad_attend, w_out[layer]).astype(jnp.bfloat16)
    dq, bias_pair, dk, dv, dt = attention.backward(kept, grad_mixed)
    grad_projected = jnp.concatenate([dq, dk, dv], axis=1)
    grad_normed = dot_back(grad_projected, layer_in[:, : 3 * D])
    grad_norm, gain_one, shift_one = norm_backward(
        inputs, gain[layer, 0], shift[layer, 0], grad_normed
    )
    small = (
        jnp.stack([gain_one, gain_two]),
        jnp.stack([shift_one, shift_two]),
        bias_pair,
        expand_bias,
        contract_bias,
    )
    early = [near(normed_two, grad_expanded), near(activated, branch), near(mixed, grad_attend)]
    late = [near(normed, grad_projected), near(attention.embedded, dt)]
    return grad_middle + grad_norm, small, early, late


def summed_pieces(groups, shapes, core, depth):
    place = (lax.axis_index("seq") // 2).astype(jnp.int32)[None]
    plan, buffers = [], []
    for pieces, targets in groups:
        plan.append(targets)
        buffers.append(reduced(pieces, place, core, depth))
    return final_outputs(plan, buffers, shapes)


def summed_plainly(groups, shapes):
    count = lax.axis_size("seq")
    outs = [[] for _ in shapes]
    for pieces, targets in groups:
        for (features, grad), (index, layer, first, columns, _) in zip(pieces, targets):
            total = outer_float(features, grad).astype(jnp.bfloat16)
            total = lax.psum_scatter(total, "seq", scatter_dimension=0, tiled=True)
            total = lax.psum(total, "dp").astype(jnp.float32)
            outs[index].append((layer, first, total))
    results = []
    for parts in outs:
        layers = []
        for layer in sorted({part[0] for part in parts}):
            chosen = sorted((p for p in parts if p[0] == layer), key=lambda p: p[1])
            layers.append(jnp.concatenate([p[2] for p in chosen], axis=1))
        results.append(jnp.stack(layers))
    return results


def per_device(
    tokens,
    doc_lengths,
    cotangent,
    norm_gain,
    norm_shift,
    relative_bias,
    attention_in,
    attention_out,
    expand_weight,
    expand_bias,
    contract_weight,
    contract_bias,
    pool_weight,
    pool_bias,
    upsample_weight,
    upsample_bias,
):
    def by_layer(weight):
        return jnp.transpose(weight, (1, 0, 2))

    params = (
        norm_gain,
        norm_shift,
        relative_bias,
        by_layer(attention_in),
        by_layer(attention_out),
        by_layer(expand_weight),
        expand_bias,
        by_layer(contract_weight),
        contract_bias,
    )
    inputs = tokens[0].astype(jnp.float32)
    row_count = inputs.shape[0]
    pooled_count = row_count // 3
    device = lax.axis_index("seq").astype(jnp.int32)
    seq_count = lax.axis_size("seq")
    usual = seq_count == 8 and lax.axis_size("dp") == 4
    core = device % 2 == 1
    depth = lax.axis_index("dp") % 2 == 1
    ends = jnp.cumsum(doc_lengths[0]).astype(jnp.int32)
    token_start = device * row_count
    token_place = token_start + jnp.arange(row_count)
    window = Window(token_start, ends, embedding(WIN, QBLK))
    pooled_level = Pooled(device, seq_count, pooled_count, ends, usual)

    def near(features, grad):
        if not usual:
            return features, grad
        own, other = halves(grad, core)
        return features, crossed(features, "seq", 1), own, crossed(other, "seq", 1)

    first_out, first_stored = block_forward(inputs, 0, params, window)
    first_low = first_out.astype(jnp.bfloat16)
    edge_rows = passed_along(first_low[row_count - 2 :], "seq", 1)
    keep_mask = (token_place >= 2) & (
        document_of(token_place - 2, ends) == document_of(token_place, ends)
    )
    shifted = jnp.concatenate([edge_rows, first_low[: row_count - 2]], axis=0)
    shifted = jnp.where(keep_mask[:, None], shifted, jnp.zeros_like(shifted))
    grouped = shifted.reshape(pooled_count, 3 * D)
    pooled = dot_float(grouped, pool_weight) + pool_bias
    short_out, short_stored = block_forward(pooled, 1, params, pooled_level)
    short_low = short_out.astype(jnp.bfloat16)
    upsampled = (dot_float(short_low, upsample_weight) + upsample_bias).reshape(row_count, D)
    output, last_stored = block_forward(first_out + upsampled, 2, params, window)
    level_squares = jnp.stack(
        [jnp.sum(first_out * first_out), jnp.sum(short_out * short_out), jnp.sum(output * output)]
    )

    grad_joined, small_last, early_last, late_last = block_backward(
        cotangent[0].astype(jnp.float32), 2, params, last_stored, window, near
    )
    grad_upsampled = grad_joined.reshape(pooled_count, 3 * D).astype(jnp.bfloat16)
    grad_upsample_bias = jnp.sum(grad_upsampled.astype(jnp.float32), axis=0)
    grad_short = dot_back(grad_upsampled, upsample_weight)
    grad_pooled, small_short, early_short, late_short = block_backward(
        grad_short, 1, params, short_stored, pooled_level, near
    )
    grad_pooled_low = grad_pooled.astype(jnp.bfloat16)
    grad_pool_bias = jnp.sum(grad_pooled_low.astype(jnp.float32), axis=0)
    grad_shifted = dot_back(grad_pooled_low, pool_weight).reshape(row_count, D)
    grad_shifted = jnp.where(keep_mask[:, None], grad_shifted, 0.0)
    came_back = passed_along(grad_shifted[:2], "seq", -1)
    grad_first = grad_joined + jnp.concatenate([grad_shifted[2:], came_back], axis=0)
    grad_inputs, small_first, early_first, late_first = block_backward(
        grad_first, 0, params, first_stored, window, near
    )

    share = D // seq_count
    shapes = [
        (3, share, 4 * D),
        (3, share, D),
        (3, share, 4 * D),
        (3, 4 * share, D),
        (3 * share, D),
        (share, 3 * D),
    ]

    def early(layer):
        return [(2, layer, 0, 4 * D, share), (3, layer, 0, D, 4 * share), (1, layer, 0, D, share)]

    def late(layer):
        return [(0, layer, 0, 3 * D, share), (0, layer, 3 * D, D, share)]

    groups = [
        (
            early_last + late_last + [near(short_low, grad_upsampled)],
            early(2) + late(2) + [(5, None, 0, 3 * D, share)],
        ),
        (
            early_short + late_short + [near(grouped, grad_pooled_low)],
            early(1) + late(1) + [(4, None, 0, D, 3 * share)],
        ),
        (early_first, early(0)),
        (late_first, late(0)),
    ]
    if usual:
        sums = summed_pieces(groups, shapes, core, depth)
    else:
        groups = [
            (pieces, [(i, l or 0, f, c, h) for i, l, f, c, h in targets])
            for pieces, targets in groups
        ]
        sums = summed_plainly(groups, shapes)
        sums[4], sums[5] = sums[4][0], sums[5][0]
    in_grad, out_grad, expand_grad, contract_grad = [by_layer(total) for total in sums[:4]]
    small = [jnp.stack(parts) for parts in zip(small_first, small_short, small_last)]
    small_sums = summed_everywhere(small + [grad_pool_bias, grad_upsample_bias, level_squares])
    whole_rows = lax.axis_size("dp") * seq_count * row_count * D
    counts = jnp.array([whole_rows, whole_rows // 3, whole_rows], jnp.float32)
    rms = jnp.sqrt(small_sums[7] / counts)
    return (
        output[None].astype(jnp.bfloat16),
        grad_inputs[None].astype(jnp.bfloat16),
        small_sums[0],
        small_sums[1],
        small_sums[2],
        in_grad,
        out_grad,
        expand_grad,
        small_sums[3],
        contract_grad,
        small_sums[4],
        sums[4],
        small_sums[5],
        sums[5],
        small_sums[6],
        rms,
    )


def solution(mesh):
    rows = P("dp", "seq", None)
    in_specs = (rows, P("dp", None), rows) + (P(),) * 13
    split = P("seq", None, None)
    flat = P("seq", None)
    out_specs = (rows, rows, P(), P(), P(), split, split, split, P(), split, P())
    out_specs += (flat, P(), flat, P(), P())
    return jax.shard_map(
        per_device, mesh=mesh, in_specs=in_specs, out_specs=out_specs, check_vma=False
    )
```

time: 1150 us -> 567 us (0.49)
  local copies, waits for them, and re-layouts: 392 us -> 49.4 us
  waiting for transfers between devices: 404 us -> 147 us
  matrix products: 218 us -> 87.4 us
  Pallas kernels: 0 us -> 106 us
  starting transfers between devices: 15.4 us -> 85.3 us
  other arithmetic: 92.1 us -> 76.6 us
  between operations: 17.6 us -> 4.43 us
    psum x2 -> x0, waiting for transfers between devices: 249 us -> none  [the longest x1 130 us: per_device(): lax.psum((stacked[0], stacked[1], stacked[2], stacked[6], stacked[8], gra...]
    ppermute x0 -> x83, waiting for transfers between devices: none -> 147 us  [crossed(): lax.ppermute(block, axis, [(index, index ^ bit) for index in range(count)])]
    reduce_scatter x6 -> x0, waiting for transfers between devices: 128 us -> none  [the longest x1 65 us: per_device(): lax.psum_scatter(stacked[3].astype(jnp.bfloat16), 'seq', scatter_dimensio...]
    unnamed x475 -> x457, local copies, waits for them, and re-layouts: 147 us -> 20.7 us
    dot_general x44 -> x0, matrix products: 123 us -> none  [the longest x17 24.2 us: outer_float(): jnp.einsum('rc,re->ce', first_matrix, second_matrix, preferred_element_ty...]
    pallas_call x0 -> x11, Pallas kernels: none -> 106 us  [the longest x3 40.3 us: attention_backward(): pl.pallas_call(kernel, grid=(HEADS // 2,), in_specs=[pl.BlockSpec(memory_...]
    reshape x9 -> x8, local copies, waits for them, and re-layouts: 100 us -> 5.23 us  [the longest x5 3.06 us: summed_everywhere(): out.append(flat[start:start + value.size].reshape(value.shape))]
    ppermute x0 -> x83, starting transfers between devices: none -> 72 us  [crossed(): lax.ppermute(block, axis, [(index, index ^ bit) for index in range(count)])]
  transfers between devices with their start and end apart: 18 -> 89, of which waited for: 7 -> 28; matrix products, arithmetic and copies ran while one was open for 45% -> 32% of each run, Pallas kernels for 0% -> 19%
where the time goes in v1:
time: 567 us; the launch traced here: 556 us
  waiting for transfers between devices  147 us (26%)
  Pallas kernels  106 us (19%)
  matrix products  87.4 us (15%)
  starting transfers between devices  85.3 us (15%)
  other arithmetic  76.6 us (14%)
  local copies, waits for them, and re-layouts  49.4 us (9%)
    ppermute x83, waiting for transfers between devices, crossed(): lax.ppermute(block, axis, [(index, index ^ bit) for index in range(count)])  147 us
    ppermute x83, starting transfers between devices, crossed(): lax.ppermute(block, axis, [(index, index ^ bit) for index in range(count)])  72 us
    dot_general x17, matrix products, dot_float(): jnp.dot(first_matrix, second_matrix, preferred_element_type=jnp.float32)  54.2 us
    pallas_call x3, Pallas kernels, attention_backward(): pl.pallas_call(kernel, grid=(HEADS // 2,), in_specs=[pl.BlockSpec(memory_...  40.3 us
    pallas_call x3, Pallas kernels, attention_forward(): pl.pallas_call(kernel, grid=(HEADS // 2,), in_specs=[pl.BlockSpec(memory_...  39 us
    dot_general x14, matrix products, dot_back(): jnp.einsum('rc,ec->re', first_matrix, second_matrix, preferred_element_ty...  33.2 us
    pallas_call x4, Pallas kernels, pair_gradients(): pl.pallas_call(partial(pair_kernel, len(pieces)), in_specs=[pl.BlockSpec(...  23.7 us
    unnamed x457, local copies, waits for them, and re-layouts  20.7 us
  transfers between devices with their start and end apart: 89, of which 28 were waited for; matrix products, arithmetic and copies ran while one was open for 32% of the time, Pallas kernels for 19%

profile of v1, /device:TPU:0, one launch (start us, length us, event | category | flops | bytes accessed | tf_op | source)
XLA Modules:
  0.0 555.9 jit_solution(2609017604432510952)
XLA Ops:
  6.0 6.1 %slice_bitcast_fusion.2 = (bf16[512,2048]{1,0:T(8,128)(2,1)}, bf16[512,2048]{1,0:T(8,128)(2,1)}, bf16[512,2048]{1,0:T(8,128)(2,1)S(1)}) fusion(bf16[3,512,2048]{2,1,0:T(8,128)(2,1)} %bitcast.417), kind=kLoop, calls=%fused_computation.43 | loop fusion | bytes 12582912 | tf_op jit(solution)/shard_map/squeeze | solution.py:650
  16.4 3.2 collective-permute-start
  30.7 4.8 fusion.38
  42.8 13.7 %shard_map.288 = (bf16[384,512]{1,0:T(8,128)(2,1)S(1)}, bf16[8,3,128,384]{3,2,1,0:T(8,128)(2,1)S(1)}) custom-call(s32[9]{0:T(128)S(1)} %get-tuple-element.279.info, bf16[384,512]{1,0:T(8,128)(2,1)S(1)} %get-tuple-element.161.content, bf16[384,512]{1,0:T(8,128)(2,1)S(1)} %get-tuple-element.160.position, bf16[640,512]{1,0:T(8,128)(2,1)S(1)} %get-tuple-element.313.keys, ...), custom_call_target="tpu_custom_call" | custom-call | tf_op jit(solution)/shard_map/pallas_call | solution.py:333
  59.0 10.4 %multiply_convert_fusion.1 = (bf16[384,2048]{1,0:T(8,128)(2,1)S(1)}, f32[384,2048]{1,0:T(8,128)}, f32[384,2048]{1,0:T(8,128)}) fusion(f32[2048]{0:T(1024)S(1)} %bitcast.470, bf16[384,512]{1,0:T(8,128)(2,1)S(1)} %add_convert_fusion.16.refs_0_, bf16[3,512,2048]{2,1,0:T(8,128)(2,1)} %bitcast.494), kind=kOutput, calls=%fused_computation.21 | convolution fusion | flops 857210880 | bytes 10362880 | tf_op jit(solution)/shard_map/dot_general | solution.py:567
  69.5 4.0 fusion.161
  73.6 2.9 collective-permute-start.1
  85.6 5.6 %collective-permute-done.3 = bf16[128,1024]{1,0:T(8,128)(2,1)S(1)} collective-permute-done((bf16[128,1024]{1,0:T(8,128)(2,1)S(1)}, bf16[128,1024]{1,0:T(8,128)(2,1)S(1)}, u32[]{:S(2)}, u32[]{:S(2)}) %collective-permute-start.3) | collective-permute-done | bytes 262176 | tf_op jit(solution)/shard_map/ppermute | solution.py:366
  93.1 3.4 collective-permute-done.7
  99.3 11.5 %shard_map.289 = (bf16[128,512]{1,0:T(8,128)(2,1)}, bf16[8,128,1024]{2,1,0:T(8,128)(2,1)S(1)}) custom-call(s32[9]{0:T(128)S(1)} %get-tuple-element.278.info, s32[9]{0:T(128)S(1)} %pad_add_fusion.2.order, bf16[128,512]{1,0:T(8,128)(2,1)S(1)} %get-tuple-element.206.content, bf16[128,512]{1,0:T(8,128)(2,1)S(1)} %get-tuple-element.205.position, ...), custom_call_target="tpu_custom_call" | custom-call | tf_op jit(solution)/shard_map/pallas_call | solution.py:333
  113.9 5.6 %multiply_convert_fusion.2 = (bf16[128,2048]{1,0:T(8,128)(2,1)}, f32[128,2048]{1,0:T(8,128)}, f32[128,2048]{1,0:T(8,128)}) fusion(f32[2048]{0:T(1024)S(1)} %bitcast.469, bf16[128,512]{1,0:T(8,128)(2,1)} %add_convert_fusion.30.refs_0_, bf16[3,512,2048]{2,1,0:T(8,128)(2,1)} %bitcast.495), kind=kOutput, calls=%fused_computation.142 | convolution fusion | flops 285736960 | bytes 4857856 | tf_op jit(solution)/shard_map/dot_general | solution.py:567
  119.5 2.9 multiply_reduce_fusion.11
  134.1 3.0 collective-permute-start.10
  142.5 13.7 %shard_map.290 = (bf16[384,512]{1,0:T(8,128)(2,1)S(1)}, bf16[8,3,128,384]{3,2,1,0:T(8,128)(2,1)S(1)}) custom-call(s32[9]{0:T(128)S(1)} %get-tuple-element.279.info, bf16[384,512]{1,0:T(8,128)(2,1)S(1)} %get-tuple-element.159.content, bf16[384,512]{1,0:T(8,128)(2,1)S(1)} %get-tuple-element.158.position, bf16[640,512]{1,0:T(8,128)(2,1)S(1)} %pad_maximum_fusion.4.keys, ...), custom_call_target="tpu_custom_call" | custom-call | tf_op jit(solution)/shard_map/pallas_call | solution.py:333
  157.2 9.7 %multiply_convert_fusion = (bf16[384,2048]{1,0:T(8,128)(2,1)}, f32[384,2048]{1,0:T(8,128)S(1)}, f32[384,2048]{1,0:T(8,128)S(1)}) fusion(f32[2048]{0:T(1024)S(1)} %bitcast.468, bf16[384,512]{1,0:T(8,128)(2,1)S(1)} %add_convert_fusion.12.refs_0_, bf16[3,512,2048]{2,1,0:T(8,128)(2,1)} %bitcast.496), kind=kOutput, calls=%fused_computation.8 | convolution fusion | flops 857210880 | bytes 10362880 | tf_op jit(solution)/shard_map/dot_general | solution.py:567
  166.9 4.1 convert_reduce_fusion
  170.9 4.0 multiply_reduce_fusion.2
  176.4 14.3 %shard_map.291 = (bf16[384,512]{1,0:T(8,128)(2,1)S(1)}, f32[2,512]{1,0:T(2,128)S(1)}, f32[640,512]{1,0:T(8,128)S(1)}, f32[640,512]{1,0:T(8,128)}, bf16[384,512]{1,0:T(8,128)(2,1)S(1)}) custom-call(bf16[384,512]{1,0:T(8,128)(2,1)S(1)} %get-tuple-element.159.content, bf16[384,512]{1,0:T(8,128)(2,1)S(1)} %get-tuple-element.158.position, ...), custom_call_target="tpu_custom_call" | custom-call | tf_op jit(solution)/shard_map/pallas_call | solution.py:351
  196.5 3.9 multiply_reduce_fusion
  209.7 3.2 convert_reduce_fusion.2
  212.9 3.2 multiply_reduce_fusion.12
  217.8 12.0 %shard_map.292 = (bf16[128,512]{1,0:T(8,128)(2,1)S(1)}, f32[2,512]{1,0:T(2,128)S(1)}, bf16[1024,512]{1,0:T(8,128)(2,1)S(1)}, bf16[1024,512]{1,0:T(8,128)(2,1)S(1)}, bf16[1152,512]{1,0:T(8,128)(2,1)S(1)}) custom-call(s32[9]{0:T(128)S(1)} %pad_add_fusion.2.order, bf16[128,512]{1,0:T(8,128)(2,1)S(1)} %copy-done.39, ...), custom_call_target="tpu_custom_call" | custom-call | tf_op jit(solution)/shard_map/pallas_call | solution.py:351
  230.3 6.5 %collective-permute-start.12 = (bf16[4,128,1024]{2,1,0:T(8,128)(2,1)S(1)}, bf16[4,128,1024]{2,1,0:T(8,128)(2,1)S(1)}, u32[]{:S(2)}, u32[]{:S(2)}) collective-permute-start(bf16[4,128,1024]{2,1,0:T(8,128)(2,1)S(1)} %slice_bitcast_fusion.37), channel_id=1, source_target_pairs={{0,1},{1,0},{2,3},{3,2},{4,5},{5,4},{6,7},{7,6},{8,9},{9,8},{10,11... | collective-permute-start | bytes 3145736 | tf_op jit(solution)/shard_map/ppermute | solution.py:366
  246.4 5.5 collective-permute-done.13
  258.8 9.1 %shard_map.294 = (bf16[2,128,2048]{2,1,0:T(8,128)(2,1)}, bf16[2,128,2048]{2,1,0:T(8,128)(2,1)}, bf16[2,128,2048]{2,1,0:T(8,128)(2,1)}, bf16[2,128,2048]{2,1,0:T(8,128)(2,1)}) custom-call(s32[1]{0:T(128)} %bitcast.103.place, bf16[384,512]{1,0:T(8,128)(2,1)S(1)} %copy-done.28, bf16[384,512]{1,0:T(8,128)(2,1)S(1)} %collective-permute-done.24.refs_1_, ...), custom_call_target="tpu_custom_call" | custom-call | tf_op jit(solution)/shard_map/pallas_call | solution.py:459
  281.5 4.6 convert_reduce_fusion.1
  287.3 3.4 multiply_reduce_fusion.4
  295.1 14.0 %shard_map.293 = (bf16[384,512]{1,0:T(8,128)(2,1)S(1)}, f32[2,512]{1,0:T(2,128)S(1)}, f32[640,512]{1,0:T(8,128)S(1)}, f32[640,512]{1,0:T(8,128)}, bf16[384,512]{1,0:T(8,128)(2,1)S(1)}) custom-call(bf16[384,512]{1,0:T(8,128)(2,1)S(1)} %copy-done.11, bf16[384,512]{1,0:T(8,128)(2,1)S(1)} %copy-done.9, bf16[640,512]{1,0:T(8,128)(2,1)S(1)} %get-tuple-element.313.keys, ...), custom_call_target="tpu_custom_call" | custom-call | tf_op jit(solution)/shard_map/pallas_call | solution.py:351
  318.6 5.8 %collective-permute-start.53 = (bf16[1152,256]{1,0:T(8,128)(2,1)}, bf16[1152,256]{1,0:T(8,128)(2,1)}, u32[]{:S(2)}, u32[]{:S(2)}) collective-permute-start(bf16[1152,256]{1,0:T(8,128)(2,1)} %get-tuple-element.174), channel_id=1, source_target_pairs={{0,1},{1,0},{2,3},{3,2},{4,5},{5,4},{6,7},{7,6},{8,9},{9,8},{10,11... | collective-permute-start | bytes 1769480 | tf_op jit(solution)/shard_map/ppermute | solution.py:366
  329.9 3.3 concatenate.134
  338.0 2.9 collective-permute-start.38
  345.4 7.0 %shard_map.295 = (bf16[2,128,2048]{2,1,0:T(8,128)(2,1)S(1)}, bf16[2,128,2048]{2,1,0:T(8,128)(2,1)}, bf16[2,128,2048]{2,1,0:T(8,128)(2,1)}, bf16[2,128,2048]{2,1,0:T(8,128)(2,1)}) custom-call(s32[1]{0:T(128)} %bitcast.103.place, bf16[128,512]{1,0:T(8,128)(2,1)} %add_convert_fusion.30.refs_0_, bf16[128,512]{1,0:T(8,128)(2,1)} %collective-permute-done.44.refs_1_, ...), custom_call_target="tpu_custom_call" | custom-call | tf_op jit(solution)/shard_map/pallas_call | solution.py:459
  353.0 13.2 %collective-permute-done.20 = f32[152,128]{1,0:T(8,128)S(1)} collective-permute-done((f32[152,128]{1,0:T(8,128)S(1)}, f32[152,128]{1,0:T(8,128)S(1)}, u32[]{:S(2)}, u32[]{:S(2)}) %collective-permute-start.20) | collective-permute-done | bytes 77856 | tf_op jit(solution)/shard_map/ppermute | solution.py:366
  383.4 4.8 shard_map.296
  401.5 2.9 shard_map.297
  405.3 12.7 %collective-permute-done.37 = bf16[128,2048]{1,0:T(8,128)(2,1)S(1)} collective-permute-done((bf16[128,2048]{1,0:T(8,128)(2,1)}, bf16[128,2048]{1,0:T(8,128)(2,1)S(1)}, u32[]{:S(2)}, u32[]{:S(2)}) %collective-permute-start.37) | collective-permute-done | bytes 524320 | tf_op jit(solution)/shard_map/ppermute | solution.py:366
  423.3 7.4 %collective-permute-done.72 = bf16[2,128,1152]{2,1,0:T(8,128)(2,1)S(1)} collective-permute-done((bf16[2,128,1152]{2,1,0:T(8,128)(2,1)}, bf16[2,128,1152]{2,1,0:T(8,128)(2,1)S(1)}, u32[]{:S(2)}, u32[]{:S(2)}) %collective-permute-start.72) | collective-permute-done | bytes 589856 | tf_op jit(solution)/shard_map/ppermute | solution.py:366
  432.4 3.4 collective-permute-done.83
  436.2 6.0 %collective-permute-done.81 = bf16[2,128,512]{2,1,0:T(8,128)(2,1)S(1)} collective-permute-done((bf16[2,128,512]{2,1,0:T(8,128)(2,1)S(1)}, bf16[2,128,512]{2,1,0:T(8,128)(2,1)S(1)}, u32[]{:S(2)}, u32[]{:S(2)}) %collective-permute-start.81) | collective-permute-done | bytes 262176 | tf_op jit(solution)/shard_map/ppermute | solution.py:366
  445.3 10.2 %collective-permute-done.84 = bf16[128,512]{1,0:T(8,128)(2,1)S(1)} collective-permute-done((bf16[128,512]{1,0:T(8,128)(2,1)S(1)}, bf16[128,512]{1,0:T(8,128)(2,1)S(1)}, u32[]{:S(2)}, u32[]{:S(2)}) %collective-permute-start.84) | collective-permute-done | bytes 131104 | tf_op jit(solution)/shard_map/ppermute | solution.py:366
  460.2 3.3 collective-permute-done.85
  479.0 10.1 %collective-permute-done.87 = bf16[128,512]{1,0:T(8,128)(2,1)S(1)} collective-permute-done((bf16[128,512]{1,0:T(8,128)(2,1)S(1)}, bf16[128,512]{1,0:T(8,128)(2,1)S(1)}, u32[]{:S(2)}, u32[]{:S(2)}) %collective-permute-start.87) | collective-permute-done | bytes 131104 | tf_op jit(solution)/shard_map/ppermute | solution.py:366
  489.5 4.3 collective-permute-start.75
  494.1 12.5 %collective-permute-done.75 = bf16[128,1152]{1,0:T(8,128)(2,1)S(1)} collective-permute-done((bf16[128,1152]{1,0:T(8,128)(2,1)S(1)}, bf16[128,1152]{1,0:T(8,128)(2,1)S(1)}, u32[]{:S(2)}, u32[]{:S(2)}) %collective-permute-start.75) | collective-permute-done | bytes 294944 | tf_op jit(solution)/shard_map/ppermute | solution.py:366
  506.7 4.3 collective-permute-start.76
  512.7 22.3 %collective-permute-done.76 = bf16[128,1152]{1,0:T(8,128)(2,1)S(1)} collective-permute-done((bf16[128,1152]{1,0:T(8,128)(2,1)S(1)}, bf16[128,1152]{1,0:T(8,128)(2,1)S(1)}, u32[]{:S(2)}, u32[]{:S(2)}) %collective-permute-start.76) | collective-permute-done | bytes 294944 | tf_op jit(solution)/shard_map/ppermute | solution.py:366
  537.1 13.0 %collective-permute-done.62 = bf16[128,2048]{1,0:T(8,128)(2,1)S(1)} collective-permute-done((bf16[128,2048]{1,0:T(8,128)(2,1)S(1)}, bf16[128,2048]{1,0:T(8,128)(2,1)S(1)}, u32[]{:S(2)}, u32[]{:S(2)}) %collective-permute-start.62) | collective-permute-done | bytes 524320 | tf_op jit(solution)/shard_map/ppermute | solution.py:366
  552.6 2.9 shard_map.298
  (842 shorter events, 210.9 us)
Async XLA Ops:
  16.4 25.2 %collective-permute-start = (bf16[2,256,512]{2,1,0:T(8,128)(2,1)}, bf16[2,256,512]{2,1,0:T(8,128)(2,1)}, u32[]{:S(2)}, u32[]{:S(2)}) collective-permute-start(bf16[2,256,512]{2,1,0:T(8,128)(2,1)} %pad_maximum_fusion.16), channel_id=1, source_target_pairs={{0,1},{1,2},{2,3},{3,4},{4,5},{5,6},{6,7},{8,9},{9,10},{10,11},{11... | collective-permute-start | bytes 1572872 | tf_op jit(solution)/shard_map/ppermute | solution.py:541
  22.1 218.5 %collective-permute-start.32 = (bf16[384,512]{1,0:T(8,128)(2,1)}, bf16[384,512]{1,0:T(8,128)(2,1)}, u32[]{:S(2)}, u32[]{:S(2)}) collective-permute-start(bf16[384,512]{1,0:T(8,128)(2,1)} %pad_maximum_fusion.20.refs_16_.refs_4_), channel_id=1, source_target_pairs={{0,1},{1,0},{2,3},{3,2},{4,5},{5,4},{6,7},{7,6},{8,9},{9,8},{10,11... | collective-permute-start | bytes 1179656 | tf_op jit(solution)/shard_map/ppermute | solution.py:366
  24.7 215.3 %collective-permute-start.27 = (bf16[384,256]{1,0:T(8,128)(2,1)}, bf16[384,256]{1,0:T(8,128)(2,1)}, u32[]{:S(2)}, u32[]{:S(2)}) collective-permute-start(bf16[384,256]{1,0:T(8,128)(2,1)} %get-tuple-element.231), channel_id=1, source_target_pairs={{0,1},{1,0},{2,3},{3,2},{4,5},{5,4},{6,7},{7,6},{8,9},{9,8},{10,11... | collective-permute-start | bytes 589832 | tf_op jit(solution)/shard_map/ppermute | solution.py:366
  81.8 9.4 %collective-permute-start.3 = (bf16[128,1024]{1,0:T(8,128)(2,1)S(1)}, bf16[128,1024]{1,0:T(8,128)(2,1)S(1)}, u32[]{:S(2)}, u32[]{:S(2)}) collective-permute-start(bf16[128,1024]{1,0:T(8,128)(2,1)S(1)} %get-tuple-element.152), channel_id=1, source_target_pairs={{0,2},{1,3},{2,0},{3,1},{4,6},{5,7},{6,4},{7,5},{8,10},{9,11},{10,... | collective-permute-start | bytes 786440 | tf_op jit(solution)/shard_map/ppermute | solution.py:366
  138.2 103.2 %collective-permute-start.30 = (bf16[384,512]{1,0:T(8,128)(2,1)}, bf16[384,512]{1,0:T(8,128)(2,1)}, u32[]{:S(2)}, u32[]{:S(2)}) collective-permute-start(bf16[384,512]{1,0:T(8,128)(2,1)} %copy-done.6), channel_id=1, source_target_pairs={{0,1},{1,0},{2,3},{3,2},{4,5},{5,4},{6,7},{7,6},{8,9},{9,8},{10,11... | collective-permute-start | bytes 1179656 | tf_op jit(solution)/shard_map/ppermute | solution.py:366
  138.7 102.2 %collective-permute-start.34 = (bf16[128,512]{1,0:T(8,128)(2,1)}, bf16[128,512]{1,0:T(8,128)(2,1)}, u32[]{:S(2)}, u32[]{:S(2)}) collective-permute-start(bf16[128,512]{1,0:T(8,128)(2,1)} %copy-done.48), channel_id=1, source_target_pairs={{0,1},{1,0},{2,3},{3,2},{4,5},{5,4},{6,7},{7,6},{8,9},{9,8},{10,11... | collective-permute-start | bytes 393224 | tf_op jit(solution)/shard_map/ppermute | solution.py:366
  230.3 9.2 %collective-permute-start.12 = (bf16[4,128,1024]{2,1,0:T(8,128)(2,1)S(1)}, bf16[4,128,1024]{2,1,0:T(8,128)(2,1)S(1)}, u32[]{:S(2)}, u32[]{:S(2)}) collective-permute-start(bf16[4,128,1024]{2,1,0:T(8,128)(2,1)S(1)} %slice_bitcast_fusion.37), channel_id=1, source_target_pairs={{0,1},{1,0},{2,3},{3,2},{4,5},{5,4},{6,7},{7,6},{8,9},{9,8},{10,11... | collective-permute-start | bytes 3145736 | tf_op jit(solution)/shard_map/ppermute | solution.py:366
  239.5 18.1 %collective-permute-start.26 = (bf16[384,2048]{1,0:T(8,128)(2,1)S(1)}, bf16[384,2048]{1,0:T(8,128)(2,1)S(1)}, u32[]{:S(2)}, u32[]{:S(2)}) collective-permute-start(bf16[384,2048]{1,0:T(8,128)(2,1)S(1)} %copy-done.110), channel_id=1, source_target_pairs={{0,1},{1,0},{2,3},{3,2},{4,5},{5,4},{6,7},{7,6},{8,9},{9,8},{10,11... | collective-permute-start | bytes 4718600 | tf_op jit(solution)/shard_map/ppermute | solution.py:366
  241.4 15.6 %collective-permute-start.25 = (bf16[384,1024]{1,0:T(8,128)(2,1)S(1)}, bf16[384,1024]{1,0:T(8,128)(2,1)S(1)}, u32[]{:S(2)}, u32[]{:S(2)}) collective-permute-start(bf16[384,1024]{1,0:T(8,128)(2,1)S(1)} %copy-done.127), channel_id=1, source_target_pairs={{0,1},{1,0},{2,3},{3,2},{4,5},{5,4},{6,7},{7,6},{8,9},{9,8},{10,11... | collective-permute-start | bytes 2359304 | tf_op jit(solution)/shard_map/ppermute | solution.py:366
  254.2 13.7 %collective-permute-start.14 = (bf16[128,512]{1,0:T(8,128)(2,1)S(1)}, bf16[128,512]{1,0:T(8,128)(2,1)S(1)}, u32[]{:S(2)}, u32[]{:S(2)}) collective-permute-start(bf16[128,512]{1,0:T(8,128)(2,1)S(1)} %get-tuple-element.194), channel_id=1, source_target_pairs={{0,4},{1,5},{2,6},{3,7},{4,0},{5,1},{6,2},{7,3},{8,12},{9,13},{10,... | collective-permute-start | bytes 393224 | tf_op jit(solution)/shard_map/ppermute | solution.py:366
  255.5 12.5 %collective-permute-start.16 = (bf16[128,512]{1,0:T(8,128)(2,1)S(1)}, bf16[128,512]{1,0:T(8,128)(2,1)S(1)}, u32[]{:S(2)}, u32[]{:S(2)}) collective-permute-start(bf16[128,512]{1,0:T(8,128)(2,1)S(1)} %get-tuple-element.195), channel_id=1, source_target_pairs={{0,2},{1,3},{2,0},{3,1},{4,6},{5,7},{6,4},{7,5},{8,10},{9,11},{10,... | collective-permute-start | bytes 393224 | tf_op jit(solution)/shard_map/ppermute | solution.py:366
  257.1 76.1 %collective-permute-start.52 = (bf16[1152,512]{1,0:T(8,128)(2,1)}, bf16[1152,512]{1,0:T(8,128)(2,1)}, u32[]{:S(2)}, u32[]{:S(2)}) collective-permute-start(bf16[1152,512]{1,0:T(8,128)(2,1)} %pad_maximum_fusion.1.refs_16_), channel_id=1, source_target_pairs={{0,1},{1,0},{2,3},{3,2},{4,5},{5,4},{6,7},{7,6},{8,9},{9,8},{10,11... | collective-permute-start | bytes 3538952 | tf_op jit(solution)/shard_map/ppermute | solution.py:366
  257.2 72.0 %collective-permute-start.50 = (bf16[128,512]{1,0:T(8,128)(2,1)S(1)}, bf16[128,512]{1,0:T(8,128)(2,1)}, u32[]{:S(2)}, u32[]{:S(2)}) collective-permute-start(bf16[128,512]{1,0:T(8,128)(2,1)S(1)} %add_convert_fusion.33.refs_12_), channel_id=1, source_target_pairs={{0,1},{1,0},{2,3},{3,2},{4,5},{5,4},{6,7},{7,6},{8,9},{9,8},{10,11... | collective-permute-start | bytes 393224 | tf_op jit(solution)/shard_map/ppermute | solution.py:366
  257.6 71.7 %collective-permute-start.54 = (bf16[128,1536]{1,0:T(8,128)(2,1)S(1)}, bf16[128,1536]{1,0:T(8,128)(2,1)}, u32[]{:S(2)}, u32[]{:S(2)}) collective-permute-start(bf16[128,1536]{1,0:T(8,128)(2,1)S(1)} %copy-done.15), channel_id=1, source_target_pairs={{0,1},{1,0},{2,3},{3,2},{4,5},{5,4},{6,7},{7,6},{8,9},{9,8},{10,11... | collective-permute-start | bytes 1179656 | tf_op jit(solution)/shard_map/ppermute | solution.py:366
  267.9 66.7 %collective-permute-start.46 = (bf16[128,2048]{1,0:T(8,128)(2,1)}, bf16[128,2048]{1,0:T(8,128)(2,1)}, u32[]{:S(2)}, u32[]{:S(2)}) collective-permute-start(bf16[128,2048]{1,0:T(8,128)(2,1)} %get-tuple-element.149.refs_4_), channel_id=1, source_target_pairs={{0,1},{1,0},{2,3},{3,2},{4,5},{5,4},{6,7},{7,6},{8,9},{9,8},{10,11... | collective-permute-start | bytes 1572872 | tf_op jit(solution)/shard_map/ppermute | solution.py:366
  318.6 19.0 %collective-permute-start.53 = (bf16[1152,256]{1,0:T(8,128)(2,1)}, bf16[1152,256]{1,0:T(8,128)(2,1)}, u32[]{:S(2)}, u32[]{:S(2)}) collective-permute-start(bf16[1152,256]{1,0:T(8,128)(2,1)} %get-tuple-element.174), channel_id=1, source_target_pairs={{0,1},{1,0},{2,3},{3,2},{4,5},{5,4},{6,7},{7,6},{8,9},{9,8},{10,11... | collective-permute-start | bytes 1769480 | tf_op jit(solution)/shard_map/ppermute | solution.py:366
  335.2 17.2 %collective-permute-start.19 = (f32[152,128]{1,0:T(8,128)S(1)}, f32[152,128]{1,0:T(8,128)S(1)}, u32[]{:S(2)}, u32[]{:S(2)}) collective-permute-start(f32[152,128]{1,0:T(8,128)S(1)} %pad_bitcast_fusion), channel_id=1, source_target_pairs={{0,1},{1,0},{2,3},{3,2},{4,5},{5,4},{6,7},{7,6},{8,9},{9,8},{10,11... | collective-permute-start | bytes 233480 | tf_op jit(solution)/shard_map/ppermute | solution.py:366
  337.5 42.9 %collective-permute-start.66 = (bf16[384,2048]{1,0:T(8,128)(2,1)}, bf16[384,2048]{1,0:T(8,128)(2,1)S(1)}, u32[]{:S(2)}, u32[]{:S(2)}) collective-permute-start(bf16[384,2048]{1,0:T(8,128)(2,1)} %copy-done.100), channel_id=1, source_target_pairs={{0,1},{1,0},{2,3},{3,2},{4,5},{5,4},{6,7},{7,6},{8,9},{9,8},{10,11... | collective-permute-start | bytes 4718600 | tf_op jit(solution)/shard_map/ppermute | solution.py:366
  337.6 38.6 %collective-permute-start.64 = (bf16[384,512]{1,0:T(8,128)(2,1)}, bf16[384,512]{1,0:T(8,128)(2,1)S(1)}, u32[]{:S(2)}, u32[]{:S(2)}) collective-permute-start(bf16[384,512]{1,0:T(8,128)(2,1)} %copy-done.25), channel_id=1, source_target_pairs={{0,1},{1,0},{2,3},{3,2},{4,5},{5,4},{6,7},{7,6},{8,9},{9,8},{10,11... | collective-permute-start | bytes 1179656 | tf_op jit(solution)/shard_map/ppermute | solution.py:366
  338.0 35.5 %collective-permute-start.38 = (bf16[2,128,2048]{2,1,0:T(8,128)(2,1)}, bf16[2,128,2048]{2,1,0:T(8,128)(2,1)S(1)}, u32[]{:S(2)}, u32[]{:S(2)}) collective-permute-start(bf16[2,128,2048]{2,1,0:T(8,128)(2,1)} %get-tuple-element.81), channel_id=1, source_target_pairs={{0,2},{1,3},{2,0},{3,1},{4,6},{5,7},{6,4},{7,5},{8,10},{9,11},{10,... | collective-permute-start | bytes 3145736 | tf_op jit(solution)/shard_map/ppermute | solution.py:366
  340.9 36.0 %collective-permute-start.36 = (bf16[2,128,2048]{2,1,0:T(8,128)(2,1)}, bf16[2,128,2048]{2,1,0:T(8,128)(2,1)S(1)}, u32[]{:S(2)}, u32[]{:S(2)}) collective-permute-start(bf16[2,128,2048]{2,1,0:T(8,128)(2,1)} %get-tuple-element.79), channel_id=1, source_target_pairs={{0,4},{1,5},{2,6},{3,7},{4,0},{5,1},{6,2},{7,3},{8,12},{9,13},{10,... | collective-permute-start | bytes 3145736 | tf_op jit(solution)/shard_map/ppermute | solution.py:366
  352.5 13.7 %collective-permute-start.20 = (f32[152,128]{1,0:T(8,128)S(1)}, f32[152,128]{1,0:T(8,128)S(1)}, u32[]{:S(2)}, u32[]{:S(2)}) collective-permute-start(f32[152,128]{1,0:T(8,128)S(1)} %fusion.139), channel_id=1, source_target_pairs={{0,2},{1,3},{2,0},{3,1},{4,6},{5,7},{6,4},{7,5},{8,10},{9,11},{10,... | collective-permute-start | bytes 233480 | tf_op jit(solution)/shard_map/ppermute | solution.py:366
  376.9 14.6 %collective-permute-start.23 = (f32[152,128]{1,0:T(8,128)S(1)}, f32[152,128]{1,0:T(8,128)S(1)}, u32[]{:S(2)}, u32[]{:S(2)}) collective-permute-start(f32[152,128]{1,0:T(8,128)S(1)} %add.611), channel_id=1, source_target_pairs={{0,16},{8,24},{16,0},{24,8},{1,17},{9,25},{17,1},{25,9},{2,18},{10... | collective-permute-start | bytes 233480 | tf_op jit(solution)/shard_map/ppermute | solution.py:366
  380.4 15.7 %collective-permute-start.78 = (bf16[384,512]{1,0:T(8,128)(2,1)S(1)}, bf16[384,512]{1,0:T(8,128)(2,1)}, u32[]{:S(2)}, u32[]{:S(2)}) collective-permute-start(bf16[384,512]{1,0:T(8,128)(2,1)S(1)} %copy-done.13), channel_id=1, source_target_pairs={{0,1},{1,0},{2,3},{3,2},{4,5},{5,4},{6,7},{7,6},{8,9},{9,8},{10,11... | collective-permute-start | bytes 1179656 | tf_op jit(solution)/shard_map/ppermute | solution.py:366
  380.6 41.3 %collective-permute-start.58 = (bf16[2,128,2048]{2,1,0:T(8,128)(2,1)}, bf16[2,128,2048]{2,1,0:T(8,128)(2,1)}, u32[]{:S(2)}, u32[]{:S(2)}) collective-permute-start(bf16[2,128,2048]{2,1,0:T(8,128)(2,1)} %get-tuple-element.86), channel_id=1, source_target_pairs={{0,2},{1,3},{2,0},{3,1},{4,6},{5,7},{6,4},{7,5},{8,10},{9,11},{10,... | collective-permute-start | bytes 3145736 | tf_op jit(solution)/shard_map/ppermute | solution.py:366
  382.4 16.5 %collective-permute-start.79 = (bf16[384,768]{1,0:T(8,128)(2,1)}, bf16[384,768]{1,0:T(8,128)(2,1)}, u32[]{:S(2)}, u32[]{:S(2)}) collective-permute-start(bf16[384,768]{1,0:T(8,128)(2,1)} %get-tuple-element.172), channel_id=1, source_target_pairs={{0,1},{1,0},{2,3},{3,2},{4,5},{5,4},{6,7},{7,6},{8,9},{9,8},{10,11... | collective-permute-start | bytes 1769480 | tf_op jit(solution)/shard_map/ppermute | solution.py:366
  382.4 21.9 %collective-permute-start.39 = (bf16[128,2048]{1,0:T(8,128)(2,1)}, bf16[128,2048]{1,0:T(8,128)(2,1)}, u32[]{:S(2)}, u32[]{:S(2)}) collective-permute-start(bf16[128,2048]{1,0:T(8,128)(2,1)} %fusion.87), channel_id=1, source_target_pairs={{0,4},{1,5},{2,6},{3,7},{4,0},{5,1},{6,2},{7,3},{8,12},{9,13},{10,... | collective-permute-start | bytes 1572872 | tf_op jit(solution)/shard_map/ppermute | solution.py:366
  391.4 26.6 %collective-permute-start.37 = (bf16[128,2048]{1,0:T(8,128)(2,1)}, bf16[128,2048]{1,0:T(8,128)(2,1)S(1)}, u32[]{:S(2)}, u32[]{:S(2)}) collective-permute-start(bf16[128,2048]{1,0:T(8,128)(2,1)} %fusion.86), channel_id=1, source_target_pairs={{0,2},{1,3},{2,0},{3,1},{4,6},{5,7},{6,4},{7,5},{8,10},{9,11},{10,... | collective-permute-start | bytes 1572872 | tf_op jit(solution)/shard_map/ppermute | solution.py:366
  397.7 60.7 %collective-permute-start.56 = (bf16[2,128,2048]{2,1,0:T(8,128)(2,1)}, bf16[2,128,2048]{2,1,0:T(8,128)(2,1)S(1)}, u32[]{:S(2)}, u32[]{:S(2)}) collective-permute-start(bf16[2,128,2048]{2,1,0:T(8,128)(2,1)} %get-tuple-element.84), channel_id=1, source_target_pairs={{0,4},{1,5},{2,6},{3,7},{4,0},{5,1},{6,2},{7,3},{8,12},{9,13},{10,... | collective-permute-start | bytes 3145736 | tf_op jit(solution)/shard_map/ppermute | solution.py:366
  398.9 31.8 %collective-permute-start.72 = (bf16[2,128,1152]{2,1,0:T(8,128)(2,1)}, bf16[2,128,1152]{2,1,0:T(8,128)(2,1)S(1)}, u32[]{:S(2)}, u32[]{:S(2)}) collective-permute-start(bf16[2,128,1152]{2,1,0:T(8,128)(2,1)} %copy-done.61), channel_id=1, source_target_pairs={{0,2},{1,3},{2,0},{3,1},{4,6},{5,7},{6,4},{7,5},{8,10},{9,11},{10,... | collective-permute-start | bytes 1769480 | tf_op jit(solution)/shard_map/ppermute | solution.py:366
  404.4 39.0 %collective-permute-start.70 = (bf16[2,128,1152]{2,1,0:T(8,128)(2,1)S(1)}, bf16[2,128,1152]{2,1,0:T(8,128)(2,1)S(1)}, u32[]{:S(2)}, u32[]{:S(2)}) collective-permute-start(bf16[2,128,1152]{2,1,0:T(8,128)(2,1)S(1)} %copy-done.60), channel_id=1, source_target_pairs={{0,4},{1,5},{2,6},{3,7},{4,0},{5,1},{6,2},{7,3},{8,12},{9,13},{10,... | collective-permute-start | bytes 1769480 | tf_op jit(solution)/shard_map/ppermute | solution.py:366
  418.1 17.7 %collective-permute-start.83 = (bf16[2,128,512]{2,1,0:T(8,128)(2,1)S(1)}, bf16[2,128,512]{2,1,0:T(8,128)(2,1)S(1)}, u32[]{:S(2)}, u32[]{:S(2)}) collective-permute-start(bf16[2,128,512]{2,1,0:T(8,128)(2,1)S(1)} %get-tuple-element.95), channel_id=1, source_target_pairs={{0,2},{1,3},{2,0},{3,1},{4,6},{5,7},{6,4},{7,5},{8,10},{9,11},{10,... | collective-permute-start | bytes 786440 | tf_op jit(solution)/shard_map/ppermute | solution.py:366
  421.9 20.3 %collective-permute-start.81 = (bf16[2,128,512]{2,1,0:T(8,128)(2,1)S(1)}, bf16[2,128,512]{2,1,0:T(8,128)(2,1)S(1)}, u32[]{:S(2)}, u32[]{:S(2)}) collective-permute-start(bf16[2,128,512]{2,1,0:T(8,128)(2,1)S(1)} %get-tuple-element.93), channel_id=1, source_target_pairs={{0,4},{1,5},{2,6},{3,7},{4,0},{5,1},{6,2},{7,3},{8,12},{9,13},{10,... | collective-permute-start | bytes 786440 | tf_op jit(solution)/shard_map/ppermute | solution.py:366
  430.7 36.8 %collective-permute-start.40 = (bf16[128,2048]{1,0:T(8,128)(2,1)S(1)}, bf16[128,2048]{1,0:T(8,128)(2,1)S(1)}, u32[]{:S(2)}, u32[]{:S(2)}) collective-permute-start(bf16[128,2048]{1,0:T(8,128)(2,1)S(1)} %broadcast_select_fusion.15), channel_id=1, source_target_pairs={{0,8},{8,0},{16,24},{24,16},{1,9},{9,1},{17,25},{25,17},{2,10},{10... | collective-permute-start | bytes 1572872 | tf_op jit(solution)/shard_map/ppermute | solution.py:366
  435.7 37.3 %collective-permute-start.59 = (bf16[128,2048]{1,0:T(8,128)(2,1)S(1)}, bf16[128,2048]{1,0:T(8,128)(2,1)S(1)}, u32[]{:S(2)}, u32[]{:S(2)}) collective-permute-start(bf16[128,2048]{1,0:T(8,128)(2,1)S(1)} %fusion.89), channel_id=1, source_target_pairs={{0,4},{1,5},{2,6},{3,7},{4,0},{5,1},{6,2},{7,3},{8,12},{9,13},{10,... | collective-permute-start | bytes 1572872 | tf_op jit(solution)/shard_map/ppermute | solution.py:366
  442.2 13.3 %collective-permute-start.84 = (bf16[128,512]{1,0:T(8,128)(2,1)S(1)}, bf16[128,512]{1,0:T(8,128)(2,1)S(1)}, u32[]{:S(2)}, u32[]{:S(2)}) collective-permute-start(bf16[128,512]{1,0:T(8,128)(2,1)S(1)} %fusion.123), channel_id=1, source_target_pairs={{0,4},{1,5},{2,6},{3,7},{4,0},{5,1},{6,2},{7,3},{8,12},{9,13},{10,... | collective-permute-start | bytes 393224 | tf_op jit(solution)/shard_map/ppermute | solution.py:366
  443.4 13.2 %collective-permute-start.82 = (bf16[128,512]{1,0:T(8,128)(2,1)S(1)}, bf16[128,512]{1,0:T(8,128)(2,1)S(1)}, u32[]{:S(2)}, u32[]{:S(2)}) collective-permute-start(bf16[128,512]{1,0:T(8,128)(2,1)S(1)} %fusion.122), channel_id=1, source_target_pairs={{0,2},{1,3},{2,0},{3,1},{4,6},{5,7},{6,4},{7,5},{8,10},{9,11},{10,... | collective-permute-start | bytes 393224 | tf_op jit(solution)/shard_map/ppermute | solution.py:366
  463.5 12.3 %collective-permute-start.57 = (bf16[128,2048]{1,0:T(8,128)(2,1)S(1)}, bf16[128,2048]{1,0:T(8,128)(2,1)S(1)}, u32[]{:S(2)}, u32[]{:S(2)}) collective-permute-start(bf16[128,2048]{1,0:T(8,128)(2,1)S(1)} %fusion.88), channel_id=1, source_target_pairs={{0,2},{1,3},{2,0},{3,1},{4,6},{5,7},{6,4},{7,5},{8,10},{9,11},{10,... | collective-permute-start | bytes 1572872 | tf_op jit(solution)/shard_map/ppermute | solution.py:366
  465.9 23.3 %collective-permute-start.74 = (bf16[128,1152]{1,0:T(8,128)(2,1)S(1)}, bf16[128,1152]{1,0:T(8,128)(2,1)S(1)}, u32[]{:S(2)}, u32[]{:S(2)}) collective-permute-start(bf16[128,1152]{1,0:T(8,128)(2,1)S(1)} %broadcast_select_fusion.27), channel_id=1, source_target_pairs={{0,8},{8,0},{16,24},{24,16},{1,9},{9,1},{17,25},{25,17},{2,10},{10... | collective-permute-start | bytes 884744 | tf_op jit(solution)/shard_map/ppermute | solution.py:366
  469.1 24.8 %collective-permute-start.41 = (bf16[128,2048]{1,0:T(8,128)(2,1)S(1)}, bf16[128,2048]{1,0:T(8,128)(2,1)S(1)}, u32[]{:S(2)}, u32[]{:S(2)}) collective-permute-start(bf16[128,2048]{1,0:T(8,128)(2,1)S(1)} %add_convert_fusion.7), channel_id=1, source_target_pairs={{0,16},{8,24},{16,0},{24,8},{1,17},{9,25},{17,1},{25,9},{2,18},{10... | collective-permute-start | bytes 1572872 | tf_op jit(solution)/shard_map/ppermute | solution.py:366
  471.0 18.0 %collective-permute-start.87 = (bf16[128,512]{1,0:T(8,128)(2,1)S(1)}, bf16[128,512]{1,0:T(8,128)(2,1)S(1)}, u32[]{:S(2)}, u32[]{:S(2)}) collective-permute-start(bf16[128,512]{1,0:T(8,128)(2,1)S(1)} %add_convert_fusion.23), channel_id=1, source_target_pairs={{0,8},{8,0},{16,24},{24,16},{1,9},{9,1},{17,25},{25,17},{2,10},{10... | collective-permute-start | bytes 393224 | tf_op jit(solution)/shard_map/ppermute | solution.py:366
  477.3 33.7 %collective-permute-start.60 = (bf16[128,2048]{1,0:T(8,128)(2,1)S(1)}, bf16[128,2048]{1,0:T(8,128)(2,1)S(1)}, u32[]{:S(2)}, u32[]{:S(2)}) collective-permute-start(bf16[128,2048]{1,0:T(8,128)(2,1)S(1)} %broadcast_select_fusion.12), channel_id=1, source_target_pairs={{0,8},{8,0},{16,24},{24,16},{1,9},{9,1},{17,25},{25,17},{2,10},{10... | collective-permute-start | bytes 1572872 | tf_op jit(solution)/shard_map/ppermute | solution.py:366
  489.5 17.2 %collective-permute-start.75 = (bf16[128,1152]{1,0:T(8,128)(2,1)S(1)}, bf16[128,1152]{1,0:T(8,128)(2,1)S(1)}, u32[]{:S(2)}, u32[]{:S(2)}) collective-permute-start(bf16[128,1152]{1,0:T(8,128)(2,1)S(1)} %add_convert_fusion.20), channel_id=1, source_target_pairs={{0,16},{8,24},{16,0},{24,8},{1,17},{9,25},{17,1},{25,9},{2,18},{10... | collective-permute-start | bytes 884744 | tf_op jit(solution)/shard_map/ppermute | solution.py:366
  494.1 41.3 %collective-permute-start.42 = (bf16[128,2048]{1,0:T(8,128)(2,1)S(1)}, bf16[128,2048]{1,0:T(8,128)(2,1)S(1)}, u32[]{:S(2)}, u32[]{:S(2)}) collective-permute-start(bf16[128,2048]{1,0:T(8,128)(2,1)S(1)} %add_convert_fusion.6), channel_id=1, source_target_pairs={{0,8},{8,0},{16,24},{24,16},{1,9},{9,1},{17,25},{25,17},{2,10},{10... | collective-permute-start | bytes 1572872 | tf_op jit(solution)/shard_map/ppermute | solution.py:366
  506.7 28.3 %collective-permute-start.76 = (bf16[128,1152]{1,0:T(8,128)(2,1)S(1)}, bf16[128,1152]{1,0:T(8,128)(2,1)S(1)}, u32[]{:S(2)}, u32[]{:S(2)}) collective-permute-start(bf16[128,1152]{1,0:T(8,128)(2,1)S(1)} %add_convert_fusion.19), channel_id=1, source_target_pairs={{0,8},{8,0},{16,24},{24,16},{1,9},{9,1},{17,25},{25,17},{2,10},{10... | collective-permute-start | bytes 884744 | tf_op jit(solution)/shard_map/ppermute | solution.py:366
  512.7 23.4 %collective-permute-start.61 = (bf16[128,2048]{1,0:T(8,128)(2,1)S(1)}, bf16[128,2048]{1,0:T(8,128)(2,1)S(1)}, u32[]{:S(2)}, u32[]{:S(2)}) collective-permute-start(bf16[128,2048]{1,0:T(8,128)(2,1)S(1)} %add_convert_fusion.3), channel_id=1, source_target_pairs={{0,16},{8,24},{16,0},{24,8},{1,17},{9,25},{17,1},{25,9},{2,18},{10... | collective-permute-start | bytes 1572872 | tf_op jit(solution)/shard_map/ppermute | solution.py:366
  535.5 14.9 %collective-permute-start.43 = (bf16[64,4096]{1,0:T(8,128)(2,1)S(1)}, bf16[64,4096]{1,0:T(8,128)(2,1)S(1)}, u32[]{:S(2)}, u32[]{:S(2)}) collective-permute-start(bf16[64,4096]{1,0:T(8,128)(2,1)S(1)} %broadcast_select_fusion.23), channel_id=1, source_target_pairs={{0,1},{1,0},{2,3},{3,2},{4,5},{5,4},{6,7},{7,6},{8,9},{9,8},{10,11... | collective-permute-start | bytes 1572872 | tf_op jit(solution)/shard_map/ppermute | solution.py:366
  536.2 13.9 %collective-permute-start.62 = (bf16[128,2048]{1,0:T(8,128)(2,1)S(1)}, bf16[128,2048]{1,0:T(8,128)(2,1)S(1)}, u32[]{:S(2)}, u32[]{:S(2)}) collective-permute-start(bf16[128,2048]{1,0:T(8,128)(2,1)S(1)} %add_convert_fusion.2), channel_id=1, source_target_pairs={{0,8},{8,0},{16,24},{24,16},{1,9},{9,1},{17,25},{25,17},{2,10},{10... | collective-permute-start | bytes 1572872 | tf_op jit(solution)/shard_map/ppermute | solution.py:366
  (264 other events, 2060.5 us)

commit v2 on v1

v2 whole, which is shorter than its diff:
```python
import math
from functools import partial

import jax
import jax.numpy as jnp
from jax import lax
from jax.experimental import pallas as pl
from jax.experimental.pallas import tpu as pltpu
from jax.sharding import PartitionSpec as P

D = 512
HEADS = 8
HD = 64
WIN = 256
QBLK = 384
DOCS = 8
epsilon = 1e-05
GAIN, SHIFT, BIAS, CONTRACT, EXPAND, POOL, UP = 0, 6, 12, 18, 21, 33, 34

VMEM = pl.BlockSpec(memory_space=pltpu.VMEM)
SMEM = pl.BlockSpec(memory_space=pltpu.SMEM)
HBM = pl.BlockSpec(memory_space=pltpu.HBM)


LANES = 128
PAIR = 2 * HD
MASKED = -1e30
PARTS = QBLK // LANES
SEEN = LANES + WIN
REACH = QBLK + WIN


def nt(first, second):
    return lax.dot_general(
        first, second, (((1,), (1,)), ((), ())), preferred_element_type=jnp.float32
    )


def nn(first, second):
    return lax.dot_general(
        first, second, (((1,), (0,)), ((), ())), preferred_element_type=jnp.float32
    )


def tn(first, second):
    return lax.dot_general(
        first, second, (((0,), (0,)), ((), ())), preferred_element_type=jnp.float32
    )


def document(places, info):
    total = jnp.zeros(places.shape, jnp.int32)
    for index in range(DOCS):
        total = total + (places >= info[1 + index]).astype(jnp.int32)
    return total


def lanes_and_rows():
    lane = lax.broadcasted_iota(jnp.int32, (LANES, LANES), 1)
    row = lax.broadcasted_iota(jnp.int32, (LANES, LANES), 0)
    return lane, row


def turned(values, index):
    return [
        jnp.take_along_axis(values[:, m * LANES : (m + 1) * LANES], index, axis=1)
        for m in range(values.shape[1] // LANES)
    ]


def skew_window(table):
    lane, row = lanes_and_rows()
    blocks = turned(table, (lane - row + LANES) % LANES)
    out = [blocks[0]] + [
        jnp.where(lane >= row, here, before) for before, here in zip(blocks, blocks[1:])
    ]
    return jnp.concatenate(out, axis=1)


def unskew_window(scores):
    lane, row = lanes_and_rows()
    blocks = turned(scores, (lane + row) % LANES)
    blocks.append(jnp.zeros_like(blocks[0]))
    out = [
        jnp.where(lane + row < LANES, here, after) for here, after in zip(blocks, blocks[1:])
    ]
    return jnp.concatenate(out, axis=1)


def skew_pooled(table):
    lane, row = lanes_and_rows()
    here, after = turned(table, (lane + LANES - 1 - row) % LANES)
    return jnp.where(lane <= row, here, after)


def unskew_pooled(scores):
    lane, row = lanes_and_rows()
    (block,) = turned(scores, (lane + row + 1) % LANES)
    zero = jnp.zeros_like(block)
    first = lane + row >= LANES - 1
    return jnp.concatenate([jnp.where(first, block, zero), jnp.where(first, zero, block)], axis=1)


def stacked(rows):
    head = lax.broadcasted_iota(jnp.int32, rows.shape, 1) // HD
    zero = jnp.zeros_like(rows)
    return jnp.concatenate([jnp.where(head == 0, rows, zero), jnp.where(head == 1, rows, zero)], axis=0)


def unstacked(rows):
    count = rows.shape[0] // 2
    head = lax.broadcasted_iota(jnp.int32, (count, PAIR), 1) // HD
    return jnp.where(head == 0, rows[:count], rows[count:])


def softmax_rows(scores):
    highest = jnp.max(scores, axis=1, keepdims=True)
    powers = jnp.exp(scores - highest)
    return powers * (1.0 / jnp.sum(powers, axis=1, keepdims=True))


def window_mask(info, part):
    place = info[0] + part * LANES
    row = lax.broadcasted_iota(jnp.int32, (LANES, SEEN), 0)
    column = lax.broadcasted_iota(jnp.int32, (LANES, SEEN), 1)
    behind = row + WIN - column
    query = place + lax.broadcasted_iota(jnp.int32, (LANES, 1), 0)
    key = place - WIN + lax.broadcasted_iota(jnp.int32, (1, SEEN), 1)
    same = document(query, info) == document(key, info)
    return (behind >= 0) & (behind <= WIN) & same & (key >= 0)


def pooled_mask(info, start):
    query = info[0] + lax.broadcasted_iota(jnp.int32, (LANES, 1), 0)
    key = start + lax.broadcasted_iota(jnp.int32, (1, LANES), 1)
    return (key <= query) & (document(3 * query, info) == document(3 * key, info))


def column_sums(first, second):
    return jnp.concatenate(
        [jnp.sum(first, axis=0, keepdims=True), jnp.sum(second, axis=0, keepdims=True)], axis=0
    )


def backward_scores(weights, grad_weights):
    delta = jnp.sum(weights * grad_weights, axis=1, keepdims=True)
    return weights * (grad_weights - delta)


def window_forward_kernel(
    raw,
    info,
    content,
    position,
    keys,
    values,
    border,
    gain,
    shift,
    key_weight,
    value_weight,
    table,
    mixed_ref,
    normed_ref,
    border_ref,
    weights_ref,
    bias,
    normed,
    places,
):
    pair = pl.program_id(0)

    @pl.when(pair == 0)
    def _():
        if raw is None:
            normed[...] = border[...]
        else:
            hat, _ = normalised(border[...].astype(jnp.float32))
            scale = gain[raw].astype(jnp.float32)[0:1, :]
            normed[...] = (hat * scale + shift[raw].astype(jnp.float32)[0:1, :]).astype(jnp.bfloat16)
        normed_ref[...] = normed[...]
        for part in range(PARTS):
            bias[part] = jnp.where(window_mask(info, part), 0.0, MASKED)

    border_keys = nn(normed[...], key_weight[...]).astype(jnp.bfloat16)
    border_values = nn(normed[...], value_weight[...]).astype(jnp.bfloat16)
    border_ref[0] = border_keys
    border_ref[1] = border_values
    all_keys = jnp.concatenate([border_keys, keys[...]], axis=0)
    all_values = jnp.concatenate([border_values, values[...]], axis=0)
    scale = jnp.asarray(HD**-0.5, jnp.bfloat16)
    order = [
        stacked(position[part * LANES : (part + 1) * LANES, :] * scale) for part in range(PARTS)
    ]
    places[...] = nt(jnp.concatenate(order, axis=0), table[...])
    for part in range(PARTS):
        rows = slice(part * LANES, (part + 1) * LANES)
        seen = slice(part * LANES, part * LANES + SEEN)
        scores = nt(stacked(content[rows, :] * scale), all_keys[seen])
        weights = []
        for index in range(2):
            start = (2 * part + index) * LANES
            score = scores[index * LANES : (index + 1) * LANES]
            score = score + skew_window(places[start : start + LANES, :]) + bias[part]
            weights.append(softmax_rows(score).astype(jnp.bfloat16))
            weights_ref[index, part] = weights[index]
        mixed = nn(jnp.concatenate(weights, axis=0), all_values[seen])
        mixed_ref[rows, :] = unstacked(mixed).astype(jnp.bfloat16)


def window_backward_kernel(
    place,
    content,
    position,
    keys,
    values,
    border,
    key_weight,
    value_weight,
    table,
    weights,
    grad,
    bias_ref,
    returned_ref,
    pack,
    dk_sum,
    dv_sum,
    returned,
    places,
    dq_out,
    dk_out,
    dv_out,
    dt_out,
    sems,
):
    pair = pl.program_id(0)
    all_keys = jnp.concatenate([border[0], keys[...]], axis=0)
    all_values = jnp.concatenate([border[1], values[...]], axis=0)
    scale = HD**-0.5
    low_scale = jnp.asarray(scale, jnp.bfloat16)
    dk_sum[...] = jnp.zeros_like(dk_sum)
    dv_sum[...] = jnp.zeros_like(dv_sum)
    contents = []
    for part in range(PARTS):
        rows = slice(part * LANES, (part + 1) * LANES)
        seen = slice(part * LANES, part * LANES + SEEN)
        grads = stacked(grad[rows, :])
        grad_weights = nt(grads, all_values[seen])
        scores, lows = [], []
        for index in range(2):
            low = weights[index, part]
            score = backward_scores(
                low.astype(jnp.float32), grad_weights[index * LANES : (index + 1) * LANES]
            ).astype(jnp.bfloat16)
            start = (2 * part + index) * LANES
            places[start : start + LANES, :] = unskew_window(score.astype(jnp.float32)).astype(
                jnp.bfloat16
            )
            scores.append(score)
            lows.append(low)
        scores = jnp.concatenate(scores, axis=0)
        contents.append(unstacked(nn(scores, all_keys[seen])) * scale)
        dk_sum[seen, :] += tn(scores, stacked(content[rows, :] * low_scale))
        dv_sum[seen, :] += tn(jnp.concatenate(lows, axis=0), grads)
    order = [
        stacked(position[part * LANES : (part + 1) * LANES, :] * low_scale)
        for part in range(PARTS)
    ]
    to_position = nn(places[...], table[...]) * scale
    positions = [
        unstacked(to_position[2 * part * LANES : 2 * (part + 1) * LANES]) for part in range(PARTS)
    ]
    grad_content = jnp.concatenate(contents, axis=0)
    grad_position = jnp.concatenate(positions, axis=0)
    bias_ref[...] = column_sums(grad_content, grad_position)
    dq_out[...] = (grad_content + grad_position).astype(jnp.bfloat16)
    dk_out[...] = dk_sum[...].astype(jnp.bfloat16)
    dv_out[...] = dv_sum[...].astype(jnp.bfloat16)
    dt_out[...] = tn(places[...], jnp.concatenate(order, axis=0)).astype(jnp.bfloat16)
    copies = pack_copies(place, pair, pack, (dq_out, dk_out, dv_out, dt_out), sems)
    back = nt(dk_out[:WIN, :], key_weight[...]) + nt(dv_out[:WIN, :], value_weight[...])

    @pl.when(pair == 0)
    def _():
        returned[...] = back

    @pl.when(pair != 0)
    def _():
        returned[...] += back

    @pl.when(pair == HEADS // 2 - 1)
    def _():
        returned_ref[...] = returned[...].astype(jnp.bfloat16)

    for copy in copies:
        copy.wait()


def pack_copies(place, pair, pack, outs, sems):
    slot = (pair // 2) ^ place[1]
    copies = []
    for index, out in enumerate(outs):
        lane = pl.multiple_of(index * D // 2 + pair % 2 * PAIR, PAIR)
        target = pack.at[slot, pl.ds(0, out.shape[0]), pl.ds(lane, PAIR)]
        copies.append(pltpu.make_async_copy(out, target, sems.at[index]))
        copies[-1].start()
    return copies


def table_rows(order, block, count):
    start = order[block] + count - 1 - order[count]
    return pl.ds(pl.multiple_of(LANES * jnp.minimum(start, count - 1), LANES), 2 * LANES)


def pooled_forward_kernel(
    info,
    order,
    content,
    position,
    normed,
    key_weight,
    value_weight,
    table,
    mixed_ref,
    keys_ref,
    values_ref,
    weights_ref,
):
    count = normed.shape[0] // LANES
    scale = jnp.asarray(HD**-0.5, jnp.bfloat16)
    keys_ref[...] = nn(normed[...], key_weight[...]).astype(jnp.bfloat16)
    values_ref[...] = nn(normed[...], value_weight[...]).astype(jnp.bfloat16)
    scores = nt(stacked(content[...] * scale), keys_ref[...])
    there = stacked(position[...] * scale)
    rows = [[], []]
    for block in range(count):
        place = nt(there, table[table_rows(order, block, count), :])
        bias = jnp.where(pooled_mask(info, LANES * order[block]), 0.0, MASKED)
        lanes = slice(block * LANES, (block + 1) * LANES)
        for index in range(2):
            half = slice(index * LANES, (index + 1) * LANES)
            rows[index].append(scores[half, lanes] + skew_pooled(place[half]) + bias)
    weights = []
    for index in range(2):
        weight = softmax_rows(jnp.concatenate(rows[index], axis=1)).astype(jnp.bfloat16)
        weights_ref[index] = weight
        weights.append(weight)
    mixed = nn(jnp.concatenate(weights, axis=0), values_ref[...])
    mixed_ref[...] = unstacked(mixed).astype(jnp.bfloat16)


def pooled_backward_kernel(
    order,
    place,
    content,
    position,
    keys,
    values,
    key_weight,
    value_weight,
    table,
    weights,
    grad,
    bias_ref,
    even_ref,
    odd_ref,
    pack,
    table_sum,
    total,
    dq_out,
    dk_out,
    dv_out,
    dt_out,
    sems,
):
    pair = pl.program_id(0)
    count = keys.shape[0] // LANES
    scale = HD**-0.5
    low_scale = jnp.asarray(scale, jnp.bfloat16)
    table_sum[...] = jnp.zeros_like(table_sum)
    grads = stacked(grad[...])
    grad_weights = nt(grads, values[...])
    lows = jnp.concatenate([weights[0], weights[1]], axis=0)
    scores = backward_scores(lows.astype(jnp.float32), grad_weights)
    low_scores = scores.astype(jnp.bfloat16)
    grad_content = unstacked(nn(low_scores, keys[...])) * scale
    positions = stacked(position[...] * low_scale)
    to_position = jnp.zeros((2 * LANES, PAIR), jnp.float32)
    for block in range(count):
        rows = table_rows(order, block, count)
        lanes = slice(block * LANES, (block + 1) * LANES)
        parts = []
        for index in range(2):
            half = low_scores[index * LANES : (index + 1) * LANES, lanes]
            parts.append(unskew_pooled(half.astype(jnp.float32)).astype(jnp.bfloat16))
        parts = jnp.concatenate(parts, axis=0)
        to_position = to_position + nn(parts, table[rows, :])
        table_sum[rows, :] += tn(parts, positions)
    grad_position = unstacked(to_position) * scale
    bias_ref[...] = column_sums(grad_content, grad_position)
    dq_out[...] = (grad_content + grad_position).astype(jnp.bfloat16)
    dk_out[...] = tn(low_scores, stacked(content[...] * low_scale)).astype(jnp.bfloat16)
    dv_out[...] = tn(lows, grads).astype(jnp.bfloat16)
    dt_out[...] = table_sum[...].astype(jnp.bfloat16)
    copies = pack_copies(place, pair, pack, (dq_out, dk_out, dv_out, dt_out), sems)
    back = nt(dk_out[...], key_weight[...]) + nt(dv_out[...], value_weight[...])

    @pl.when(pair == 0)
    def _():
        total[...] = back

    @pl.when(pair != 0)
    def _():
        total[...] += back

    @pl.when(pair == HEADS // 2 - 1)
    def _():
        for block in range(count):
            target = (even_ref, odd_ref)[block % 2]
            start = block // 2 * LANES
            rows = total[block * LANES : (block + 1) * LANES, :]
            target[start : start + LANES, :] = rows.astype(jnp.bfloat16)

    for copy in copies:
        copy.wait()


def by_pair(shape, first=0):
    front = tuple(shape[:-1])
    zeros = (0,) * len(front)
    return pl.BlockSpec(front + (PAIR,), lambda pair: zeros + (first + pair,))


def entire(shape):
    zeros = (0,) * len(shape)
    return pl.BlockSpec(tuple(shape), lambda pair: zeros)


def of_layer(shape, layer, first):
    return pl.BlockSpec((None, shape[1], PAIR), lambda pair: (layer, 0, first + pair))


def weights_block(shape):
    return pl.BlockSpec((2,) + tuple(shape[1:]), lambda pair: (pair,) + (0,) * (len(shape) - 1))


def attention_call(micros, kernel, scalars, operands, outs, scratch, mib):
    return pl.pallas_call(
        kernel,
        grid=(HEADS // 2,),
        in_specs=[SMEM] * len(scalars) + [spec for _, spec in operands],
        out_specs=[HBM if spec is None else spec for _, _, spec in outs],
        out_shape=[pltpu.HBM(shape, kind) for shape, kind, _ in outs],
        scratch_shapes=scratch,
        compiler_params=pltpu.CompilerParams(vmem_limit_bytes=mib * 2**20),
        cost_estimate=lasting(micros),
    )(*scalars, *[in_hbm(array) for array, _ in operands])


def vector(vectors, row):
    gain, shift, bias, contract, expand, pool, up = vectors
    for start, ref in ((GAIN, gain), (SHIFT, shift), (BIAS, bias)):
        if start <= row < start + 6:
            layer, index = divmod(row - start, 2)
            return ref[layer].astype(jnp.float32)[index : index + 1, :]
    if row < EXPAND:
        return contract[...].astype(jnp.float32)[row - CONTRACT : row - CONTRACT + 1, :]
    if row < POOL:
        layer, part = divmod(row - EXPAND, 4)
        lanes = slice(part * D, (part + 1) * D)
        return expand[:, lanes].astype(jnp.float32)[layer : layer + 1, :]
    if row < UP:
        return pool[...].astype(jnp.float32)
    part = row - UP
    return up[:, part * D : (part + 1) * D].astype(jnp.float32)


def normalised(values):
    centre = values - jnp.mean(values, axis=1, keepdims=True)
    spread = jnp.mean(centre * centre, axis=1, keepdims=True)
    rate = lax.rsqrt(spread + epsilon)
    return centre * rate, rate


def norm_forward(values, vectors, layer, index):
    hat, _ = normalised(values)
    gain = vector(vectors, GAIN + 2 * layer + index)
    return (hat * gain + vector(vectors, SHIFT + 2 * layer + index)).astype(jnp.bfloat16)


def norm_backward(values, vectors, layer, index, grad):
    hat, rate = normalised(values)
    scaled = grad * vector(vectors, GAIN + 2 * layer + index)
    mean = jnp.mean(scaled, axis=1, keepdims=True)
    along = jnp.mean(scaled * hat, axis=1, keepdims=True)
    result = rate * (scaled - mean - hat * along)
    return result, jnp.sum(grad * hat, axis=0, keepdims=True), jnp.sum(grad, axis=0, keepdims=True)


class Copies:
    def __init__(self, sems):
        self.sems, self.used, self.open = sems, 0, []

    def start(self, source, target):
        copy = pltpu.make_async_copy(source, target, self.sems.at[self.used])
        self.used += 1
        copy.start()
        return copy

    def send(self, source, target):
        self.open.append(self.start(source, target))

    def finish(self):
        for copy in self.open:
            copy.wait()


class Output:
    def __init__(self, buffer, target, copies):
        self.buffer, self.target, self.copies, self.sent = buffer, target, copies, False
        self.shape, self.dtype = buffer.shape, buffer.dtype

    def __setitem__(self, index, value):
        self.buffer[index] = value

    def __getitem__(self, index):
        return self.buffer[index]

    def send(self, lanes=None):
        self.sent = True
        if lanes is None:
            self.copies.send(self.buffer, self.target)
        else:
            self.copies.send(self.buffer.at[:, lanes], self.target.at[:, lanes])


def queries(layer, normed, vectors, weight, content, position):
    value = nn(normed, weight[:, :D])
    content[...] = (value + vector(vectors, BIAS + 2 * layer)).astype(jnp.bfloat16)
    position[...] = (value + vector(vectors, BIAS + 2 * layer + 1)).astype(jnp.bfloat16)
    content.send()
    position.send()


def window_project_kernel(
    layer, inputs, vectors, embedded, w_in, content, position, keys, values, table, *normed
):
    weight, copy = w_in
    rows = inputs[...]
    if normed:
        rows = norm_forward(rows.astype(jnp.float32), vectors, layer, 0)
        normed[0][...] = rows
        normed[0].send()
    copy.wait()
    queries(layer, rows, vectors, weight, content, position)
    for index, out in ((1, keys), (2, values)):
        out[...] = nn(rows, weight[:, index * D : (index + 1) * D]).astype(jnp.bfloat16)
        out.send()
    table[...] = nn(embedded[...], weight[:, 3 * D :]).astype(jnp.bfloat16)


def third_rows(ref, start):
    rows = pl.ds(start, LANES, stride=3)
    return jnp.concatenate([ref[index, rows, :] for index in range(D // LANES)], axis=1)


def put_third_rows(ref, start, values):
    for index in range(D // LANES):
        lanes = slice(index * LANES, (index + 1) * LANES)
        ref[index, pl.ds(start, LANES, stride=3), :] = values[:, lanes]


def put_rows(ref, start, values):
    for index in range(D // LANES):
        lanes = slice(index * LANES, (index + 1) * LANES)
        ref[index, start : start + values.shape[0], :] = values[:, lanes]


def all_rows(ref):
    return jnp.concatenate([ref[index] for index in range(D // LANES)], axis=1)


def kept(info, offset):
    count = LANES
    place = info[0] + 3 * lax.broadcasted_iota(jnp.int32, (count, 1), 0) + offset
    return (place >= 2) & (document(place - 2, info) == document(place, info))


def pool_kernel(info, full, edge, vectors, w_pool, normed, inputs, grouped, moved):
    pool_weight, pool_copy = w_pool
    put_rows(moved, 8, full[...])
    put_rows(moved, 6, edge[...].astype(jnp.float32))
    parts = []
    for offset in range(3):
        rows = third_rows(moved, offset + 6)
        parts.append(jnp.where(kept(info, offset), rows, 0.0).astype(jnp.bfloat16))
        grouped[:, offset * D : (offset + 1) * D] = parts[offset]
    pool_copy.wait()
    total = vector(vectors, POOL)
    for offset in range(3):
        total = total + nn(parts[offset], pool_weight[offset * D : (offset + 1) * D, :])
    normed[...] = norm_forward(total, vectors, 1, 0)
    normed.send()
    inputs[...] = total


def pooled_project_kernel(normed, vectors, embedded, w_in, content, position, table):
    weight, copy = w_in
    copy.wait()
    queries(1, normed[...], vectors, weight, content, position)
    table[...] = nn(embedded[...], weight[:, 3 * D :]).astype(jnp.bfloat16)


def feed(layer, mixed, inputs, vectors, weights, middle_ref, slope, pack):
    w_out, w_expand, w_contract = [buffer for buffer, _ in weights]
    copies = [copy for _, copy in weights]
    pack[:, :D] = mixed[...]
    copies[0].wait()
    middle = inputs[...].astype(jnp.float32) + nn(mixed[...], w_out[...])
    middle_ref[...] = middle
    middle_ref.send()
    normed_two = norm_forward(middle, vectors, layer, 1)
    pack[:, D : 2 * D] = normed_two
    pack.send(slice(0, 2 * D))
    copies[1].wait()
    copies[2].wait()
    total = middle + vector(vectors, CONTRACT + layer)
    for part in range(4):
        lanes = slice(part * D, (part + 1) * D)
        value = nn(normed_two, w_expand[:, lanes]) + vector(vectors, EXPAND + 4 * layer + part)
        below = 0.5 + 0.5 * lax.erf(value * 0.5**0.5)
        density = jnp.exp(value * value * -0.5) * (0.5 / math.pi) ** 0.5
        slope[:, lanes] = (below + value * density).astype(jnp.bfloat16)
        active = (value * below).astype(jnp.bfloat16)
        pack[:, (2 + part) * D : (3 + part) * D] = active
        slope.send(lanes)
        pack.send(slice((2 + part) * D, (3 + part) * D))
        total = total + nn(active, w_contract[lanes, :])
    return total


def window_feed_kernel(
    layer,
    mixed,
    inputs,
    vectors,
    w_out,
    w_expand,
    w_contract,
    middle,
    slope,
    pack,
    result,
    squares,
):
    weights = (w_out, w_expand, w_contract)
    total = feed(layer, mixed, inputs, vectors, weights, middle, slope, pack)
    result[...] = total.astype(result.dtype)
    squares[...] = jnp.sum(total * total, axis=0, keepdims=True)


def pooled_feed_kernel(
    mixed,
    inputs,
    grouped,
    full,
    vectors,
    w_out,
    w_expand,
    w_contract,
    w_up,
    middle,
    slope,
    pack,
    next_normed,
    result,
    squares,
    spread,
):
    weights = (w_out, w_expand, w_contract)
    total = feed(1, mixed, inputs, vectors, weights, middle, slope, pack)
    squares[...] = jnp.sum(total * total, axis=0, keepdims=True)
    low = total.astype(jnp.bfloat16)
    pack[:, 6 * D : 7 * D] = low
    pack[:, 7 * D :] = grouped[...]
    pack.send(slice(6 * D, 10 * D))
    up_buffer, copy = w_up
    copy.wait()
    for offset in range(3):
        raised = nn(low, up_buffer[:, offset * D : (offset + 1) * D])
        put_third_rows(spread, offset, raised + vector(vectors, UP + offset))
    raised = full[...] + all_rows(spread)
    next_normed[...] = norm_forward(raised, vectors, 2, 0)
    next_normed.send()
    result[...] = raised


def store_halves(core, own, other, offset, values):
    half = values.shape[1] // 2
    low = values[:, :half].astype(jnp.bfloat16)
    high = values[:, half:].astype(jnp.bfloat16)
    rows = values.shape[0]

    @pl.when(core == 0)
    def _():
        own[:rows, offset : offset + half] = low
        other[:rows, offset : offset + half] = high

    @pl.when(core != 0)
    def _():
        own[:rows, offset : offset + half] = high
        other[:rows, offset : offset + half] = low


def feed_backward(
    layer,
    place,
    grad,
    slope,
    middle,
    vectors,
    w_contract,
    w_expand,
    w_out,
    middle_grad,
    mixed_grad,
    own,
    other,
    small,
):
    contract, expand, out = [weight[0] for weight in (w_contract, w_expand, w_out)]
    copies = [weight[1] for weight in (w_contract, w_expand, w_out)]
    core = place[1]
    branch = grad.astype(jnp.bfloat16)
    small[...] = jnp.zeros_like(small)
    small[0:1, :] = jnp.sum(branch.astype(jnp.float32), axis=0, keepdims=True)
    store_halves(core, own, other, 2 * D, branch)
    copies[0].wait()
    copies[1].wait()
    normed_grad = jnp.zeros(grad.shape, jnp.float32)
    changes = []
    for part in range(4):
        lanes = slice(part * D, (part + 1) * D)
        change = nt(branch, contract[lanes, :]) * slope[:, lanes].astype(jnp.float32)
        change = change.astype(jnp.bfloat16)
        changes.append(change)
        small[3 + part : 4 + part, :] = jnp.sum(
            change.astype(jnp.float32), axis=0, keepdims=True
        )
        normed_grad = normed_grad + nt(change, expand[:, lanes])
    store_halves(core, own, other, 0, jnp.concatenate(changes, axis=1))
    norm, gain, shift = norm_backward(middle[...], vectors, layer, 1, normed_grad)
    small[1:2, :] = gain
    small[2:3, :] = shift
    total = grad + norm
    middle_grad[...] = total
    attend = total.astype(jnp.bfloat16)
    store_halves(core, own, other, 2 * D + D // 2, attend)
    other.send()
    copies[2].wait()
    mixed_grad[...] = nt(attend, out[...]).astype(jnp.bfloat16)


def feed_backward_kernel(layer, place, grad, *refs):
    feed_backward(layer, place, grad[...].astype(jnp.float32), *refs)


def first_feed_backward_kernel(place, joined, shifted, came_back, *refs):
    moved = refs[-1]
    rows = shifted.shape[0]
    moved[:rows, :] = shifted[...]
    moved[rows : rows + 2, :] = came_back[...]
    feed_backward(0, place, joined[...] + moved[2 : rows + 2, :], *refs[:-1])


def project_backward(layer, core, pack, rows, weight, extra, inputs, middle_grad, vectors, small):
    small[...] = jnp.zeros_like(small)
    normed_grad = extra
    for index, chosen in enumerate(rows):
        for slot in range(2):
            half = slot ^ core
            begin = pl.multiple_of(index * D + half * (D // 2), D // 2)
            grad = pack[slot, chosen, index * D // 2 : (index + 1) * D // 2]
            normed_grad = normed_grad + nt(grad, weight[:, pl.ds(begin, D // 2)])
    norm, gain, shift = norm_backward(inputs, vectors, layer, 0, normed_grad)
    small[0:1, :] = gain
    small[1:2, :] = shift
    return middle_grad[...] + norm


def window_project_backward(layer, core, pack, returned, weight, *rest):
    extra = jnp.concatenate(
        [jnp.zeros((QBLK - WIN, D), jnp.float32), returned[...].astype(jnp.float32)], axis=0
    )
    rows = (slice(0, QBLK), slice(WIN, REACH), slice(WIN, REACH))
    return project_backward(layer, core, pack, rows, weight, extra, *rest)


def first_project_backward_kernel(
    place, pack, returned, inputs, middle_grad, vectors, w_in, inputs_grad, small
):
    weight, copy = w_in
    copy.wait()
    rows = inputs[...].astype(jnp.float32)
    total = window_project_backward(
        0, place[1], pack, returned, weight, rows, middle_grad, vectors, small
    )
    inputs_grad[...] = total.astype(inputs_grad.dtype)


def last_project_backward_kernel(
    place,
    pack,
    returned,
    inputs,
    middle_grad,
    vectors,
    w_in,
    w_up,
    inputs_grad,
    short_grad,
    own,
    other,
    small,
    spread,
):
    (weight, copy), (up_weight, up_copy) = w_in, w_up
    copy.wait()
    total = window_project_backward(
        2, place[1], pack, returned, weight, inputs[...], middle_grad, vectors, small
    )
    inputs_grad[...] = total
    inputs_grad.send()
    put_rows(spread, 0, total)
    parts = [third_rows(spread, offset).astype(jnp.bfloat16) for offset in range(3)]
    up_copy.wait()
    result = jnp.zeros((LANES, D), jnp.float32)
    for offset in range(3):
        small[2 + offset : 3 + offset, :] = jnp.sum(
            parts[offset].astype(jnp.float32), axis=0, keepdims=True
        )
        result = result + nt(parts[offset], up_weight[:, offset * D : (offset + 1) * D])
    short_grad[...] = result
    joined = jnp.concatenate(parts, axis=1)
    half = 3 * D // 2
    quarter = half // 3

    def place_parts(target, values):
        for index in range(3):
            target[index * LANES : (index + 1) * LANES, :] = values[
                :, index * quarter : (index + 1) * quarter
            ]

    @pl.when(place[1] == 0)
    def _():
        place_parts(own, joined[:, :half])
        place_parts(other, joined[:, half:])

    @pl.when(place[1] != 0)
    def _():
        place_parts(own, joined[:, half:])
        place_parts(other, joined[:, :half])


def pooled_project_backward_kernel(
    info,
    place,
    pack,
    normed_grad,
    inputs,
    middle_grad,
    vectors,
    w_in,
    w_pool,
    shifted_grad,
    own,
    other,
    small,
    spread,
):
    (weight, copy), (pool_weight, pool_copy) = w_in, w_pool
    copy.wait()
    total = project_backward(
        1,
        place[1],
        pack,
        (slice(0, LANES),),
        weight,
        normed_grad[...],
        inputs[...],
        middle_grad,
        vectors,
        small,
    )
    low = total.astype(jnp.bfloat16)
    small[2:3, :] = jnp.sum(low.astype(jnp.float32), axis=0, keepdims=True)
    store_halves(place[1], own, other, 0, low)
    pool_copy.wait()
    for offset in range(3):
        rows = nt(low, pool_weight[offset * D : (offset + 1) * D, :])
        put_third_rows(spread, offset, jnp.where(kept(info, offset), rows, 0.0))
    shifted_grad[...] = all_rows(spread)


def lasting(micros):
    return pl.CostEstimate(
        flops=int(micros * 1e8), bytes_accessed=int(micros * 3e5), transcendentals=0
    )


class Part:
    def __init__(self, array, shape):
        self.array, self.shape = array, tuple(shape)

    def of(self, ref):
        if self.shape == self.array.shape:
            return ref
        return ref.at[tuple(slice(0, size) for size in self.shape)]


def whole(micros, kernel, scalars, arrays, weights, outs, scratch=(), mib=24):
    flat, groups, parts = [], [], []
    for array in arrays:
        groups.append(len(array) if isinstance(array, tuple) else 0)
        for item in array if isinstance(array, tuple) else (array,):
            part = item if isinstance(item, Part) else Part(item, item.shape)
            flat.append(part.array)
            parts.append(part)
    shapes = [(part.shape, part.array.dtype) for part in parts]
    shapes += [(w.shape if layer is None else w.shape[1:], w.dtype) for w, layer in weights]
    shapes += list(outs) + list(scratch)
    scalar_count, flat_count, weight_count = len(scalars), len(flat), len(weights)
    sem_count = 64

    def run(*refs):
        copies = Copies(refs[-1])
        refs = list(refs[:-1])

        def take(count):
            taken, refs[:count] = refs[:count], []
            return taken

        taken = take(scalar_count)
        sources, weight_sources, targets = take(flat_count), take(weight_count), take(len(outs))
        buffers, weight_buffers, out_buffers = take(flat_count), take(weight_count), take(len(outs))
        loads = [copies.start(p.of(s), b) for p, s, b in zip(parts, sources, buffers)]
        loaded = []
        for (_, layer), source, buffer in zip(weights, weight_sources, weight_buffers):
            source = source if layer is None else source.at[layer]
            loaded.append((buffer, copies.start(source, buffer)))
        for copy in loads:
            copy.wait()
        position = 0
        for size in groups:
            taken.append(buffers[position : position + size] if size else buffers[position])
            position += size or 1
        results = [Output(b, t, copies) for b, t in zip(out_buffers, targets)]
        kernel(*taken, *loaded, *results, *refs)
        for result in results:
            if not result.sent:
                result.send()
        copies.finish()

    return pl.pallas_call(
        run,
        in_specs=[SMEM] * scalar_count + [HBM] * (flat_count + weight_count),
        out_specs=[HBM] * len(outs),
        out_shape=[pltpu.HBM(shape, kind) for shape, kind in outs],
        scratch_shapes=[pltpu.VMEM(*item) for item in shapes]
        + [pltpu.SemaphoreType.DMA((sem_count,))],
        compiler_params=pltpu.CompilerParams(vmem_limit_bytes=mib * 2**20),
        cost_estimate=lasting(micros),
    )(*scalars, *[in_hbm(a) for a in flat + [w for w, _ in weights]])


def in_hbm(array):
    return pltpu.with_memory_space_constraint(array, pltpu.HBM)


def crossed(block, axis, bit):
    count = lax.axis_size(axis)
    return lax.ppermute(block, axis, [(index, index ^ bit) for index in range(count)])


def passed_along(block, axis, distance):
    devices = range(lax.axis_size(axis))
    route = [(i - distance, i) for i in devices if i - distance in devices]
    return lax.ppermute(block, axis, route)


def both(low, high, bit):
    return jnp.where(bit, high, low), jnp.where(bit, low, high)


def rounded_sum(*terms):
    return sum(term.astype(jnp.float32) for term in terms).astype(jnp.bfloat16)


def gather_pooled(rows):
    half = rows.shape[0] // 2
    from_x = crossed(rows, "seq", 2)
    from_y = crossed(rows, "seq", 4)
    from_core = crossed(rows, "seq", 1)
    first = crossed(from_x[:half], "seq", 4)
    second = crossed(from_y[half:], "seq", 2)
    core_x = crossed(from_x, "seq", 1)
    core_y = crossed(from_y, "seq", 1)
    opposite = jnp.concatenate([first, second], axis=0)
    core_opposite = crossed(opposite, "seq", 1)
    return jnp.concatenate(
        [rows, from_core, from_x, core_x, from_y, core_y, opposite, core_opposite], axis=0
    )


def scatter_pooled(even, odd, meanwhile):
    arrived = crossed(odd, "seq", 1)
    total = rounded_sum(even, arrived).reshape(4, LANES, D)
    made = meanwhile(total)
    left, right = total[:, :, : D // 2], total[:, :, D // 2 :]
    left_arrived = crossed(jnp.stack([left[1], left[3]]), "seq", 2)
    right_arrived = crossed(right[2:], "seq", 4)
    (left_arrived, right_arrived), _ = together((left_arrived, right_arrived), made)
    left_next = crossed(rounded_sum(left[2], left_arrived[1]), "seq", 4)
    right_next = crossed(rounded_sum(right[1], right_arrived[1]), "seq", 2)

    def added(*terms):
        return sum(term.astype(jnp.float32) for term in terms)

    total = jnp.concatenate(
        [
            added(left[0], left_arrived[0], left_next),
            added(right[0], right_arrived[0], right_next),
        ],
        axis=1,
    )
    return total, made


class Piece:
    def __init__(self, features, halves, reads, compute):
        self.height, self.halves, self.reads, self.compute = features // 4, halves, reads, compute
        self.lanes = sum(features // D * half // 2 for half in halves)


def plain_piece(x, first, features, dy, start, half):
    def compute(refs, chosen):
        return [sum(tn(a[:, chosen], b[...]) for a, b in zip(refs[x], refs[dy]))]

    return Piece(features, [half], {x: (first, features), dy: (start, half)}, compute)


def table_part(embedded, grads, chosen):
    rows = embedded.shape[0]
    lanes = slice(3 * D // 2, 2 * D)
    summed = sum(grad[:rows, lanes].astype(jnp.float32) for grad in grads)
    return tn(embedded[:, chosen], summed.astype(jnp.bfloat16))


def window_piece(normed, grads, table):
    def compute(refs, chosen):
        totals = []
        for index, (rows, grad_rows) in enumerate(
            ((slice(WIN, REACH), slice(0, QBLK)),) + ((slice(0, REACH),) * 2,) * 2
        ):
            lanes = slice(index * D // 2, (index + 1) * D // 2)
            totals.append(
                sum(
                    tn(features[rows, chosen], grad[grad_rows, lanes])
                    for features, grad in zip(refs[normed], refs[grads])
                )
            )
        return totals + [table_part(refs[table][0], refs[grads], chosen)]

    return Piece(D, [D // 2] * 4, {normed: (0, D), grads: (0, 2 * D), table: (0, D)}, compute)


def pooled_piece(normed, grads, table):
    def compute(refs, chosen):
        (features,) = refs[normed]
        own, pair = refs[grads]
        count = features.shape[0] // LANES
        lanes = slice(0, D // 2)
        query = sum(
            tn(features[index * LANES : (index + 1) * LANES, chosen], grad[:LANES, lanes])
            for index, grad in enumerate((own, pair))
        )
        totals = [query]
        for index in (1, 2):
            lanes = slice(index * D // 2, (index + 1) * D // 2)
            parts = []
            for block in range(count):
                near, far = block * LANES, (block ^ 1) * LANES
                parts.append(
                    rounded_sum(own[near : near + LANES, lanes], pair[far : far + LANES, lanes])
                )
            totals.append(tn(features[:, chosen], jnp.concatenate(parts, axis=0)))
        return totals + [table_part(refs[table][0], refs[grads], chosen)]

    return Piece(D, [D // 2] * 4, {normed: (0, D), grads: (0, 2 * D), table: (0, D)}, compute)


def upsample_piece(x, first, dy):
    def compute(refs, chosen):
        parts = []
        for index in range(3):
            rows = slice(index * LANES, (index + 1) * LANES)
            parts.append(sum(tn(a[:, chosen], b[rows, :]) for a, b in zip(refs[x], refs[dy])))
        return [jnp.concatenate(parts, axis=1)]

    return Piece(D, [3 * D // 2], {x: (first, D), dy: (0, D // 2)}, compute)


def pair_gradients(micros, place, sources, pieces):
    lanes = sum(piece.lanes for piece in pieces)
    flat, first = [], {}
    for name, arrays in sources.items():
        first[name] = len(flat)
        flat.extend(arrays)
    buffers = []
    for piece in pieces:
        for name, (_, width) in piece.reads.items():
            for array in sources[name]:
                buffers.append(pltpu.VMEM((array.shape[-2], width), array.dtype))
    count = len(flat)
    out = (2, LANES, lanes)

    def kernel(place, *refs):
        arrays, targets = refs[:count], refs[count : count + 4]
        spaces, sems = list(refs[count + 4 : -5]), refs[-1]
        copies = Copies(sems)
        keep_one, send_one, keep_two, send_two = refs[-5:-1]
        ready = []
        for piece in pieces:
            inputs, loads = {}, []
            for name, (start, width) in piece.reads.items():
                inputs[name] = []
                for index in range(len(sources[name])):
                    source = arrays[first[name] + index]
                    space = spaces.pop(0)
                    if len(source.shape) == 3:
                        source = source.at[0]
                    if width != source.shape[1]:
                        source = source.at[:, start : start + width]
                    loads.append(copies.start(source, space))
                    inputs[name].append(space)
            ready.append((inputs, loads))
        offset = 0
        for piece, (inputs, loads) in zip(pieces, ready):
            for load in loads:
                load.wait()
            groups = piece.height // LANES
            for block in range(4):
                begin = pl.multiple_of((place[0] ^ block) * piece.height, LANES)
                totals = piece.compute(inputs, pl.ds(begin, piece.height))
                position = offset
                for total in totals:
                    total = total.astype(jnp.bfloat16)
                    quarter = total.shape[1] // 2
                    for space, slot, part in (
                        ((keep_one, send_one)[block % 2], block // 2, total[:, :quarter]),
                        ((keep_two, send_two)[block // 2], block % 2, total[:, quarter:]),
                    ):
                        if groups == 1:
                            space[slot, :, position : position + quarter] = part
                            continue
                        for group in range(groups):
                            start = position + quarter * group
                            low = HD * group
                            high = piece.height // 2 + low
                            space[slot, :HD, start : start + quarter] = part[low : low + HD]
                            space[slot, HD:, start : start + quarter] = part[high : high + HD]
                    position += quarter * groups
            done = slice(offset, offset + piece.lanes)
            for space, target in zip((keep_one, send_one, keep_two, send_two), targets):
                copies.send(space.at[:, :, done], target.at[:, :, done])
            offset += piece.lanes
        copies.finish()

    return pl.pallas_call(
        kernel,
        in_specs=[SMEM] + [HBM] * count,
        out_specs=[HBM] * 4,
        out_shape=[pltpu.HBM(out, jnp.bfloat16)] * 4,
        scratch_shapes=buffers
        + [pltpu.VMEM(out, jnp.bfloat16)] * 4
        + [pltpu.SemaphoreType.DMA((64,))],
        compiler_params=pltpu.CompilerParams(vmem_limit_bytes=32 * 2**20),
        cost_estimate=lasting(micros),
    )(place, *[in_hbm(a) for a in flat])


def first_step(keep_one, send_one, keep_two, send_two):
    return keep_one, crossed(send_one, "seq", 2), keep_two, crossed(send_two, "seq", 4)


def first_sums(*groups):
    parts = [[], [], [], []]
    for keep_one, one, keep_two, two in groups:
        for index in range(2):
            parts[index].append(rounded_sum(keep_one[index], one[index]))
            parts[2 + index].append(rounded_sum(keep_two[index], two[index]))
    return tuple(jnp.concatenate(part, axis=1) for part in parts)


def second_step(one, send_one, two, send_two):
    return one, crossed(send_one, "seq", 4), two, crossed(send_two, "seq", 2)


def second_sums(one, add_one, two, add_two):
    return rounded_sum(one, add_one), rounded_sum(two, add_two)


def depth_halves(first, second, depth):
    keep, send = both(first, second, depth)
    return keep, crossed(send, "dp", 1)


def depth_quarters(keep, arrived):
    keep = rounded_sum(keep, arrived)
    return keep, crossed(keep, "dp", 2)


def depth_back(keep, arrived):
    keep = rounded_sum(keep, arrived)
    return keep, crossed(keep, "dp", 1)


def shared(keep, other, depth, core):
    first, second = both(keep, other, depth)
    share = jnp.concatenate([first, second], axis=1)
    keep, send = both(share[:HD], share[HD:], core)
    return both(keep, crossed(send, "seq", 1), core)


def together(*groups):
    return lax.optimization_barrier(tuple(tuple(group) for group in groups))


def final_kernel(plan, *refs):
    groups = len(plan)
    buffers, outs = refs[: 2 * groups], refs[2 * groups :]
    for index, pieces in enumerate(plan):
        lanes = buffers[2 * index].shape[1] // 2
        offset = 0
        for out_index, layer, first_column, columns, height in pieces:
            out = outs[out_index]
            quarter = columns // 4
            for group in range(height // HD):
                rows = pl.ds(HD * group, HD)
                for part in range(4):
                    buffer = buffers[2 * index + part // 2]
                    start = (part % 2) * lanes + offset
                    value = buffer[:, start : start + quarter].astype(jnp.float32)
                    begin = first_column + part * quarter
                    if layer is None:
                        out[rows, begin : begin + quarter] = value
                    else:
                        out[layer, rows, begin : begin + quarter] = value
                offset += quarter


def final_outputs(plan, buffers, shapes):
    flat = [array for pair in buffers for array in pair]
    return pl.pallas_call(
        partial(final_kernel, plan),
        in_specs=[VMEM] * len(flat),
        out_specs=[VMEM] * len(shapes),
        out_shape=[jax.ShapeDtypeStruct(shape, jnp.float32) for shape in shapes],
        compiler_params=pltpu.CompilerParams(vmem_limit_bytes=16 * 2**20),
        cost_estimate=lasting(3),
    )(*flat)


def summed_everywhere(flat):
    for axis in ("seq", "dp"):
        for bit in range(lax.axis_size(axis).bit_length() - 1):
            flat = flat + crossed(flat, axis, 1 << bit)
    return flat


def phases(distance):
    frequency = jnp.power(10000.0, -2.0 * jnp.arange(D // 2, dtype=jnp.float32) / D)
    angle = distance.astype(jnp.float32)[:, None] * frequency[None, :]
    return jnp.sin(angle), jnp.cos(angle)


def embedding(first, count):
    step = 32
    high_sin, high_cos = phases(first - step * jnp.arange(count // step))
    low_sin, low_cos = phases(-jnp.arange(step))
    high_sin, high_cos = high_sin[:, None], high_cos[:, None]
    sines = high_sin * low_cos[None] + high_cos * low_sin[None]
    cosines = high_cos * low_cos[None] - high_sin * low_sin[None]
    return jnp.concatenate([sines, cosines], axis=2).astype(jnp.bfloat16).reshape(count, D)


def outer_float(first_matrix, second_matrix):
    return jnp.einsum("rc,re->ce", first_matrix, second_matrix, preferred_element_type=jnp.float32)


BF, FL = jnp.bfloat16, jnp.float32


def window_project(layer, inputs, vectors, embedded, w_in, normalise):
    one = (inputs.shape, BF)
    outs = [one, one, one, one, (embedded.shape, BF)] + [one] * normalise
    return whole(
        4,
        partial(window_project_kernel, layer),
        [],
        [inputs, vectors, embedded],
        [(w_in, layer)],
        outs,
    )


def window_attention(layer, raw, info, heads, border, vectors, w_in, table):
    rows = heads[0].shape[0]
    operands = [(a, by_pair(a.shape)) for a in heads]
    operands += [(a, entire(a.shape)) for a in (border, vectors[0], vectors[1])]
    operands += [(w_in, of_layer(w_in.shape, layer, first)) for first in (4, 8)]
    operands.append((table, by_pair(table.shape)))
    weights = (HEADS, PARTS, LANES, SEEN)
    pair_border = (2, WIN, D)
    outs = [
        ((rows, D), BF, by_pair((rows, D))),
        (border.shape, BF, entire(border.shape)),
        (pair_border, BF, by_pair(pair_border)),
        (weights, BF, weights_block(weights)),
    ]
    scratch = [
        pltpu.VMEM((PARTS, LANES, SEEN), FL),
        pltpu.VMEM(border.shape, BF),
        pltpu.VMEM((2 * rows, SEEN), FL),
    ]
    kernel = partial(window_forward_kernel, layer if raw else None)
    return attention_call(11, kernel, [info], operands, outs, scratch, 20)


def window_attention_back(layer, place, heads, border, w_in, table, weights, grad):
    rows = heads[0].shape[0]
    operands = [(a, by_pair(a.shape)) for a in (*heads, border)]
    operands += [(w_in, of_layer(w_in.shape, layer, first)) for first in (4, 8)]
    operands += [(table, by_pair(table.shape)), (weights, weights_block(weights.shape))]
    operands.append((grad, by_pair(grad.shape)))
    outs = [
        ((2, D), FL, by_pair((2, D))),
        ((WIN, D), BF, entire((WIN, D))),
        ((2, REACH, 2 * D), BF, None),
    ]
    scratch = [pltpu.VMEM((REACH, PAIR), FL)] * 2
    scratch += [pltpu.VMEM((WIN, D), FL), pltpu.VMEM((2 * rows, SEEN), BF)]
    scratch += [pltpu.VMEM((size, PAIR), BF) for size in (rows, REACH, REACH, table.shape[0])]
    scratch.append(pltpu.SemaphoreType.DMA((4,)))
    return attention_call(13, window_backward_kernel, [place], operands, outs, scratch, 20)


def pooled_attention(info, order, content, position, normed, w_in, table):
    rows, total = content.shape[0], normed.shape[0]
    operands = [(a, by_pair(a.shape)) for a in (content, position)]
    operands.append((normed, entire(normed.shape)))
    operands += [(w_in, of_layer(w_in.shape, 1, first)) for first in (4, 8)]
    operands.append((table, by_pair(table.shape)))
    weights = (HEADS, LANES, total)
    outs = [
        ((rows, D), BF, by_pair((rows, D))),
        ((total, D), BF, by_pair((total, D))),
        ((total, D), BF, by_pair((total, D))),
        (weights, BF, weights_block(weights)),
    ]
    mib = 10 + total // LANES * 3 // 2
    return attention_call(13, pooled_forward_kernel, [info, order], operands, outs, [], mib)


def pooled_attention_back(order, place, heads, w_in, table, weights, grad):
    rows, total = heads[0].shape[0], heads[2].shape[0]
    operands = [(a, by_pair(a.shape)) for a in heads]
    operands += [(w_in, of_layer(w_in.shape, 1, first)) for first in (4, 8)]
    operands += [(table, by_pair(table.shape)), (weights, weights_block(weights.shape))]
    operands.append((grad, by_pair(grad.shape)))
    half = ((total // LANES + 1) // 2 * LANES, D)
    outs = [
        ((2, D), FL, by_pair((2, D))),
        (half, BF, entire(half)),
        (half, BF, entire(half)),
        ((2, table.shape[0], 2 * D), BF, None),
    ]
    scratch = [pltpu.VMEM((table.shape[0], PAIR), FL), pltpu.VMEM((total, D), FL)]
    scratch += [pltpu.VMEM((size, PAIR), BF) for size in (rows, total, total, table.shape[0])]
    scratch.append(pltpu.SemaphoreType.DMA((4,)))
    mib = 10 + total // LANES * 3 // 2
    return attention_call(13, pooled_backward_kernel, [order, place], operands, outs, scratch, mib)


def window_feed(layer, mixed, inputs, vectors, weights, kind):
    rows = mixed.shape[0]
    outs = [
        ((rows, D), FL),
        ((rows, 4 * D), BF),
        ((rows, 6 * D), BF),
        ((rows, D), kind),
        ((1, D), FL),
    ]
    return whole(
        7,
        partial(window_feed_kernel, layer),
        [],
        [mixed, inputs, vectors],
        [(w, layer) for w in weights],
        outs,
    )


def feed_back(kernel, layer, place, arrays, rows, weights, extra=()):
    outs = [((rows, D), FL), ((rows, D), BF), ((rows, 3 * D), BF), ((rows, 3 * D), BF)]
    outs.append(((8, D), FL))
    return whole(8, kernel, [place], arrays, [(w, layer) for w in weights], outs, extra)


def per_device(
    tokens,
    doc_lengths,
    cotangent,
    norm_gain,
    norm_shift,
    relative_bias,
    attention_in,
    attention_out,
    expand_weight,
    expand_bias,
    contract_weight,
    contract_bias,
    pool_weight,
    pool_bias,
    upsample_weight,
    upsample_bias,
):
    def by_layer(weight):
        return jnp.transpose(weight, (1, 0, 2))

    w_in, w_out = by_layer(attention_in), by_layer(attention_out)
    w_expand, w_contract = by_layer(expand_weight), by_layer(contract_weight)
    ff_weights = [w_out, w_expand, w_contract]
    vectors = (norm_gain, norm_shift, relative_bias, contract_bias, expand_bias)
    vectors += (pool_bias[None], upsample_bias[None])

    inputs = tokens[0]
    rows = inputs.shape[0]
    pooled_rows = rows // 3
    device = lax.axis_index("seq").astype(jnp.int32)
    seq_count = lax.axis_size("seq")
    usual = seq_count == 8 and lax.axis_size("dp") == 4
    core_index = device % 2
    core = core_index == 1
    depth = lax.axis_index("dp") % 2 == 1
    place = jnp.stack([device // 2, core_index])
    ends = jnp.cumsum(doc_lengths[0]).astype(jnp.int32)
    info = jnp.concatenate([(device * rows)[None], ends]).astype(jnp.int32)
    pooled_info = jnp.concatenate([(device * pooled_rows)[None], ends]).astype(jnp.int32)
    order = jnp.arange(seq_count, dtype=jnp.int32)
    if usual:
        order = order ^ device
    order = jnp.concatenate([order, device[None]])
    near_table = embedding(WIN, QBLK)
    far_table = embedding(seq_count * pooled_rows - 1, (seq_count + 1) * pooled_rows)

    def swapped(array):
        return (array, crossed(array, "seq", 1)) if usual else array

    def swapped_halves(own, other):
        return (own, crossed(other, "seq", 1)) if usual else (own, other)

    border0 = passed_along(inputs[rows - WIN :], "seq", 1)
    *heads0, table0, normed0 = window_project(0, inputs, vectors, near_table, w_in, True)
    mixed0, edge_normed0, border0, weights0 = window_attention(
        0, True, info, heads0, border0, vectors, w_in, table0
    )
    middle0, slope0, pack0, full0, squares0 = window_feed(
        0, mixed0, inputs, vectors, ff_weights, FL
    )
    edge = passed_along(full0[rows - 2 :].astype(BF), "seq", 1)
    x0, n0 = swapped(pack0), swapped(jnp.concatenate([edge_normed0, normed0], axis=0))

    one = ((pooled_rows, D), BF)
    spread = ((D // LANES, rows, LANES), FL)
    normed1, inputs1, grouped = whole(
        4,
        pool_kernel,
        [info],
        [full0, edge, vectors],
        [(pool_weight, None)],
        [one, ((pooled_rows, D), FL), ((pooled_rows, 3 * D), BF)],
        [((D // LANES, rows + 8, LANES), FL)],
    )
    if usual:
        normed1_all = gather_pooled(normed1)
    else:
        normed1_all = lax.all_gather(normed1, "seq", axis=0, tiled=True)
    content1, position1, table1 = whole(
        4,
        pooled_project_kernel,
        [],
        [normed1, vectors, far_table],
        [(w_in, 1)],
        [one, one, (far_table.shape, BF)],
    )
    mixed1, keys1, values1, weights1 = pooled_attention(
        pooled_info, order, content1, position1, normed1_all, w_in, table1
    )
    if usual:
        (mixed1,), x0, n0 = together((mixed1,), x0, n0)
    middle1, slope1, pack1, normed2, inputs2, squares1 = whole(
        7,
        pooled_feed_kernel,
        [],
        [mixed1, inputs1, grouped, full0, vectors],
        [(w, 1) for w in ff_weights] + [(upsample_weight, None)],
        [
            ((pooled_rows, D), FL),
            ((pooled_rows, 4 * D), BF),
            ((pooled_rows, 10 * D), BF),
            ((rows, D), BF),
            ((rows, D), FL),
            ((1, D), FL),
        ],
        [spread],
    )

    border2 = passed_along(normed2[rows - WIN :], "seq", 1)
    *heads2, table2 = window_project(2, normed2, vectors, near_table, w_in, False)
    mixed2, edge_normed2, border2, weights2 = window_attention(
        2, False, info, heads2, border2, vectors, w_in, table2
    )
    x1, n2 = swapped(pack1), swapped(jnp.concatenate([edge_normed2, normed2], axis=0))
    if usual:
        (mixed2,), x1, n2 = together((mixed2,), x1, n2)
    middle2, slope2, pack2, output, squares2 = window_feed(
        2, mixed2, inputs2, vectors, ff_weights, BF
    )

    share = D // seq_count
    shapes = [
        (3, share, 4 * D),
        (3, share, D),
        (3, share, 4 * D),
        (3, 4 * share, D),
        (3 * share, D),
        (share, 3 * D),
    ]

    every = {"near": (near_table,), "far": (far_table,)}

    def feed_pieces(x, dy, layer):
        pieces = [
            plain_piece(x, D, D, dy, 0, 2 * D),
            plain_piece(x, 2 * D, 4 * D, dy, 2 * D, D // 2),
            plain_piece(x, 0, D, dy, 2 * D + D // 2, D // 2),
        ]
        targets = [
            (2, layer, 0, 4 * D, share),
            (3, layer, 0, D, 4 * share),
            (1, layer, 0, D, share),
        ]
        return pieces, targets

    def project_targets(layer):
        return [(0, layer, index * D, D, share) for index in range(4)]

    feed2 = feed_pieces("x2", "a2", 2)
    project2 = [window_piece("n2", "b2", "near")], project_targets(2)
    up = [upsample_piece("x1", 6 * D, "u2")], [(5, None, 0, 3 * D, share)]
    feed1 = feed_pieces("x1", "a1", 1)
    project1 = [pooled_piece("n1", "b1", "far")], project_targets(1)
    pool = [plain_piece("x1", 7 * D, 3 * D, "p1", 0, D // 2)], [(4, None, 0, D, 3 * share)]
    feed0 = feed_pieces("x0", "a0", 0)
    project0 = [window_piece("n0", "b0", "near")], project_targets(0)

    def gradients(names, follows, *parts):
        if not usual:
            return ()
        pieces = sum((part[0] for part in parts), [])
        sources = {name: every[name] for name in names}
        first = names[0]
        sources[first], _ = together(sources[first], follows)
        return tuple(pair_gradients(7, place, sources, pieces))

    def step(function, values, *options):
        return tuple(function(*values, *options)) if usual else ()

    back_weights = [w_contract, w_expand, w_out]
    x2 = swapped(pack2)
    every["x0"], every["x1"], every["x2"] = x0, x1, x2
    every["n0"], every["n1"], every["n2"] = n0, (normed1_all,), n2

    def swapped_pack(pack):
        return (pack, crossed(pack[1], "seq", 1)) if usual else pack

    middle_grad2, mixed_grad2, own_a2, other_a2, small_a2 = feed_back(
        partial(feed_backward_kernel, 2),
        2,
        place,
        [cotangent[0], slope2, middle2, vectors],
        rows,
        back_weights,
    )
    every["a2"] = swapped_halves(own_a2, other_a2)
    if usual:
        (mixed_grad2,), every["x2"] = together((mixed_grad2,), x2)
    bias2, leaving2, grads2 = window_attention_back(
        2, place, heads2, border2, w_in, table2, weights2, mixed_grad2
    )
    returned2 = passed_along(leaving2, "seq", -1)
    every["b2"] = swapped_pack(grads2)
    group2a = gradients(("a2", "x2", "b2", "n2", "near"), (bias2,), feed2, project2)
    (returned2,), group2a = together((returned2,), group2a)
    group2a = step(first_step, group2a)
    joined, short_grad, own_u2, other_u2, small_b2 = whole(
        6,
        last_project_backward_kernel,
        [place],
        [Part(grads2, (2, REACH, 3 * D // 2)), returned2, inputs2, middle_grad2, vectors],
        [(w_in, 2), (upsample_weight, None)],
        [
            ((rows, D), FL),
            ((pooled_rows, D), FL),
            ((rows, D // 2), BF),
            ((rows, D // 2), BF),
            ((8, D), FL),
        ],
        [spread],
    )
    every["u2"] = swapped_halves(own_u2, other_u2)

    middle_grad1, mixed_grad1, own_a1, other_a1, small_a1 = feed_back(
        partial(feed_backward_kernel, 1),
        1,
        place,
        [short_grad, slope1, middle1, vectors],
        pooled_rows,
        back_weights,
    )
    every["a1"] = swapped_halves(own_a1, other_a1)
    (mixed_grad1,), group2a = together((mixed_grad1,), group2a)
    group2a = step(first_sums, (group2a,))
    (mixed_grad1,), group2a = together((mixed_grad1,), group2a)
    group2a = step(second_step, group2a)
    heads1 = (content1, position1, keys1, values1)
    bias1, even, odd, grads1 = pooled_attention_back(
        order, place, heads1, w_in, table1, weights1, mixed_grad1
    )
    every["b1"] = swapped_pack(grads1)

    def group1_gradients(total):
        return gradients(("a1", "x1", "u2"), (total,), up, feed1)

    if usual:
        (even, odd), group2a = together((even, odd), group2a)
        normed_grad1, group1 = scatter_pooled(even, odd, group1_gradients)
    else:
        group1 = ()
        split = (seq_count // 2, 1, LANES, D)
        summed = jnp.concatenate([even.reshape(split), odd.reshape(split)], axis=1)
        summed = summed.reshape(seq_count * LANES, D)
        normed_grad1 = lax.psum_scatter(summed, "seq", scatter_dimension=0, tiled=True).astype(FL)
    (normed_grad1,), group1, group2a = together((normed_grad1,), group1, group2a)
    group1 = step(first_step, group1)
    group2a = step(second_sums, group2a)
    group2a = step(depth_halves, group2a, depth)
    shifted_grad, own_p1, other_p1, small_b1 = whole(
        5,
        pooled_project_backward_kernel,
        [info, place],
        [Part(grads1, (2, LANES, D // 2)), normed_grad1, inputs1, middle_grad1, vectors],
        [(w_in, 1), (pool_weight, None)],
        [((rows, D), FL), ((pooled_rows, D // 2), BF), ((pooled_rows, D // 2), BF), ((8, D), FL)],
        [spread],
    )
    every["p1"] = swapped_halves(own_p1, other_p1)
    came_back = passed_along(shifted_grad[:2], "seq", -1)
    group1b = gradients(("p1", "x1", "b1", "n1", "far"), (shifted_grad,), pool, project1)
    (came_back,), group1b, group2a = together((came_back,), group1b, group2a)
    group1b = step(first_step, group1b)
    group2a = step(depth_quarters, group2a)
    middle_grad0, mixed_grad0, own_a0, other_a0, small_a0 = feed_back(
        first_feed_backward_kernel,
        0,
        place,
        [joined, shifted_grad, came_back, slope0, middle0, vectors],
        rows,
        back_weights,
        [((rows + 8, D), FL)],
    )
    every["a0"] = swapped_halves(own_a0, other_a0)
    (mixed_grad0,), group1, group1b = together((mixed_grad0,), group1, group1b)
    group1 = step(first_sums, (group1, group1b))
    (mixed_grad0,), group1 = together((mixed_grad0,), group1)
    group1 = step(second_step, group1)
    bias0, leaving0, grads0 = window_attention_back(
        0, place, heads0, border0, w_in, table0, weights0, mixed_grad0
    )
    every["b0"] = swapped_pack(grads0)
    returned0 = passed_along(leaving0, "seq", -1)

    clock = (bias0,)
    if usual:
        clock, group1, group2a = together(clock, group1, group2a)
        group1 = step(second_sums, group1)
        group1 = step(depth_halves, group1, depth)
        group2a = step(depth_back, group2a)
        group0 = gradients(("a0", "x0"), clock, feed0)
        clock, group0 = together(clock, group0)
        group0 = step(first_step, group0)
        last = gradients(("b0", "n0", "near"), clock, project0)
        clock, last = together(clock, last)
        last = step(first_step, last)
    (returned0,), clock = together((returned0,), clock)
    tokens_grad, small_b0 = whole(
        5,
        first_project_backward_kernel,
        [place],
        [Part(grads0, (2, REACH, 3 * D // 2)), returned0, inputs, middle_grad0, vectors],
        [(w_in, 0)],
        [((rows, D), BF), ((8, D), FL)],
    )
    small = jnp.concatenate(
        [
            small_b0[:2],
            small_b1[:3],
            small_b2[:5],
            small_a0[:7],
            small_a1[:7],
            small_a2[:7],
            bias0,
            bias1,
            bias2,
            squares0,
            squares1,
            squares2,
        ],
        axis=0,
    )
    if usual:
        clock, (small,), group1 = together(clock, (small,), group1)
        group1 = step(depth_quarters, group1)
        small = small + crossed(small, "seq", 1)
        clock, (small,), group0 = together(clock, (small,), group0)
        group0 = step(first_sums, (group0,))
        group0 = step(second_step, group0)
        small = small + crossed(small, "seq", 2)
        clock, (small,), last = together(clock, (small,), last)
        last = step(first_sums, (last,))
        last = step(second_step, last)
        small = small + crossed(small, "seq", 4)
        clock, (small,), group0, group1 = together(clock, (small,), group0, group1)
        group0 = step(second_sums, group0)
        group0 = step(depth_halves, group0, depth)
        group1 = step(depth_back, group1)
        clock, last = together(clock, last)
        last = step(second_sums, last)
        last = step(depth_halves, last, depth)
        clock, group0 = together(clock, group0)
        group0 = step(depth_quarters, group0)
        clock, last, group1 = together(clock, last, group1)
        last = step(depth_quarters, last)
        small = small + crossed(small, "dp", 1)
        clock, (small,), group0 = together(clock, (small,), group0)
        group0 = step(depth_back, group0)
        clock, last = together(clock, last)
        last = step(depth_back, last)
        small = small + crossed(small, "dp", 2)
        plan = [feed2[1] + project2[1], up[1] + feed1[1] + pool[1] + project1[1]]
        plan += [feed0[1], project0[1]]
        buffers = [shared(*group, depth, core) for group in (group2a, group1, group0, last)]
        sums = final_outputs(plan, buffers, shapes)
    else:
        small = summed_everywhere(small)
        sums = plain_sums(
            shapes,
            core,
            (pack0, pack1, pack2),
            (every["n0"], normed1, every["n2"]),
            (every["n0"], normed1_all, every["n2"]),
            (every["a0"], every["a1"], every["a2"]),
            (grads0, grads1, grads2),
            every["p1"],
            every["u2"],
            (near_table, far_table),
        )
    in_grad, out_grad, expand_grad, contract_grad = [by_layer(total) for total in sums[:4]]

    gain, shift, expand_sum, contract_sum = [], [], [], []
    for layer, b in enumerate((0, 2, 5)):
        a = 10 + 7 * layer
        gain.append(jnp.stack([small[b], small[a + 1]]))
        shift.append(jnp.stack([small[b + 1], small[a + 2]]))
        contract_sum.append(small[a])
        expand_sum.append(small[a + 3 : a + 7].reshape(4 * D))
    bias_sum = small[31:37].reshape(3, 2, D)
    whole_rows = lax.axis_size("dp") * seq_count * rows * D
    counts = jnp.array([whole_rows, whole_rows // 3, whole_rows], FL)
    rms = jnp.sqrt(jnp.sum(small[37:40], axis=1) / counts)
    return (
        output[None],
        tokens_grad[None],
        jnp.stack(gain),
        jnp.stack(shift),
        bias_sum,
        in_grad,
        out_grad,
        expand_grad,
        jnp.stack(expand_sum),
        contract_grad,
        jnp.stack(contract_sum),
        sums[4],
        small[4],
        sums[5],
        small[7:10].reshape(3 * D),
        rms,
    )


def plain_sums(
    shapes, core, packs, normed, normed_all, a_pairs, grads, pool_pair, up_pair, tables
):
    def full(pair, start, half):
        own, other = (array[:, start : start + half] for array in pair)
        return jnp.concatenate(both(own, other, core), axis=1)

    def summed(features, grad):
        total = outer_float(features, grad).astype(BF)
        total = lax.psum_scatter(total, "seq", scatter_dimension=0, tiled=True)
        return lax.psum(total, "dp").astype(FL)

    into, out, expand, contract = [], [], [], []
    for layer in range(3):
        x, a, b = packs[layer], a_pairs[layer], (grads[layer][0], grads[layer][1])
        table, near, every = tables[layer % 2], normed[layer], normed_all[layer]
        own = x.shape[0]
        near = near[near.shape[0] - own :]
        columns = [
            summed(near, full(b, 0, D // 2)[:own]),
            summed(every, full(b, D // 2, D // 2)[: every.shape[0]]),
            summed(every, full(b, D, D // 2)[: every.shape[0]]),
            summed(table, full(b, 3 * D // 2, D // 2)[: table.shape[0]]),
        ]
        into.append(jnp.concatenate(columns, axis=1))
        out.append(summed(x[:, :D], full(a, 2 * D + D // 2, D // 2)))
        expand.append(summed(x[:, D : 2 * D], full(a, 0, 2 * D)))
        contract.append(summed(x[:, 2 * D : 6 * D], full(a, 2 * D, D // 2)))
    pool = summed(packs[1][:, 7 * D :], full(pool_pair, 0, D // 2))
    sides = []
    for array in up_pair:
        parts = [array[index * LANES : (index + 1) * LANES] for index in range(3)]
        sides.append(jnp.concatenate(parts, axis=1))
    up = summed(packs[1][:, 6 * D : 7 * D], jnp.concatenate(both(*sides, core), axis=1))
    stacks = [jnp.stack(parts) for parts in (into, out, expand, contract)]
    return stacks + [pool, up]


def solution(mesh):
    rows = P("dp", "seq", None)
    in_specs = (rows, P("dp", None), rows) + (P(),) * 13
    split = P("seq", None, None)
    flat = P("seq", None)
    out_specs = (rows, rows, P(), P(), P(), split, split, split, P(), split, P())
    out_specs += (flat, P(), flat, P(), P())
    return jax.shard_map(
        per_device, mesh=mesh, in_specs=in_specs, out_specs=out_specs, check_vma=False
    )
```

time: 567 us -> 419 us (0.74)
  Pallas kernels: 106 us -> 196 us
  matrix products: 87.4 us -> 0 us
  other arithmetic: 76.6 us -> 25.1 us
  waiting for transfers between devices: 147 us -> 97.2 us
  local copies, waits for them, and re-layouts: 49.4 us -> 25.1 us
  starting transfers between devices: 85.3 us -> 65.7 us
    pallas_call x11 -> x25, Pallas kernels: 106 us -> 196 us  [the longest x13 82.9 us: whole(): pl.pallas_call(run, in_specs=[SMEM] * scalar_count + [HBM] * (flat_count...]
    dot_general x31 -> x0, matrix products: 87.4 us -> none  [the longest x17 54.2 us: dot_float(): jnp.dot(first_matrix, second_matrix, preferred_element_type=jnp.float32)]
    ppermute x83 -> x65, waiting for transfers between devices: 147 us -> 96.3 us  [crossed(): lax.ppermute(block, axis, [(index, index ^ bit) for index in range(count)])]
    ppermute x83 -> x65, starting transfers between devices: 72 us -> 54.4 us  [crossed(): lax.ppermute(block, axis, [(index, index ^ bit) for index in range(count)])]
    select_n x33 -> x16, other arithmetic: 20.7 us -> 5.38 us  [both(): return (jnp.where(bit, high, low), jnp.where(bit, low, high))]
    another operation x22 -> x14, other arithmetic: 17.3 us -> 3.92 us
    convert_element_type x22 -> x3, other arithmetic: 12.6 us -> 0.02 us  [phases(): angle = distance.astype(jnp.float32)[:, None] * frequency[None, :]]
    unnamed x457 -> x110, local copies, waits for them, and re-layouts: 20.7 us -> 8.95 us
  transfers between devices with their start and end apart: 89 -> 71, of which waited for: 28 -> 28; matrix products, arithmetic and copies ran while one was open for 32% -> 8% of each run, Pallas kernels for 19% -> 35%
where the time goes in v2:
time: 419 us; the launch traced here: 412 us
  Pallas kernels  196 us (47%)
  waiting for transfers between devices  97.2 us (23%)
  starting transfers between devices  65.7 us (16%)
  local copies, waits for them, and re-layouts  25.1 us (6%)
  other arithmetic  25.1 us (6%)
    ppermute x65, waiting for transfers between devices, crossed(): lax.ppermute(block, axis, [(index, index ^ bit) for index in range(count)])  96.3 us
    pallas_call x13, Pallas kernels, whole(): pl.pallas_call(run, in_specs=[SMEM] * scalar_count + [HBM] * (flat_count...  82.9 us
    pallas_call x6, Pallas kernels, attention_call(): pl.pallas_call(kernel, grid=(HEADS // 2,), in_specs=[SMEM] * len(scalars)...  76.8 us
    ppermute x65, starting transfers between devices, crossed(): lax.ppermute(block, axis, [(index, index ^ bit) for index in range(count)])  54.4 us
    pallas_call x5, Pallas kernels, pair_gradients(): pl.pallas_call(kernel, in_specs=[SMEM] + [HBM] * count, out_specs=[HBM] *...  33.4 us
    ppermute x6, starting transfers between devices, passed_along(): return lax.ppermute(block, axis, route)  11.3 us
    convert_element_type x19, other arithmetic, rounded_sum(): sum((term.astype(jnp.float32) for term in terms)).astype(jnp.bfloat16)  8.97 us
    unnamed x110, local copies, waits for them, and re-layouts  8.95 us
  transfers between devices with their start and end apart: 71, of which 28 were waited for; matrix products, arithmetic and copies ran while one was open for 8% of the time, Pallas kernels for 35%

profile of v2, /device:TPU:0, one launch (start us, length us, event | category | flops | bytes accessed | tf_op | source)
XLA Modules:
  0.0 411.6 jit_solution(12978077834808535934)
XLA Ops:
  1.6 2.4 collective-permute-start
  8.7 4.3 %shard_map.288 = (bf16[384,512]{1,0:T(8,128)(2,1)}, bf16[384,512]{1,0:T(8,128)(2,1)}, bf16[384,512]{1,0:T(8,128)(2,1)}, bf16[384,512]{1,0:T(8,128)(2,1)}, bf16[3...) custom-call(bf16[384,512]{1,0:T(8,128)(2,1)} %bitcast.145, bf16[3,2,512]{2,1,0:T(2,128)(2,1)} %refs_5_.21, ...), custom_call_target="tpu_custom_call" | custom-call | flops 400000000 | bytes 1200000 | tf_op jit(solution)/shard_map/pallas_call | solution.py:964
  13.7 10.8 %shard_map.289 = (bf16[384,512]{1,0:T(8,128)(2,1)}, bf16[256,512]{1,0:T(8,128)(2,1)}, bf16[2,256,512]{2,1,0:T(8,128)(2,1)}, bf16[8,3,128,384]{3,2,1,0:T(8,128)(2,1)}) custom-call(s32[9]{0:T(128)S(1)} %get-tuple-element.566.info.refs_0_, bf16[384,512]{1,0:T(8,128)(2,1)} %get-tuple-element.250.content, bf16[384,512]{1,0:T(8,128)(2,1)} %get-tuple-element.251.position, ...), custom_call_target="tpu_custom_call" | custom-call | flops 1100000000 | bytes 3300000 | tf_op jit(solution)/shard_map/pallas_call | solution.py:448
  24.5 7.0 %shard_map.290 = (f32[384,512]{1,0:T(8,128)}, bf16[384,2048]{1,0:T(8,128)(2,1)}, bf16[384,3072]{1,0:T(8,128)(2,1)}, f32[384,512]{1,0:T(8,128)}, f32[1,512]{1,0:T(1,128)}) custom-call(bf16[384,512]{1,0:T(8,128)(2,1)} %get-tuple-element.255.refs_0_, bf16[384,512]{1,0:T(8,128)(2,1)} %bitcast.146, bf16[3,2,512]{2,1,0:T(2,128)(2,1)} %refs_5_.21, ...), custom_call_target="tpu_custom_call" | custom-call | flops 700000000 | bytes 2100000 | tf_op jit(solution)/shard_map/pallas_call | solution.py:964
  31.6 2.7 collective-permute-start.10
  36.8 2.1 collective-permute-start.1
  41.2 4.3 %shard_map.291 = (bf16[128,512]{1,0:T(8,128)(2,1)}, f32[128,512]{1,0:T(8,128)}, bf16[128,1536]{1,0:T(8,128)(2,1)}) custom-call(s32[9]{0:T(128)S(1)} %get-tuple-element.566.info.refs_0_, f32[384,512]{1,0:T(8,128)} %get-tuple-element.256.refs_1_.refs_3_, bf16[2,512]{1,0:T(2,128)(2,1)} %copy-done.42, bf16[3,2,512]{2,1,0:T(2,128)(2,1)} %refs_5_.21, ...), custom_call_target="tpu_custom_call" | custom-call | flops 400000000 | bytes 1200000 | tf_op jit(solution)/shard_map/pallas_call | solution.py:964
  45.6 3.5 collective-permute-start.5
  49.1 4.6 %shard_map.292 = (bf16[128,512]{1,0:T(8,128)(2,1)}, bf16[128,512]{1,0:T(8,128)(2,1)}, bf16[1152,512]{1,0:T(8,128)(2,1)}) custom-call(bf16[128,512]{1,0:T(8,128)(2,1)} %get-tuple-element.257.refs_0_, bf16[3,2,512]{2,1,0:T(2,128)(2,1)} %refs_5_.21, bf16[3,2,512]{2,1,0:T(2,128)(2,1)} %refs_6_.19, bf16[3,2,512]{2,1,0:T(2,128)(2,1)} %refs_7_.15, ...), custom_call_target="tpu_custom_call" | custom-call | flops 400000000 | bytes 1200000 | tf_op jit(solution)/shard_map/pallas_call | solution.py:964
  53.7 2.1 collective-permute-start.8
  56.2 2.3 collective-permute-done.8
  62.6 13.8 %shard_map.293 = (bf16[128,512]{1,0:T(8,128)(2,1)}, bf16[1024,512]{1,0:T(8,128)(2,1)}, bf16[1024,512]{1,0:T(8,128)(2,1)}, bf16[8,128,1024]{2,1,0:T(8,128)(2,1)}) custom-call(s32[9]{0:T(128)S(1)} %get-tuple-element.565.info, s32[9]{0:T(128)S(1)} %pad_add_fusion.2.order, bf16[128,512]{1,0:T(8,128)(2,1)} %get-tuple-element.258.content, ...), custom_call_target="tpu_custom_call" | custom-call | flops 1300000000 | bytes 3900000 | tf_op jit(solution)/shard_map/pallas_call | solution.py:448
  76.4 7.8 %shard_map.294 = (f32[128,512]{1,0:T(8,128)}, bf16[128,2048]{1,0:T(8,128)(2,1)}, bf16[128,5120]{1,0:T(8,128)(2,1)}, bf16[384,512]{1,0:T(8,128)(2,1)}, f32[384,512]{1,0:T(8,128)}, /*index=5*/f32[1,512]{1,0:T(1,128)}) custom-call(bf16[128,512]{1,0:T(8,128)(2,1)} %get-tuple-element.265.refs_0_, f32[128,512]{1,0:T(8,128)} %get-tuple-element.266.refs_1_.refs_4_, ...), custom_call_target="tpu_custom_call" | custom-call | flops 700000000 | bytes 2100000 | tf_op jit(solution)/shard_map/pallas_call | solution.py:964
  85.5 2.5 collective-permute-start.12
  88.0 4.3 %shard_map.295 = (bf16[384,512]{1,0:T(8,128)(2,1)}, bf16[384,512]{1,0:T(8,128)(2,1)}, bf16[384,512]{1,0:T(8,128)(2,1)}, bf16[384,512]{1,0:T(8,128)(2,1)}, bf16[384,512]{1,0:T(8,128)(2,1)}) custom-call(bf16[384,512]{1,0:T(8,128)(2,1)} %get-tuple-element.268.refs_0_, bf16[3,2,512]{2,1,0:T(2,128)(2,1)} %refs_5_.21, bf16[3,2,512]{2,1,0:T(2,128)(2,1)} %refs_6_.19, ...), custom_call_target="tpu_custom_call" | custom-call | flops 400000000 | bytes 1200000 | tf_op jit(solution)/shard_map/pallas_call | solution.py:964
  93.0 10.5 %shard_map.296 = (bf16[384,512]{1,0:T(8,128)(2,1)}, bf16[256,512]{1,0:T(8,128)(2,1)}, bf16[2,256,512]{2,1,0:T(8,128)(2,1)}, bf16[8,3,128,384]{3,2,1,0:T(8,128)(2,1)}) custom-call(s32[9]{0:T(128)S(1)} %get-tuple-element.566.info.refs_0_, bf16[384,512]{1,0:T(8,128)(2,1)} %get-tuple-element.269.content, bf16[384,512]{1,0:T(8,128)(2,1)} %get-tuple-element.270.position, ...), custom_call_target="tpu_custom_call" | custom-call | flops 1100000000 | bytes 3300000 | tf_op jit(solution)/shard_map/pallas_call | solution.py:448
  106.8 7.7 %shard_map.297 = (f32[384,512]{1,0:T(8,128)}, bf16[384,2048]{1,0:T(8,128)(2,1)}, bf16[384,3072]{1,0:T(8,128)(2,1)}, bf16[384,512]{1,0:T(8,128)(2,1)}, f32[1,512]{1,0:T(1,128)}) custom-call(bf16[384,512]{1,0:T(8,128)(2,1)} %get-tuple-element.277.refs_0_, f32[384,512]{1,0:T(8,128)} %get-tuple-element.278.refs_1_.refs_3_, bf16[3,2,512]{2,1,0:T(2,128)(2,1)} %refs_5_.21, ...), custom_call_target="tpu_custom_call" | custom-call | flops 700000000 | bytes 2100000 | tf_op jit(solution)/shard_map/pallas_call | solution.py:964
  114.9 8.9 %shard_map.298 = (f32[384,512]{1,0:T(8,128)}, bf16[384,512]{1,0:T(8,128)(2,1)}, bf16[384,1536]{1,0:T(8,128)(2,1)}, bf16[384,1536]{1,0:T(8,128)(2,1)}, f32[8,512]{1,0:T(8,128)}) custom-call(s32[2]{0:T(128)S(1)} %pad_add_fusion.3.refs_0_.place.refs_1_, bf16[384,512]{1,0:T(8,128)(2,1)} %bitcast.156, bf16[384,2048]{1,0:T(8,128)(2,1)} %get-tuple-element.284.refs_2_, ...), custom_call_target="tpu_custom_call" | custom-call | flops 800000000 | bytes 2400000 | tf_op jit(solution)/shard_map/pallas_call | solution.py:964
  123.9 14.2 %shard_map.299 = (f32[2,512]{1,0:T(2,128)}, bf16[256,512]{1,0:T(8,128)(2,1)}, bf16[2,640,1024]{2,1,0:T(8,128)(2,1)}) custom-call(s32[2]{0:T(128)S(1)} %pad_add_fusion.3.refs_0_.place.refs_1_, bf16[384,512]{1,0:T(8,128)(2,1)} %get-tuple-element.269.content, bf16[384,512]{1,0:T(8,128)(2,1)} %get-tuple-element.270.position, ...), custom_call_target="tpu_custom_call" | custom-call | flops 1300000000 | bytes 3900000 | tf_op jit(solution)/shard_map/pallas_call | solution.py:448
  142.0 2.5 collective-permute-done.17.refs_1_
  146.5 8.3 %shard_map.300 = (bf16[2,128,1664]{2,1,0:T(8,128)(2,1)}, bf16[2,128,1664]{2,1,0:T(8,128)(2,1)}, bf16[2,128,1664]{2,1,0:T(8,128)(2,1)}, bf16[2,128,1664]{2,1,0:T(8,128)(2,1)}) custom-call(s32[2]{0:T(128)S(1)} %pad_add_fusion.3.refs_0_.place.refs_1_, bf16[384,1536]{1,0:T(8,128)(2,1)} %get-tuple-element.294.refs_0_, bf16[384,1536]{1,0:T(8,128)(2,1)} %copy-done.9, ...), custom_call_target="tpu_custom_call" | custom-call | flops 700000000 | bytes 2100000 | tf_op jit(solution)/shard_map/pallas_call | solution.py:1179
  156.9 6.7 %shard_map.301 = (f32[384,512]{1,0:T(8,128)}, f32[128,512]{1,0:T(8,128)}, bf16[384,256]{1,0:T(8,128)(2,1)}, bf16[384,256]{1,0:T(8,128)(2,1)}, f32[8,512]{1,0:T(8,128)}) custom-call(s32[2]{0:T(128)S(1)} %pad_add_fusion.3.refs_0_.place.refs_1_, bf16[2,640,1024]{2,1,0:T(8,128)(2,1)} %get-tuple-element.289.refs_4_.refs_1_, bf16[256,512]{1,0:T(8,128)(2,1)} %copy-done.32, ...), custom_call_target="tpu_custom_call" | custom-call | flops 600000000 | bytes 1800000 | tf_op jit(solution)/shard_map/pallas_call | solution.py:964
  163.7 7.0 %shard_map.302 = (f32[128,512]{1,0:T(8,128)}, bf16[128,512]{1,0:T(8,128)(2,1)}, bf16[128,1536]{1,0:T(8,128)(2,1)}, bf16[128,1536]{1,0:T(8,128)(2,1)}, f32[8,512]{1,0:T(8,128)}) custom-call(s32[2]{0:T(128)S(1)} %pad_add_fusion.3.refs_0_.place.refs_1_, f32[128,512]{1,0:T(8,128)} %get-tuple-element.310.refs_1_, bf16[128,2048]{1,0:T(8,128)(2,1)} %get-tuple-element.311.refs_2_, ...), custom_call_target="tpu_custom_call" | custom-call | flops 800000000 | bytes 2400000 | tf_op jit(solution)/shard_map/pallas_call | solution.py:964
  170.7 5.5 %collective-permute-done.19 = bf16[2,128,1664]{2,1,0:T(8,128)(2,1)S(1)} collective-permute-done((bf16[2,128,1664]{2,1,0:T(8,128)(2,1)}, bf16[2,128,1664]{2,1,0:T(8,128)(2,1)S(1)}, u32[]{:S(2)}, u32[]{:S(2)}) %collective-permute-start.19) | collective-permute-done | bytes 852000 | tf_op jit(solution)/shard_map/ppermute | solution.py:982
  181.1 14.1 %shard_map.303 = (f32[2,512]{1,0:T(2,128)}, bf16[512,512]{1,0:T(8,128)(2,1)}, bf16[512,512]{1,0:T(8,128)(2,1)}, bf16[2,1152,1024]{2,1,0:T(8,128)(2,1)}) custom-call(s32[9]{0:T(128)S(1)} %pad_add_fusion.2.order, s32[2]{0:T(128)S(1)} %pad_add_fusion.3.refs_0_.place.refs_1_, bf16[128,512]{1,0:T(8,128)(2,1)} %get-tuple-element.258.content, ...), custom_call_target="tpu_custom_call" | custom-call | flops 1300000000 | bytes 3900000 | tf_op jit(solution)/shard_map/pallas_call | solution.py:448
  200.4 2.7 collective-permute-done.26.refs_1_
  203.9 5.5 %shard_map.304 = (bf16[2,128,1536]{2,1,0:T(8,128)(2,1)}, bf16[2,128,1536]{2,1,0:T(8,128)(2,1)}, bf16[2,128,1536]{2,1,0:T(8,128)(2,1)}, bf16[2,128,1536]{2,1,0:T(8,128)(2,1)}) custom-call(s32[2]{0:T(128)S(1)} %pad_add_fusion.3.refs_0_.place.refs_1_, bf16[128,1536]{1,0:T(8,128)(2,1)} %get-tuple-element.335.refs_0_, bf16[128,1536]{1,0:T(8,128)(2,1)} %copy-done.26, ...), custom_call_target="tpu_custom_call" | custom-call | flops 700000000 | bytes 2100000 | tf_op jit(solution)/shard_map/pallas_call | solution.py:1179
  212.5 3.1 collective-permute-done.28
  222.6 5.3 %shard_map.305 = (f32[384,512]{1,0:T(8,128)}, bf16[128,256]{1,0:T(8,128)(2,1)}, bf16[128,256]{1,0:T(8,128)(2,1)}, f32[8,512]{1,0:T(8,128)}) custom-call(s32[9]{0:T(128)S(1)} %get-tuple-element.566.info.refs_0_, s32[2]{0:T(128)S(1)} %pad_add_fusion.3.refs_0_.place.refs_1_, bf16[2,1152,1024]{2,1,0:T(8,128)(2,1)} %get-tuple-element.324.refs_2_.refs_4_, ...), custom_call_target="tpu_custom_call" | custom-call | flops 500000000 | bytes 1500000 | tf_op jit(solution)/shard_map/pallas_call | solution.py:964
  230.7 7.5 %shard_map.306 = (bf16[2,128,896]{2,1,0:T(8,128)(2,1)}, bf16[2,128,896]{2,1,0:T(8,128)(2,1)}, bf16[2,128,896]{2,1,0:T(8,128)(2,1)}, bf16[2,128,896]{2,1,0:T(8,128)(2,1)}) custom-call(s32[2]{0:T(128)S(1)} %pad_add_fusion.3.refs_0_.place.refs_1_, bf16[128,256]{1,0:T(8,128)(2,1)} %get-tuple-element.356.refs_0_, bf16[128,256]{1,0:T(8,128)(2,1)} %copy-done.36, ...), custom_call_target="tpu_custom_call" | custom-call | flops 700000000 | bytes 2100000 | tf_op jit(solution)/shard_map/pallas_call | solution.py:1179
  239.0 2.4 collective-permute-start.36
  242.5 9.2 %shard_map.307 = (f32[384,512]{1,0:T(8,128)}, bf16[384,512]{1,0:T(8,128)(2,1)}, bf16[384,1536]{1,0:T(8,128)(2,1)}, bf16[384,1536]{1,0:T(8,128)(2,1)}, f32[8,512]{1,0:T(8,128)}) custom-call(s32[2]{0:T(128)S(1)} %pad_add_fusion.3.refs_0_.place.refs_1_, f32[384,512]{1,0:T(8,128)} %get-tuple-element.306.refs_1_, f32[384,512]{1,0:T(8,128)} %get-tuple-element.353.refs_2_, ...), custom_call_target="tpu_custom_call" | custom-call | flops 800000000 | bytes 2400000 | tf_op jit(solution)/shard_map/pallas_call | solution.py:964
  262.5 2.7 collective-permute-start.41
  265.1 13.4 %shard_map.308 = (f32[2,512]{1,0:T(2,128)}, bf16[256,512]{1,0:T(8,128)(2,1)}, bf16[2,640,1024]{2,1,0:T(8,128)(2,1)}) custom-call(s32[2]{0:T(128)S(1)} %pad_add_fusion.3.refs_0_.place.refs_1_, bf16[384,512]{1,0:T(8,128)(2,1)} %get-tuple-element.250.content, bf16[384,512]{1,0:T(8,128)(2,1)} %get-tuple-element.251.position, ...), custom_call_target="tpu_custom_call" | custom-call | flops 1300000000 | bytes 3900000 | tf_op jit(solution)/shard_map/pallas_call | solution.py:448
  282.2 4.8 %collective-permute-start.48 = (bf16[640,1024]{1,0:T(8,128)(2,1)S(1)}, bf16[640,1024]{1,0:T(8,128)(2,1)}, u32[]{:S(2)}, u32[]{:S(2)}) collective-permute-start(bf16[640,1024]{1,0:T(8,128)(2,1)S(1)} %slice_bitcast_fusion.1), channel_id=1, source_target_pairs={{0,1},{1,0},{2,3},{3,2},{4,5},{5,4},{6,7},{7,6},{8,9},{9,8},{10,11... | collective-permute-start | bytes 3932168 | tf_op jit(solution)/shard_map/ppermute | solution.py:982
  286.9 5.7 %shard_map.309 = (bf16[384,512]{1,0:T(8,128)(2,1)}, f32[8,512]{1,0:T(8,128)}) custom-call(s32[2]{0:T(128)S(1)} %pad_add_fusion.3.refs_0_.place.refs_1_, bf16[2,640,1024]{2,1,0:T(8,128)(2,1)} %get-tuple-element.431.refs_1_.refs_0_, bf16[256,512]{1,0:T(8,128)(2,1)} %copy-done.33, bf16[384,512]{1,0:T(8,128)(2,1)} %bitcast.147, ...), custom_call_target="tpu_custom_call" | custom-call | flops 500000000 | bytes 1500000 | tf_op jit(solution)/shard_map/pallas_call | solution.py:964
  293.4 2.7 concatenate.76
  300.1 6.5 %shard_map.310 = (bf16[2,128,1152]{2,1,0:T(8,128)(2,1)}, bf16[2,128,1152]{2,1,0:T(8,128)(2,1)}, bf16[2,128,1152]{2,1,0:T(8,128)(2,1)}, bf16[2,128,1152]{2,1,0:T(8,128)(2,1)}) custom-call(s32[2]{0:T(128)S(1)} %pad_add_fusion.3.refs_0_.place.refs_1_, bf16[384,1536]{1,0:T(8,128)(2,1)} %get-tuple-element.417.refs_0_, ...), custom_call_target="tpu_custom_call" | custom-call | flops 700000000 | bytes 2100000 | tf_op jit(solution)/shard_map/pallas_call | solution.py:1179
  309.3 12.8 %collective-permute-done.42 = bf16[128,2432]{1,0:T(8,128)(2,1)S(1)} collective-permute-done((bf16[128,2432]{1,0:T(8,128)(2,1)S(1)}, bf16[128,2432]{1,0:T(8,128)(2,1)S(1)}, u32[]{:S(2)}, u32[]{:S(2)}) %collective-permute-start.42) | collective-permute-done | bytes 622624 | tf_op jit(solution)/shard_map/ppermute | solution.py:982
  322.7 5.6 %shard_map.311 = (bf16[2,128,512]{2,1,0:T(8,128)(2,1)}, bf16[2,128,512]{2,1,0:T(8,128)(2,1)}, bf16[2,128,512]{2,1,0:T(8,128)(2,1)}, bf16[2,128,512]{2,1,0:T(8,128)(2,1)}) custom-call(s32[2]{0:T(128)S(1)} %pad_add_fusion.3.refs_0_.place.refs_1_, bf16[2,640,1024]{2,1,0:T(8,128)(2,1)} %get-tuple-element.431.refs_1_.refs_0_, ...), custom_call_target="tpu_custom_call" | custom-call | flops 700000000 | bytes 2100000 | tf_op jit(solution)/shard_map/pallas_call | solution.py:1179
  331.5 7.3 %collective-permute-done.47 = f32[40,512]{1,0:T(8,128)S(1)} collective-permute-done((f32[40,512]{1,0:T(8,128)S(1)}, f32[40,512]{1,0:T(8,128)S(1)}, u32[]{:S(2)}, u32[]{:S(2)}) %collective-permute-start.47) | collective-permute-done | bytes 81952 | tf_op jit(solution)/shard_map/ppermute | solution.py:982
  342.5 6.4 %collective-permute-done.51 = f32[40,512]{1,0:T(8,128)S(1)} collective-permute-done((f32[40,512]{1,0:T(8,128)S(1)}, f32[40,512]{1,0:T(8,128)S(1)}, u32[]{:S(2)}, u32[]{:S(2)}) %collective-permute-start.51) | collective-permute-done | bytes 81952 | tf_op jit(solution)/shard_map/ppermute | solution.py:982
  350.7 2.2 collective-permute-done.54
  355.5 7.5 %collective-permute-done.56 = bf16[128,1152]{1,0:T(8,128)(2,1)S(1)} collective-permute-done((bf16[128,1152]{1,0:T(8,128)(2,1)S(1)}, bf16[128,1152]{1,0:T(8,128)(2,1)S(1)}, u32[]{:S(2)}, u32[]{:S(2)}) %collective-permute-start.56) | collective-permute-done | bytes 294944 | tf_op jit(solution)/shard_map/ppermute | solution.py:982
  365.6 12.1 %collective-permute-done.57 = bf16[128,1152]{1,0:T(8,128)(2,1)S(1)} collective-permute-done((bf16[128,1152]{1,0:T(8,128)(2,1)S(1)}, bf16[128,1152]{1,0:T(8,128)(2,1)S(1)}, u32[]{:S(2)}, u32[]{:S(2)}) %collective-permute-start.57) | collective-permute-done | bytes 294944 | tf_op jit(solution)/shard_map/ppermute | solution.py:982
  378.8 13.7 %collective-permute-done.63 = bf16[128,512]{1,0:T(8,128)(2,1)S(1)} collective-permute-done((bf16[128,512]{1,0:T(8,128)(2,1)S(1)}, bf16[128,512]{1,0:T(8,128)(2,1)S(1)}, u32[]{:S(2)}, u32[]{:S(2)}) %collective-permute-start.63) | collective-permute-done | bytes 131104 | tf_op jit(solution)/shard_map/ppermute | solution.py:982
  401.4 4.5 %collective-permute-done.69 = bf16[128,512]{1,0:T(8,128)(2,1)S(1)} collective-permute-done((bf16[128,512]{1,0:T(8,128)(2,1)S(1)}, bf16[128,512]{1,0:T(8,128)(2,1)S(1)}, u32[]{:S(2)}, u32[]{:S(2)}) %collective-permute-start.69) | collective-permute-done | bytes 131104 | tf_op jit(solution)/shard_map/ppermute | solution.py:982
  408.4 2.7 shard_map.312
  (328 shorter events, 102.7 us)
Async XLA Ops:
  1.6 11.4 %collective-permute-start = (bf16[256,512]{1,0:T(8,128)(2,1)S(1)}, bf16[256,512]{1,0:T(8,128)(2,1)S(1)}, u32[]{:S(2)}, u32[]{:S(2)}) collective-permute-start(bf16[256,512]{1,0:T(8,128)(2,1)S(1)} %slice_bitcast_fusion.3), channel_id=1, source_target_pairs={{0,1},{1,2},{2,3},{3,4},{4,5},{5,6},{6,7},{8,9},{9,10},{10,11},{11... | collective-permute-start | bytes 786440 | tf_op jit(solution)/shard_map/ppermute | solution.py:988
  31.6 44.8 %collective-permute-start.10 = (bf16[384,3072]{1,0:T(8,128)(2,1)}, bf16[384,3072]{1,0:T(8,128)(2,1)S(1)}, u32[]{:S(2)}, u32[]{:S(2)}) collective-permute-start(bf16[384,3072]{1,0:T(8,128)(2,1)} %get-tuple-element.419.refs_2_), channel_id=1, source_target_pairs={{0,1},{1,0},{2,3},{3,2},{4,5},{5,4},{6,7},{7,6},{8,9},{9,8},{10,11... | collective-permute-start | bytes 7077896 | tf_op jit(solution)/shard_map/ppermute | solution.py:982
  39.0 37.4 %collective-permute-start.11 = (bf16[640,512]{1,0:T(8,128)(2,1)S(1)}, bf16[640,512]{1,0:T(8,128)(2,1)S(1)}, u32[]{:S(2)}, u32[]{:S(2)}) collective-permute-start(bf16[640,512]{1,0:T(8,128)(2,1)S(1)} %constant_dynamic-update-slice_fusion.9.refs_2_), channel_id=1, source_target_pairs={{0,1},{1,0},{2,3},{3,2},{4,5},{5,4},{6,7},{7,6},{8,9},{9,8},{10,11... | collective-permute-start | bytes 1966088 | tf_op jit(solution)/shard_map/ppermute | solution.py:982
  45.6 8.1 %collective-permute-start.5 = (bf16[128,512]{1,0:T(8,128)(2,1)}, bf16[128,512]{1,0:T(8,128)(2,1)S(1)}, u32[]{:S(2)}, u32[]{:S(2)}) collective-permute-start(bf16[128,512]{1,0:T(8,128)(2,1)} %get-tuple-element.257.refs_0_), channel_id=1, source_target_pairs={{0,4},{1,5},{2,6},{3,7},{4,0},{5,1},{6,2},{7,3},{8,12},{9,13},{10,... | collective-permute-start | bytes 393224 | tf_op jit(solution)/shard_map/ppermute | solution.py:982
  49.1 6.9 %collective-permute-start.2 = (bf16[128,512]{1,0:T(8,128)(2,1)}, bf16[128,512]{1,0:T(8,128)(2,1)S(1)}, u32[]{:S(2)}, u32[]{:S(2)}) collective-permute-start(bf16[128,512]{1,0:T(8,128)(2,1)} %get-tuple-element.257.refs_0_), channel_id=1, source_target_pairs={{0,1},{1,0},{2,3},{3,2},{4,5},{5,4},{6,7},{7,6},{8,9},{9,8},{10,11... | collective-permute-start | bytes 393224 | tf_op jit(solution)/shard_map/ppermute | solution.py:982
  84.3 22.5 %collective-permute-start.13 = (bf16[128,5120]{1,0:T(8,128)(2,1)}, bf16[128,5120]{1,0:T(8,128)(2,1)S(1)}, u32[]{:S(2)}, u32[]{:S(2)}) collective-permute-start(bf16[128,5120]{1,0:T(8,128)(2,1)} %get-tuple-element.337.refs_2_), channel_id=1, source_target_pairs={{0,1},{1,0},{2,3},{3,2},{4,5},{5,4},{6,7},{7,6},{8,9},{9,8},{10,11... | collective-permute-start | bytes 3932168 | tf_op jit(solution)/shard_map/ppermute | solution.py:982
  85.5 6.8 %collective-permute-start.12 = (bf16[256,512]{1,0:T(8,128)(2,1)S(1)}, bf16[256,512]{1,0:T(8,128)(2,1)S(1)}, u32[]{:S(2)}, u32[]{:S(2)}) collective-permute-start(bf16[256,512]{1,0:T(8,128)(2,1)S(1)} %slice.306), channel_id=1, source_target_pairs={{0,1},{1,2},{2,3},{3,4},{4,5},{5,6},{6,7},{8,9},{9,10},{10,11},{11... | collective-permute-start | bytes 786440 | tf_op jit(solution)/shard_map/ppermute | solution.py:988
  114.5 9.3 %collective-permute-start.15 = (bf16[384,3072]{1,0:T(8,128)(2,1)}, bf16[384,3072]{1,0:T(8,128)(2,1)S(1)}, u32[]{:S(2)}, u32[]{:S(2)}) collective-permute-start(bf16[384,3072]{1,0:T(8,128)(2,1)} %get-tuple-element.296.refs_2_), channel_id=1, source_target_pairs={{0,1},{1,0},{2,3},{3,2},{4,5},{5,4},{6,7},{7,6},{8,9},{9,8},{10,11... | collective-permute-start | bytes 7077896 | tf_op jit(solution)/shard_map/ppermute | solution.py:982
  140.2 14.6 %collective-permute-start.16 = (bf16[256,512]{1,0:T(8,128)(2,1)S(1)}, bf16[256,512]{1,0:T(8,128)(2,1)S(1)}, u32[]{:S(2)}, u32[]{:S(2)}) collective-permute-start(bf16[256,512]{1,0:T(8,128)(2,1)S(1)} %copy-done.45), channel_id=1, source_target_pairs={{1,0},{2,1},{3,2},{4,3},{5,4},{6,5},{7,6},{9,8},{10,9},{11,10},{12... | collective-permute-start | bytes 786440 | tf_op jit(solution)/shard_map/ppermute | solution.py:988
  154.8 21.4 %collective-permute-start.19 = (bf16[2,128,1664]{2,1,0:T(8,128)(2,1)}, bf16[2,128,1664]{2,1,0:T(8,128)(2,1)S(1)}, u32[]{:S(2)}, u32[]{:S(2)}) collective-permute-start(bf16[2,128,1664]{2,1,0:T(8,128)(2,1)} %get-tuple-element.315), channel_id=1, source_target_pairs={{0,2},{1,3},{2,0},{3,1},{4,6},{5,7},{6,4},{7,5},{8,10},{9,11},{10,... | collective-permute-start | bytes 2555912 | tf_op jit(solution)/shard_map/ppermute | solution.py:982
  156.1 21.1 %collective-permute-start.20 = (bf16[2,128,1664]{2,1,0:T(8,128)(2,1)}, bf16[2,128,1664]{2,1,0:T(8,128)(2,1)S(1)}, u32[]{:S(2)}, u32[]{:S(2)}) collective-permute-start(bf16[2,128,1664]{2,1,0:T(8,128)(2,1)} %get-tuple-element.317), channel_id=1, source_target_pairs={{0,4},{1,5},{2,6},{3,7},{4,0},{5,1},{6,2},{7,3},{8,12},{9,13},{10,... | collective-permute-start | bytes 2555912 | tf_op jit(solution)/shard_map/ppermute | solution.py:982
  178.5 16.8 %collective-permute-start.21 = (bf16[128,1664]{1,0:T(8,128)(2,1)S(1)}, bf16[128,1664]{1,0:T(8,128)(2,1)S(1)}, u32[]{:S(2)}, u32[]{:S(2)}) collective-permute-start(bf16[128,1664]{1,0:T(8,128)(2,1)S(1)} %get-tuple-element.328), channel_id=1, source_target_pairs={{0,4},{1,5},{2,6},{3,7},{4,0},{5,1},{6,2},{7,3},{8,12},{9,13},{10,... | collective-permute-start | bytes 1277960 | tf_op jit(solution)/shard_map/ppermute | solution.py:982
  179.4 15.8 %collective-permute-start.22 = (bf16[128,1664]{1,0:T(8,128)(2,1)S(1)}, bf16[128,1664]{1,0:T(8,128)(2,1)}, u32[]{:S(2)}, u32[]{:S(2)}) collective-permute-start(bf16[128,1664]{1,0:T(8,128)(2,1)S(1)} %get-tuple-element.330), channel_id=1, source_target_pairs={{0,2},{1,3},{2,0},{3,1},{4,6},{5,7},{6,4},{7,5},{8,10},{9,11},{10,... | collective-permute-start | bytes 1277960 | tf_op jit(solution)/shard_map/ppermute | solution.py:982
  198.0 32.7 %collective-permute-start.32 = (bf16[1152,1024]{1,0:T(8,128)(2,1)S(1)}, bf16[1152,1024]{1,0:T(8,128)(2,1)}, u32[]{:S(2)}, u32[]{:S(2)}) collective-permute-start(bf16[1152,1024]{1,0:T(8,128)(2,1)S(1)} %slice_bitcast_fusion), channel_id=1, source_target_pairs={{0,1},{1,0},{2,3},{3,2},{4,5},{5,4},{6,7},{7,6},{8,9},{9,8},{10,11... | collective-permute-start | bytes 7077896 | tf_op jit(solution)/shard_map/ppermute | solution.py:982
  198.9 10.6 %collective-permute-start.24 = (bf16[2,128,256]{2,1,0:T(8,128)(2,1)S(1)}, bf16[2,128,256]{2,1,0:T(8,128)(2,1)S(1)}, u32[]{:S(2)}, u32[]{:S(2)}) collective-permute-start(bf16[2,128,256]{2,1,0:T(8,128)(2,1)S(1)} %pad_maximum_fusion.12), channel_id=1, source_target_pairs={{0,2},{1,3},{2,0},{3,1},{4,6},{5,7},{6,4},{7,5},{8,10},{9,11},{10,... | collective-permute-start | bytes 393224 | tf_op jit(solution)/shard_map/ppermute | solution.py:982
  199.3 10.2 %collective-permute-start.25 = (bf16[2,128,256]{2,1,0:T(8,128)(2,1)S(1)}, bf16[2,128,256]{2,1,0:T(8,128)(2,1)}, u32[]{:S(2)}, u32[]{:S(2)}) collective-permute-start(bf16[2,128,256]{2,1,0:T(8,128)(2,1)S(1)} %slice.404), channel_id=1, source_target_pairs={{0,4},{1,5},{2,6},{3,7},{4,0},{5,1},{6,2},{7,3},{8,12},{9,13},{10,... | collective-permute-start | bytes 393224 | tf_op jit(solution)/shard_map/ppermute | solution.py:982
  218.9 19.4 %collective-permute-start.33 = (bf16[128,1664]{1,0:T(8,128)(2,1)S(1)}, bf16[128,1664]{1,0:T(8,128)(2,1)S(1)}, u32[]{:S(2)}, u32[]{:S(2)}) collective-permute-start(bf16[128,1664]{1,0:T(8,128)(2,1)S(1)} %get-tuple-element.488), channel_id=1, source_target_pairs={{0,8},{8,0},{16,24},{24,16},{1,9},{9,1},{17,25},{25,17},{2,10},{10... | collective-permute-start | bytes 1277960 | tf_op jit(solution)/shard_map/ppermute | solution.py:982
  220.5 31.3 %collective-permute-start.34 = (bf16[2,128,1536]{2,1,0:T(8,128)(2,1)}, bf16[2,128,1536]{2,1,0:T(8,128)(2,1)}, u32[]{:S(2)}, u32[]{:S(2)}) collective-permute-start(bf16[2,128,1536]{2,1,0:T(8,128)(2,1)} %get-tuple-element.371), channel_id=1, source_target_pairs={{0,2},{1,3},{2,0},{3,1},{4,6},{5,7},{6,4},{7,5},{8,10},{9,11},{10,... | collective-permute-start | bytes 2359304 | tf_op jit(solution)/shard_map/ppermute | solution.py:982
  221.6 30.1 %collective-permute-start.35 = (bf16[2,128,1536]{2,1,0:T(8,128)(2,1)}, bf16[2,128,1536]{2,1,0:T(8,128)(2,1)}, u32[]{:S(2)}, u32[]{:S(2)}) collective-permute-start(bf16[2,128,1536]{2,1,0:T(8,128)(2,1)} %get-tuple-element.373), channel_id=1, source_target_pairs={{0,4},{1,5},{2,6},{3,7},{4,0},{5,1},{6,2},{7,3},{8,12},{9,13},{10,... | collective-permute-start | bytes 2359304 | tf_op jit(solution)/shard_map/ppermute | solution.py:982
  229.4 8.8 %collective-permute-start.30 = (f32[2,512]{1,0:T(2,128)S(1)}, f32[2,512]{1,0:T(2,128)S(1)}, u32[]{:S(2)}, u32[]{:S(2)}) collective-permute-start(f32[2,512]{1,0:T(2,128)S(1)} %slice.327), channel_id=1, source_target_pairs={{1,0},{2,1},{3,2},{4,3},{5,4},{6,5},{7,6},{9,8},{10,9},{11,10},{12... | collective-permute-start | bytes 12296 | tf_op jit(solution)/shard_map/ppermute | solution.py:988
  239.0 13.9 %collective-permute-start.36 = (bf16[2,128,896]{2,1,0:T(8,128)(2,1)}, bf16[2,128,896]{2,1,0:T(8,128)(2,1)}, u32[]{:S(2)}, u32[]{:S(2)}) collective-permute-start(bf16[2,128,896]{2,1,0:T(8,128)(2,1)} %get-tuple-element.375), channel_id=1, source_target_pairs={{0,2},{1,3},{2,0},{3,1},{4,6},{5,7},{6,4},{7,5},{8,10},{9,11},{10,... | collective-permute-start | bytes 1376264 | tf_op jit(solution)/shard_map/ppermute | solution.py:982
  241.5 12.7 %collective-permute-start.37 = (bf16[2,128,896]{2,1,0:T(8,128)(2,1)}, bf16[2,128,896]{2,1,0:T(8,128)(2,1)S(1)}, u32[]{:S(2)}, u32[]{:S(2)}) collective-permute-start(bf16[2,128,896]{2,1,0:T(8,128)(2,1)} %get-tuple-element.377), channel_id=1, source_target_pairs={{0,4},{1,5},{2,6},{3,7},{4,0},{5,1},{6,2},{7,3},{8,12},{9,13},{10,... | collective-permute-start | bytes 1376264 | tf_op jit(solution)/shard_map/ppermute | solution.py:982
  260.5 35.6 %collective-permute-start.39 = (bf16[128,2432]{1,0:T(8,128)(2,1)}, bf16[128,2432]{1,0:T(8,128)(2,1)}, u32[]{:S(2)}, u32[]{:S(2)}) collective-permute-start(bf16[128,2432]{1,0:T(8,128)(2,1)} %pad_maximum_fusion.3), channel_id=1, source_target_pairs={{0,4},{1,5},{2,6},{3,7},{4,0},{5,1},{6,2},{7,3},{8,12},{9,13},{10,... | collective-permute-start | bytes 1867784 | tf_op jit(solution)/shard_map/ppermute | solution.py:982
  260.8 35.3 %collective-permute-start.40 = (bf16[128,2432]{1,0:T(8,128)(2,1)}, bf16[128,2432]{1,0:T(8,128)(2,1)}, u32[]{:S(2)}, u32[]{:S(2)}) collective-permute-start(bf16[128,2432]{1,0:T(8,128)(2,1)} %pad_maximum_fusion.5), channel_id=1, source_target_pairs={{0,2},{1,3},{2,0},{3,1},{4,6},{5,7},{6,4},{7,5},{8,10},{9,11},{10,... | collective-permute-start | bytes 1867784 | tf_op jit(solution)/shard_map/ppermute | solution.py:982
  262.5 33.6 %collective-permute-start.41 = (bf16[128,1664]{1,0:T(8,128)(2,1)S(1)}, bf16[128,1664]{1,0:T(8,128)(2,1)S(1)}, u32[]{:S(2)}, u32[]{:S(2)}) collective-permute-start(bf16[128,1664]{1,0:T(8,128)(2,1)S(1)} %add_convert_fusion.7), channel_id=1, source_target_pairs={{0,16},{8,24},{16,0},{24,8},{1,17},{9,25},{17,1},{25,9},{2,18},{10... | collective-permute-start | bytes 1277960 | tf_op jit(solution)/shard_map/ppermute | solution.py:982
  265.1 34.9 %collective-permute-start.44 = (bf16[384,1536]{1,0:T(8,128)(2,1)}, bf16[384,1536]{1,0:T(8,128)(2,1)}, u32[]{:S(2)}, u32[]{:S(2)}) collective-permute-start(bf16[384,1536]{1,0:T(8,128)(2,1)} %get-tuple-element.416), channel_id=1, source_target_pairs={{0,1},{1,0},{2,3},{3,2},{4,5},{5,4},{6,7},{7,6},{8,9},{9,8},{10,11... | collective-permute-start | bytes 3538952 | tf_op jit(solution)/shard_map/ppermute | solution.py:982
  282.2 40.1 %collective-permute-start.48 = (bf16[640,1024]{1,0:T(8,128)(2,1)S(1)}, bf16[640,1024]{1,0:T(8,128)(2,1)}, u32[]{:S(2)}, u32[]{:S(2)}) collective-permute-start(bf16[640,1024]{1,0:T(8,128)(2,1)S(1)} %slice_bitcast_fusion.1), channel_id=1, source_target_pairs={{0,1},{1,0},{2,3},{3,2},{4,5},{5,4},{6,7},{7,6},{8,9},{9,8},{10,11... | collective-permute-start | bytes 3932168 | tf_op jit(solution)/shard_map/ppermute | solution.py:982
  296.2 12.8 %collective-permute-start.59 = (bf16[128,1664]{1,0:T(8,128)(2,1)S(1)}, bf16[128,1664]{1,0:T(8,128)(2,1)S(1)}, u32[]{:S(2)}, u32[]{:S(2)}) collective-permute-start(bf16[128,1664]{1,0:T(8,128)(2,1)S(1)} %add_convert_fusion.6), channel_id=1, source_target_pairs={{0,8},{8,0},{16,24},{24,16},{1,9},{9,1},{17,25},{25,17},{2,10},{10... | collective-permute-start | bytes 1277960 | tf_op jit(solution)/shard_map/ppermute | solution.py:982
  298.4 23.6 %collective-permute-start.42 = (bf16[128,2432]{1,0:T(8,128)(2,1)S(1)}, bf16[128,2432]{1,0:T(8,128)(2,1)S(1)}, u32[]{:S(2)}, u32[]{:S(2)}) collective-permute-start(bf16[128,2432]{1,0:T(8,128)(2,1)S(1)} %get-tuple-element.484), channel_id=1, source_target_pairs={{0,8},{8,0},{16,24},{24,16},{1,9},{9,1},{17,25},{25,17},{2,10},{10... | collective-permute-start | bytes 1867784 | tf_op jit(solution)/shard_map/ppermute | solution.py:982
  306.6 23.3 %collective-permute-start.45 = (bf16[2,128,1152]{2,1,0:T(8,128)(2,1)}, bf16[2,128,1152]{2,1,0:T(8,128)(2,1)S(1)}, u32[]{:S(2)}, u32[]{:S(2)}) collective-permute-start(bf16[2,128,1152]{2,1,0:T(8,128)(2,1)} %get-tuple-element.426), channel_id=1, source_target_pairs={{0,2},{1,3},{2,0},{3,1},{4,6},{5,7},{6,4},{7,5},{8,10},{9,11},{10,... | collective-permute-start | bytes 1769480 | tf_op jit(solution)/shard_map/ppermute | solution.py:982
  308.1 21.8 %collective-permute-start.46 = (bf16[2,128,1152]{2,1,0:T(8,128)(2,1)}, bf16[2,128,1152]{2,1,0:T(8,128)(2,1)S(1)}, u32[]{:S(2)}, u32[]{:S(2)}) collective-permute-start(bf16[2,128,1152]{2,1,0:T(8,128)(2,1)} %get-tuple-element.428), channel_id=1, source_target_pairs={{0,4},{1,5},{2,6},{3,7},{4,0},{5,1},{6,2},{7,3},{8,12},{9,13},{10,... | collective-permute-start | bytes 1769480 | tf_op jit(solution)/shard_map/ppermute | solution.py:982
  309.2 44.0 %collective-permute-start.60 = (bf16[64,3328]{1,0:T(8,128)(2,1)S(1)}, bf16[64,3328]{1,0:T(8,128)(2,1)S(1)}, u32[]{:S(2)}, u32[]{:S(2)}) collective-permute-start(bf16[64,3328]{1,0:T(8,128)(2,1)S(1)} %broadcast_select_fusion.11), channel_id=1, source_target_pairs={{0,1},{1,0},{2,3},{3,2},{4,5},{5,4},{6,7},{7,6},{8,9},{9,8},{10,11... | collective-permute-start | bytes 1277960 | tf_op jit(solution)/shard_map/ppermute | solution.py:982
  322.3 30.6 %collective-permute-start.54 = (bf16[128,2432]{1,0:T(8,128)(2,1)S(1)}, bf16[128,2432]{1,0:T(8,128)(2,1)S(1)}, u32[]{:S(2)}, u32[]{:S(2)}) collective-permute-start(bf16[128,2432]{1,0:T(8,128)(2,1)S(1)} %add_convert_fusion.1), channel_id=1, source_target_pairs={{0,16},{8,24},{16,0},{24,8},{1,17},{9,25},{17,1},{25,9},{2,18},{10... | collective-permute-start | bytes 1867784 | tf_op jit(solution)/shard_map/ppermute | solution.py:982
  328.3 11.1 %collective-permute-start.49 = (bf16[2,128,512]{2,1,0:T(8,128)(2,1)}, bf16[2,128,512]{2,1,0:T(8,128)(2,1)S(1)}, u32[]{:S(2)}, u32[]{:S(2)}) collective-permute-start(bf16[2,128,512]{2,1,0:T(8,128)(2,1)} %get-tuple-element.440), channel_id=1, source_target_pairs={{0,2},{1,3},{2,0},{3,1},{4,6},{5,7},{6,4},{7,5},{8,10},{9,11},{10,... | collective-permute-start | bytes 786440 | tf_op jit(solution)/shard_map/ppermute | solution.py:982
  329.8 10.5 %collective-permute-start.50 = (bf16[2,128,512]{2,1,0:T(8,128)(2,1)}, bf16[2,128,512]{2,1,0:T(8,128)(2,1)S(1)}, u32[]{:S(2)}, u32[]{:S(2)}) collective-permute-start(bf16[2,128,512]{2,1,0:T(8,128)(2,1)} %get-tuple-element.442), channel_id=1, source_target_pairs={{0,4},{1,5},{2,6},{3,7},{4,0},{5,1},{6,2},{7,3},{8,12},{9,13},{10,... | collective-permute-start | bytes 786440 | tf_op jit(solution)/shard_map/ppermute | solution.py:982
  329.9 8.9 %collective-permute-start.47 = (f32[40,512]{1,0:T(8,128)S(1)}, f32[40,512]{1,0:T(8,128)S(1)}, u32[]{:S(2)}, u32[]{:S(2)}) collective-permute-start(f32[40,512]{1,0:T(8,128)S(1)} %add.226), channel_id=1, source_target_pairs={{0,2},{1,3},{2,0},{3,1},{4,6},{5,7},{6,4},{7,5},{8,10},{9,11},{10,... | collective-permute-start | bytes 245768 | tf_op jit(solution)/shard_map/ppermute | solution.py:982
  338.8 10.7 %collective-permute-start.52 = (bf16[128,1152]{1,0:T(8,128)(2,1)S(1)}, bf16[128,1152]{1,0:T(8,128)(2,1)S(1)}, u32[]{:S(2)}, u32[]{:S(2)}) collective-permute-start(bf16[128,1152]{1,0:T(8,128)(2,1)S(1)} %get-tuple-element.506), channel_id=1, source_target_pairs={{0,4},{1,5},{2,6},{3,7},{4,0},{5,1},{6,2},{7,3},{8,12},{9,13},{10,... | collective-permute-start | bytes 884744 | tf_op jit(solution)/shard_map/ppermute | solution.py:982
  339.5 11.2 %collective-permute-start.53 = (bf16[128,1152]{1,0:T(8,128)(2,1)S(1)}, bf16[128,1152]{1,0:T(8,128)(2,1)S(1)}, u32[]{:S(2)}, u32[]{:S(2)}) collective-permute-start(bf16[128,1152]{1,0:T(8,128)(2,1)S(1)} %get-tuple-element.504), channel_id=1, source_target_pairs={{0,2},{1,3},{2,0},{3,1},{4,6},{5,7},{6,4},{7,5},{8,10},{9,11},{10,... | collective-permute-start | bytes 884744 | tf_op jit(solution)/shard_map/ppermute | solution.py:982
  340.3 8.6 %collective-permute-start.51 = (f32[40,512]{1,0:T(8,128)S(1)}, f32[40,512]{1,0:T(8,128)S(1)}, u32[]{:S(2)}, u32[]{:S(2)}) collective-permute-start(f32[40,512]{1,0:T(8,128)S(1)} %add.227), channel_id=1, source_target_pairs={{0,4},{1,5},{2,6},{3,7},{4,0},{5,1},{6,2},{7,3},{8,12},{9,13},{10,... | collective-permute-start | bytes 245768 | tf_op jit(solution)/shard_map/ppermute | solution.py:982
  353.1 9.9 %collective-permute-start.56 = (bf16[128,1152]{1,0:T(8,128)(2,1)S(1)}, bf16[128,1152]{1,0:T(8,128)(2,1)S(1)}, u32[]{:S(2)}, u32[]{:S(2)}) collective-permute-start(bf16[128,1152]{1,0:T(8,128)(2,1)S(1)} %get-tuple-element.502), channel_id=1, source_target_pairs={{0,8},{8,0},{16,24},{24,16},{1,9},{9,1},{17,25},{25,17},{2,10},{10... | collective-permute-start | bytes 884744 | tf_op jit(solution)/shard_map/ppermute | solution.py:982
  354.6 11.0 %collective-permute-start.55 = (f32[40,512]{1,0:T(8,128)S(1)}, f32[40,512]{1,0:T(8,128)S(1)}, u32[]{:S(2)}, u32[]{:S(2)}) collective-permute-start(f32[40,512]{1,0:T(8,128)S(1)} %add.228), channel_id=1, source_target_pairs={{0,8},{8,0},{16,24},{24,16},{1,9},{9,1},{17,25},{25,17},{2,10},{10... | collective-permute-start | bytes 245768 | tf_op jit(solution)/shard_map/ppermute | solution.py:982
  363.1 14.6 %collective-permute-start.57 = (bf16[128,1152]{1,0:T(8,128)(2,1)S(1)}, bf16[128,1152]{1,0:T(8,128)(2,1)S(1)}, u32[]{:S(2)}, u32[]{:S(2)}) collective-permute-start(bf16[128,1152]{1,0:T(8,128)(2,1)S(1)} %add_convert_fusion.19), channel_id=1, source_target_pairs={{0,16},{8,24},{16,0},{24,8},{1,17},{9,25},{17,1},{25,9},{2,18},{10... | collective-permute-start | bytes 884744 | tf_op jit(solution)/shard_map/ppermute | solution.py:982
  363.3 29.1 %collective-permute-start.64 = (bf16[128,2432]{1,0:T(8,128)(2,1)S(1)}, bf16[128,2432]{1,0:T(8,128)(2,1)S(1)}, u32[]{:S(2)}, u32[]{:S(2)}) collective-permute-start(bf16[128,2432]{1,0:T(8,128)(2,1)S(1)} %add_convert_fusion), channel_id=1, source_target_pairs={{0,8},{8,0},{16,24},{24,16},{1,9},{9,1},{17,25},{25,17},{2,10},{10... | collective-permute-start | bytes 1867784 | tf_op jit(solution)/shard_map/ppermute | solution.py:982
  364.0 28.5 %collective-permute-start.63 = (bf16[128,512]{1,0:T(8,128)(2,1)S(1)}, bf16[128,512]{1,0:T(8,128)(2,1)S(1)}, u32[]{:S(2)}, u32[]{:S(2)}) collective-permute-start(bf16[128,512]{1,0:T(8,128)(2,1)S(1)} %get-tuple-element.518), channel_id=1, source_target_pairs={{0,8},{8,0},{16,24},{24,16},{1,9},{9,1},{17,25},{25,17},{2,10},{10... | collective-permute-start | bytes 393224 | tf_op jit(solution)/shard_map/ppermute | solution.py:982
  377.7 16.0 %collective-permute-start.58 = (f32[40,512]{1,0:T(8,128)S(1)}, f32[40,512]{1,0:T(8,128)S(1)}, u32[]{:S(2)}, u32[]{:S(2)}) collective-permute-start(f32[40,512]{1,0:T(8,128)S(1)} %add.234), channel_id=1, source_target_pairs={{0,16},{8,24},{16,0},{24,8},{1,17},{9,25},{17,1},{25,9},{2,18},{10... | collective-permute-start | bytes 245768 | tf_op jit(solution)/shard_map/ppermute | solution.py:982
  377.8 23.6 %collective-permute-start.66 = (bf16[128,1152]{1,0:T(8,128)(2,1)S(1)}, bf16[128,1152]{1,0:T(8,128)(2,1)S(1)}, u32[]{:S(2)}, u32[]{:S(2)}) collective-permute-start(bf16[128,1152]{1,0:T(8,128)(2,1)S(1)} %add_convert_fusion.18), channel_id=1, source_target_pairs={{0,8},{8,0},{16,24},{24,16},{1,9},{9,1},{17,25},{25,17},{2,10},{10... | collective-permute-start | bytes 884744 | tf_op jit(solution)/shard_map/ppermute | solution.py:982
  392.5 7.4 %collective-permute-start.68 = (bf16[128,512]{1,0:T(8,128)(2,1)S(1)}, bf16[128,512]{1,0:T(8,128)(2,1)}, u32[]{:S(2)}, u32[]{:S(2)}) collective-permute-start(bf16[128,512]{1,0:T(8,128)(2,1)S(1)} %add_convert_fusion.32), channel_id=1, source_target_pairs={{0,16},{8,24},{16,0},{24,8},{1,17},{9,25},{17,1},{25,9},{2,18},{10... | collective-permute-start | bytes 393224 | tf_op jit(solution)/shard_map/ppermute | solution.py:982
  393.7 14.4 %collective-permute-start.65 = (bf16[64,4864]{1,0:T(8,128)(2,1)}, bf16[64,4864]{1,0:T(8,128)(2,1)S(1)}, u32[]{:S(2)}, u32[]{:S(2)}) collective-permute-start(bf16[64,4864]{1,0:T(8,128)(2,1)} %broadcast_select_fusion.3), channel_id=1, source_target_pairs={{0,1},{1,0},{2,3},{3,2},{4,5},{5,4},{6,7},{7,6},{8,9},{9,8},{10,11... | collective-permute-start | bytes 1867784 | tf_op jit(solution)/shard_map/ppermute | solution.py:982
  (71 other events, 345.2 us)

commit v3 on v2

--- a/solution.py
+++ b/solution.py
@@ -14,12 +14,14 @@
 WIN = 256
 QBLK = 384
 DOCS = 8
+EDGE = 16
 epsilon = 1e-05
 GAIN, SHIFT, BIAS, CONTRACT, EXPAND, POOL, UP = 0, 6, 12, 18, 21, 33, 34
 
 VMEM = pl.BlockSpec(memory_space=pltpu.VMEM)
 SMEM = pl.BlockSpec(memory_space=pltpu.SMEM)
 HBM = pl.BlockSpec(memory_space=pltpu.HBM)
+ANY = pl.BlockSpec(memory_space=pl.ANY)
 
 
 LANES = 128
@@ -85,12 +87,6 @@
         jnp.where(lane + row < LANES, here, after) for here, after in zip(blocks, blocks[1:])
     ]
     return jnp.concatenate(out, axis=1)
-
-
-def skew_pooled(table):
-    lane, row = lanes_and_rows()
-    here, after = turned(table, (lane + LANES - 1 - row) % LANES)
-    return jnp.where(lane <= row, here, after)
 
 
 def unskew_pooled(scores):
@@ -222,7 +218,8 @@
     grad,
     bias_ref,
     returned_ref,
-    pack,
+    own_pack,
+    other_pack,
     dk_sum,
     dv_sum,
     returned,
@@ -273,12 +270,16 @@
     grad_content = jnp.concatenate(contents, axis=0)
     grad_position = jnp.concatenate(positions, axis=0)
     bias_ref[...] = column_sums(grad_content, grad_position)
-    dq_out[...] = (grad_content + grad_position).astype(jnp.bfloat16)
-    dk_out[...] = dk_sum[...].astype(jnp.bfloat16)
-    dv_out[...] = dv_sum[...].astype(jnp.bfloat16)
-    dt_out[...] = tn(places[...], jnp.concatenate(order, axis=0)).astype(jnp.bfloat16)
-    copies = pack_copies(place, pair, pack, (dq_out, dk_out, dv_out, dt_out), sems)
-    back = nt(dk_out[:WIN, :], key_weight[...]) + nt(dv_out[:WIN, :], value_weight[...])
+    slot = pair % 2
+    grad_keys = dk_sum[...].astype(jnp.bfloat16)
+    grad_values = dv_sum[...].astype(jnp.bfloat16)
+    dq_out[slot] = (grad_content + grad_position).astype(jnp.bfloat16)
+    dk_out[slot] = grad_keys
+    dv_out[slot] = grad_values
+    dt_out[slot] = tn(places[...], jnp.concatenate(order, axis=0)).astype(jnp.bfloat16)
+    outs = (dq_out, dk_out, dv_out, dt_out)
+    send_pack(place, pair, (own_pack, other_pack), outs, sems)
+    back = nt(grad_keys[:WIN], key_weight[...]) + nt(grad_values[:WIN], value_weight[...])
 
     @pl.when(pair == 0)
     def _():
@@ -292,24 +293,45 @@
     def _():
         returned_ref[...] = returned[...].astype(jnp.bfloat16)
 
-    for copy in copies:
+
+def pack_copies(place, pair, packs, outs, sems, act):
+    for slot, pack in enumerate(packs):
+
+        @pl.when((pair // 2) ^ place[1] == slot)
+        def _(pack=pack):
+            for index, out in enumerate(outs):
+                lane = pl.multiple_of(index * D // 2 + pair % 2 * PAIR, PAIR)
+                source = out.at[pair % 2]
+                target = pack.at[pl.ds(0, source.shape[0]), pl.ds(lane, PAIR)]
+                act(pltpu.make_async_copy(source, target, sems.at[pair % 2, index]))
+
+
+def send_pack(place, pair, packs, outs, sems):
+    def start(copy):
+        copy.start()
+
+    def wait(copy):
         copy.wait()
 
-
-def pack_copies(place, pair, pack, outs, sems):
-    slot = (pair // 2) ^ place[1]
-    copies = []
-    for index, out in enumerate(outs):
-        lane = pl.multiple_of(index * D // 2 + pair % 2 * PAIR, PAIR)
-        target = pack.at[slot, pl.ds(0, out.shape[0]), pl.ds(lane, PAIR)]
-        copies.append(pltpu.make_async_copy(out, target, sems.at[index]))
-        copies[-1].start()
-    return copies
+    pack_copies(place, pair, packs, outs, sems, start)
+
+    @pl.when(pair > 0)
+    def _():
+        pack_copies(place, pair - 1, packs, outs, sems, wait)
+
+    @pl.when(pair == HEADS // 2 - 1)
+    def _():
+        pack_copies(place, pair, packs, outs, sems, wait)
 
 
 def table_rows(order, block, count):
-    start = order[block] + count - 1 - order[count]
-    return pl.ds(pl.multiple_of(LANES * jnp.minimum(start, count - 1), LANES), 2 * LANES)
+    start = jnp.minimum(order[block] + count - 1 - order[count], count - 1)
+    return pl.ds(pl.multiple_of(LANES * start, LANES), 2 * LANES)
+
+
+def table_lanes(order, block, count, offset):
+    start = jnp.minimum(order[block] + count - 1 - order[count], count - 1) + offset
+    return pl.ds(pl.multiple_of(LANES * start, LANES), LANES)
 
 
 def pooled_forward_kernel(
@@ -325,21 +347,33 @@
     keys_ref,
     values_ref,
     weights_ref,
+    bias,
+    places,
 ):
     count = normed.shape[0] // LANES
+
+    @pl.when(pl.program_id(0) == 0)
+    def _():
+        for block in range(count):
+            visible = pooled_mask(info, LANES * order[block])
+            bias[block] = jnp.where(visible, 0.0, MASKED)
+
     scale = jnp.asarray(HD**-0.5, jnp.bfloat16)
     keys_ref[...] = nn(normed[...], key_weight[...]).astype(jnp.bfloat16)
     values_ref[...] = nn(normed[...], value_weight[...]).astype(jnp.bfloat16)
     scores = nt(stacked(content[...] * scale), keys_ref[...])
-    there = stacked(position[...] * scale)
+    lane, row = lanes_and_rows()
+    place = nt(stacked(position[...] * scale), table[...])
+    turn = (lane + LANES - 1 - row) % LANES
     rows = [[], []]
-    for block in range(count):
-        place = nt(there, table[table_rows(order, block, count), :])
-        bias = jnp.where(pooled_mask(info, LANES * order[block]), 0.0, MASKED)
-        lanes = slice(block * LANES, (block + 1) * LANES)
-        for index in range(2):
-            half = slice(index * LANES, (index + 1) * LANES)
-            rows[index].append(scores[half, lanes] + skew_pooled(place[half]) + bias)
+    for index in range(2):
+        half = slice(index * LANES, (index + 1) * LANES)
+        places[half, :] = jnp.concatenate(turned(place[half], turn), axis=1)
+        for block in range(count):
+            here = places[half, table_lanes(order, block, count, 0)]
+            there = places[half, table_lanes(order, block, count, 1)]
+            score = scores[half, block * LANES : (block + 1) * LANES]
+            rows[index].append(score + jnp.where(lane <= row, here, there) + bias[block])
     weights = []
     for index in range(2):
         weight = softmax_rows(jnp.concatenate(rows[index], axis=1)).astype(jnp.bfloat16)
@@ -364,7 +398,8 @@
     bias_ref,
     even_ref,
     odd_ref,
-    pack,
+    own_pack,
+    other_pack,
     table_sum,
     total,
     dq_out,
@@ -398,12 +433,16 @@
         table_sum[rows, :] += tn(parts, positions)
     grad_position = unstacked(to_position) * scale
     bias_ref[...] = column_sums(grad_content, grad_position)
-    dq_out[...] = (grad_content + grad_position).astype(jnp.bfloat16)
-    dk_out[...] = tn(low_scores, stacked(content[...] * low_scale)).astype(jnp.bfloat16)
-    dv_out[...] = tn(lows, grads).astype(jnp.bfloat16)
-    dt_out[...] = table_sum[...].astype(jnp.bfloat16)
-    copies = pack_copies(place, pair, pack, (dq_out, dk_out, dv_out, dt_out), sems)
-    back = nt(dk_out[...], key_weight[...]) + nt(dv_out[...], value_weight[...])
+    slot = pair % 2
+    grad_keys = tn(low_scores, stacked(content[...] * low_scale)).astype(jnp.bfloat16)
+    grad_values = tn(lows, grads).astype(jnp.bfloat16)
+    dq_out[slot] = (grad_content + grad_position).astype(jnp.bfloat16)
+    dk_out[slot] = grad_keys
+    dv_out[slot] = grad_values
+    dt_out[slot] = table_sum[...].astype(jnp.bfloat16)
+    outs = (dq_out, dk_out, dv_out, dt_out)
+    send_pack(place, pair, (own_pack, other_pack), outs, sems)
+    back = nt(grad_keys, key_weight[...]) + nt(grad_values, value_weight[...])
 
     @pl.when(pair == 0)
     def _():
@@ -421,9 +460,6 @@
             rows = total[block * LANES : (block + 1) * LANES, :]
             target[start : start + LANES, :] = rows.astype(jnp.bfloat16)
 
-    for copy in copies:
-        copy.wait()
-
 
 def by_pair(shape, first=0):
     front = tuple(shape[:-1])
@@ -444,17 +480,22 @@
     return pl.BlockSpec((2,) + tuple(shape[1:]), lambda pair: (pair,) + (0,) * (len(shape) - 1))
 
 
-def attention_call(micros, kernel, scalars, operands, outs, scratch, mib):
+def attention_call(micros, kernel, scalars, operands, outs, scratch, mib, follows=()):
+    first = len(scalars) + len(operands)
+
+    def run(*refs):
+        kernel(*refs[:first], *refs[first + len(follows) :])
+
     return pl.pallas_call(
-        kernel,
+        run,
         grid=(HEADS // 2,),
-        in_specs=[SMEM] * len(scalars) + [spec for _, spec in operands],
+        in_specs=[SMEM] * len(scalars) + [spec for _, spec in operands] + [HBM] * len(follows),
         out_specs=[HBM if spec is None else spec for _, _, spec in outs],
         out_shape=[pltpu.HBM(shape, kind) for shape, kind, _ in outs],
         scratch_shapes=scratch,
         compiler_params=pltpu.CompilerParams(vmem_limit_bytes=mib * 2**20),
         cost_estimate=lasting(micros),
-    )(*scalars, *[in_hbm(array) for array, _ in operands])
+    )(*scalars, *[in_hbm(array) for array, _ in operands], *[in_hbm(a) for a in follows])
 
 
 def vector(vectors, row):
@@ -534,6 +575,25 @@
             self.copies.send(self.buffer.at[:, lanes], self.target.at[:, lanes])
 
 
+def write_table(frequency, first, out):
+    step = 32
+    count = out.shape[0]
+
+    def waves(start, change, rows):
+        distance = start + change * lax.broadcasted_iota(jnp.int32, (rows, 1), 0)
+        angle = distance.astype(jnp.float32) * frequency[...]
+        return jnp.sin(angle), jnp.cos(angle)
+
+    high_sin, high_cos = waves(first, -step, count // step)
+    low_sin, low_cos = waves(0, -1, step)
+    for index in range(count // step):
+        rows = slice(index * step, (index + 1) * step)
+        sine, cosine = high_sin[index : index + 1], high_cos[index : index + 1]
+        out[rows, : D // 2] = (sine * low_cos + cosine * low_sin).astype(jnp.bfloat16)
+        out[rows, D // 2 :] = (cosine * low_cos - sine * low_sin).astype(jnp.bfloat16)
+    out.send()
+
+
 def queries(layer, normed, vectors, weight, content, position):
     value = nn(normed, weight[:, :D])
     content[...] = (value + vector(vectors, BIAS + 2 * layer)).astype(jnp.bfloat16)
@@ -543,14 +603,17 @@
 
 
 def window_project_kernel(
-    layer, inputs, vectors, embedded, w_in, content, position, keys, values, table, *normed
+    layer, inputs, vectors, embedded, w_in, content, position, keys, values, table, *more
 ):
     weight, copy = w_in
     rows = inputs[...]
-    if normed:
+    if more:
+        normed, waves = more
         rows = norm_forward(rows.astype(jnp.float32), vectors, layer, 0)
-        normed[0][...] = rows
-        normed[0].send()
+        normed[...] = rows
+        normed.send()
+        write_table(embedded, WIN, waves)
+        embedded = waves
     copy.wait()
     queries(layer, rows, vectors, weight, content, position)
     for index, out in ((1, keys), (2, values)):
@@ -589,7 +652,7 @@
 def pool_kernel(info, full, edge, vectors, w_pool, normed, inputs, grouped, moved):
     pool_weight, pool_copy = w_pool
     put_rows(moved, 8, full[...])
-    put_rows(moved, 6, edge[...].astype(jnp.float32))
+    put_rows(moved, 6, edge[-2:, :].astype(jnp.float32))
     parts = []
     for offset in range(3):
         rows = third_rows(moved, offset + 6)
@@ -604,11 +667,12 @@
     inputs[...] = total
 
 
-def pooled_project_kernel(normed, vectors, embedded, w_in, content, position, table):
+def pooled_project_kernel(normed, vectors, frequency, w_in, content, position, table, waves):
     weight, copy = w_in
+    write_table(frequency, waves.shape[0] - LANES - 1, waves)
     copy.wait()
     queries(1, normed[...], vectors, weight, content, position)
-    table[...] = nn(embedded[...], weight[:, 3 * D :]).astype(jnp.bfloat16)
+    table[...] = nn(waves[...], weight[:, 3 * D :]).astype(jnp.bfloat16)
 
 
 def feed(layer, mixed, inputs, vectors, weights, middle_ref, slope, pack):
@@ -652,10 +716,12 @@
     pack,
     result,
     squares,
+    edge,
 ):
     weights = (w_out, w_expand, w_contract)
     total = feed(layer, mixed, inputs, vectors, weights, middle, slope, pack)
     result[...] = total.astype(result.dtype)
+    edge[...] = total[-EDGE:].astype(jnp.bfloat16)
     squares[...] = jnp.sum(total * total, axis=0, keepdims=True)
 
 
@@ -769,18 +835,18 @@
     moved = refs[-1]
     rows = shifted.shape[0]
     moved[:rows, :] = shifted[...]
-    moved[rows : rows + 2, :] = came_back[...]
+    moved[rows : rows + 2, :] = came_back[:2, :]
     feed_backward(0, place, joined[...] + moved[2 : rows + 2, :], *refs[:-1])
 
 
-def project_backward(layer, core, pack, rows, weight, extra, inputs, middle_grad, vectors, small):
+def project_backward(layer, core, packs, rows, weight, extra, inputs, middle_grad, vectors, small):
     small[...] = jnp.zeros_like(small)
     normed_grad = extra
     for index, chosen in enumerate(rows):
         for slot in range(2):
             half = slot ^ core
             begin = pl.multiple_of(index * D + half * (D // 2), D // 2)
-            grad = pack[slot, chosen, index * D // 2 : (index + 1) * D // 2]
+            grad = packs[slot][chosen, index * D // 2 : (index + 1) * D // 2]
             normed_grad = normed_grad + nt(grad, weight[:, pl.ds(begin, D // 2)])
     norm, gain, shift = norm_backward(inputs, vectors, layer, 0, normed_grad)
     small[0:1, :] = gain
@@ -788,29 +854,29 @@
     return middle_grad[...] + norm
 
 
-def window_project_backward(layer, core, pack, returned, weight, *rest):
+def window_project_backward(layer, core, packs, returned, weight, *rest):
     extra = jnp.concatenate(
         [jnp.zeros((QBLK - WIN, D), jnp.float32), returned[...].astype(jnp.float32)], axis=0
     )
     rows = (slice(0, QBLK), slice(WIN, REACH), slice(WIN, REACH))
-    return project_backward(layer, core, pack, rows, weight, extra, *rest)
+    return project_backward(layer, core, packs, rows, weight, extra, *rest)
 
 
 def first_project_backward_kernel(
-    place, pack, returned, inputs, middle_grad, vectors, w_in, inputs_grad, small
+    place, packs, returned, inputs, middle_grad, vectors, w_in, inputs_grad, small
 ):
     weight, copy = w_in
     copy.wait()
     rows = inputs[...].astype(jnp.float32)
     total = window_project_backward(
-        0, place[1], pack, returned, weight, rows, middle_grad, vectors, small
+        0, place[1], packs, returned, weight, rows, middle_grad, vectors, small
     )
     inputs_grad[...] = total.astype(inputs_grad.dtype)
 
 
 def last_project_backward_kernel(
     place,
-    pack,
+    packs,
     returned,
     inputs,
     middle_grad,
@@ -827,7 +893,7 @@
     (weight, copy), (up_weight, up_copy) = w_in, w_up
     copy.wait()
     total = window_project_backward(
-        2, place[1], pack, returned, weight, inputs[...], middle_grad, vectors, small
+        2, place[1], packs, returned, weight, inputs[...], middle_grad, vectors, small
     )
     inputs_grad[...] = total
     inputs_grad.send()
@@ -865,7 +931,7 @@
 def pooled_project_backward_kernel(
     info,
     place,
-    pack,
+    packs,
     normed_grad,
     inputs,
     middle_grad,
@@ -873,6 +939,7 @@
     w_in,
     w_pool,
     shifted_grad,
+    first_rows,
     own,
     other,
     small,
@@ -883,7 +950,7 @@
     total = project_backward(
         1,
         place[1],
-        pack,
+        packs,
         (slice(0, LANES),),
         weight,
         normed_grad[...],
@@ -900,25 +967,29 @@
         rows = nt(low, pool_weight[offset * D : (offset + 1) * D, :])
         put_third_rows(spread, offset, jnp.where(kept(info, offset), rows, 0.0))
     shifted_grad[...] = all_rows(spread)
+    first_rows[...] = shifted_grad[:EDGE, :]
 
 
 def lasting(micros):
     return pl.CostEstimate(
-        flops=int(micros * 1e8), bytes_accessed=int(micros * 3e5), transcendentals=0
+        flops=int(micros * 1e9), bytes_accessed=int(micros * 3e6), transcendentals=0
     )
 
 
 class Part:
-    def __init__(self, array, shape):
-        self.array, self.shape = array, tuple(shape)
+    def __init__(self, array, shape=None, place=None):
+        self.array, self.place = array, place
+        self.shape = tuple(shape or (array.shape if place is None else array.shape[1:]))
 
     def of(self, ref):
+        if self.place is not None:
+            return ref.at[self.place]
         if self.shape == self.array.shape:
             return ref
         return ref.at[tuple(slice(0, size) for size in self.shape)]
 
 
-def whole(micros, kernel, scalars, arrays, weights, outs, scratch=(), mib=24):
+def whole(micros, kernel, scalars, arrays, weights, outs, scratch=(), mib=24, follows=()):
     flat, groups, parts = [], [], []
     for array in arrays:
         groups.append(len(array) if isinstance(array, tuple) else 0)
@@ -941,7 +1012,9 @@
             return taken
 
         taken = take(scalar_count)
-        sources, weight_sources, targets = take(flat_count), take(weight_count), take(len(outs))
+        sources, weight_sources = take(flat_count), take(weight_count)
+        take(len(follows))
+        targets = take(len(outs))
         buffers, weight_buffers, out_buffers = take(flat_count), take(weight_count), take(len(outs))
         loads = [copies.start(p.of(s), b) for p, s, b in zip(parts, sources, buffers)]
         loaded = []
@@ -963,14 +1036,14 @@
 
     return pl.pallas_call(
         run,
-        in_specs=[SMEM] * scalar_count + [HBM] * (flat_count + weight_count),
+        in_specs=[SMEM] * scalar_count + [HBM] * (flat_count + weight_count + len(follows)),
         out_specs=[HBM] * len(outs),
         out_shape=[pltpu.HBM(shape, kind) for shape, kind in outs],
         scratch_shapes=[pltpu.VMEM(*item) for item in shapes]
         + [pltpu.SemaphoreType.DMA((sem_count,))],
         compiler_params=pltpu.CompilerParams(vmem_limit_bytes=mib * 2**20),
         cost_estimate=lasting(micros),
-    )(*scalars, *[in_hbm(a) for a in flat + [w for w, _ in weights]])
+    )(*scalars, *[in_hbm(a) for a in flat + [w for w, _ in weights] + list(follows)])
 
 
 def in_hbm(array):
@@ -1110,7 +1183,7 @@
     return Piece(D, [3 * D // 2], {x: (first, D), dy: (0, D // 2)}, compute)
 
 
-def pair_gradients(micros, place, sources, pieces):
+def pair_gradients(micros, place, sources, pieces, follows, natural=False):
     lanes = sum(piece.lanes for piece in pieces)
     flat, first = [], {}
     for name, arrays in sources.items():
@@ -1123,12 +1196,15 @@
                 buffers.append(pltpu.VMEM((array.shape[-2], width), array.dtype))
     count = len(flat)
     out = (2, LANES, lanes)
+    shapes = [(4, LANES, 2 * lanes)] if natural else [out] * 4
+    total_outs = len(shapes)
 
     def kernel(place, *refs):
-        arrays, targets = refs[:count], refs[count : count + 4]
-        spaces, sems = list(refs[count + 4 : -5]), refs[-1]
+        arrays = refs[:count]
+        refs = refs[count + len(follows) :]
+        targets, spaces, sems = refs[:total_outs], list(refs[total_outs : -1 - total_outs]), refs[-1]
         copies = Copies(sems)
-        keep_one, send_one, keep_two, send_two = refs[-5:-1]
+        results = refs[-1 - total_outs : -1]
         ready = []
         for piece in pieces:
             inputs, loads = {}, []
@@ -1150,43 +1226,52 @@
                 load.wait()
             groups = piece.height // LANES
             for block in range(4):
-                begin = pl.multiple_of((place[0] ^ block) * piece.height, LANES)
+                chip = block if natural else place[0] ^ block
+                begin = chip * piece.height
+                if not natural:
+                    begin = pl.multiple_of(begin, LANES)
                 totals = piece.compute(inputs, pl.ds(begin, piece.height))
                 position = offset
                 for total in totals:
                     total = total.astype(jnp.bfloat16)
                     quarter = total.shape[1] // 2
-                    for space, slot, part in (
-                        ((keep_one, send_one)[block % 2], block // 2, total[:, :quarter]),
-                        ((keep_two, send_two)[block // 2], block % 2, total[:, quarter:]),
-                    ):
+                    halves = (total[:, :quarter], total[:, quarter:])
+                    for index, part in enumerate(halves):
+                        if natural:
+                            space, slot, lane = results[0], block, position + index * lanes
+                        else:
+                            which = (block % 2, block // 2)[index]
+                            space, slot, lane = results[2 * index + which], block // 2, position
+                            if index == 1:
+                                slot = block % 2
                         if groups == 1:
-                            space[slot, :, position : position + quarter] = part
+                            space[slot, :, lane : lane + quarter] = part
                             continue
                         for group in range(groups):
-                            start = position + quarter * group
+                            start = lane + quarter * group
                             low = HD * group
                             high = piece.height // 2 + low
                             space[slot, :HD, start : start + quarter] = part[low : low + HD]
                             space[slot, HD:, start : start + quarter] = part[high : high + HD]
                     position += quarter * groups
-            done = slice(offset, offset + piece.lanes)
-            for space, target in zip((keep_one, send_one, keep_two, send_two), targets):
-                copies.send(space.at[:, :, done], target.at[:, :, done])
+            for begin in (offset, offset + lanes) if natural else (offset,):
+                done = slice(begin, begin + piece.lanes)
+                for space, target in zip(results, targets):
+                    copies.send(space.at[:, :, done], target.at[:, :, done])
             offset += piece.lanes
         copies.finish()
 
     return pl.pallas_call(
         kernel,
-        in_specs=[SMEM] + [HBM] * count,
-        out_specs=[HBM] * 4,
-        out_shape=[pltpu.HBM(out, jnp.bfloat16)] * 4,
+        in_specs=[SMEM] + [ANY] * count + [HBM] * len(follows),
+        out_specs=[HBM] * total_outs,
+        out_shape=[pltpu.HBM(shape, jnp.bfloat16) for shape in shapes],
         scratch_shapes=buffers
-        + [pltpu.VMEM(out, jnp.bfloat16)] * 4
+        + [pltpu.VMEM(shape, jnp.bfloat16) for shape in shapes]
         + [pltpu.SemaphoreType.DMA((64,))],
         compiler_params=pltpu.CompilerParams(vmem_limit_bytes=32 * 2**20),
         cost_estimate=lasting(micros),
-    )(place, *[in_hbm(a) for a in flat])
+    )(place, *flat, *[in_hbm(a) for a in follows])
 
 
 def first_step(keep_one, send_one, keep_two, send_two):
@@ -1225,50 +1310,45 @@
     return keep, crossed(keep, "dp", 1)
 
 
-def shared(keep, other, depth, core):
-    first, second = both(keep, other, depth)
-    share = jnp.concatenate([first, second], axis=1)
+def depth_share(keep, other, depth):
+    return jnp.concatenate(both(keep, other, depth), axis=1)
+
+
+def core_rows(share, core):
     keep, send = both(share[:HD], share[HD:], core)
-    return both(keep, crossed(send, "seq", 1), core)
+    return keep, crossed(send, "seq", 1)
 
 
 def together(*groups):
     return lax.optimization_barrier(tuple(tuple(group) for group in groups))
 
 
-def final_kernel(plan, *refs):
+def final_kernel(plan, place, *refs):
     groups = len(plan)
     buffers, outs = refs[: 2 * groups], refs[2 * groups :]
     for index, pieces in enumerate(plan):
-        lanes = buffers[2 * index].shape[1] // 2
+        mine, other = buffers[2 * index : 2 * index + 2]
+        lanes = mine.shape[1] // 2
         offset = 0
         for out_index, layer, first_column, columns, height in pieces:
             out = outs[out_index]
             quarter = columns // 4
             for group in range(height // HD):
-                rows = pl.ds(HD * group, HD)
+                rows = slice(HD * group, HD * (group + 1))
                 for part in range(4):
-                    buffer = buffers[2 * index + part // 2]
                     start = (part % 2) * lanes + offset
-                    value = buffer[:, start : start + quarter].astype(jnp.float32)
+                    chosen = slice(start, start + quarter)
+                    value = jnp.where(place[1] == part // 2, mine[:, chosen], other[:, chosen])
                     begin = first_column + part * quarter
-                    if layer is None:
-                        out[rows, begin : begin + quarter] = value
-                    else:
-                        out[layer, rows, begin : begin + quarter] = value
+                    where = (rows, slice(begin, begin + quarter))
+                    out[where if layer is None else (layer, *where)] = value.astype(jnp.float32)
                 offset += quarter
 
 
-def final_outputs(plan, buffers, shapes):
+def final_outputs(place, plan, buffers, shapes):
     flat = [array for pair in buffers for array in pair]
-    return pl.pallas_call(
-        partial(final_kernel, plan),
-        in_specs=[VMEM] * len(flat),
-        out_specs=[VMEM] * len(shapes),
-        out_shape=[jax.ShapeDtypeStruct(shape, jnp.float32) for shape in shapes],
-        compiler_params=pltpu.CompilerParams(vmem_limit_bytes=16 * 2**20),
-        cost_estimate=lasting(3),
-    )(*flat)
+    outs = [(shape, jnp.float32) for shape in shapes]
+    return whole(3, partial(final_kernel, plan), [place], flat, [], outs, mib=32)
 
 
 def summed_everywhere(flat):
@@ -1278,22 +1358,6 @@
     return flat
 
 
-def phases(distance):
-    frequency = jnp.power(10000.0, -2.0 * jnp.arange(D // 2, dtype=jnp.float32) / D)
-    angle = distance.astype(jnp.float32)[:, None] * frequency[None, :]
-    return jnp.sin(angle), jnp.cos(angle)
-
-
-def embedding(first, count):
-    step = 32
-    high_sin, high_cos = phases(first - step * jnp.arange(count // step))
-    low_sin, low_cos = phases(-jnp.arange(step))
-    high_sin, high_cos = high_sin[:, None], high_cos[:, None]
-    sines = high_sin * low_cos[None] + high_cos * low_sin[None]
-    cosines = high_cos * low_cos[None] - high_sin * low_sin[None]
-    return jnp.concatenate([sines, cosines], axis=2).astype(jnp.bfloat16).reshape(count, D)
-
-
 def outer_float(first_matrix, second_matrix):
     return jnp.einsum("rc,re->ce", first_matrix, second_matrix, preferred_element_type=jnp.float32)
 
@@ -1301,9 +1365,9 @@
 BF, FL = jnp.bfloat16, jnp.float32
 
 
-def window_project(layer, inputs, vectors, embedded, w_in, normalise):
+def window_project(layer, inputs, vectors, embedded, w_in, first):
     one = (inputs.shape, BF)
-    outs = [one, one, one, one, (embedded.shape, BF)] + [one] * normalise
+    outs = [one, one, one, one, ((QBLK, D), BF)] + [one, ((QBLK, D), BF)] * first
     return whole(
         4,
         partial(window_project_kernel, layer),
@@ -1337,7 +1401,9 @@
     return attention_call(11, kernel, [info], operands, outs, scratch, 20)
 
 
-def window_attention_back(layer, place, heads, border, w_in, table, weights, grad):
+def window_attention_back(
+    layer, place, heads, border, w_in, table, weights, grad, follows=()
+):
     rows = heads[0].shape[0]
     operands = [(a, by_pair(a.shape)) for a in (*heads, border)]
     operands += [(w_in, of_layer(w_in.shape, layer, first)) for first in (4, 8)]
@@ -1346,13 +1412,16 @@
     outs = [
         ((2, D), FL, by_pair((2, D))),
         ((WIN, D), BF, entire((WIN, D))),
-        ((2, REACH, 2 * D), BF, None),
+        ((REACH, 2 * D), BF, None),
+        ((REACH, 2 * D), BF, None),
     ]
     scratch = [pltpu.VMEM((REACH, PAIR), FL)] * 2
     scratch += [pltpu.VMEM((WIN, D), FL), pltpu.VMEM((2 * rows, SEEN), BF)]
-    scratch += [pltpu.VMEM((size, PAIR), BF) for size in (rows, REACH, REACH, table.shape[0])]
-    scratch.append(pltpu.SemaphoreType.DMA((4,)))
-    return attention_call(13, window_backward_kernel, [place], operands, outs, scratch, 20)
+    scratch += [pltpu.VMEM((2, size, PAIR), BF) for size in (rows, REACH, REACH, table.shape[0])]
+    scratch.append(pltpu.SemaphoreType.DMA((2, 4)))
+    return attention_call(
+        13, window_backward_kernel, [place], operands, outs, scratch, 20, follows
+    )
 
 
 def pooled_attention(info, order, content, position, normed, w_in, table):
@@ -1368,11 +1437,15 @@
         ((total, D), BF, by_pair((total, D))),
         (weights, BF, weights_block(weights)),
     ]
+    scratch = [
+        pltpu.VMEM((total // LANES, LANES, LANES), FL),
+        pltpu.VMEM((2 * rows, table.shape[0]), FL),
+    ]
     mib = 10 + total // LANES * 3 // 2
-    return attention_call(13, pooled_forward_kernel, [info, order], operands, outs, [], mib)
-
-
-def pooled_attention_back(order, place, heads, w_in, table, weights, grad):
+    return attention_call(13, pooled_forward_kernel, [info, order], operands, outs, scratch, mib)
+
+
+def pooled_attention_back(order, place, heads, w_in, table, weights, grad, follows):
     rows, total = heads[0].shape[0], heads[2].shape[0]
     operands = [(a, by_pair(a.shape)) for a in heads]
     operands += [(w_in, of_layer(w_in.shape, 1, first)) for first in (4, 8)]
@@ -1383,16 +1456,19 @@
         ((2, D), FL, by_pair((2, D))),
         (half, BF, entire(half)),
         (half, BF, entire(half)),
-        ((2, table.shape[0], 2 * D), BF, None),
+        ((table.shape[0], 2 * D), BF, None),
+        ((table.shape[0], 2 * D), BF, None),
     ]
     scratch = [pltpu.VMEM((table.shape[0], PAIR), FL), pltpu.VMEM((total, D), FL)]
-    scratch += [pltpu.VMEM((size, PAIR), BF) for size in (rows, total, total, table.shape[0])]
-    scratch.append(pltpu.SemaphoreType.DMA((4,)))
+    scratch += [pltpu.VMEM((2, size, PAIR), BF) for size in (rows, total, total, table.shape[0])]
+    scratch.append(pltpu.SemaphoreType.DMA((2, 4)))
     mib = 10 + total // LANES * 3 // 2
-    return attention_call(13, pooled_backward_kernel, [order, place], operands, outs, scratch, mib)
-
-
-def window_feed(layer, mixed, inputs, vectors, weights, kind):
+    return attention_call(
+        13, pooled_backward_kernel, [order, place], operands, outs, scratch, mib, follows
+    )
+
+
+def window_feed(layer, mixed, inputs, vectors, weights, kind, follows=()):
     rows = mixed.shape[0]
     outs = [
         ((rows, D), FL),
@@ -1400,6 +1476,7 @@
         ((rows, 6 * D), BF),
         ((rows, D), kind),
         ((1, D), FL),
+        ((EDGE, D), BF),
     ]
     return whole(
         7,
@@ -1408,13 +1485,20 @@
         [mixed, inputs, vectors],
         [(w, layer) for w in weights],
         outs,
-    )
-
-
-def feed_back(kernel, layer, place, arrays, rows, weights, extra=()):
+        follows=follows,
+    )
+
+
+def feed_back(kernel, layer, place, arrays, rows, weights, extra=(), follows=()):
     outs = [((rows, D), FL), ((rows, D), BF), ((rows, 3 * D), BF), ((rows, 3 * D), BF)]
     outs.append(((8, D), FL))
-    return whole(8, kernel, [place], arrays, [(w, layer) for w in weights], outs, extra)
+    return whole(
+        8, kernel, [place], arrays, [(w, layer) for w in weights], outs, extra, follows=follows
+    )
+
+
+def first_lanes(arrays, rows, lanes):
+    return tuple(Part(array, (rows, lanes)) for array in arrays)
 
 
 def per_device(
@@ -1454,15 +1538,16 @@
     core = core_index == 1
     depth = lax.axis_index("dp") % 2 == 1
     place = jnp.stack([device // 2, core_index])
-    ends = jnp.cumsum(doc_lengths[0]).astype(jnp.int32)
+    cores = [[core + chip for chip in range(0, seq_count, 2)] for core in range(2)]
+    document = jnp.arange(DOCS)
+    ends = jnp.sum(jnp.where(document[None] <= document[:, None], doc_lengths, 0), axis=1)
     info = jnp.concatenate([(device * rows)[None], ends]).astype(jnp.int32)
     pooled_info = jnp.concatenate([(device * pooled_rows)[None], ends]).astype(jnp.int32)
     order = jnp.arange(seq_count, dtype=jnp.int32)
     if usual:
         order = order ^ device
     order = jnp.concatenate([order, device[None]])
-    near_table = embedding(WIN, QBLK)
-    far_table = embedding(seq_count * pooled_rows - 1, (seq_count + 1) * pooled_rows)
+    frequency = jnp.power(10000.0, -2.0 * jnp.arange(D // 2, dtype=FL) / D)[None]
 
     def swapped(array):
         return (array, crossed(array, "seq", 1)) if usual else array
@@ -1471,14 +1556,16 @@
         return (own, crossed(other, "seq", 1)) if usual else (own, other)
 
     border0 = passed_along(inputs[rows - WIN :], "seq", 1)
-    *heads0, table0, normed0 = window_project(0, inputs, vectors, near_table, w_in, True)
+    *heads0, table0, normed0, near_table = window_project(
+        0, inputs, vectors, frequency, w_in, True
+    )
     mixed0, edge_normed0, border0, weights0 = window_attention(
         0, True, info, heads0, border0, vectors, w_in, table0
     )
-    middle0, slope0, pack0, full0, squares0 = window_feed(
+    middle0, slope0, pack0, full0, squares0, edge = window_feed(
         0, mixed0, inputs, vectors, ff_weights, FL
     )
-    edge = passed_along(full0[rows - 2 :].astype(BF), "seq", 1)
+    edge = passed_along(edge, "seq", 1)
     x0, n0 = swapped(pack0), swapped(jnp.concatenate([edge_normed0, normed0], axis=0))
 
     one = ((pooled_rows, D), BF)
@@ -1492,23 +1579,22 @@
         [one, ((pooled_rows, D), FL), ((pooled_rows, 3 * D), BF)],
         [((D // LANES, rows + 8, LANES), FL)],
     )
+    far_shape = (((seq_count + 1) * pooled_rows, D), BF)
     if usual:
         normed1_all = gather_pooled(normed1)
     else:
         normed1_all = lax.all_gather(normed1, "seq", axis=0, tiled=True)
-    content1, position1, table1 = whole(
+    content1, position1, table1, far_table = whole(
         4,
         pooled_project_kernel,
         [],
-        [normed1, vectors, far_table],
+        [normed1, vectors, frequency],
         [(w_in, 1)],
-        [one, one, (far_table.shape, BF)],
+        [one, one, far_shape, far_shape],
     )
     mixed1, keys1, values1, weights1 = pooled_attention(
         pooled_info, order, content1, position1, normed1_all, w_in, table1
     )
-    if usual:
-        (mixed1,), x0, n0 = together((mixed1,), x0, n0)
     middle1, slope1, pack1, normed2, inputs2, squares1 = whole(
         7,
         pooled_feed_kernel,
@@ -1524,6 +1610,7 @@
             ((1, D), FL),
         ],
         [spread],
+        follows=(x0[1], n0[1]) if usual else (),
     )
 
     border2 = passed_along(normed2[rows - WIN :], "seq", 1)
@@ -1532,10 +1619,8 @@
         2, False, info, heads2, border2, vectors, w_in, table2
     )
     x1, n2 = swapped(pack1), swapped(jnp.concatenate([edge_normed2, normed2], axis=0))
-    if usual:
-        (mixed2,), x1, n2 = together((mixed2,), x1, n2)
-    middle2, slope2, pack2, output, squares2 = window_feed(
-        2, mixed2, inputs2, vectors, ff_weights, BF
+    middle2, slope2, pack2, output, squares2, _ = window_feed(
+        2, mixed2, inputs2, vectors, ff_weights, BF, x1[1:] if usual else ()
     )
 
     share = D // seq_count
@@ -1548,7 +1633,7 @@
         (share, 3 * D),
     ]
 
-    every = {"near": (near_table,), "far": (far_table,)}
+    every = {}
 
     def feed_pieces(x, dy, layer):
         pieces = [
@@ -1575,25 +1660,21 @@
     feed0 = feed_pieces("x0", "a0", 0)
     project0 = [window_piece("n0", "b0", "near")], project_targets(0)
 
-    def gradients(names, follows, *parts):
+    def gradients(names, follows, *parts, natural=False):
         if not usual:
             return ()
         pieces = sum((part[0] for part in parts), [])
         sources = {name: every[name] for name in names}
-        first = names[0]
-        sources[first], _ = together(sources[first], follows)
-        return tuple(pair_gradients(7, place, sources, pieces))
+        return tuple(pair_gradients(7, place, sources, pieces, follows, natural))
 
     def step(function, values, *options):
         return tuple(function(*values, *options)) if usual else ()
 
     back_weights = [w_contract, w_expand, w_out]
     x2 = swapped(pack2)
+    every["near"], every["far"] = (near_table,), (far_table,)
     every["x0"], every["x1"], every["x2"] = x0, x1, x2
     every["n0"], every["n1"], every["n2"] = n0, (normed1_all,), n2
-
-    def swapped_pack(pack):
-        return (pack, crossed(pack[1], "seq", 1)) if usual else pack
 
     middle_grad2, mixed_grad2, own_a2, other_a2, small_a2 = feed_back(
         partial(feed_backward_kernel, 2),
@@ -1604,21 +1685,19 @@
         back_weights,
     )
     every["a2"] = swapped_halves(own_a2, other_a2)
-    if usual:
-        (mixed_grad2,), every["x2"] = together((mixed_grad2,), x2)
-    bias2, leaving2, grads2 = window_attention_back(
-        2, place, heads2, border2, w_in, table2, weights2, mixed_grad2
+    bias2, leaving2, *grads2 = window_attention_back(
+        2, place, heads2, border2, w_in, table2, weights2, mixed_grad2, (x2[1], n2[1]) if usual else ()
     )
     returned2 = passed_along(leaving2, "seq", -1)
-    every["b2"] = swapped_pack(grads2)
-    group2a = gradients(("a2", "x2", "b2", "n2", "near"), (bias2,), feed2, project2)
-    (returned2,), group2a = together((returned2,), group2a)
-    group2a = step(first_step, group2a)
+    every["b2"] = swapped_halves(*grads2)
+    sent2 = gradients(
+        ("a2", "x2", "b2", "n2", "near"), (bias2,), feed2, project2, natural=True
+    )
     joined, short_grad, own_u2, other_u2, small_b2 = whole(
         6,
         last_project_backward_kernel,
         [place],
-        [Part(grads2, (2, REACH, 3 * D // 2)), returned2, inputs2, middle_grad2, vectors],
+        [first_lanes(grads2, REACH, 3 * D // 2), returned2, inputs2, middle_grad2, vectors],
         [(w_in, 2), (upsample_weight, None)],
         [
             ((rows, D), FL),
@@ -1628,6 +1707,7 @@
             ((8, D), FL),
         ],
         [spread],
+        follows=sent2[:1],
     )
     every["u2"] = swapped_halves(own_u2, other_u2)
 
@@ -1640,21 +1720,25 @@
         back_weights,
     )
     every["a1"] = swapped_halves(own_a1, other_a1)
-    (mixed_grad1,), group2a = together((mixed_grad1,), group2a)
-    group2a = step(first_sums, (group2a,))
-    (mixed_grad1,), group2a = together((mixed_grad1,), group2a)
-    group2a = step(second_step, group2a)
+    if usual:
+        share2 = sent2[0].reshape(4 * LANES, -1)
+        share2 = lax.psum_scatter(
+            share2, "seq", scatter_dimension=0, tiled=True, axis_index_groups=cores
+        )
+        follows0 = (share2,)
+        share2 = lax.psum(share2, "dp")
+    else:
+        follows0 = ()
     heads1 = (content1, position1, keys1, values1)
-    bias1, even, odd, grads1 = pooled_attention_back(
-        order, place, heads1, w_in, table1, weights1, mixed_grad1
-    )
-    every["b1"] = swapped_pack(grads1)
+    bias1, even, odd, *grads1 = pooled_attention_back(
+        order, place, heads1, w_in, table1, weights1, mixed_grad1, ()
+    )
+    every["b1"] = swapped_halves(*grads1)
 
     def group1_gradients(total):
         return gradients(("a1", "x1", "u2"), (total,), up, feed1)
 
     if usual:
-        (even, odd), group2a = together((even, odd), group2a)
         normed_grad1, group1 = scatter_pooled(even, odd, group1_gradients)
     else:
         group1 = ()
@@ -1662,25 +1746,29 @@
         summed = jnp.concatenate([even.reshape(split), odd.reshape(split)], axis=1)
         summed = summed.reshape(seq_count * LANES, D)
         normed_grad1 = lax.psum_scatter(summed, "seq", scatter_dimension=0, tiled=True).astype(FL)
-    (normed_grad1,), group1, group2a = together((normed_grad1,), group1, group2a)
+    (normed_grad1,), group1 = together((normed_grad1,), group1)
     group1 = step(first_step, group1)
-    group2a = step(second_sums, group2a)
-    group2a = step(depth_halves, group2a, depth)
-    shifted_grad, own_p1, other_p1, small_b1 = whole(
+    shifted_grad, first_rows, own_p1, other_p1, small_b1 = whole(
         5,
         pooled_project_backward_kernel,
         [info, place],
-        [Part(grads1, (2, LANES, D // 2)), normed_grad1, inputs1, middle_grad1, vectors],
+        [first_lanes(grads1, LANES, D // 2), normed_grad1, inputs1, middle_grad1, vectors],
         [(w_in, 1), (pool_weight, None)],
-        [((rows, D), FL), ((pooled_rows, D // 2), BF), ((pooled_rows, D // 2), BF), ((8, D), FL)],
+        [
+            ((rows, D), FL),
+            ((EDGE, D), FL),
+            ((pooled_rows, D // 2), BF),
+            ((pooled_rows, D // 2), BF),
+            ((8, D), FL),
+        ],
         [spread],
+        follows=follows0,
     )
     every["p1"] = swapped_halves(own_p1, other_p1)
-    came_back = passed_along(shifted_grad[:2], "seq", -1)
-    group1b = gradients(("p1", "x1", "b1", "n1", "far"), (shifted_grad,), pool, project1)
-    (came_back,), group1b, group2a = together((came_back,), group1b, group2a)
+    came_back = passed_along(first_rows, "seq", -1)
+    group1b = gradients(("p1", "x1", "b1", "n1", "far"), (small_b1,), pool, project1)
+    (came_back,), group1b = together((came_back,), group1b)
     group1b = step(first_step, group1b)
-    group2a = step(depth_quarters, group2a)
     middle_grad0, mixed_grad0, own_a0, other_a0, small_a0 = feed_back(
         first_feed_backward_kernel,
         0,
@@ -1695,32 +1783,31 @@
     group1 = step(first_sums, (group1, group1b))
     (mixed_grad0,), group1 = together((mixed_grad0,), group1)
     group1 = step(second_step, group1)
-    bias0, leaving0, grads0 = window_attention_back(
+    bias0, leaving0, *grads0 = window_attention_back(
         0, place, heads0, border0, w_in, table0, weights0, mixed_grad0
     )
-    every["b0"] = swapped_pack(grads0)
+    every["b0"] = swapped_halves(*grads0)
     returned0 = passed_along(leaving0, "seq", -1)
 
-    clock = (bias0,)
+    follows = ()
     if usual:
-        clock, group1, group2a = together(clock, group1, group2a)
+        group0 = gradients(("a0", "x0"), (bias0,), feed0)
+        last = gradients(("b0", "n0", "near"), group0[:1], project0)
+        last_sent = last[0]
+        group0 = step(first_step, group0)
+        last = step(first_step, last)
         group1 = step(second_sums, group1)
         group1 = step(depth_halves, group1, depth)
-        group2a = step(depth_back, group2a)
-        group0 = gradients(("a0", "x0"), clock, feed0)
-        clock, group0 = together(clock, group0)
-        group0 = step(first_step, group0)
-        last = gradients(("b0", "n0", "near"), clock, project0)
-        clock, last = together(clock, last)
-        last = step(first_step, last)
-    (returned0,), clock = together((returned0,), clock)
+        group1 = step(depth_quarters, group1)
+        follows = (last_sent, share2, group1[0])
     tokens_grad, small_b0 = whole(
         5,
         first_project_backward_kernel,
         [place],
-        [Part(grads0, (2, REACH, 3 * D // 2)), returned0, inputs, middle_grad0, vectors],
+        [first_lanes(grads0, REACH, 3 * D // 2), returned0, inputs, middle_grad0, vectors],
         [(w_in, 0)],
         [((rows, D), BF), ((8, D), FL)],
+        follows=follows,
     )
     small = jnp.concatenate(
         [
@@ -1740,8 +1827,7 @@
         axis=0,
     )
     if usual:
-        clock, (small,), group1 = together(clock, (small,), group1)
-        group1 = step(depth_quarters, group1)
+        clock = (small_b0,)
         small = small + crossed(small, "seq", 1)
         clock, (small,), group0 = together(clock, (small,), group0)
         group0 = step(first_sums, (group0,))
@@ -1770,8 +1856,9 @@
         small = small + crossed(small, "dp", 2)
         plan = [feed2[1] + project2[1], up[1] + feed1[1] + pool[1] + project1[1]]
         plan += [feed0[1], project0[1]]
-        buffers = [shared(*group, depth, core) for group in (group2a, group1, group0, last)]
-        sums = final_outputs(plan, buffers, shapes)
+        shares = [share2] + [depth_share(*group, depth) for group in (group1, group0, last)]
+        buffers = [core_rows(share, core) for share in shares]
+        sums = final_outputs(place, plan, buffers, shapes)
     else:
         small = summed_everywhere(small)
         sums = plain_sums(
@@ -1833,7 +1920,7 @@
 
     into, out, expand, contract = [], [], [], []
     for layer in range(3):
-        x, a, b = packs[layer], a_pairs[layer], (grads[layer][0], grads[layer][1])
+        x, a, b = packs[layer], a_pairs[layer], grads[layer]
         table, near, every = tables[layer % 2], normed[layer], normed_all[layer]
         own = x.shape[0]
         near = near[near.shape[0] - own :]

time: 419 us -> 409 us (0.976)
  waiting for transfers between devices: 97.2 us -> 78.5 us
  between operations: 2.48 us -> 15.9 us
  other arithmetic: 25.1 us -> 17.2 us
    ppermute x65 -> x58, waiting for transfers between devices: 96.3 us -> 76.1 us  [crossed(): lax.ppermute(block, axis, [(index, index ^ bit) for index in range(count)])]
    unnamed x110 -> x140, local copies, waits for them, and re-layouts: 8.95 us -> 19.2 us
    pallas_call x12 -> x11, Pallas kernels: 113 us -> 107 us  [the longest x6 77.6 us: attention_call(): pl.pallas_call(run, grid=(HEADS // 2,), in_specs=[SMEM] * len(scalars) +...]
    squeeze x3 -> x0, local copies, waits for them, and re-layouts: 4.89 us -> none  [swapped_pack(): return (pack, crossed(pack[1], 'seq', 1)) if usual else pack]
    pallas_call x13 -> x14, Pallas kernels: 82.9 us -> 87.3 us  [whole(): pl.pallas_call(run, in_specs=[SMEM] * scalar_count + [HBM] * (flat_count...]
    convert_element_type x19 -> x14, other arithmetic: 8.97 us -> 6.29 us  [rounded_sum(): sum((term.astype(jnp.float32) for term in terms)).astype(jnp.bfloat16)]
    ppermute x65 -> x58, starting transfers between devices: 54.4 us -> 56.2 us  [crossed(): lax.ppermute(block, axis, [(index, index ^ bit) for index in range(count)])]
  transfers between devices with their start and end apart: 71 -> 66, of which waited for: 28 -> 21; matrix products, arithmetic and copies ran while one was open for 8% -> 6% of each run, Pallas kernels for 35% -> 34%
where the time goes in v3:
time: 409 us; the launch traced here: 402 us
  Pallas kernels  194 us (47%)
  waiting for transfers between devices  78.5 us (19%)
  starting transfers between devices  69.5 us (17%)
  local copies, waits for them, and re-layouts  27.4 us (7%)
  other arithmetic  17.2 us (4%)
  between operations  15.9 us (4%)
    pallas_call x14, Pallas kernels, whole(): pl.pallas_call(run, in_specs=[SMEM] * scalar_count + [HBM] * (flat_count...  87.3 us
    pallas_call x6, Pallas kernels, attention_call(): pl.pallas_call(run, grid=(HEADS // 2,), in_specs=[SMEM] * len(scalars) +...  77.6 us
    ppermute x58, waiting for transfers between devices, crossed(): lax.ppermute(block, axis, [(index, index ^ bit) for index in range(count)])  76.1 us
    ppermute x58, starting transfers between devices, crossed(): lax.ppermute(block, axis, [(index, index ^ bit) for index in range(count)])  56.2 us
    pallas_call x5, Pallas kernels, pair_gradients(): pl.pallas_call(kernel, in_specs=[SMEM] + [ANY] * count + [HBM] * len(foll...  29 us
    unnamed x140, local copies, waits for them, and re-layouts  19.2 us
    ppermute x6, starting transfers between devices, passed_along(): return lax.ppermute(block, axis, route)  13.2 us
  transfers between devices with their start and end apart: 66, of which 21 were waited for; matrix products, arithmetic and copies ran while one was open for 6% of the time, Pallas kernels for 34%

profile of v3, /device:TPU:0, one launch (start us, length us, event | category | flops | bytes accessed | tf_op | source)
XLA Modules:
  0.0 402.5 jit_solution(6046762935139465709)
XLA Ops:
  8.2 2.4 collective-permute-start
  14.6 4.2 %shard_map.288 = (bf16[384,512]{1,0:T(8,128)(2,1)}, bf16[384,512]{1,0:T(8,128)(2,1)}, bf16[384,512]{1,0:T(8,128)(2,1)}, bf16[384,512]{1,0:T(8,128)(2,1)}, bf16[3...) custom-call(bf16[384,512]{1,0:T(8,128)(2,1)} %bitcast.97, bf16[3,2,512]{2,1,0:T(2,128)(2,1)} %refs_6_.21, ...), custom_call_target="tpu_custom_call" | custom-call | flops 4000000000 | bytes 12000000 | tf_op jit(solution)/shard_map/pallas_call | solution.py:1037
  19.5 10.7 %shard_map.289 = (bf16[384,512]{1,0:T(8,128)(2,1)}, bf16[256,512]{1,0:T(8,128)(2,1)}, bf16[2,256,512]{2,1,0:T(8,128)(2,1)}, bf16[8,3,128,384]{3,2,1,0:T(8,128)(2,1)}) custom-call(s32[9]{0:T(128)S(1)} %get-tuple-element.414.refs_0_, bf16[384,512]{1,0:T(8,128)(2,1)} %get-tuple-element.184.refs_1_, bf16[384,512]{1,0:T(8,128)(2,1)} %get-tuple-element.185.refs_2_, ...), custom_call_target="tpu_custom_call" | custom-call | flops 11000000512 | bytes 33000000 | tf_op jit(solution)/shard_map/pallas_call | solution.py:489
  31.3 7.1 %shard_map.290 = (f32[384,512]{1,0:T(8,128)}, bf16[384,2048]{1,0:T(8,128)(2,1)}, bf16[384,3072]{1,0:T(8,128)(2,1)}, f32[384,512]{1,0:T(8,128)}, f32[1,512]{1,0:T(1,128)}, /*index=5*/bf16[16,512]{1,0:T(8,128)(2,1)}) custom-call(bf16[384,512]{1,0:T(8,128)(2,1)} %get-tuple-element.189.refs_0_, bf16[384,512]{1,0:T(8,128)(2,1)} %bitcast.98, ...), custom_call_target="tpu_custom_call" | custom-call | flops 7000000000 | bytes 21000000 | tf_op jit(solution)/shard_map/pallas_call | solution.py:1037
  38.3 4.7 %collective-permute-start.1 = (bf16[16,512]{1,0:T(8,128)(2,1)}, bf16[16,512]{1,0:T(8,128)(2,1)S(1)}, u32[]{:S(2)}, u32[]{:S(2)}) collective-permute-start(bf16[16,512]{1,0:T(8,128)(2,1)} %get-tuple-element.191), channel_id=1, source_target_pairs={{0,1},{1,2},{2,3},{3,4},{4,5},{5,6},{6,7},{8,9},{9,10},{10,11},{11... | collective-permute-start | bytes 49160 | tf_op jit(solution)/shard_map/ppermute | solution.py:1061
  44.5 4.3 %shard_map.291 = (bf16[128,512]{1,0:T(8,128)(2,1)}, f32[128,512]{1,0:T(8,128)}, bf16[128,1536]{1,0:T(8,128)(2,1)}) custom-call(s32[9]{0:T(128)S(1)} %get-tuple-element.414.refs_0_, f32[384,512]{1,0:T(8,128)} %get-tuple-element.190.refs_1_.refs_3_, bf16[16,512]{1,0:T(8,128)(2,1)} %copy-done.61, bf16[3,2,512]{2,1,0:T(2,128)(2,1)} %refs_6_.21, ...), custom_call_target="tpu_custom_call" | custom-call | flops 4000000000 | bytes 12000000 | tf_op jit(solution)/shard_map/pallas_call | solution.py:1037
  48.8 3.2 collective-permute-start.5
  52.6 4.3 %shard_map.292 = (bf16[128,512]{1,0:T(8,128)(2,1)}, bf16[128,512]{1,0:T(8,128)(2,1)}, bf16[1152,512]{1,0:T(8,128)(2,1)}, bf16[1152,512]{1,0:T(8,128)(2,1)}) custom-call(bf16[128,512]{1,0:T(8,128)(2,1)} %get-tuple-element.192.refs_0_, bf16[3,2,512]{2,1,0:T(2,128)(2,1)} %refs_6_.21, bf16[3,2,512]{2,1,0:T(2,128)(2,1)} %refs_7_.19, bf16[3,2,512]{2,1,0:T(2,128)(2,1)} %refs_8_.13, ...), custom_call_target="tpu_custom_call" | custom-call | flops 4000000000 | bytes 12000000 | tf_op jit(solution)/shard_map/pallas_call | solution.py:1037
  58.9 2.7 collective-permute-done.8
  65.2 12.8 %shard_map.293 = (bf16[128,512]{1,0:T(8,128)(2,1)}, bf16[1024,512]{1,0:T(8,128)(2,1)}, bf16[1024,512]{1,0:T(8,128)(2,1)}, bf16[8,128,1024]{2,1,0:T(8,128)(2,1)}) custom-call(s32[9]{0:T(128)S(1)} %get-tuple-element.413.refs_0_, s32[9]{0:T(128)S(1)} %pad_add_fusion.2.refs_1_.refs_0_, bf16[128,512]{1,0:T(8,128)(2,1)} %get-tuple-element.193.refs_2_, ...), custom_call_target="tpu_custom_call" | custom-call | flops 12999999488 | bytes 39000000 | tf_op jit(solution)/shard_map/pallas_call | solution.py:489
  79.7 6.8 %shard_map.294 = (f32[128,512]{1,0:T(8,128)}, bf16[128,2048]{1,0:T(8,128)(2,1)}, bf16[128,5120]{1,0:T(8,128)(2,1)}, bf16[384,512]{1,0:T(8,128)(2,1)}, f32[384,512]{1,0:T(8,128)}, /*index=5*/f32[1,512]{1,0:T(1,128)}) custom-call(bf16[128,512]{1,0:T(8,128)(2,1)} %get-tuple-element.196.refs_0_, f32[128,512]{1,0:T(8,128)} %get-tuple-element.197.refs_1_.refs_5_, ...), custom_call_target="tpu_custom_call" | custom-call | flops 7000000000 | bytes 21000000 | tf_op jit(solution)/shard_map/pallas_call | solution.py:1037
  90.5 4.3 %shard_map.295 = (bf16[384,512]{1,0:T(8,128)(2,1)}, bf16[384,512]{1,0:T(8,128)(2,1)}, bf16[384,512]{1,0:T(8,128)(2,1)}, bf16[384,512]{1,0:T(8,128)(2,1)}, bf16[384,512]{1,0:T(8,128)(2,1)}) custom-call(bf16[384,512]{1,0:T(8,128)(2,1)} %get-tuple-element.202.refs_0_, bf16[3,2,512]{2,1,0:T(2,128)(2,1)} %refs_6_.21, bf16[3,2,512]{2,1,0:T(2,128)(2,1)} %refs_7_.19, ...), custom_call_target="tpu_custom_call" | custom-call | flops 4000000000 | bytes 12000000 | tf_op jit(solution)/shard_map/pallas_call | solution.py:1037
  95.5 10.5 %shard_map.296 = (bf16[384,512]{1,0:T(8,128)(2,1)}, bf16[256,512]{1,0:T(8,128)(2,1)}, bf16[2,256,512]{2,1,0:T(8,128)(2,1)}, bf16[8,3,128,384]{3,2,1,0:T(8,128)(2,1)}) custom-call(s32[9]{0:T(128)S(1)} %get-tuple-element.414.refs_0_, bf16[384,512]{1,0:T(8,128)(2,1)} %get-tuple-element.204.refs_1_, bf16[384,512]{1,0:T(8,128)(2,1)} %get-tuple-element.205.refs_2_, ...), custom_call_target="tpu_custom_call" | custom-call | flops 11000000512 | bytes 33000000 | tf_op jit(solution)/shard_map/pallas_call | solution.py:489
  107.1 7.0 %shard_map.297 = (f32[384,512]{1,0:T(8,128)}, bf16[384,2048]{1,0:T(8,128)(2,1)}, bf16[384,3072]{1,0:T(8,128)(2,1)}, bf16[384,512]{1,0:T(8,128)(2,1)}, f32[1,512]{1,0:T(1,128)}, /*index=5*/bf16[16,512]{1,0:T(8,128)(2,1)}) custom-call(bf16[384,512]{1,0:T(8,128)(2,1)} %get-tuple-element.209.refs_0_, f32[384,512]{1,0:T(8,128)} %get-tuple-element.210.refs_1_.refs_4_, ...), custom_call_target="tpu_custom_call" | custom-call | flops 7000000000 | bytes 21000000 | tf_op jit(solution)/shard_map/pallas_call | solution.py:1037
  115.0 9.3 %shard_map.298 = (f32[384,512]{1,0:T(8,128)}, bf16[384,512]{1,0:T(8,128)(2,1)}, bf16[384,1536]{1,0:T(8,128)(2,1)}, bf16[384,1536]{1,0:T(8,128)(2,1)}, f32[8,512]{1,0:T(8,128)}) custom-call(s32[2]{0:T(128)S(1)} %pad_add_fusion.3.refs_0_.place.refs_1_, bf16[384,512]{1,0:T(8,128)(2,1)} %bitcast.144, bf16[384,2048]{1,0:T(8,128)(2,1)} %get-tuple-element.217.refs_2_, ...), custom_call_target="tpu_custom_call" | custom-call | flops 8000000000 | bytes 24000000 | tf_op jit(solution)/shard_map/pallas_call | solution.py:1037
  125.1 14.1 %shard_map.299 = (f32[2,512]{1,0:T(2,128)}, bf16[256,512]{1,0:T(8,128)(2,1)}, bf16[640,1024]{1,0:T(8,128)(2,1)}, bf16[640,1024]{1,0:T(8,128)(2,1)}) custom-call(s32[2]{0:T(128)S(1)} %pad_add_fusion.3.refs_0_.place.refs_1_, bf16[384,512]{1,0:T(8,128)(2,1)} %get-tuple-element.204.refs_1_, bf16[384,512]{1,0:T(8,128)(2,1)} %get-tuple-element.205.refs_2_, ...), custom_call_target="tpu_custom_call" | custom-call | flops 12999999488 | bytes 39000000 | tf_op jit(solution)/shard_map/pallas_call | solution.py:489
  139.8 4.2 %collective-permute-done.17.refs_1_ = bf16[384,1536]{1,0:T(8,128)(2,1)S(1)} collective-permute-done((bf16[384,1536]{1,0:T(8,128)(2,1)S(1)}, bf16[384,1536]{1,0:T(8,128)(2,1)S(1)}, u32[]{:S(2)}, u32[]{:S(2)}) %collective-permute-start.17) | collective-permute-done | bytes 1179680 | tf_op jit(solution)/shard_map/ppermute | solution.py:1055
  146.4 7.9 %shard_map.300.refs_15_ = bf16[4,128,3328]{2,1,0:T(8,128)(2,1)} custom-call(s32[2]{0:T(128)S(1)} %pad_add_fusion.3.refs_0_.place.refs_1_, bf16[384,1536]{1,0:T(8,128)(2,1)S(1)} %copy-done.18, bf16[384,1536]{1,0:T(8,128)(2,1)S(1)} %collective-permute-done.17.refs_1_, bf16[384,3072]{1,0:T(8,128)(2,1)S(1)} %copy-done.5, ...), custom_call_target="tpu_custom_call" | custom-call | flops 7000000000 | bytes 21000000 | tf_op jit(solution)/shard_map/pallas_call | solution.py:1264
  159.3 7.3 %shard_map.301 = (f32[384,512]{1,0:T(8,128)}, f32[128,512]{1,0:T(8,128)}, bf16[384,256]{1,0:T(8,128)(2,1)}, bf16[384,256]{1,0:T(8,128)(2,1)}, f32[8,512]{1,0:T(8,128)}) custom-call(s32[2]{0:T(128)S(1)} %pad_add_fusion.3.refs_0_.place.refs_1_, bf16[640,1024]{1,0:T(8,128)(2,1)} %get-tuple-element.222.refs_4_.refs_1_, ...), custom_call_target="tpu_custom_call" | custom-call | flops 6000000000 | bytes 18000000 | tf_op jit(solution)/shard_map/pallas_call | solution.py:1037
  166.6 7.1 %shard_map.302 = (f32[128,512]{1,0:T(8,128)}, bf16[128,512]{1,0:T(8,128)(2,1)}, bf16[128,1536]{1,0:T(8,128)(2,1)}, bf16[128,1536]{1,0:T(8,128)(2,1)}, f32[8,512]{1,0:T(8,128)}) custom-call(s32[2]{0:T(128)S(1)} %pad_add_fusion.3.refs_0_.place.refs_1_, f32[128,512]{1,0:T(8,128)} %get-tuple-element.233.refs_1_, bf16[128,2048]{1,0:T(8,128)(2,1)} %get-tuple-element.234.refs_2_, ...), custom_call_target="tpu_custom_call" | custom-call | flops 8000000000 | bytes 24000000 | tf_op jit(solution)/shard_map/pallas_call | solution.py:1037
  173.7 15.5 %shard_map.303 = (f32[2,512]{1,0:T(2,128)}, bf16[512,512]{1,0:T(8,128)(2,1)}, bf16[512,512]{1,0:T(8,128)(2,1)}, bf16[1152,1024]{1,0:T(8,128)(2,1)}, bf16[1152,1024]{1,0:T(8,128)(2,1)}) custom-call(s32[9]{0:T(128)S(1)} %pad_add_fusion.2.refs_1_.refs_0_, s32[2]{0:T(128)S(1)} %pad_add_fusion.3.refs_0_.place.refs_1_, ...), custom_call_target="tpu_custom_call" | custom-call | flops 12999999488 | bytes 39000000 | tf_op jit(solution)/shard_map/pallas_call | solution.py:489
  189.3 3.9 collective-permute-start.19
  196.3 3.0 collective-permute-start.20
  199.3 5.1 %shard_map.304 = (bf16[2,128,1536]{2,1,0:T(8,128)(2,1)}, bf16[2,128,1536]{2,1,0:T(8,128)(2,1)}, bf16[2,128,1536]{2,1,0:T(8,128)(2,1)}, bf16[2,128,1536]{2,1,0:T(8,128)(2,1)}) custom-call(s32[2]{0:T(128)S(1)} %pad_add_fusion.3.refs_0_.place.refs_1_, bf16[128,1536]{1,0:T(8,128)(2,1)S(1)} %copy-done.23, bf16[128,1536]{1,0:T(8,128)(2,1)S(1)} %collective-permute-done.22.refs_1_, ...), custom_call_target="tpu_custom_call" | custom-call | flops 7000000000 | bytes 21000000 | tf_op jit(solution)/shard_map/pallas_call | solution.py:1264
  207.5 2.5 collective-permute-done.24
  213.3 5.2 %shard_map.305 = (f32[384,512]{1,0:T(8,128)}, f32[16,512]{1,0:T(8,128)}, bf16[128,256]{1,0:T(8,128)(2,1)}, bf16[128,256]{1,0:T(8,128)(2,1)}, f32[8,512]{1,0:T(8,128)}) custom-call(s32[9]{0:T(128)S(1)} %get-tuple-element.414.refs_0_, s32[2]{0:T(128)S(1)} %pad_add_fusion.3.refs_0_.place.refs_1_, bf16[1152,1024]{1,0:T(8,128)(2,1)} %get-tuple-element.237.refs_2_.refs_4_, ...), custom_call_target="tpu_custom_call" | custom-call | flops 5000000000 | bytes 15000000 | tf_op jit(solution)/shard_map/pallas_call | solution.py:1037
  227.3 6.1 %shard_map.306 = (bf16[2,128,896]{2,1,0:T(8,128)(2,1)}, bf16[2,128,896]{2,1,0:T(8,128)(2,1)}, bf16[2,128,896]{2,1,0:T(8,128)(2,1)}, bf16[2,128,896]{2,1,0:T(8,128)(2,1)}) custom-call(s32[2]{0:T(128)S(1)} %pad_add_fusion.3.refs_0_.place.refs_1_, bf16[128,256]{1,0:T(8,128)(2,1)S(1)} %copy-done.22, bf16[128,256]{1,0:T(8,128)(2,1)S(1)} %collective-permute-done.27.refs_1_, ...), custom_call_target="tpu_custom_call" | custom-call | flops 7000000000 | bytes 21000000 | tf_op jit(solution)/shard_map/pallas_call | solution.py:1264
  233.4 5.5 %collective-permute-start.31 = (bf16[2,128,896]{2,1,0:T(8,128)(2,1)}, bf16[2,128,896]{2,1,0:T(8,128)(2,1)S(1)}, u32[]{:S(2)}, u32[]{:S(2)}) collective-permute-start(bf16[2,128,896]{2,1,0:T(8,128)(2,1)} %get-tuple-element.272), channel_id=1, source_target_pairs={{0,2},{1,3},{2,0},{3,1},{4,6},{5,7},{6,4},{7,5},{8,10},{9,11},{10,... | collective-permute-start | bytes 1376264 | tf_op jit(solution)/shard_map/ppermute | solution.py:1055
  239.2 9.3 %shard_map.307 = (f32[384,512]{1,0:T(8,128)}, bf16[384,512]{1,0:T(8,128)(2,1)}, bf16[384,1536]{1,0:T(8,128)(2,1)}, bf16[384,1536]{1,0:T(8,128)(2,1)}, f32[8,512]{1,0:T(8,128)}) custom-call(s32[2]{0:T(128)S(1)} %pad_add_fusion.3.refs_0_.place.refs_1_, f32[384,512]{1,0:T(8,128)} %get-tuple-element.229.refs_1_, f32[384,512]{1,0:T(8,128)} %get-tuple-element.253.refs_2_, ...), custom_call_target="tpu_custom_call" | custom-call | flops 8000000000 | bytes 24000000 | tf_op jit(solution)/shard_map/pallas_call | solution.py:1037
  249.8 2.6 collective-permute-done.32
  257.1 14.0 %shard_map.308 = (f32[2,512]{1,0:T(2,128)}, bf16[256,512]{1,0:T(8,128)(2,1)}, bf16[640,1024]{1,0:T(8,128)(2,1)}, bf16[640,1024]{1,0:T(8,128)(2,1)}) custom-call(s32[2]{0:T(128)S(1)} %pad_add_fusion.3.refs_0_.place.refs_1_, bf16[384,512]{1,0:T(8,128)(2,1)} %get-tuple-element.184.refs_1_, bf16[384,512]{1,0:T(8,128)(2,1)} %get-tuple-element.185.refs_2_, ...), custom_call_target="tpu_custom_call" | custom-call | flops 12999999488 | bytes 39000000 | tf_op jit(solution)/shard_map/pallas_call | solution.py:489
  275.6 5.8 %shard_map.309 = (bf16[2,128,1152]{2,1,0:T(8,128)(2,1)}, bf16[2,128,1152]{2,1,0:T(8,128)(2,1)}, bf16[2,128,1152]{2,1,0:T(8,128)(2,1)}, bf16[2,128,1152]{2,1,0:T(8,128)(2,1)}) custom-call(s32[2]{0:T(128)S(1)} %pad_add_fusion.3.refs_0_.place.refs_1_, bf16[384,1536]{1,0:T(8,128)(2,1)S(1)} %copy-done.19, bf16[384,1536]{1,0:T(8,128)(2,1)S(1)} %collective-permute-done.35.refs_1_, ...), custom_call_target="tpu_custom_call" | custom-call | flops 7000000000 | bytes 21000000 | tf_op jit(solution)/shard_map/pallas_call | solution.py:1264
  282.6 2.4 collective-permute-start.41
  285.0 5.0 %collective-permute-done.38 = bf16[128,2432]{1,0:T(8,128)(2,1)S(1)} collective-permute-done((bf16[128,2432]{1,0:T(8,128)(2,1)S(1)}, bf16[128,2432]{1,0:T(8,128)(2,1)S(1)}, u32[]{:S(2)}, u32[]{:S(2)}) %collective-permute-start.38) | collective-permute-done | bytes 622624 | tf_op jit(solution)/shard_map/ppermute | solution.py:1055
  291.3 4.3 %shard_map.310 = (bf16[2,128,512]{2,1,0:T(8,128)(2,1)}, bf16[2,128,512]{2,1,0:T(8,128)(2,1)}, bf16[2,128,512]{2,1,0:T(8,128)(2,1)}, bf16[2,128,512]{2,1,0:T(8,128)(2,1)}) custom-call(s32[2]{0:T(128)S(1)} %pad_add_fusion.3.refs_0_.place.refs_1_, bf16[640,1024]{1,0:T(8,128)(2,1)S(1)} %copy-done.15, bf16[640,1024]{1,0:T(8,128)(2,1)S(1)} %collective-permute-done.34.refs_1_, ...), custom_call_target="tpu_custom_call" | custom-call | flops 7000000000 | bytes 21000000 | tf_op jit(solution)/shard_map/pallas_call | solution.py:1264
  295.7 5.7 %shard_map.311 = (bf16[384,512]{1,0:T(8,128)(2,1)}, f32[8,512]{1,0:T(8,128)}) custom-call(s32[2]{0:T(128)S(1)} %pad_add_fusion.3.refs_0_.place.refs_1_, bf16[640,1024]{1,0:T(8,128)(2,1)} %get-tuple-element.285.refs_0_.refs_1_, bf16[640,1024]{1,0:T(8,128)(2,1)} %get-tuple-element.286.refs_2_, bf16[256,512]{1,0:T(8,128)(2,1)} %collective-permute-done.33.refs_3_, ...), custom_call_target="tpu_custom_call" | custom-call | flops 5000000000 | bytes 15000000 | tf_op jit(solution)/shard_map/pallas_call | solution.py:1037
  302.7 2.4 collective-permute-start.48
  306.9 2.4 collective-permute-start.44
  309.8 5.7 %collective-permute-done.42 = f32[40,512]{1,0:T(8,128)S(1)} collective-permute-done((f32[40,512]{1,0:T(8,128)S(1)}, f32[40,512]{1,0:T(8,128)S(1)}, u32[]{:S(2)}, u32[]{:S(2)}) %collective-permute-start.42) | collective-permute-done | bytes 81952 | tf_op jit(solution)/shard_map/ppermute | solution.py:1055
  317.3 2.4 collective-permute-start.45
  320.0 4.7 %collective-permute-done.45 = f32[40,512]{1,0:T(8,128)S(1)} collective-permute-done((f32[40,512]{1,0:T(8,128)S(1)}, f32[40,512]{1,0:T(8,128)S(1)}, u32[]{:S(2)}, u32[]{:S(2)}) %collective-permute-start.45) | collective-permute-done | bytes 81952 | tf_op jit(solution)/shard_map/ppermute | solution.py:1055
  324.7 8.7 %collective-permute-done.48 = bf16[128,2432]{1,0:T(8,128)(2,1)S(1)} collective-permute-done((bf16[128,2432]{1,0:T(8,128)(2,1)S(1)}, bf16[128,2432]{1,0:T(8,128)(2,1)S(1)}, u32[]{:S(2)}, u32[]{:S(2)}) %collective-permute-start.48) | collective-permute-done | bytes 622624 | tf_op jit(solution)/shard_map/ppermute | solution.py:1055
  336.6 6.5 %collective-permute-done.50 = bf16[128,1152]{1,0:T(8,128)(2,1)S(1)} collective-permute-done((bf16[128,1152]{1,0:T(8,128)(2,1)S(1)}, bf16[128,1152]{1,0:T(8,128)(2,1)S(1)}, u32[]{:S(2)}, u32[]{:S(2)}) %collective-permute-start.50) | collective-permute-done | bytes 294944 | tf_op jit(solution)/shard_map/ppermute | solution.py:1055
  347.9 10.1 %collective-permute-done.51 = bf16[128,1152]{1,0:T(8,128)(2,1)S(1)} collective-permute-done((bf16[128,1152]{1,0:T(8,128)(2,1)S(1)}, bf16[128,1152]{1,0:T(8,128)(2,1)S(1)}, u32[]{:S(2)}, u32[]{:S(2)}) %collective-permute-start.51) | collective-permute-done | bytes 294944 | tf_op jit(solution)/shard_map/ppermute | solution.py:1055
  358.1 4.1 %collective-permute-start.59 = (bf16[128,1152]{1,0:T(8,128)(2,1)S(1)}, bf16[128,1152]{1,0:T(8,128)(2,1)S(1)}, u32[]{:S(2)}, u32[]{:S(2)}) collective-permute-start(bf16[128,1152]{1,0:T(8,128)(2,1)S(1)} %add_convert_fusion.9), channel_id=1, source_target_pairs={{0,8},{8,0},{16,24},{24,16},{1,9},{9,1},{17,25},{25,17},{2,10},{10... | collective-permute-start | bytes 884744 | tf_op jit(solution)/shard_map/ppermute | solution.py:1055
  362.2 11.7 %collective-permute-done.56 = bf16[128,512]{1,0:T(8,128)(2,1)S(1)} collective-permute-done((bf16[128,512]{1,0:T(8,128)(2,1)S(1)}, bf16[128,512]{1,0:T(8,128)(2,1)S(1)}, u32[]{:S(2)}, u32[]{:S(2)}) %collective-permute-start.56) | collective-permute-done | bytes 131104 | tf_op jit(solution)/shard_map/ppermute | solution.py:1055
  382.6 3.4 collective-permute-done.62
  389.7 5.5 %shard_map.312 = (f32[3,64,2048]{2,1,0:T(8,128)}, f32[3,64,512]{2,1,0:T(8,128)}, f32[3,64,2048]{2,1,0:T(8,128)}, f32[3,256,512]{2,1,0:T(8,128)}, f32[192,512]{1,0:T(8,128)}, /*index=5*/f32[64,1536]{1,0:T(8,128)}) custom-call(s32[2]{0:T(128)S(1)} %pad_add_fusion.3.refs_0_.place.refs_1_, bf16[64,3328]{1,0:T(8,128)(2,1)} %get-tuple-element.371.refs_1_, ...), custom_call_target="tpu_custom_call" | custom-call | flops 3000000000 | bytes 9000000 | tf_op jit(solution)/shard_map/pallas_call | solution.py:1037
  (324 shorter events, 88.4 us)
Async XLA Ops:
  7.2 206.2 %reduce-scatter.2.cloned.1.call-start = ((), (), s32[]{:S(2)}) async-start(), calls=%async_computation.1 | async-start | bytes 4259840 | tf_op jit(solution)/shard_map/reduce_scatter | solution.py:1725
  8.2 10.6 %collective-permute-start = (bf16[256,512]{1,0:T(8,128)(2,1)S(1)}, bf16[256,512]{1,0:T(8,128)(2,1)S(1)}, u32[]{:S(2)}, u32[]{:S(2)}) collective-permute-start(bf16[256,512]{1,0:T(8,128)(2,1)S(1)} %slice_bitcast_fusion), channel_id=1, source_target_pairs={{0,1},{1,2},{2,3},{3,4},{4,5},{5,6},{6,7},{8,9},{9,10},{10,11},{11... | collective-permute-start | bytes 786440 | tf_op jit(solution)/shard_map/ppermute | solution.py:1061
  43.1 34.9 %collective-permute-start.11 = (bf16[640,512]{1,0:T(8,128)(2,1)S(1)}, bf16[640,512]{1,0:T(8,128)(2,1)S(1)}, u32[]{:S(2)}, u32[]{:S(2)}) collective-permute-start(bf16[640,512]{1,0:T(8,128)(2,1)S(1)} %constant_dynamic-update-slice_fusion.9.refs_2_), channel_id=1, source_target_pairs={{0,1},{1,0},{2,3},{3,2},{4,5},{5,4},{6,7},{7,6},{8,9},{9,8},{10,11... | collective-permute-start | bytes 1966088 | tf_op jit(solution)/shard_map/ppermute | solution.py:1055
  43.2 34.9 %collective-permute-start.10 = (bf16[384,3072]{1,0:T(8,128)(2,1)}, bf16[384,3072]{1,0:T(8,128)(2,1)S(1)}, u32[]{:S(2)}, u32[]{:S(2)}) collective-permute-start(bf16[384,3072]{1,0:T(8,128)(2,1)} %get-tuple-element.199.refs_2_), channel_id=1, source_target_pairs={{0,1},{1,0},{2,3},{3,2},{4,5},{5,4},{6,7},{7,6},{8,9},{9,8},{10,11... | collective-permute-start | bytes 7077896 | tf_op jit(solution)/shard_map/ppermute | solution.py:1055
  48.8 8.1 %collective-permute-start.5 = (bf16[128,512]{1,0:T(8,128)(2,1)}, bf16[128,512]{1,0:T(8,128)(2,1)S(1)}, u32[]{:S(2)}, u32[]{:S(2)}) collective-permute-start(bf16[128,512]{1,0:T(8,128)(2,1)} %get-tuple-element.192.refs_0_), channel_id=1, source_target_pairs={{0,4},{1,5},{2,6},{3,7},{4,0},{5,1},{6,2},{7,3},{8,12},{9,13},{10,... | collective-permute-start | bytes 393224 | tf_op jit(solution)/shard_map/ppermute | solution.py:1055
  52.0 6.4 %collective-permute-start.3 = (bf16[128,512]{1,0:T(8,128)(2,1)}, bf16[128,512]{1,0:T(8,128)(2,1)S(1)}, u32[]{:S(2)}, u32[]{:S(2)}) collective-permute-start(bf16[128,512]{1,0:T(8,128)(2,1)} %get-tuple-element.192.refs_0_), channel_id=1, source_target_pairs={{0,2},{1,3},{2,0},{3,1},{4,6},{5,7},{6,4},{7,5},{8,10},{9,11},{10,... | collective-permute-start | bytes 393224 | tf_op jit(solution)/shard_map/ppermute | solution.py:1055
  52.6 6.0 %collective-permute-start.2 = (bf16[128,512]{1,0:T(8,128)(2,1)}, bf16[128,512]{1,0:T(8,128)(2,1)S(1)}, u32[]{:S(2)}, u32[]{:S(2)}) collective-permute-start(bf16[128,512]{1,0:T(8,128)(2,1)} %get-tuple-element.192.refs_0_), channel_id=1, source_target_pairs={{0,1},{1,0},{2,3},{3,2},{4,5},{5,4},{6,7},{7,6},{8,9},{9,8},{10,11... | collective-permute-start | bytes 393224 | tf_op jit(solution)/shard_map/ppermute | solution.py:1055
  87.5 7.3 %collective-permute-start.12 = (bf16[256,512]{1,0:T(8,128)(2,1)S(1)}, bf16[256,512]{1,0:T(8,128)(2,1)S(1)}, u32[]{:S(2)}, u32[]{:S(2)}) collective-permute-start(bf16[256,512]{1,0:T(8,128)(2,1)S(1)} %slice.265), channel_id=1, source_target_pairs={{0,1},{1,2},{2,3},{3,4},{4,5},{5,6},{6,7},{8,9},{9,10},{10,11},{11... | collective-permute-start | bytes 786440 | tf_op jit(solution)/shard_map/ppermute | solution.py:1061
  89.8 16.2 %collective-permute-start.13 = (bf16[128,5120]{1,0:T(8,128)(2,1)}, bf16[128,5120]{1,0:T(8,128)(2,1)S(1)}, u32[]{:S(2)}, u32[]{:S(2)}) collective-permute-start(bf16[128,5120]{1,0:T(8,128)(2,1)} %get-tuple-element.211.refs_2_), channel_id=1, source_target_pairs={{0,1},{1,0},{2,3},{3,2},{4,5},{5,4},{6,7},{7,6},{8,9},{9,8},{10,11... | collective-permute-start | bytes 3932168 | tf_op jit(solution)/shard_map/ppermute | solution.py:1055
  114.2 10.1 %collective-permute-start.14 = (bf16[384,3072]{1,0:T(8,128)(2,1)}, bf16[384,3072]{1,0:T(8,128)(2,1)}, u32[]{:S(2)}, u32[]{:S(2)}) collective-permute-start(bf16[384,3072]{1,0:T(8,128)(2,1)} %get-tuple-element.220.refs_2_), channel_id=1, source_target_pairs={{0,1},{1,0},{2,3},{3,2},{4,5},{5,4},{6,7},{7,6},{8,9},{9,8},{10,11... | collective-permute-start | bytes 7077896 | tf_op jit(solution)/shard_map/ppermute | solution.py:1055
  114.4 9.9 %collective-permute-start.15 = (bf16[640,512]{1,0:T(8,128)(2,1)S(1)}, bf16[640,512]{1,0:T(8,128)(2,1)S(1)}, u32[]{:S(2)}, u32[]{:S(2)}) collective-permute-start(bf16[640,512]{1,0:T(8,128)(2,1)S(1)} %constant_dynamic-update-slice_fusion.11.refs_6_), channel_id=1, source_target_pairs={{0,1},{1,0},{2,3},{3,2},{4,5},{5,4},{6,7},{7,6},{8,9},{9,8},{10,11... | collective-permute-start | bytes 1966088 | tf_op jit(solution)/shard_map/ppermute | solution.py:1055
  193.2 6.0 %collective-permute-start.23 = (bf16[384,256]{1,0:T(8,128)(2,1)S(1)}, bf16[384,256]{1,0:T(8,128)(2,1)S(1)}, u32[]{:S(2)}, u32[]{:S(2)}) collective-permute-start(bf16[384,256]{1,0:T(8,128)(2,1)S(1)} %copy-done.58), channel_id=1, source_target_pairs={{0,1},{1,0},{2,3},{3,2},{4,5},{5,4},{6,7},{7,6},{8,9},{9,8},{10,11... | collective-permute-start | bytes 589832 | tf_op jit(solution)/shard_map/ppermute | solution.py:1055
  193.7 28.4 %collective-permute-start.28 = (bf16[1152,1024]{1,0:T(8,128)(2,1)}, bf16[1152,1024]{1,0:T(8,128)(2,1)}, u32[]{:S(2)}, u32[]{:S(2)}) collective-permute-start(bf16[1152,1024]{1,0:T(8,128)(2,1)} %get-tuple-element.238.refs_3_), channel_id=1, source_target_pairs={{0,1},{1,0},{2,3},{3,2},{4,5},{5,4},{6,7},{7,6},{8,9},{9,8},{10,11... | collective-permute-start | bytes 7077896 | tf_op jit(solution)/shard_map/ppermute | solution.py:1055
  196.3 8.1 %collective-permute-start.20 = (bf16[2,128,256]{2,1,0:T(8,128)(2,1)S(1)}, bf16[2,128,256]{2,1,0:T(8,128)(2,1)S(1)}, u32[]{:S(2)}, u32[]{:S(2)}) collective-permute-start(bf16[2,128,256]{2,1,0:T(8,128)(2,1)S(1)} %pad_maximum_fusion.9), channel_id=1, source_target_pairs={{0,2},{1,3},{2,0},{3,1},{4,6},{5,7},{6,4},{7,5},{8,10},{9,11},{10,... | collective-permute-start | bytes 393224 | tf_op jit(solution)/shard_map/ppermute | solution.py:1055
  218.6 77.0 %all-reduce.2.cloned.1.call-start = ((), (), s32[]{:S(2)}) async-start(), calls=%async_computation.2 | async-start | bytes 1703936 | tf_op jit(solution)/shard_map/psum | solution.py:1729
  218.7 30.7 %collective-permute-start.29 = (bf16[2,128,1536]{2,1,0:T(8,128)(2,1)}, bf16[2,128,1536]{2,1,0:T(8,128)(2,1)}, u32[]{:S(2)}, u32[]{:S(2)}) collective-permute-start(bf16[2,128,1536]{2,1,0:T(8,128)(2,1)} %get-tuple-element.268), channel_id=1, source_target_pairs={{0,2},{1,3},{2,0},{3,1},{4,6},{5,7},{6,4},{7,5},{8,10},{9,11},{10,... | collective-permute-start | bytes 2359304 | tf_op jit(solution)/shard_map/ppermute | solution.py:1055
  218.9 30.5 %collective-permute-start.30 = (bf16[2,128,1536]{2,1,0:T(8,128)(2,1)}, bf16[2,128,1536]{2,1,0:T(8,128)(2,1)}, u32[]{:S(2)}, u32[]{:S(2)}) collective-permute-start(bf16[2,128,1536]{2,1,0:T(8,128)(2,1)} %get-tuple-element.270), channel_id=1, source_target_pairs={{0,4},{1,5},{2,6},{3,7},{4,0},{5,1},{6,2},{7,3},{8,12},{9,13},{10,... | collective-permute-start | bytes 2359304 | tf_op jit(solution)/shard_map/ppermute | solution.py:1055
  220.9 12.5 %collective-permute-start.26 = (f32[16,512]{1,0:T(8,128)}, f32[16,512]{1,0:T(8,128)S(1)}, u32[]{:S(2)}, u32[]{:S(2)}) collective-permute-start(f32[16,512]{1,0:T(8,128)} %get-tuple-element.254), channel_id=1, source_target_pairs={{1,0},{2,1},{3,2},{4,3},{5,4},{6,5},{7,6},{9,8},{10,9},{11,10},{12... | collective-permute-start | bytes 98312 | tf_op jit(solution)/shard_map/ppermute | solution.py:1061
  233.4 16.4 %collective-permute-start.31 = (bf16[2,128,896]{2,1,0:T(8,128)(2,1)}, bf16[2,128,896]{2,1,0:T(8,128)(2,1)S(1)}, u32[]{:S(2)}, u32[]{:S(2)}) collective-permute-start(bf16[2,128,896]{2,1,0:T(8,128)(2,1)} %get-tuple-element.272), channel_id=1, source_target_pairs={{0,2},{1,3},{2,0},{3,1},{4,6},{5,7},{6,4},{7,5},{8,10},{9,11},{10,... | collective-permute-start | bytes 1376264 | tf_op jit(solution)/shard_map/ppermute | solution.py:1055
  238.9 13.5 %collective-permute-start.32 = (bf16[2,128,896]{2,1,0:T(8,128)(2,1)}, bf16[2,128,896]{2,1,0:T(8,128)(2,1)S(1)}, u32[]{:S(2)}, u32[]{:S(2)}) collective-permute-start(bf16[2,128,896]{2,1,0:T(8,128)(2,1)} %get-tuple-element.274), channel_id=1, source_target_pairs={{0,4},{1,5},{2,6},{3,7},{4,0},{5,1},{6,2},{7,3},{8,12},{9,13},{10,... | collective-permute-start | bytes 1376264 | tf_op jit(solution)/shard_map/ppermute | solution.py:1055
  248.5 27.1 %collective-permute-start.35 = (bf16[384,1536]{1,0:T(8,128)(2,1)}, bf16[384,1536]{1,0:T(8,128)(2,1)S(1)}, u32[]{:S(2)}, u32[]{:S(2)}) collective-permute-start(bf16[384,1536]{1,0:T(8,128)(2,1)} %get-tuple-element.290), channel_id=1, source_target_pairs={{0,1},{1,0},{2,3},{3,2},{4,5},{5,4},{6,7},{7,6},{8,9},{9,8},{10,11... | collective-permute-start | bytes 3538952 | tf_op jit(solution)/shard_map/ppermute | solution.py:1055
  255.9 17.7 %collective-permute-start.36 = (bf16[128,2432]{1,0:T(8,128)(2,1)S(1)}, bf16[128,2432]{1,0:T(8,128)(2,1)S(1)}, u32[]{:S(2)}, u32[]{:S(2)}) collective-permute-start(bf16[128,2432]{1,0:T(8,128)(2,1)S(1)} %pad_maximum_fusion.4), channel_id=1, source_target_pairs={{0,2},{1,3},{2,0},{3,1},{4,6},{5,7},{6,4},{7,5},{8,10},{9,11},{10,... | collective-permute-start | bytes 1867784 | tf_op jit(solution)/shard_map/ppermute | solution.py:1055
  256.0 17.6 %collective-permute-start.37 = (bf16[128,2432]{1,0:T(8,128)(2,1)S(1)}, bf16[128,2432]{1,0:T(8,128)(2,1)S(1)}, u32[]{:S(2)}, u32[]{:S(2)}) collective-permute-start(bf16[128,2432]{1,0:T(8,128)(2,1)S(1)} %pad_maximum_fusion.2), channel_id=1, source_target_pairs={{0,4},{1,5},{2,6},{3,7},{4,0},{5,1},{6,2},{7,3},{8,12},{9,13},{10,... | collective-permute-start | bytes 1867784 | tf_op jit(solution)/shard_map/ppermute | solution.py:1055
  271.1 24.4 %collective-permute-start.33 = (bf16[256,512]{1,0:T(8,128)(2,1)}, bf16[256,512]{1,0:T(8,128)(2,1)}, u32[]{:S(2)}, u32[]{:S(2)}) collective-permute-start(bf16[256,512]{1,0:T(8,128)(2,1)} %get-tuple-element.287), channel_id=1, source_target_pairs={{1,0},{2,1},{3,2},{4,3},{5,4},{6,5},{7,6},{9,8},{10,9},{11,10},{12... | collective-permute-start | bytes 786440 | tf_op jit(solution)/shard_map/ppermute | solution.py:1061
  272.4 18.8 %collective-permute-start.34 = (bf16[640,1024]{1,0:T(8,128)(2,1)}, bf16[640,1024]{1,0:T(8,128)(2,1)S(1)}, u32[]{:S(2)}, u32[]{:S(2)}) collective-permute-start(bf16[640,1024]{1,0:T(8,128)(2,1)} %get-tuple-element.286.refs_2_), channel_id=1, source_target_pairs={{0,1},{1,0},{2,3},{3,2},{4,5},{5,4},{6,7},{7,6},{8,9},{9,8},{10,11... | collective-permute-start | bytes 3932168 | tf_op jit(solution)/shard_map/ppermute | solution.py:1055
  274.0 16.0 %collective-permute-start.38 = (bf16[128,2432]{1,0:T(8,128)(2,1)S(1)}, bf16[128,2432]{1,0:T(8,128)(2,1)S(1)}, u32[]{:S(2)}, u32[]{:S(2)}) collective-permute-start(bf16[128,2432]{1,0:T(8,128)(2,1)S(1)} %broadcast_select_fusion.4), channel_id=1, source_target_pairs={{0,8},{8,0},{16,24},{24,16},{1,9},{9,1},{17,25},{25,17},{2,10},{10... | collective-permute-start | bytes 1867784 | tf_op jit(solution)/shard_map/ppermute | solution.py:1055
  281.3 28.0 %collective-permute-start.40 = (bf16[2,128,1152]{2,1,0:T(8,128)(2,1)}, bf16[2,128,1152]{2,1,0:T(8,128)(2,1)S(1)}, u32[]{:S(2)}, u32[]{:S(2)}) collective-permute-start(bf16[2,128,1152]{2,1,0:T(8,128)(2,1)} %get-tuple-element.308), channel_id=1, source_target_pairs={{0,2},{1,3},{2,0},{3,1},{4,6},{5,7},{6,4},{7,5},{8,10},{9,11},{10,... | collective-permute-start | bytes 1769480 | tf_op jit(solution)/shard_map/ppermute | solution.py:1055
  282.6 26.7 %collective-permute-start.41 = (bf16[2,128,1152]{2,1,0:T(8,128)(2,1)}, bf16[2,128,1152]{2,1,0:T(8,128)(2,1)S(1)}, u32[]{:S(2)}, u32[]{:S(2)}) collective-permute-start(bf16[2,128,1152]{2,1,0:T(8,128)(2,1)} %get-tuple-element.310), channel_id=1, source_target_pairs={{0,4},{1,5},{2,6},{3,7},{4,0},{5,1},{6,2},{7,3},{8,12},{9,13},{10,... | collective-permute-start | bytes 1769480 | tf_op jit(solution)/shard_map/ppermute | solution.py:1055
  302.7 30.7 %collective-permute-start.48 = (bf16[128,2432]{1,0:T(8,128)(2,1)S(1)}, bf16[128,2432]{1,0:T(8,128)(2,1)S(1)}, u32[]{:S(2)}, u32[]{:S(2)}) collective-permute-start(bf16[128,2432]{1,0:T(8,128)(2,1)S(1)} %copy-done.24), channel_id=1, source_target_pairs={{0,16},{8,24},{16,0},{24,8},{1,17},{9,25},{17,1},{25,9},{2,18},{10... | collective-permute-start | bytes 1867784 | tf_op jit(solution)/shard_map/ppermute | solution.py:1055
  305.1 12.1 %collective-permute-start.43 = (bf16[2,128,512]{2,1,0:T(8,128)(2,1)}, bf16[2,128,512]{2,1,0:T(8,128)(2,1)S(1)}, u32[]{:S(2)}, u32[]{:S(2)}) collective-permute-start(bf16[2,128,512]{2,1,0:T(8,128)(2,1)} %get-tuple-element.312), channel_id=1, source_target_pairs={{0,2},{1,3},{2,0},{3,1},{4,6},{5,7},{6,4},{7,5},{8,10},{9,11},{10,... | collective-permute-start | bytes 786440 | tf_op jit(solution)/shard_map/ppermute | solution.py:1055
  306.9 10.4 %collective-permute-start.44 = (bf16[2,128,512]{2,1,0:T(8,128)(2,1)}, bf16[2,128,512]{2,1,0:T(8,128)(2,1)S(1)}, u32[]{:S(2)}, u32[]{:S(2)}) collective-permute-start(bf16[2,128,512]{2,1,0:T(8,128)(2,1)} %get-tuple-element.314), channel_id=1, source_target_pairs={{0,4},{1,5},{2,6},{3,7},{4,0},{5,1},{6,2},{7,3},{8,12},{9,13},{10,... | collective-permute-start | bytes 786440 | tf_op jit(solution)/shard_map/ppermute | solution.py:1055
  309.3 6.2 %collective-permute-start.42 = (f32[40,512]{1,0:T(8,128)S(1)}, f32[40,512]{1,0:T(8,128)S(1)}, u32[]{:S(2)}, u32[]{:S(2)}) collective-permute-start(f32[40,512]{1,0:T(8,128)S(1)} %add.178), channel_id=1, source_target_pairs={{0,2},{1,3},{2,0},{3,1},{4,6},{5,7},{6,4},{7,5},{8,10},{9,11},{10,... | collective-permute-start | bytes 245768 | tf_op jit(solution)/shard_map/ppermute | solution.py:1055
  309.6 15.1 %collective-permute-start.46 = (bf16[128,1152]{1,0:T(8,128)(2,1)S(1)}, bf16[128,1152]{1,0:T(8,128)(2,1)S(1)}, u32[]{:S(2)}, u32[]{:S(2)}) collective-permute-start(bf16[128,1152]{1,0:T(8,128)(2,1)S(1)} %get-tuple-element.364), channel_id=1, source_target_pairs={{0,4},{1,5},{2,6},{3,7},{4,0},{5,1},{6,2},{7,3},{8,12},{9,13},{10,... | collective-permute-start | bytes 884744 | tf_op jit(solution)/shard_map/ppermute | solution.py:1055
  315.5 9.2 %collective-permute-start.47 = (bf16[128,1152]{1,0:T(8,128)(2,1)S(1)}, bf16[128,1152]{1,0:T(8,128)(2,1)S(1)}, u32[]{:S(2)}, u32[]{:S(2)}) collective-permute-start(bf16[128,1152]{1,0:T(8,128)(2,1)S(1)} %get-tuple-element.362), channel_id=1, source_target_pairs={{0,2},{1,3},{2,0},{3,1},{4,6},{5,7},{6,4},{7,5},{8,10},{9,11},{10,... | collective-permute-start | bytes 884744 | tf_op jit(solution)/shard_map/ppermute | solution.py:1055
  317.3 7.4 %collective-permute-start.45 = (f32[40,512]{1,0:T(8,128)S(1)}, f32[40,512]{1,0:T(8,128)S(1)}, u32[]{:S(2)}, u32[]{:S(2)}) collective-permute-start(f32[40,512]{1,0:T(8,128)S(1)} %add.179), channel_id=1, source_target_pairs={{0,4},{1,5},{2,6},{3,7},{4,0},{5,1},{6,2},{7,3},{8,12},{9,13},{10,... | collective-permute-start | bytes 245768 | tf_op jit(solution)/shard_map/ppermute | solution.py:1055
  319.8 15.1 %collective-permute-start.54 = (bf16[128,512]{1,0:T(8,128)(2,1)S(1)}, bf16[128,512]{1,0:T(8,128)(2,1)S(1)}, u32[]{:S(2)}, u32[]{:S(2)}) collective-permute-start(bf16[128,512]{1,0:T(8,128)(2,1)S(1)} %get-tuple-element.380), channel_id=1, source_target_pairs={{0,4},{1,5},{2,6},{3,7},{4,0},{5,1},{6,2},{7,3},{8,12},{9,13},{10,... | collective-permute-start | bytes 393224 | tf_op jit(solution)/shard_map/ppermute | solution.py:1055
  324.7 10.2 %collective-permute-start.55 = (bf16[128,512]{1,0:T(8,128)(2,1)S(1)}, bf16[128,512]{1,0:T(8,128)(2,1)S(1)}, u32[]{:S(2)}, u32[]{:S(2)}) collective-permute-start(bf16[128,512]{1,0:T(8,128)(2,1)S(1)} %get-tuple-element.378), channel_id=1, source_target_pairs={{0,2},{1,3},{2,0},{3,1},{4,6},{5,7},{6,4},{7,5},{8,10},{9,11},{10,... | collective-permute-start | bytes 393224 | tf_op jit(solution)/shard_map/ppermute | solution.py:1055
  333.6 9.5 %collective-permute-start.50 = (bf16[128,1152]{1,0:T(8,128)(2,1)S(1)}, bf16[128,1152]{1,0:T(8,128)(2,1)S(1)}, u32[]{:S(2)}, u32[]{:S(2)}) collective-permute-start(bf16[128,1152]{1,0:T(8,128)(2,1)S(1)} %get-tuple-element.360), channel_id=1, source_target_pairs={{0,8},{8,0},{16,24},{24,16},{1,9},{9,1},{17,25},{25,17},{2,10},{10... | collective-permute-start | bytes 884744 | tf_op jit(solution)/shard_map/ppermute | solution.py:1055
  334.9 53.6 %collective-permute-start.53 = (bf16[64,3328]{1,0:T(8,128)(2,1)S(1)}, bf16[64,3328]{1,0:T(8,128)(2,1)S(1)}, u32[]{:S(2)}, u32[]{:S(2)}) collective-permute-start(bf16[64,3328]{1,0:T(8,128)(2,1)S(1)} %get-tuple-element.370), channel_id=1, source_target_pairs={{0,1},{1,0},{2,3},{3,2},{4,5},{5,4},{6,7},{7,6},{8,9},{9,8},{10,11... | collective-permute-start | bytes 1277960 | tf_op jit(solution)/shard_map/ppermute | solution.py:1055
  334.9 12.9 %collective-permute-start.49 = (f32[40,512]{1,0:T(8,128)S(1)}, f32[40,512]{1,0:T(8,128)S(1)}, u32[]{:S(2)}, u32[]{:S(2)}) collective-permute-start(f32[40,512]{1,0:T(8,128)S(1)} %add.180), channel_id=1, source_target_pairs={{0,8},{8,0},{16,24},{24,16},{1,9},{9,1},{17,25},{25,17},{2,10},{10... | collective-permute-start | bytes 245768 | tf_op jit(solution)/shard_map/ppermute | solution.py:1055
  343.2 14.8 %collective-permute-start.51 = (bf16[128,1152]{1,0:T(8,128)(2,1)S(1)}, bf16[128,1152]{1,0:T(8,128)(2,1)S(1)}, u32[]{:S(2)}, u32[]{:S(2)}) collective-permute-start(bf16[128,1152]{1,0:T(8,128)(2,1)S(1)} %add_convert_fusion.10), channel_id=1, source_target_pairs={{0,16},{8,24},{16,0},{24,8},{1,17},{9,25},{17,1},{25,9},{2,18},{10... | collective-permute-start | bytes 884744 | tf_op jit(solution)/shard_map/ppermute | solution.py:1055
  345.6 28.4 %collective-permute-start.57 = (bf16[128,2432]{1,0:T(8,128)(2,1)S(1)}, bf16[128,2432]{1,0:T(8,128)(2,1)S(1)}, u32[]{:S(2)}, u32[]{:S(2)}) collective-permute-start(bf16[128,2432]{1,0:T(8,128)(2,1)S(1)} %add_convert_fusion), channel_id=1, source_target_pairs={{0,8},{8,0},{16,24},{24,16},{1,9},{9,1},{17,25},{25,17},{2,10},{10... | collective-permute-start | bytes 1867784 | tf_op jit(solution)/shard_map/ppermute | solution.py:1055
  347.8 26.2 %collective-permute-start.56 = (bf16[128,512]{1,0:T(8,128)(2,1)S(1)}, bf16[128,512]{1,0:T(8,128)(2,1)S(1)}, u32[]{:S(2)}, u32[]{:S(2)}) collective-permute-start(bf16[128,512]{1,0:T(8,128)(2,1)S(1)} %get-tuple-element.376), channel_id=1, source_target_pairs={{0,8},{8,0},{16,24},{24,16},{1,9},{9,1},{17,25},{25,17},{2,10},{10... | collective-permute-start | bytes 393224 | tf_op jit(solution)/shard_map/ppermute | solution.py:1055
  358.0 17.5 %collective-permute-start.52 = (f32[40,512]{1,0:T(8,128)S(1)}, f32[40,512]{1,0:T(8,128)S(1)}, u32[]{:S(2)}, u32[]{:S(2)}) collective-permute-start(f32[40,512]{1,0:T(8,128)S(1)} %add.185), channel_id=1, source_target_pairs={{0,16},{8,24},{16,0},{24,8},{1,17},{9,25},{17,1},{25,9},{2,18},{10... | collective-permute-start | bytes 245768 | tf_op jit(solution)/shard_map/ppermute | solution.py:1055
  358.1 23.4 %collective-permute-start.59 = (bf16[128,1152]{1,0:T(8,128)(2,1)S(1)}, bf16[128,1152]{1,0:T(8,128)(2,1)S(1)}, u32[]{:S(2)}, u32[]{:S(2)}) collective-permute-start(bf16[128,1152]{1,0:T(8,128)(2,1)S(1)} %add_convert_fusion.9), channel_id=1, source_target_pairs={{0,8},{8,0},{16,24},{24,16},{1,9},{9,1},{17,25},{25,17},{2,10},{10... | collective-permute-start | bytes 884744 | tf_op jit(solution)/shard_map/ppermute | solution.py:1055
  374.0 6.9 %collective-permute-start.61 = (bf16[128,512]{1,0:T(8,128)(2,1)S(1)}, bf16[128,512]{1,0:T(8,128)(2,1)S(1)}, u32[]{:S(2)}, u32[]{:S(2)}) collective-permute-start(bf16[128,512]{1,0:T(8,128)(2,1)S(1)} %add_convert_fusion.22), channel_id=1, source_target_pairs={{0,16},{8,24},{16,0},{24,8},{1,17},{9,25},{17,1},{25,9},{2,18},{10... | collective-permute-start | bytes 393224 | tf_op jit(solution)/shard_map/ppermute | solution.py:1055
  375.5 13.1 %collective-permute-start.58 = (bf16[64,4864]{1,0:T(8,128)(2,1)S(1)}, bf16[64,4864]{1,0:T(8,128)(2,1)S(1)}, u32[]{:S(2)}, u32[]{:S(2)}) collective-permute-start(bf16[64,4864]{1,0:T(8,128)(2,1)S(1)} %get-tuple-element.356), channel_id=1, source_target_pairs={{0,1},{1,0},{2,3},{3,2},{4,5},{5,4},{6,7},{7,6},{8,9},{9,8},{10,11... | collective-permute-start | bytes 1867784 | tf_op jit(solution)/shard_map/ppermute | solution.py:1055
  382.3 6.2 %collective-permute-start.60 = (bf16[64,2304]{1,0:T(8,128)(2,1)S(1)}, bf16[64,2304]{1,0:T(8,128)(2,1)S(1)}, u32[]{:S(2)}, u32[]{:S(2)}) collective-permute-start(bf16[64,2304]{1,0:T(8,128)(2,1)S(1)} %get-tuple-element.372), channel_id=1, source_target_pairs={{0,1},{1,0},{2,3},{3,2},{4,5},{5,4},{6,7},{7,6},{8,9},{9,8},{10,11... | collective-permute-start | bytes 884744 | tf_op jit(solution)/shard_map/ppermute | solution.py:1055
  (81 other events, 530.7 us)
Sparse Core Ops, SparseCore 0:
  154.4 47.0 reduce-scatter.1
  222.3 48.0 all-reduce.1

commit v4 on v3

--- a/solution.py
+++ b/solution.py
@@ -972,7 +972,7 @@
 
 def lasting(micros):
     return pl.CostEstimate(
-        flops=int(micros * 1e9), bytes_accessed=int(micros * 3e6), transcendentals=0
+        flops=int(micros * 4e9), bytes_accessed=int(micros * 1.2e7), transcendentals=0
     )
 
 

time: 409 us -> 405 us (level)
  local copies, waits for them, and re-layouts: 27.4 us -> 32.3 us
  starting transfers between devices: 69.5 us -> 64.7 us
    ppermute x58, starting transfers between devices: 56.2 us -> 50.9 us  [crossed(): lax.ppermute(block, axis, [(index, index ^ bit) for index in range(count)])]
    unnamed x140 -> x158, local copies, waits for them, and re-layouts: 19.2 us -> 23.5 us
  transfers between devices with their start and end apart: 66 -> 66, of which waited for: 21 -> 20; matrix products, arithmetic and copies ran while one was open for 6% -> 6% of each run, Pallas kernels for 34% -> 37%
where the time goes in v4:
time: 405 us; the launch traced here: 399 us
  Pallas kernels  193 us (48%)
  waiting for transfers between devices  76.4 us (19%)
  starting transfers between devices  64.7 us (16%)
  local copies, waits for them, and re-layouts  32.3 us (8%)
  other arithmetic  16.5 us (4%)
  between operations  15.9 us (4%)
    pallas_call x14, Pallas kernels, whole(): pl.pallas_call(run, in_specs=[SMEM] * scalar_count + [HBM] * (flat_count...  86.3 us
    pallas_call x6, Pallas kernels, attention_call(): pl.pallas_call(run, grid=(HEADS // 2,), in_specs=[SMEM] * len(scalars) +...  77.8 us
    ppermute x58, waiting for transfers between devices, crossed(): lax.ppermute(block, axis, [(index, index ^ bit) for index in range(count)])  76.2 us
    ppermute x58, starting transfers between devices, crossed(): lax.ppermute(block, axis, [(index, index ^ bit) for index in range(count)])  50.9 us
    pallas_call x5, Pallas kernels, pair_gradients(): pl.pallas_call(kernel, in_specs=[SMEM] + [ANY] * count + [HBM] * len(foll...  28.6 us
    unnamed x158, local copies, waits for them, and re-layouts  23.5 us
    ppermute x6, starting transfers between devices, passed_along(): return lax.ppermute(block, axis, route)  13.7 us
  transfers between devices with their start and end apart: 66, of which 20 were waited for; matrix products, arithmetic and copies ran while one was open for 6% of the time, Pallas kernels for 37%

profile of v4, /device:TPU:0, one launch (start us, length us, event | category | flops | bytes accessed | tf_op | source)
XLA Modules:
  0.0 398.5 jit_solution(17546730941108842550)
XLA Ops:
  8.2 2.4 collective-permute-start
  13.8 4.1 %shard_map.288 = (bf16[384,512]{1,0:T(8,128)(2,1)}, bf16[384,512]{1,0:T(8,128)(2,1)}, bf16[384,512]{1,0:T(8,128)(2,1)}, bf16[384,512]{1,0:T(8,128)(2,1)}, bf16[3...) custom-call(bf16[384,512]{1,0:T(8,128)(2,1)} %bitcast.97, bf16[3,2,512]{2,1,0:T(2,128)(2,1)} %refs_6_.21, ...), custom_call_target="tpu_custom_call" | custom-call | flops 16000000000 | bytes 48000000 | tf_op jit(solution)/shard_map/pallas_call | solution.py:1037
  18.9 10.7 %shard_map.289 = (bf16[384,512]{1,0:T(8,128)(2,1)}, bf16[256,512]{1,0:T(8,128)(2,1)}, bf16[2,256,512]{2,1,0:T(8,128)(2,1)}, bf16[8,3,128,384]{3,2,1,0:T(8,128)(2,1)}) custom-call(s32[9]{0:T(128)S(1)} %get-tuple-element.414.refs_0_, bf16[384,512]{1,0:T(8,128)(2,1)} %get-tuple-element.184.refs_1_, bf16[384,512]{1,0:T(8,128)(2,1)} %get-tuple-element.185.refs_2_, ...), custom_call_target="tpu_custom_call" | custom-call | flops 44000002048 | bytes 132000000 | tf_op jit(solution)/shard_map/pallas_call | solution.py:489
  30.7 7.1 %shard_map.290 = (f32[384,512]{1,0:T(8,128)}, bf16[384,2048]{1,0:T(8,128)(2,1)}, bf16[384,3072]{1,0:T(8,128)(2,1)}, f32[384,512]{1,0:T(8,128)}, f32[1,512]{1,0:T(1,128)}, /*index=5*/bf16[16,512]{1,0:T(8,128)(2,1)}) custom-call(bf16[384,512]{1,0:T(8,128)(2,1)} %get-tuple-element.189.refs_0_, bf16[384,512]{1,0:T(8,128)(2,1)} %bitcast.98, ...), custom_call_target="tpu_custom_call" | custom-call | flops 28000000000 | bytes 84000000 | tf_op jit(solution)/shard_map/pallas_call | solution.py:1037
  37.8 4.7 %collective-permute-start.1 = (bf16[16,512]{1,0:T(8,128)(2,1)}, bf16[16,512]{1,0:T(8,128)(2,1)S(1)}, u32[]{:S(2)}, u32[]{:S(2)}) collective-permute-start(bf16[16,512]{1,0:T(8,128)(2,1)} %get-tuple-element.191), channel_id=1, source_target_pairs={{0,1},{1,2},{2,3},{3,4},{4,5},{5,6},{6,7},{8,9},{9,10},{10,11},{11... | collective-permute-start | bytes 49160 | tf_op jit(solution)/shard_map/ppermute | solution.py:1061
  43.9 4.3 %shard_map.291 = (bf16[128,512]{1,0:T(8,128)(2,1)}, f32[128,512]{1,0:T(8,128)}, bf16[128,1536]{1,0:T(8,128)(2,1)}) custom-call(s32[9]{0:T(128)S(1)} %get-tuple-element.414.refs_0_, f32[384,512]{1,0:T(8,128)} %get-tuple-element.190.refs_1_.refs_3_, bf16[16,512]{1,0:T(8,128)(2,1)} %copy-done.69, bf16[3,2,512]{2,1,0:T(2,128)(2,1)} %refs_6_.21, ...), custom_call_target="tpu_custom_call" | custom-call | flops 16000000000 | bytes 48000000 | tf_op jit(solution)/shard_map/pallas_call | solution.py:1037
  48.2 3.2 collective-permute-start.5
  52.0 4.2 %shard_map.292 = (bf16[128,512]{1,0:T(8,128)(2,1)}, bf16[128,512]{1,0:T(8,128)(2,1)}, bf16[1152,512]{1,0:T(8,128)(2,1)}, bf16[1152,512]{1,0:T(8,128)(2,1)}) custom-call(bf16[128,512]{1,0:T(8,128)(2,1)} %get-tuple-element.192.refs_0_, bf16[3,2,512]{2,1,0:T(2,128)(2,1)} %refs_6_.21, bf16[3,2,512]{2,1,0:T(2,128)(2,1)} %refs_7_.19, bf16[3,2,512]{2,1,0:T(2,128)(2,1)} %refs_8_.13, ...), custom_call_target="tpu_custom_call" | custom-call | flops 16000000000 | bytes 48000000 | tf_op jit(solution)/shard_map/pallas_call | solution.py:1037
  58.3 2.6 collective-permute-done.8
  64.6 12.8 %shard_map.293 = (bf16[128,512]{1,0:T(8,128)(2,1)}, bf16[1024,512]{1,0:T(8,128)(2,1)}, bf16[1024,512]{1,0:T(8,128)(2,1)}, bf16[8,128,1024]{2,1,0:T(8,128)(2,1)}) custom-call(s32[9]{0:T(128)S(1)} %get-tuple-element.413.refs_0_, s32[9]{0:T(128)S(1)} %pad_add_fusion.2.refs_1_.refs_0_, bf16[128,512]{1,0:T(8,128)(2,1)} %get-tuple-element.193.refs_2_, ...), custom_call_target="tpu_custom_call" | custom-call | flops 51999997952 | bytes 156000000 | tf_op jit(solution)/shard_map/pallas_call | solution.py:489
  79.0 6.8 %shard_map.294 = (f32[128,512]{1,0:T(8,128)}, bf16[128,2048]{1,0:T(8,128)(2,1)}, bf16[128,5120]{1,0:T(8,128)(2,1)}, bf16[384,512]{1,0:T(8,128)(2,1)}, f32[384,512]{1,0:T(8,128)}, /*index=5*/f32[1,512]{1,0:T(1,128)}) custom-call(bf16[128,512]{1,0:T(8,128)(2,1)} %get-tuple-element.196.refs_0_, f32[128,512]{1,0:T(8,128)} %get-tuple-element.197.refs_1_.refs_5_, ...), custom_call_target="tpu_custom_call" | custom-call | flops 28000000000 | bytes 84000000 | tf_op jit(solution)/shard_map/pallas_call | solution.py:1037
  86.8 2.3 collective-permute-start.12
  89.8 4.3 %shard_map.295 = (bf16[384,512]{1,0:T(8,128)(2,1)}, bf16[384,512]{1,0:T(8,128)(2,1)}, bf16[384,512]{1,0:T(8,128)(2,1)}, bf16[384,512]{1,0:T(8,128)(2,1)}, bf16[384,512]{1,0:T(8,128)(2,1)}) custom-call(bf16[384,512]{1,0:T(8,128)(2,1)} %get-tuple-element.202.refs_0_, bf16[3,2,512]{2,1,0:T(2,128)(2,1)} %refs_6_.21, bf16[3,2,512]{2,1,0:T(2,128)(2,1)} %refs_7_.19, ...), custom_call_target="tpu_custom_call" | custom-call | flops 16000000000 | bytes 48000000 | tf_op jit(solution)/shard_map/pallas_call | solution.py:1037
  94.7 10.6 %shard_map.296 = (bf16[384,512]{1,0:T(8,128)(2,1)}, bf16[256,512]{1,0:T(8,128)(2,1)}, bf16[2,256,512]{2,1,0:T(8,128)(2,1)}, bf16[8,3,128,384]{3,2,1,0:T(8,128)(2,1)}) custom-call(s32[9]{0:T(128)S(1)} %get-tuple-element.414.refs_0_, bf16[384,512]{1,0:T(8,128)(2,1)} %get-tuple-element.204.refs_1_, bf16[384,512]{1,0:T(8,128)(2,1)} %get-tuple-element.205.refs_2_, ...), custom_call_target="tpu_custom_call" | custom-call | flops 44000002048 | bytes 132000000 | tf_op jit(solution)/shard_map/pallas_call | solution.py:489
  107.5 7.0 %shard_map.297 = (f32[384,512]{1,0:T(8,128)}, bf16[384,2048]{1,0:T(8,128)(2,1)}, bf16[384,3072]{1,0:T(8,128)(2,1)}, bf16[384,512]{1,0:T(8,128)(2,1)}, f32[1,512]{1,0:T(1,128)}, /*index=5*/bf16[16,512]{1,0:T(8,128)(2,1)}) custom-call(bf16[384,512]{1,0:T(8,128)(2,1)} %get-tuple-element.209.refs_0_, f32[384,512]{1,0:T(8,128)} %get-tuple-element.210.refs_1_.refs_4_, ...), custom_call_target="tpu_custom_call" | custom-call | flops 28000000000 | bytes 84000000 | tf_op jit(solution)/shard_map/pallas_call | solution.py:1037
  115.1 8.9 %shard_map.298 = (f32[384,512]{1,0:T(8,128)}, bf16[384,512]{1,0:T(8,128)(2,1)}, bf16[384,1536]{1,0:T(8,128)(2,1)}, bf16[384,1536]{1,0:T(8,128)(2,1)}, f32[8,512]{1,0:T(8,128)}) custom-call(s32[2]{0:T(128)S(1)} %pad_add_fusion.3.refs_0_.place.refs_1_, bf16[384,512]{1,0:T(8,128)(2,1)} %bitcast.144, bf16[384,2048]{1,0:T(8,128)(2,1)} %get-tuple-element.217.refs_2_, ...), custom_call_target="tpu_custom_call" | custom-call | flops 32000000000 | bytes 96000000 | tf_op jit(solution)/shard_map/pallas_call | solution.py:1037
  125.6 14.1 %shard_map.299 = (f32[2,512]{1,0:T(2,128)}, bf16[256,512]{1,0:T(8,128)(2,1)}, bf16[640,1024]{1,0:T(8,128)(2,1)}, bf16[640,1024]{1,0:T(8,128)(2,1)}) custom-call(s32[2]{0:T(128)S(1)} %pad_add_fusion.3.refs_0_.place.refs_1_, bf16[384,512]{1,0:T(8,128)(2,1)} %get-tuple-element.204.refs_1_, bf16[384,512]{1,0:T(8,128)(2,1)} %get-tuple-element.205.refs_2_, ...), custom_call_target="tpu_custom_call" | custom-call | flops 51999997952 | bytes 156000000 | tf_op jit(solution)/shard_map/pallas_call | solution.py:489
  142.0 2.8 collective-permute-done.17.refs_1_
  149.0 8.0 %shard_map.300.refs_15_ = bf16[4,128,3328]{2,1,0:T(8,128)(2,1)} custom-call(s32[2]{0:T(128)S(1)} %pad_add_fusion.3.refs_0_.place.refs_1_, bf16[384,1536]{1,0:T(8,128)(2,1)S(1)} %copy-done.25, bf16[384,1536]{1,0:T(8,128)(2,1)S(1)} %collective-permute-done.17.refs_1_, bf16[384,3072]{1,0:T(8,128)(2,1)S(1)} %copy-done.9, bf16[384,3072]{1,0:T(8,128)(2,1)S(1)} %copy-done.11, ...), custom_call_target="tpu_custom_call" | custom-call | flops 28000000000 | bytes 84000000 | tf_op jit(solution)/shard_map/pallas_call | solution.py:1264
  157.7 6.7 %shard_map.301 = (f32[384,512]{1,0:T(8,128)}, f32[128,512]{1,0:T(8,128)}, bf16[384,256]{1,0:T(8,128)(2,1)}, bf16[384,256]{1,0:T(8,128)(2,1)}, f32[8,512]{1,0:T(8,128)}) custom-call(s32[2]{0:T(128)S(1)} %pad_add_fusion.3.refs_0_.place.refs_1_, bf16[640,1024]{1,0:T(8,128)(2,1)} %get-tuple-element.222.refs_4_.refs_1_, ...), custom_call_target="tpu_custom_call" | custom-call | flops 24000000000 | bytes 72000000 | tf_op jit(solution)/shard_map/pallas_call | solution.py:1037
  164.3 7.0 %shard_map.302 = (f32[128,512]{1,0:T(8,128)}, bf16[128,512]{1,0:T(8,128)(2,1)}, bf16[128,1536]{1,0:T(8,128)(2,1)}, bf16[128,1536]{1,0:T(8,128)(2,1)}, f32[8,512]{1,0:T(8,128)}) custom-call(s32[2]{0:T(128)S(1)} %pad_add_fusion.3.refs_0_.place.refs_1_, f32[128,512]{1,0:T(8,128)} %get-tuple-element.233.refs_1_, bf16[128,2048]{1,0:T(8,128)(2,1)} %get-tuple-element.234.refs_2_, ...), custom_call_target="tpu_custom_call" | custom-call | flops 32000000000 | bytes 96000000 | tf_op jit(solution)/shard_map/pallas_call | solution.py:1037
  171.4 15.6 %shard_map.303 = (f32[2,512]{1,0:T(2,128)}, bf16[512,512]{1,0:T(8,128)(2,1)}, bf16[512,512]{1,0:T(8,128)(2,1)}, bf16[1152,1024]{1,0:T(8,128)(2,1)}, bf16[1152,1024]{1,0:T(8,128)(2,1)}) custom-call(s32[9]{0:T(128)S(1)} %pad_add_fusion.2.refs_1_.refs_0_, s32[2]{0:T(128)S(1)} %pad_add_fusion.3.refs_0_.place.refs_1_, ...), custom_call_target="tpu_custom_call" | custom-call | flops 51999997952 | bytes 156000000 | tf_op jit(solution)/shard_map/pallas_call | solution.py:489
  192.8 5.1 %shard_map.304 = (bf16[2,128,1536]{2,1,0:T(8,128)(2,1)}, bf16[2,128,1536]{2,1,0:T(8,128)(2,1)}, bf16[2,128,1536]{2,1,0:T(8,128)(2,1)}, bf16[2,128,1536]{2,1,0:T(8,128)(2,1)}) custom-call(s32[2]{0:T(128)S(1)} %pad_add_fusion.3.refs_0_.place.refs_1_, bf16[128,1536]{1,0:T(8,128)(2,1)S(1)} %copy-done.29, bf16[128,1536]{1,0:T(8,128)(2,1)S(1)} %collective-permute-done.22.refs_1_, ...), custom_call_target="tpu_custom_call" | custom-call | flops 28000000000 | bytes 84000000 | tf_op jit(solution)/shard_map/pallas_call | solution.py:1264
  203.9 2.5 collective-permute-done.24
  208.4 5.2 %shard_map.305 = (f32[384,512]{1,0:T(8,128)}, f32[16,512]{1,0:T(8,128)}, bf16[128,256]{1,0:T(8,128)(2,1)}, bf16[128,256]{1,0:T(8,128)(2,1)}, f32[8,512]{1,0:T(8,128)}) custom-call(s32[9]{0:T(128)S(1)} %copy-done.5, s32[2]{0:T(128)S(1)} %pad_add_fusion.3.refs_0_.place.refs_1_, bf16[1152,1024]{1,0:T(8,128)(2,1)} %get-tuple-element.237.refs_2_.refs_4_, ...), custom_call_target="tpu_custom_call" | custom-call | flops 20000000000 | bytes 60000000 | tf_op jit(solution)/shard_map/pallas_call | solution.py:1037
  224.7 5.5 %shard_map.306 = (bf16[2,128,896]{2,1,0:T(8,128)(2,1)}, bf16[2,128,896]{2,1,0:T(8,128)(2,1)}, bf16[2,128,896]{2,1,0:T(8,128)(2,1)}, bf16[2,128,896]{2,1,0:T(8,128)(2,1)}) custom-call(s32[2]{0:T(128)S(1)} %pad_add_fusion.3.refs_0_.place.refs_1_, bf16[128,256]{1,0:T(8,128)(2,1)S(1)} %copy-done.31, bf16[128,256]{1,0:T(8,128)(2,1)S(1)} %collective-permute-done.27.refs_1_, ...), custom_call_target="tpu_custom_call" | custom-call | flops 28000000000 | bytes 84000000 | tf_op jit(solution)/shard_map/pallas_call | solution.py:1264
  230.2 3.7 collective-permute-start.31
  235.2 9.3 %shard_map.307 = (f32[384,512]{1,0:T(8,128)}, bf16[384,512]{1,0:T(8,128)(2,1)}, bf16[384,1536]{1,0:T(8,128)(2,1)}, bf16[384,1536]{1,0:T(8,128)(2,1)}, f32[8,512]{1,0:T(8,128)}) custom-call(s32[2]{0:T(128)S(1)} %pad_add_fusion.3.refs_0_.place.refs_1_, f32[384,512]{1,0:T(8,128)} %get-tuple-element.229.refs_1_, f32[384,512]{1,0:T(8,128)} %get-tuple-element.253.refs_2_, ...), custom_call_target="tpu_custom_call" | custom-call | flops 32000000000 | bytes 96000000 | tf_op jit(solution)/shard_map/pallas_call | solution.py:1037
  244.9 2.3 collective-permute-done.32
  248.5 1.9 fusion.2
  252.2 14.0 %shard_map.308 = (f32[2,512]{1,0:T(2,128)}, bf16[256,512]{1,0:T(8,128)(2,1)}, bf16[640,1024]{1,0:T(8,128)(2,1)}, bf16[640,1024]{1,0:T(8,128)(2,1)}) custom-call(s32[2]{0:T(128)S(1)} %pad_add_fusion.3.refs_0_.place.refs_1_, bf16[384,512]{1,0:T(8,128)(2,1)} %get-tuple-element.184.refs_1_, bf16[384,512]{1,0:T(8,128)(2,1)} %get-tuple-element.185.refs_2_, ...), custom_call_target="tpu_custom_call" | custom-call | flops 51999997952 | bytes 156000000 | tf_op jit(solution)/shard_map/pallas_call | solution.py:489
  270.6 5.8 %shard_map.309 = (bf16[2,128,1152]{2,1,0:T(8,128)(2,1)}, bf16[2,128,1152]{2,1,0:T(8,128)(2,1)}, bf16[2,128,1152]{2,1,0:T(8,128)(2,1)}, bf16[2,128,1152]{2,1,0:T(8,128)(2,1)}) custom-call(s32[2]{0:T(128)S(1)} %pad_add_fusion.3.refs_0_.place.refs_1_, bf16[384,1536]{1,0:T(8,128)(2,1)S(1)} %copy-done.28, bf16[384,1536]{1,0:T(8,128)(2,1)S(1)} %collective-permute-done.35.refs_1_, ...), custom_call_target="tpu_custom_call" | custom-call | flops 28000000000 | bytes 84000000 | tf_op jit(solution)/shard_map/pallas_call | solution.py:1264
  279.0 6.0 %collective-permute-done.38 = bf16[128,2432]{1,0:T(8,128)(2,1)S(1)} collective-permute-done((bf16[128,2432]{1,0:T(8,128)(2,1)S(1)}, bf16[128,2432]{1,0:T(8,128)(2,1)S(1)}, u32[]{:S(2)}, u32[]{:S(2)}) %collective-permute-start.38) | collective-permute-done | bytes 622624 | tf_op jit(solution)/shard_map/ppermute | solution.py:1055
  286.3 4.3 %shard_map.310 = (bf16[2,128,512]{2,1,0:T(8,128)(2,1)}, bf16[2,128,512]{2,1,0:T(8,128)(2,1)}, bf16[2,128,512]{2,1,0:T(8,128)(2,1)}, bf16[2,128,512]{2,1,0:T(8,128)(2,1)}) custom-call(s32[2]{0:T(128)S(1)} %pad_add_fusion.3.refs_0_.place.refs_1_, bf16[640,1024]{1,0:T(8,128)(2,1)S(1)} %copy-done.23, bf16[640,1024]{1,0:T(8,128)(2,1)S(1)} %collective-permute-done.34.refs_1_, ...), custom_call_target="tpu_custom_call" | custom-call | flops 28000000000 | bytes 84000000 | tf_op jit(solution)/shard_map/pallas_call | solution.py:1264
  291.4 5.7 %shard_map.311 = (bf16[384,512]{1,0:T(8,128)(2,1)}, f32[8,512]{1,0:T(8,128)}) custom-call(s32[2]{0:T(128)S(1)} %pad_add_fusion.3.refs_0_.place.refs_1_, bf16[640,1024]{1,0:T(8,128)(2,1)} %get-tuple-element.285.refs_0_.refs_1_, bf16[640,1024]{1,0:T(8,128)(2,1)} %get-tuple-element.286.refs_2_, bf16[256,512]{1,0:T(8,128)(2,1)} %copy-done.63, ...), custom_call_target="tpu_custom_call" | custom-call | flops 20000000000 | bytes 60000000 | tf_op jit(solution)/shard_map/pallas_call | solution.py:1037
  298.4 2.7 collective-permute-start.48
  305.7 5.8 %collective-permute-done.42 = f32[40,512]{1,0:T(8,128)S(1)} collective-permute-done((f32[40,512]{1,0:T(8,128)S(1)}, f32[40,512]{1,0:T(8,128)S(1)}, u32[]{:S(2)}, u32[]{:S(2)}) %collective-permute-start.42) | collective-permute-done | bytes 81952 | tf_op jit(solution)/shard_map/ppermute | solution.py:1055
  315.4 4.8 %collective-permute-done.45 = f32[40,512]{1,0:T(8,128)S(1)} collective-permute-done((f32[40,512]{1,0:T(8,128)S(1)}, f32[40,512]{1,0:T(8,128)S(1)}, u32[]{:S(2)}, u32[]{:S(2)}) %collective-permute-start.45) | collective-permute-done | bytes 81952 | tf_op jit(solution)/shard_map/ppermute | solution.py:1055
  320.7 8.4 %collective-permute-done.48 = bf16[128,2432]{1,0:T(8,128)(2,1)S(1)} collective-permute-done((bf16[128,2432]{1,0:T(8,128)(2,1)S(1)}, bf16[128,2432]{1,0:T(8,128)(2,1)S(1)}, u32[]{:S(2)}, u32[]{:S(2)}) %collective-permute-start.48) | collective-permute-done | bytes 622624 | tf_op jit(solution)/shard_map/ppermute | solution.py:1055
  332.3 6.5 %collective-permute-done.50 = bf16[128,1152]{1,0:T(8,128)(2,1)S(1)} collective-permute-done((bf16[128,1152]{1,0:T(8,128)(2,1)S(1)}, bf16[128,1152]{1,0:T(8,128)(2,1)S(1)}, u32[]{:S(2)}, u32[]{:S(2)}) %collective-permute-start.50) | collective-permute-done | bytes 294944 | tf_op jit(solution)/shard_map/ppermute | solution.py:1055
  338.8 2.6 collective-permute-start.51
  341.6 2.1 collective-permute-start.57
  343.9 10.1 %collective-permute-done.51 = bf16[128,1152]{1,0:T(8,128)(2,1)S(1)} collective-permute-done((bf16[128,1152]{1,0:T(8,128)(2,1)S(1)}, bf16[128,1152]{1,0:T(8,128)(2,1)S(1)}, u32[]{:S(2)}, u32[]{:S(2)}) %collective-permute-start.51) | collective-permute-done | bytes 294944 | tf_op jit(solution)/shard_map/ppermute | solution.py:1055
  354.1 4.1 %collective-permute-start.59 = (bf16[128,1152]{1,0:T(8,128)(2,1)S(1)}, bf16[128,1152]{1,0:T(8,128)(2,1)S(1)}, u32[]{:S(2)}, u32[]{:S(2)}) collective-permute-start(bf16[128,1152]{1,0:T(8,128)(2,1)S(1)} %add_convert_fusion.9), channel_id=1, source_target_pairs={{0,8},{8,0},{16,24},{24,16},{1,9},{9,1},{17,25},{25,17},{2,10},{10... | collective-permute-start | bytes 884744 | tf_op jit(solution)/shard_map/ppermute | solution.py:1055
  358.2 11.7 %collective-permute-done.56 = bf16[128,512]{1,0:T(8,128)(2,1)S(1)} collective-permute-done((bf16[128,512]{1,0:T(8,128)(2,1)S(1)}, bf16[128,512]{1,0:T(8,128)(2,1)S(1)}, u32[]{:S(2)}, u32[]{:S(2)}) %collective-permute-start.56) | collective-permute-done | bytes 131104 | tf_op jit(solution)/shard_map/ppermute | solution.py:1055
  374.7 2.2 collective-permute-done.61
  378.6 3.4 collective-permute-done.62
  385.7 5.5 %shard_map.312 = (f32[3,64,2048]{2,1,0:T(8,128)}, f32[3,64,512]{2,1,0:T(8,128)}, f32[3,64,2048]{2,1,0:T(8,128)}, f32[3,256,512]{2,1,0:T(8,128)}, f32[192,512]{1,0:T(8,128)}, /*index=5*/f32[64,1536]{1,0:T(8,128)}) custom-call(s32[2]{0:T(128)S(1)} %pad_add_fusion.3.refs_0_.place.refs_1_, bf16[64,3328]{1,0:T(8,128)(2,1)} %get-tuple-element.371.refs_1_, ...), custom_call_target="tpu_custom_call" | custom-call | flops 12000000000 | bytes 36000000 | tf_op jit(solution)/shard_map/pallas_call | solution.py:1037
  (342 shorter events, 90.9 us)
Async XLA Ops:
  7.2 201.2 %reduce-scatter.2.cloned.1.call-start = ((), (), s32[]{:S(2)}) async-start(), calls=%async_computation.1 | async-start | bytes 4259840 | tf_op jit(solution)/shard_map/reduce_scatter | solution.py:1725
  8.2 10.0 %collective-permute-start = (bf16[256,512]{1,0:T(8,128)(2,1)S(1)}, bf16[256,512]{1,0:T(8,128)(2,1)S(1)}, u32[]{:S(2)}, u32[]{:S(2)}) collective-permute-start(bf16[256,512]{1,0:T(8,128)(2,1)S(1)} %slice_bitcast_fusion), channel_id=1, source_target_pairs={{0,1},{1,2},{2,3},{3,4},{4,5},{5,6},{6,7},{8,9},{9,10},{10,11},{11... | collective-permute-start | bytes 786440 | tf_op jit(solution)/shard_map/ppermute | solution.py:1061
  42.5 34.9 %collective-permute-start.11 = (bf16[640,512]{1,0:T(8,128)(2,1)S(1)}, bf16[640,512]{1,0:T(8,128)(2,1)S(1)}, u32[]{:S(2)}, u32[]{:S(2)}) collective-permute-start(bf16[640,512]{1,0:T(8,128)(2,1)S(1)} %constant_dynamic-update-slice_fusion.9.refs_2_), channel_id=1, source_target_pairs={{0,1},{1,0},{2,3},{3,2},{4,5},{5,4},{6,7},{7,6},{8,9},{9,8},{10,11... | collective-permute-start | bytes 1966088 | tf_op jit(solution)/shard_map/ppermute | solution.py:1055
  42.6 34.8 %collective-permute-start.10 = (bf16[384,3072]{1,0:T(8,128)(2,1)}, bf16[384,3072]{1,0:T(8,128)(2,1)S(1)}, u32[]{:S(2)}, u32[]{:S(2)}) collective-permute-start(bf16[384,3072]{1,0:T(8,128)(2,1)} %get-tuple-element.199.refs_2_), channel_id=1, source_target_pairs={{0,1},{1,0},{2,3},{3,2},{4,5},{5,4},{6,7},{7,6},{8,9},{9,8},{10,11... | collective-permute-start | bytes 7077896 | tf_op jit(solution)/shard_map/ppermute | solution.py:1055
  48.2 8.1 %collective-permute-start.5 = (bf16[128,512]{1,0:T(8,128)(2,1)}, bf16[128,512]{1,0:T(8,128)(2,1)S(1)}, u32[]{:S(2)}, u32[]{:S(2)}) collective-permute-start(bf16[128,512]{1,0:T(8,128)(2,1)} %get-tuple-element.192.refs_0_), channel_id=1, source_target_pairs={{0,4},{1,5},{2,6},{3,7},{4,0},{5,1},{6,2},{7,3},{8,12},{9,13},{10,... | collective-permute-start | bytes 393224 | tf_op jit(solution)/shard_map/ppermute | solution.py:1055
  51.5 6.4 %collective-permute-start.3 = (bf16[128,512]{1,0:T(8,128)(2,1)}, bf16[128,512]{1,0:T(8,128)(2,1)S(1)}, u32[]{:S(2)}, u32[]{:S(2)}) collective-permute-start(bf16[128,512]{1,0:T(8,128)(2,1)} %get-tuple-element.192.refs_0_), channel_id=1, source_target_pairs={{0,2},{1,3},{2,0},{3,1},{4,6},{5,7},{6,4},{7,5},{8,10},{9,11},{10,... | collective-permute-start | bytes 393224 | tf_op jit(solution)/shard_map/ppermute | solution.py:1055
  86.8 7.2 %collective-permute-start.12 = (bf16[256,512]{1,0:T(8,128)(2,1)S(1)}, bf16[256,512]{1,0:T(8,128)(2,1)S(1)}, u32[]{:S(2)}, u32[]{:S(2)}) collective-permute-start(bf16[256,512]{1,0:T(8,128)(2,1)S(1)} %slice.265), channel_id=1, source_target_pairs={{0,1},{1,2},{2,3},{3,4},{4,5},{5,6},{6,7},{8,9},{9,10},{10,11},{11... | collective-permute-start | bytes 786440 | tf_op jit(solution)/shard_map/ppermute | solution.py:1061
  89.1 17.3 %collective-permute-start.13 = (bf16[128,5120]{1,0:T(8,128)(2,1)}, bf16[128,5120]{1,0:T(8,128)(2,1)S(1)}, u32[]{:S(2)}, u32[]{:S(2)}) collective-permute-start(bf16[128,5120]{1,0:T(8,128)(2,1)} %get-tuple-element.211.refs_2_), channel_id=1, source_target_pairs={{0,1},{1,0},{2,3},{3,2},{4,5},{5,4},{6,7},{7,6},{8,9},{9,8},{10,11... | collective-permute-start | bytes 3932168 | tf_op jit(solution)/shard_map/ppermute | solution.py:1055
  106.3 17.7 %collective-permute-start.15 = (bf16[640,512]{1,0:T(8,128)(2,1)S(1)}, bf16[640,512]{1,0:T(8,128)(2,1)S(1)}, u32[]{:S(2)}, u32[]{:S(2)}) collective-permute-start(bf16[640,512]{1,0:T(8,128)(2,1)S(1)} %constant_dynamic-update-slice_fusion.11.refs_6_), channel_id=1, source_target_pairs={{0,1},{1,0},{2,3},{3,2},{4,5},{5,4},{6,7},{7,6},{8,9},{9,8},{10,11... | collective-permute-start | bytes 1966088 | tf_op jit(solution)/shard_map/ppermute | solution.py:1055
  114.5 9.5 %collective-permute-start.14 = (bf16[384,3072]{1,0:T(8,128)(2,1)}, bf16[384,3072]{1,0:T(8,128)(2,1)S(1)}, u32[]{:S(2)}, u32[]{:S(2)}) collective-permute-start(bf16[384,3072]{1,0:T(8,128)(2,1)} %get-tuple-element.220.refs_2_), channel_id=1, source_target_pairs={{0,1},{1,0},{2,3},{3,2},{4,5},{5,4},{6,7},{7,6},{8,9},{9,8},{10,11... | collective-permute-start | bytes 7077896 | tf_op jit(solution)/shard_map/ppermute | solution.py:1055
  140.3 16.7 %collective-permute-start.16 = (bf16[256,512]{1,0:T(8,128)(2,1)}, bf16[256,512]{1,0:T(8,128)(2,1)S(1)}, u32[]{:S(2)}, u32[]{:S(2)}) collective-permute-start(bf16[256,512]{1,0:T(8,128)(2,1)} %get-tuple-element.224), channel_id=1, source_target_pairs={{1,0},{2,1},{3,2},{4,3},{5,4},{6,5},{7,6},{9,8},{10,9},{11,10},{12... | collective-permute-start | bytes 786440 | tf_op jit(solution)/shard_map/ppermute | solution.py:1061
  190.5 8.6 %collective-permute-start.20 = (bf16[2,128,256]{2,1,0:T(8,128)(2,1)S(1)}, bf16[2,128,256]{2,1,0:T(8,128)(2,1)S(1)}, u32[]{:S(2)}, u32[]{:S(2)}) collective-permute-start(bf16[2,128,256]{2,1,0:T(8,128)(2,1)S(1)} %pad_maximum_fusion.9), channel_id=1, source_target_pairs={{0,2},{1,3},{2,0},{3,1},{4,6},{5,7},{6,4},{7,5},{8,10},{9,11},{10,... | collective-permute-start | bytes 393224 | tf_op jit(solution)/shard_map/ppermute | solution.py:1055
  191.7 8.7 %collective-permute-start.21 = (bf16[2,128,256]{2,1,0:T(8,128)(2,1)S(1)}, bf16[2,128,256]{2,1,0:T(8,128)(2,1)S(1)}, u32[]{:S(2)}, u32[]{:S(2)}) collective-permute-start(bf16[2,128,256]{2,1,0:T(8,128)(2,1)S(1)} %slice.350), channel_id=1, source_target_pairs={{0,4},{1,5},{2,6},{3,7},{4,0},{5,1},{6,2},{7,3},{8,12},{9,13},{10,... | collective-permute-start | bytes 393224 | tf_op jit(solution)/shard_map/ppermute | solution.py:1055
  203.9 14.4 %collective-permute-start.28 = (bf16[1152,1024]{1,0:T(8,128)(2,1)}, bf16[1152,1024]{1,0:T(8,128)(2,1)S(1)}, u32[]{:S(2)}, u32[]{:S(2)}) collective-permute-start(bf16[1152,1024]{1,0:T(8,128)(2,1)} %get-tuple-element.238.refs_3_), channel_id=1, source_target_pairs={{0,1},{1,0},{2,3},{3,2},{4,5},{5,4},{6,7},{7,6},{8,9},{9,8},{10,11... | collective-permute-start | bytes 7077896 | tf_op jit(solution)/shard_map/ppermute | solution.py:1055
  213.7 76.9 %all-reduce.2.cloned.1.call-start = ((), (), s32[]{:S(2)}) async-start(), calls=%async_computation.2 | async-start | bytes 1703936 | tf_op jit(solution)/shard_map/psum | solution.py:1729
  213.8 31.1 %collective-permute-start.29 = (bf16[2,128,1536]{2,1,0:T(8,128)(2,1)}, bf16[2,128,1536]{2,1,0:T(8,128)(2,1)}, u32[]{:S(2)}, u32[]{:S(2)}) collective-permute-start(bf16[2,128,1536]{2,1,0:T(8,128)(2,1)} %get-tuple-element.268), channel_id=1, source_target_pairs={{0,2},{1,3},{2,0},{3,1},{4,6},{5,7},{6,4},{7,5},{8,10},{9,11},{10,... | collective-permute-start | bytes 2359304 | tf_op jit(solution)/shard_map/ppermute | solution.py:1055
  215.3 29.6 %collective-permute-start.30 = (bf16[2,128,1536]{2,1,0:T(8,128)(2,1)}, bf16[2,128,1536]{2,1,0:T(8,128)(2,1)}, u32[]{:S(2)}, u32[]{:S(2)}) collective-permute-start(bf16[2,128,1536]{2,1,0:T(8,128)(2,1)} %get-tuple-element.270), channel_id=1, source_target_pairs={{0,4},{1,5},{2,6},{3,7},{4,0},{5,1},{6,2},{7,3},{8,12},{9,13},{10,... | collective-permute-start | bytes 2359304 | tf_op jit(solution)/shard_map/ppermute | solution.py:1055
  216.9 13.3 %collective-permute-start.26 = (f32[16,512]{1,0:T(8,128)}, f32[16,512]{1,0:T(8,128)S(1)}, u32[]{:S(2)}, u32[]{:S(2)}) collective-permute-start(f32[16,512]{1,0:T(8,128)} %get-tuple-element.254), channel_id=1, source_target_pairs={{1,0},{2,1},{3,2},{4,3},{5,4},{6,5},{7,6},{9,8},{10,9},{11,10},{12... | collective-permute-start | bytes 98312 | tf_op jit(solution)/shard_map/ppermute | solution.py:1061
  230.2 14.6 %collective-permute-start.31 = (bf16[2,128,896]{2,1,0:T(8,128)(2,1)}, bf16[2,128,896]{2,1,0:T(8,128)(2,1)S(1)}, u32[]{:S(2)}, u32[]{:S(2)}) collective-permute-start(bf16[2,128,896]{2,1,0:T(8,128)(2,1)} %get-tuple-element.272), channel_id=1, source_target_pairs={{0,2},{1,3},{2,0},{3,1},{4,6},{5,7},{6,4},{7,5},{8,10},{9,11},{10,... | collective-permute-start | bytes 1376264 | tf_op jit(solution)/shard_map/ppermute | solution.py:1055
  234.0 13.2 %collective-permute-start.32 = (bf16[2,128,896]{2,1,0:T(8,128)(2,1)}, bf16[2,128,896]{2,1,0:T(8,128)(2,1)S(1)}, u32[]{:S(2)}, u32[]{:S(2)}) collective-permute-start(bf16[2,128,896]{2,1,0:T(8,128)(2,1)} %get-tuple-element.274), channel_id=1, source_target_pairs={{0,4},{1,5},{2,6},{3,7},{4,0},{5,1},{6,2},{7,3},{8,12},{9,13},{10,... | collective-permute-start | bytes 1376264 | tf_op jit(solution)/shard_map/ppermute | solution.py:1055
  244.5 26.2 %collective-permute-start.35 = (bf16[384,1536]{1,0:T(8,128)(2,1)}, bf16[384,1536]{1,0:T(8,128)(2,1)S(1)}, u32[]{:S(2)}, u32[]{:S(2)}) collective-permute-start(bf16[384,1536]{1,0:T(8,128)(2,1)} %get-tuple-element.290), channel_id=1, source_target_pairs={{0,1},{1,0},{2,3},{3,2},{4,5},{5,4},{6,7},{7,6},{8,9},{9,8},{10,11... | collective-permute-start | bytes 3538952 | tf_op jit(solution)/shard_map/ppermute | solution.py:1055
  250.6 18.1 %collective-permute-start.36 = (bf16[128,2432]{1,0:T(8,128)(2,1)S(1)}, bf16[128,2432]{1,0:T(8,128)(2,1)S(1)}, u32[]{:S(2)}, u32[]{:S(2)}) collective-permute-start(bf16[128,2432]{1,0:T(8,128)(2,1)S(1)} %pad_maximum_fusion.4), channel_id=1, source_target_pairs={{0,2},{1,3},{2,0},{3,1},{4,6},{5,7},{6,4},{7,5},{8,10},{9,11},{10,... | collective-permute-start | bytes 1867784 | tf_op jit(solution)/shard_map/ppermute | solution.py:1055
  250.7 18.0 %collective-permute-start.37 = (bf16[128,2432]{1,0:T(8,128)(2,1)S(1)}, bf16[128,2432]{1,0:T(8,128)(2,1)S(1)}, u32[]{:S(2)}, u32[]{:S(2)}) collective-permute-start(bf16[128,2432]{1,0:T(8,128)(2,1)S(1)} %pad_maximum_fusion.2), channel_id=1, source_target_pairs={{0,4},{1,5},{2,6},{3,7},{4,0},{5,1},{6,2},{7,3},{8,12},{9,13},{10,... | collective-permute-start | bytes 1867784 | tf_op jit(solution)/shard_map/ppermute | solution.py:1055
  266.2 24.4 %collective-permute-start.33 = (bf16[256,512]{1,0:T(8,128)(2,1)}, bf16[256,512]{1,0:T(8,128)(2,1)S(1)}, u32[]{:S(2)}, u32[]{:S(2)}) collective-permute-start(bf16[256,512]{1,0:T(8,128)(2,1)} %get-tuple-element.287), channel_id=1, source_target_pairs={{1,0},{2,1},{3,2},{4,3},{5,4},{6,5},{7,6},{9,8},{10,9},{11,10},{12... | collective-permute-start | bytes 786440 | tf_op jit(solution)/shard_map/ppermute | solution.py:1061
  267.5 18.8 %collective-permute-start.34 = (bf16[640,1024]{1,0:T(8,128)(2,1)}, bf16[640,1024]{1,0:T(8,128)(2,1)S(1)}, u32[]{:S(2)}, u32[]{:S(2)}) collective-permute-start(bf16[640,1024]{1,0:T(8,128)(2,1)} %get-tuple-element.286.refs_2_), channel_id=1, source_target_pairs={{0,1},{1,0},{2,3},{3,2},{4,5},{5,4},{6,7},{7,6},{8,9},{9,8},{10,11... | collective-permute-start | bytes 3932168 | tf_op jit(solution)/shard_map/ppermute | solution.py:1055
  269.0 16.0 %collective-permute-start.38 = (bf16[128,2432]{1,0:T(8,128)(2,1)S(1)}, bf16[128,2432]{1,0:T(8,128)(2,1)S(1)}, u32[]{:S(2)}, u32[]{:S(2)}) collective-permute-start(bf16[128,2432]{1,0:T(8,128)(2,1)S(1)} %broadcast_select_fusion.4), channel_id=1, source_target_pairs={{0,8},{8,0},{16,24},{24,16},{1,9},{9,1},{17,25},{25,17},{2,10},{10... | collective-permute-start | bytes 1867784 | tf_op jit(solution)/shard_map/ppermute | solution.py:1055
  276.4 27.2 %collective-permute-start.40 = (bf16[2,128,1152]{2,1,0:T(8,128)(2,1)}, bf16[2,128,1152]{2,1,0:T(8,128)(2,1)S(1)}, u32[]{:S(2)}, u32[]{:S(2)}) collective-permute-start(bf16[2,128,1152]{2,1,0:T(8,128)(2,1)} %get-tuple-element.308), channel_id=1, source_target_pairs={{0,2},{1,3},{2,0},{3,1},{4,6},{5,7},{6,4},{7,5},{8,10},{9,11},{10,... | collective-permute-start | bytes 1769480 | tf_op jit(solution)/shard_map/ppermute | solution.py:1055
  278.3 25.4 %collective-permute-start.41 = (bf16[2,128,1152]{2,1,0:T(8,128)(2,1)}, bf16[2,128,1152]{2,1,0:T(8,128)(2,1)S(1)}, u32[]{:S(2)}, u32[]{:S(2)}) collective-permute-start(bf16[2,128,1152]{2,1,0:T(8,128)(2,1)} %get-tuple-element.310), channel_id=1, source_target_pairs={{0,4},{1,5},{2,6},{3,7},{4,0},{5,1},{6,2},{7,3},{8,12},{9,13},{10,... | collective-permute-start | bytes 1769480 | tf_op jit(solution)/shard_map/ppermute | solution.py:1055
  298.4 30.7 %collective-permute-start.48 = (bf16[128,2432]{1,0:T(8,128)(2,1)S(1)}, bf16[128,2432]{1,0:T(8,128)(2,1)S(1)}, u32[]{:S(2)}, u32[]{:S(2)}) collective-permute-start(bf16[128,2432]{1,0:T(8,128)(2,1)S(1)} %copy-done.32), channel_id=1, source_target_pairs={{0,16},{8,24},{16,0},{24,8},{1,17},{9,25},{17,1},{25,9},{2,18},{10... | collective-permute-start | bytes 1867784 | tf_op jit(solution)/shard_map/ppermute | solution.py:1055
  301.1 11.9 %collective-permute-start.43 = (bf16[2,128,512]{2,1,0:T(8,128)(2,1)}, bf16[2,128,512]{2,1,0:T(8,128)(2,1)S(1)}, u32[]{:S(2)}, u32[]{:S(2)}) collective-permute-start(bf16[2,128,512]{2,1,0:T(8,128)(2,1)} %get-tuple-element.312), channel_id=1, source_target_pairs={{0,2},{1,3},{2,0},{3,1},{4,6},{5,7},{6,4},{7,5},{8,10},{9,11},{10,... | collective-permute-start | bytes 786440 | tf_op jit(solution)/shard_map/ppermute | solution.py:1055
  302.7 10.4 %collective-permute-start.44 = (bf16[2,128,512]{2,1,0:T(8,128)(2,1)}, bf16[2,128,512]{2,1,0:T(8,128)(2,1)S(1)}, u32[]{:S(2)}, u32[]{:S(2)}) collective-permute-start(bf16[2,128,512]{2,1,0:T(8,128)(2,1)} %get-tuple-element.314), channel_id=1, source_target_pairs={{0,4},{1,5},{2,6},{3,7},{4,0},{5,1},{6,2},{7,3},{8,12},{9,13},{10,... | collective-permute-start | bytes 786440 | tf_op jit(solution)/shard_map/ppermute | solution.py:1055
  303.7 7.8 %collective-permute-start.42 = (f32[40,512]{1,0:T(8,128)S(1)}, f32[40,512]{1,0:T(8,128)S(1)}, u32[]{:S(2)}, u32[]{:S(2)}) collective-permute-start(f32[40,512]{1,0:T(8,128)S(1)} %add.178), channel_id=1, source_target_pairs={{0,2},{1,3},{2,0},{3,1},{4,6},{5,7},{6,4},{7,5},{8,10},{9,11},{10,... | collective-permute-start | bytes 245768 | tf_op jit(solution)/shard_map/ppermute | solution.py:1055
  305.3 15.4 %collective-permute-start.46 = (bf16[128,1152]{1,0:T(8,128)(2,1)S(1)}, bf16[128,1152]{1,0:T(8,128)(2,1)S(1)}, u32[]{:S(2)}, u32[]{:S(2)}) collective-permute-start(bf16[128,1152]{1,0:T(8,128)(2,1)S(1)} %get-tuple-element.364), channel_id=1, source_target_pairs={{0,4},{1,5},{2,6},{3,7},{4,0},{5,1},{6,2},{7,3},{8,12},{9,13},{10,... | collective-permute-start | bytes 884744 | tf_op jit(solution)/shard_map/ppermute | solution.py:1055
  311.5 9.2 %collective-permute-start.47 = (bf16[128,1152]{1,0:T(8,128)(2,1)S(1)}, bf16[128,1152]{1,0:T(8,128)(2,1)S(1)}, u32[]{:S(2)}, u32[]{:S(2)}) collective-permute-start(bf16[128,1152]{1,0:T(8,128)(2,1)S(1)} %get-tuple-element.362), channel_id=1, source_target_pairs={{0,2},{1,3},{2,0},{3,1},{4,6},{5,7},{6,4},{7,5},{8,10},{9,11},{10,... | collective-permute-start | bytes 884744 | tf_op jit(solution)/shard_map/ppermute | solution.py:1055
  313.1 7.1 %collective-permute-start.45 = (f32[40,512]{1,0:T(8,128)S(1)}, f32[40,512]{1,0:T(8,128)S(1)}, u32[]{:S(2)}, u32[]{:S(2)}) collective-permute-start(f32[40,512]{1,0:T(8,128)S(1)} %add.179), channel_id=1, source_target_pairs={{0,4},{1,5},{2,6},{3,7},{4,0},{5,1},{6,2},{7,3},{8,12},{9,13},{10,... | collective-permute-start | bytes 245768 | tf_op jit(solution)/shard_map/ppermute | solution.py:1055
  314.1 16.8 %collective-permute-start.54 = (bf16[128,512]{1,0:T(8,128)(2,1)S(1)}, bf16[128,512]{1,0:T(8,128)(2,1)S(1)}, u32[]{:S(2)}, u32[]{:S(2)}) collective-permute-start(bf16[128,512]{1,0:T(8,128)(2,1)S(1)} %get-tuple-element.380), channel_id=1, source_target_pairs={{0,4},{1,5},{2,6},{3,7},{4,0},{5,1},{6,2},{7,3},{8,12},{9,13},{10,... | collective-permute-start | bytes 393224 | tf_op jit(solution)/shard_map/ppermute | solution.py:1055
  320.2 10.8 %collective-permute-start.55 = (bf16[128,512]{1,0:T(8,128)(2,1)S(1)}, bf16[128,512]{1,0:T(8,128)(2,1)S(1)}, u32[]{:S(2)}, u32[]{:S(2)}) collective-permute-start(bf16[128,512]{1,0:T(8,128)(2,1)S(1)} %get-tuple-element.378), channel_id=1, source_target_pairs={{0,2},{1,3},{2,0},{3,1},{4,6},{5,7},{6,4},{7,5},{8,10},{9,11},{10,... | collective-permute-start | bytes 393224 | tf_op jit(solution)/shard_map/ppermute | solution.py:1055
  329.3 9.5 %collective-permute-start.50 = (bf16[128,1152]{1,0:T(8,128)(2,1)S(1)}, bf16[128,1152]{1,0:T(8,128)(2,1)S(1)}, u32[]{:S(2)}, u32[]{:S(2)}) collective-permute-start(bf16[128,1152]{1,0:T(8,128)(2,1)S(1)} %get-tuple-element.360), channel_id=1, source_target_pairs={{0,8},{8,0},{16,24},{24,16},{1,9},{9,1},{17,25},{25,17},{2,10},{10... | collective-permute-start | bytes 884744 | tf_op jit(solution)/shard_map/ppermute | solution.py:1055
  330.9 53.6 %collective-permute-start.53 = (bf16[64,3328]{1,0:T(8,128)(2,1)S(1)}, bf16[64,3328]{1,0:T(8,128)(2,1)S(1)}, u32[]{:S(2)}, u32[]{:S(2)}) collective-permute-start(bf16[64,3328]{1,0:T(8,128)(2,1)S(1)} %get-tuple-element.370), channel_id=1, source_target_pairs={{0,1},{1,0},{2,3},{3,2},{4,5},{5,4},{6,7},{7,6},{8,9},{9,8},{10,11... | collective-permute-start | bytes 1277960 | tf_op jit(solution)/shard_map/ppermute | solution.py:1055
  330.9 12.9 %collective-permute-start.49 = (f32[40,512]{1,0:T(8,128)S(1)}, f32[40,512]{1,0:T(8,128)S(1)}, u32[]{:S(2)}, u32[]{:S(2)}) collective-permute-start(f32[40,512]{1,0:T(8,128)S(1)} %add.180), channel_id=1, source_target_pairs={{0,8},{8,0},{16,24},{24,16},{1,9},{9,1},{17,25},{25,17},{2,10},{10... | collective-permute-start | bytes 245768 | tf_op jit(solution)/shard_map/ppermute | solution.py:1055
  338.8 15.1 %collective-permute-start.51 = (bf16[128,1152]{1,0:T(8,128)(2,1)S(1)}, bf16[128,1152]{1,0:T(8,128)(2,1)S(1)}, u32[]{:S(2)}, u32[]{:S(2)}) collective-permute-start(bf16[128,1152]{1,0:T(8,128)(2,1)S(1)} %add_convert_fusion.10), channel_id=1, source_target_pairs={{0,16},{8,24},{16,0},{24,8},{1,17},{9,25},{17,1},{25,9},{2,18},{10... | collective-permute-start | bytes 884744 | tf_op jit(solution)/shard_map/ppermute | solution.py:1055
  341.6 28.4 %collective-permute-start.57 = (bf16[128,2432]{1,0:T(8,128)(2,1)S(1)}, bf16[128,2432]{1,0:T(8,128)(2,1)S(1)}, u32[]{:S(2)}, u32[]{:S(2)}) collective-permute-start(bf16[128,2432]{1,0:T(8,128)(2,1)S(1)} %add_convert_fusion), channel_id=1, source_target_pairs={{0,8},{8,0},{16,24},{24,16},{1,9},{9,1},{17,25},{25,17},{2,10},{10... | collective-permute-start | bytes 1867784 | tf_op jit(solution)/shard_map/ppermute | solution.py:1055
  343.8 26.2 %collective-permute-start.56 = (bf16[128,512]{1,0:T(8,128)(2,1)S(1)}, bf16[128,512]{1,0:T(8,128)(2,1)S(1)}, u32[]{:S(2)}, u32[]{:S(2)}) collective-permute-start(bf16[128,512]{1,0:T(8,128)(2,1)S(1)} %get-tuple-element.376), channel_id=1, source_target_pairs={{0,8},{8,0},{16,24},{24,16},{1,9},{9,1},{17,25},{25,17},{2,10},{10... | collective-permute-start | bytes 393224 | tf_op jit(solution)/shard_map/ppermute | solution.py:1055
  354.0 17.5 %collective-permute-start.52 = (f32[40,512]{1,0:T(8,128)S(1)}, f32[40,512]{1,0:T(8,128)S(1)}, u32[]{:S(2)}, u32[]{:S(2)}) collective-permute-start(f32[40,512]{1,0:T(8,128)S(1)} %add.185), channel_id=1, source_target_pairs={{0,16},{8,24},{16,0},{24,8},{1,17},{9,25},{17,1},{25,9},{2,18},{10... | collective-permute-start | bytes 245768 | tf_op jit(solution)/shard_map/ppermute | solution.py:1055
  354.1 23.4 %collective-permute-start.59 = (bf16[128,1152]{1,0:T(8,128)(2,1)S(1)}, bf16[128,1152]{1,0:T(8,128)(2,1)S(1)}, u32[]{:S(2)}, u32[]{:S(2)}) collective-permute-start(bf16[128,1152]{1,0:T(8,128)(2,1)S(1)} %add_convert_fusion.9), channel_id=1, source_target_pairs={{0,8},{8,0},{16,24},{24,16},{1,9},{9,1},{17,25},{25,17},{2,10},{10... | collective-permute-start | bytes 884744 | tf_op jit(solution)/shard_map/ppermute | solution.py:1055
  370.0 6.9 %collective-permute-start.61 = (bf16[128,512]{1,0:T(8,128)(2,1)S(1)}, bf16[128,512]{1,0:T(8,128)(2,1)S(1)}, u32[]{:S(2)}, u32[]{:S(2)}) collective-permute-start(bf16[128,512]{1,0:T(8,128)(2,1)S(1)} %add_convert_fusion.22), channel_id=1, source_target_pairs={{0,16},{8,24},{16,0},{24,8},{1,17},{9,25},{17,1},{25,9},{2,18},{10... | collective-permute-start | bytes 393224 | tf_op jit(solution)/shard_map/ppermute | solution.py:1055
  371.5 13.1 %collective-permute-start.58 = (bf16[64,4864]{1,0:T(8,128)(2,1)S(1)}, bf16[64,4864]{1,0:T(8,128)(2,1)S(1)}, u32[]{:S(2)}, u32[]{:S(2)}) collective-permute-start(bf16[64,4864]{1,0:T(8,128)(2,1)S(1)} %get-tuple-element.356), channel_id=1, source_target_pairs={{0,1},{1,0},{2,3},{3,2},{4,5},{5,4},{6,7},{7,6},{8,9},{9,8},{10,11... | collective-permute-start | bytes 1867784 | tf_op jit(solution)/shard_map/ppermute | solution.py:1055
  378.3 6.2 %collective-permute-start.60 = (bf16[64,2304]{1,0:T(8,128)(2,1)S(1)}, bf16[64,2304]{1,0:T(8,128)(2,1)S(1)}, u32[]{:S(2)}, u32[]{:S(2)}) collective-permute-start(bf16[64,2304]{1,0:T(8,128)(2,1)S(1)} %get-tuple-element.372), channel_id=1, source_target_pairs={{0,1},{1,0},{2,3},{3,2},{4,5},{5,4},{6,7},{7,6},{8,9},{9,8},{10,11... | collective-permute-start | bytes 884744 | tf_op jit(solution)/shard_map/ppermute | solution.py:1055
  (90 other events, 624.4 us)
Sparse Core Ops, SparseCore 0:
  157.1 50.5 reduce-scatter.1
  218.4 47.6 all-reduce.1
